TPU v7x, 32 devices: a whole 2x2x4 slice. The times are simulated.
32 devices in a mesh: lat: 4 (over y, x), lon: 8 (over z, core).
Axes of the slice: x: 2, y: 2, z: 4, core: 2. Of those that a mesh axis runs over, the one named last changes fastest.
Arguments:
- sea_heat_deviations: bfloat16 [16, 1024, 3840], P('lat', 'lon'), may hold values from -6 to 6
- missing_date_bitmask: int32 [16, 1024, 256], P('lat', 'lon'), may hold values from 0 to 32704
- ocean_binary_mask: int32 [16, 1024], P('lat', 'lon'), may hold values 0 or 1
- mode_maps: float32 [48, 16, 1024], P(None, 'lat', 'lon'), may hold values from -1 to 1
- mode_series: float32 [48, 3840], P(None, 'lon'), may hold values from -6 to 6
Outputs:
- spatial_out: float32 [48, 16, 1024], P(None, 'lat', 'lon')
- temporal_out: float32 [48, 3840], P(None, 'lon')
Inputs may be any that keep to these rules, and one draw needn't show every extreme that they name: `missing_date_bitmask`: bit b of word w of a cell flags day 15 w + b as missing when it is 1; words run up to 32704.
All inputs are finite; a program needn't handle non-finite values. No bound on the sum of `ocean_binary_mask` on one device may be relied on, other than what follows from the above.
Results may differ from a plain program's by a relative error of at most 0.0003.
Values sent between devices are 32-bit elements; how exact they have to be, the bound alone decides.
No kernel may reach another device: no remote copies, remote signals or barrier semaphores. Data moves between devices by JAX's collectives and lax.ppermute only.
A program may use at most 128 MiB of HBM per device.

v0:
```python
import jax
import jax.numpy as jnp
from jax import lax
from jax.sharding import PartitionSpec as P

STEPS = 4
SWEEPS = 4


KLAT = 0.2
KLON = 0.05
EPS = 1e-06
HIGH = lax.Precision.HIGHEST


def with_halo(x, sides, width):
    for axis, dim in sides:
        count, length = (lax.axis_size(axis), x.shape[dim])
        up = [(i, (i + 1) % count) for i in range(count)]
        down = [(j, i) for i, j in up]
        last = lax.slice_in_dim(x, length - width, length, axis=dim)
        first = lax.slice_in_dim(x, 0, width, axis=dim)
        before = lax.ppermute(last, axis, up)
        after = lax.ppermute(first, axis, down)
        x = jnp.concatenate([before, x, after], axis=dim)
    return x


def latitude_cos(rows, nrows):
    degree = -60.0 + 120.0 * (rows.astype(jnp.float32) + 0.5) / nrows
    return jnp.cos(degree * (jnp.pi / 180.0))


def unpack_days(words):
    shifts = jnp.arange(15, dtype=jnp.int32)
    flags = jnp.right_shift(words[..., None], shifts) & 1
    return flags.reshape(words.shape[:-1] + (words.shape[-1] * 15,))


def solve_pair(gram, right):
    determ = gram[0, 0] * gram[1, 1] - gram[0, 1] * gram[1, 0]
    first = (gram[1, 1] * right[0] - gram[0, 1] * right[1]) / determ
    second = (gram[0, 0] * right[1] - gram[1, 0] * right[0]) / determ
    return jnp.stack([first, second])


def sweep(padded, coast, klon_rows):
    center = padded[:, 1:-1, 1:-1]
    north = coast[:-2, 1:-1] * (padded[:, :-2, 1:-1] - center)
    south = coast[2:, 1:-1] * (padded[:, 2:, 1:-1] - center)
    west = coast[1:-1, :-2] * (padded[:, 1:-1, :-2] - center)
    east = coast[1:-1, 2:] * (padded[:, 1:-1, 2:] - center)
    flux = KLAT * (north + south) + klon_rows[1:-1, None] * (west + east)
    return center + coast[1:-1, 1:-1] * flux


def shards(sea_heat_deviations, missing_date_bitmask, ocean_binary_mask, mode_maps, mode_series):
    polar_coordinate, zonal_coordinate, calendar_dates = sea_heat_deviations.shape
    modes = mode_maps.shape[0]
    nlat = polar_coordinate * lax.axis_size("lat")
    total = modes * nlat * zonal_coordinate * lax.axis_size("lon")
    row_start = lax.axis_index("lat") * polar_coordinate
    cosl = latitude_cos(row_start + jnp.arange(polar_coordinate), nlat)
    weight = jnp.broadcast_to(cosl[:, None], (polar_coordinate, zonal_coordinate)).reshape(-1)
    coast = ocean_binary_mask.astype(jnp.float32)
    coast_flat = coast.reshape(-1)
    depth = 1
    coast_pad = with_halo(coast, (("lat", 0), ("lon", 1)), depth)
    pad_rows = row_start - depth + jnp.arange(polar_coordinate + 2 * depth)
    inside = ((pad_rows >= 0) & (pad_rows < nlat)).astype(jnp.float32)
    coast_pad = coast_pad * inside[:, None]
    pad_cos = latitude_cos(pad_rows, nlat)
    klon_pad = KLON / (pad_cos * pad_cos)
    miss = unpack_days(missing_date_bitmask).reshape(-1, calendar_dates) == 1
    given_deviation = sea_heat_deviations.astype(jnp.float32).reshape(-1, calendar_dates)
    panel = lax.all_gather(mode_series, "lon", axis=1, tiled=True)
    modes_now = mode_maps.reshape(modes, -1)
    recon = jnp.dot(modes_now.T, panel, precision=HIGH)
    for step in range(STEPS):
        low = 2 * step
        pair_u = modes_now[low : low + 2]
        pair_v = panel[low : low + 2]
        others = recon - jnp.dot(pair_u.T, pair_v, precision=HIGH)
        filled = coast_flat[:, None] * jnp.where(miss, recon, given_deviation)
        resid = filled - others
        proj = jnp.dot(resid, pair_v.T, precision=HIGH).T
        gram = jnp.dot(pair_v, pair_v.T, precision=HIGH)
        fresh = (coast_flat * solve_pair(gram, proj)).reshape(2, polar_coordinate, zonal_coordinate)
        for sweep_index in range(SWEEPS):
            padded = with_halo(fresh, (("lat", 1), ("lon", 2)), 1)
            fresh = sweep(padded, coast_pad, klon_pad)
        fresh = fresh.reshape(2, -1)
        sums = lax.psum(jnp.sum(weight * fresh * fresh, axis=1), ("lat", "lon"))
        scale = jnp.sqrt(sums / total + EPS)
        unit = fresh / scale[:, None]
        weighted = unit * weight
        proj_days, gram_u = lax.psum(
            (jnp.dot(weighted, resid, precision=HIGH), jnp.dot(weighted, unit.T, precision=HIGH)),
            ("lat", "lon"),
        )
        new_v = solve_pair(gram_u, proj_days)
        recon = others + jnp.dot(unit.T, new_v, precision=HIGH)
        modes_now = modes_now.at[low : low + 2].set(unit)
        panel = panel.at[low : low + 2].set(new_v)
    share = mode_series.shape[1]
    own_days = lax.dynamic_slice_in_dim(panel, lax.axis_index("lon") * share, share, 1)
    return (modes_now.reshape(modes, polar_coordinate, zonal_coordinate), own_days)


def solution(mesh):
    in_specs = (
        P("lat", "lon", None),
        P("lat", "lon", None),
        P("lat", "lon"),
        P(None, "lat", "lon"),
        P(None, "lon"),
    )
    out_specs = (P(None, "lat", "lon"), P(None, "lon"))
    return jax.shard_map(shards, mesh=mesh, in_specs=in_specs, out_specs=out_specs, check_vma=False)
```

profile of v0, /device:TPU:0, one launch (start us, length us, event | category | flops | bytes accessed | tf_op | source)
XLA Modules:
  0.0 726.5 jit_solution(397510755848207824)
XLA Ops:
  1.3 2.9 collective-permute-start
  7.4 16.4 %all-gather = f32[8,480,48]{1,2,0:T(8,128)S(1)} all-gather(f32[1,480,48]{1,2,0:T(8,128)} %bitcast.158), channel_id=1, replica_groups=mesh['lat'=4,'lon'=8] {'lon'}, dimensions={0}, use_global_device_ids=true | all-gather | bytes 829440 | tf_op jit(solution)/shard_map/all_gather | solution.py:76
  26.8 4.0 copy.60
  30.8 9.4 %copy.39 = s32[512,3840]{1,0:T(8,128)} copy(s32[512,3840]{0,1:T(8,128)} %bitcast.150) | data formatting | bytes 15728640 | tf_op jit(solution)/shard_map/shift_right_arithmetic | solution.py:36
  40.2 8.4 %fusion.231 = f32[512,3840]{1,0:T(8,128)} fusion(f32[3840,48]{0,1:T(8,128)S(1)} %reshape.373, f32[6,8,4,128]{3,2,1,0:T(4,128)S(1)} %bitcast.155), kind=kOutput, calls=%fused_computation.458 | convolution fusion | flops 1132462080 | bytes 8699904 | tf_op jit(solution)/shard_map/dot_general | solution.py:78
  48.6 15.2 %fusion.1 = (f32[512,3840]{1,0:T(8,128)S(1)}, pred[512,3840]{1,0:T(32,128)(4,1)S(1)}, f32[512,3840]{1,0:T(8,128)}) fusion(f32[512,3840]{1,0:T(8,128)} %fusion.231, bf16[4,128,3840]{2,1,0:T(8,128)(2,1)S(1)} %copy-done.4, f32[512]{0:T(512)S(1)} %get-tuple-element.206, s32[512,3840]{1,0:T(8,128)} %copy.39, s32[3840]{0:T(1024)S(1)} %shift_right_arithmetic.23, ...), kind=kOutput, calls=%fused_computation.5 | convolution fusion | flops 62914560 | bytes 37408768 | tf_op jit(solution)/shard_map/dot_general | solution.py:83
  63.8 3.2 copy-done
  66.9 6.7 convolution_bitcast_fusion
  76.2 2.5 divide_bitcast_fusion.7
  79.4 2.3 collective-permute-start.5
  81.9 3.5 collective-permute-start.3
  87.1 3.5 collective-permute-start.7
  92.2 2.9 collective-permute-start.9
  96.7 3.5 collective-permute-start.11
  101.7 3.0 collective-permute-start.12
  108.4 3.5 collective-permute-start.15
  118.0 3.5 collective-permute-start.19
  123.1 39.3 %psum.84 = f32[2]{0:T(128)S(1)} all-reduce(f32[2]{0:T(128)S(1)} %get-tuple-element.112), channel_id=1, replica_groups=mesh['lat'=4,'lon'=8] {'lat','lon'}, use_global_device_ids=true, to_apply=%region_1.2 | all-reduce | flops 2 | bytes 16 | tf_op jit(solution)/shard_map/psum | solution.py:93
  162.6 6.0 fusion.210
  168.7 41.9 %all-reduce.3 = (f32[2,3840]{1,0:T(2,128)S(1)}, f32[2,2]{1,0:T(2,128)S(1)}) all-reduce(f32[2,3840]{1,0:T(2,128)S(1)} %fusion.210, f32[2,2]{1,0:T(2,128)S(1)} %convolution_bitcast_fusion.4), channel_id=1, replica_groups=mesh['lat'=4,'lon'=8] {'lat','lon'}, use_global_device_ids=true, to_apply=%region_3.4 | all-reduce | flops 7684 | bytes 61472 | tf_op jit(solution)/shard_map/psum | solution.py:97
  213.9 2.7 subtract_divide_fusion.7
  216.7 9.0 %convolution_add_fusion.1 = f32[512,3840]{1,0:T(8,128)S(1)} fusion(f32[512,3840]{1,0:T(8,128)} %get-tuple-element.239, f32[1,3840]{1,0:T(1,128)S(1)} %get-tuple-element.123, f32[1,3840]{1,0:T(1,128)S(1)} %get-tuple-element.122, f32[2,4,128]{2,0,1:T(2,128)S(1)} %get-tuple-element.113, f32[2]{0:T(128)S(1)} %add_sqrt_fusion.3), kind=kOutput, calls=%fused_computation.17 | convolution fusion | flops 49160704 | bytes 15763464 | tf_op jit(solution)/shard_map/dot_general | solution.py:102
  226.7 10.4 %fusion.3 = (f32[512,3840]{1,0:T(8,128)S(1)}, f32[512,3840]{1,0:T(8,128)}) fusion(pred[512,3840]{1,0:T(32,128)(4,1)S(1)} %get-tuple-element.115, f32[512,3840]{1,0:T(8,128)S(1)} %convolution_add_fusion.1, bf16[4,128,3840]{2,1,0:T(8,128)(2,1)S(1)} %copy-done.5, f32[512]{0:T(512)S(1)} %get-tuple-element.206, f32[48,3840]{1,0:T(8,128)S(1)} %fusion.30, ...), kind=kOutput, calls=%fused_computation.7 | convolution fusion | flops 57016320 | bytes 29528064 | tf_op jit(solution)/shard_map/dot_general | solution.py:83
  237.1 3.1 copy-done.2
  240.2 6.5 fusion.18
  249.2 2.5 divide_bitcast_fusion.5
  257.7 3.5 collective-permute-start.23
  262.7 2.4 collective-permute-start.24
  268.7 3.5 collective-permute-start.27
  278.4 3.5 collective-permute-start.31
  288.3 3.5 collective-permute-start.35
  293.4 39.5 %psum.87 = f32[2]{0:T(128)S(1)} all-reduce(f32[2]{0:T(128)S(1)} %get-tuple-element.110), channel_id=1, replica_groups=mesh['lat'=4,'lon'=8] {'lat','lon'}, use_global_device_ids=true, to_apply=%region_5.6 | all-reduce | flops 2 | bytes 16 | tf_op jit(solution)/shard_map/psum | solution.py:93
  332.9 6.0 fusion.208
  339.1 41.8 %all-reduce.2 = (f32[2,3840]{1,0:T(2,128)S(1)}, f32[2,2]{1,0:T(2,128)S(1)}) all-reduce(f32[2,3840]{1,0:T(2,128)S(1)} %fusion.208, f32[2,2]{1,0:T(2,128)S(1)} %convolution_bitcast_fusion.3), channel_id=1, replica_groups=mesh['lat'=4,'lon'=8] {'lat','lon'}, use_global_device_ids=true, to_apply=%region_7.8 | all-reduce | flops 7684 | bytes 61472 | tf_op jit(solution)/shard_map/psum | solution.py:97
  384.1 2.6 subtract_divide_fusion.5
  386.7 9.0 %convolution_add_fusion = f32[512,3840]{1,0:T(8,128)S(1)} fusion(f32[512,3840]{1,0:T(8,128)} %get-tuple-element.241, f32[1,3840]{1,0:T(1,128)S(1)} %get-tuple-element.121, f32[1,3840]{1,0:T(1,128)S(1)} %get-tuple-element.120, f32[2,4,128]{2,0,1:T(2,128)S(1)} %get-tuple-element.111, f32[2]{0:T(128)S(1)} %add_sqrt_fusion.2), kind=kOutput, calls=%fused_computation.15 | convolution fusion | flops 49160704 | bytes 15763464 | tf_op jit(solution)/shard_map/dot_general | solution.py:102
  396.7 10.4 %fusion.5 = (f32[512,3840]{1,0:T(8,128)S(1)}, f32[512,3840]{1,0:T(8,128)}) fusion(pred[512,3840]{1,0:T(32,128)(4,1)S(1)} %get-tuple-element.115, f32[512,3840]{1,0:T(8,128)S(1)} %convolution_add_fusion, bf16[4,128,3840]{2,1,0:T(8,128)(2,1)S(1)} %copy-done.6, f32[512]{0:T(512)S(1)} %get-tuple-element.206, f32[48,3840]{1,0:T(8,128)S(1)} %fusion.29, ...), kind=kOutput, calls=%fused_computation.9 | convolution fusion | flops 57016320 | bytes 29528064 | tf_op jit(solution)/shard_map/dot_general | solution.py:83
  407.1 3.1 copy-done.3
  410.2 6.5 fusion.13
  419.2 2.5 divide_bitcast_fusion.3
  421.7 2.3 collective-permute-start.36
  427.7 3.5 collective-permute-start.39
  432.6 2.4 collective-permute-start.40
  438.7 3.5 collective-permute-start.43
  448.6 3.5 collective-permute-start.47
  458.3 3.5 collective-permute-start.51
  463.3 39.5 %psum.90 = f32[2]{0:T(128)S(1)} all-reduce(f32[2]{0:T(128)S(1)} %get-tuple-element.108), channel_id=1, replica_groups=mesh['lat'=4,'lon'=8] {'lat','lon'}, use_global_device_ids=true, to_apply=%region_9.10 | all-reduce | flops 2 | bytes 16 | tf_op jit(solution)/shard_map/psum | solution.py:93
  502.9 6.0 fusion.206
  509.1 41.7 %all-reduce.1 = (f32[2,3840]{1,0:T(2,128)S(1)}, f32[2,2]{1,0:T(2,128)S(1)}) all-reduce(f32[2,3840]{1,0:T(2,128)S(1)} %fusion.206, f32[2,2]{1,0:T(2,128)S(1)} %convolution_bitcast_fusion.2), channel_id=1, replica_groups=mesh['lat'=4,'lon'=8] {'lat','lon'}, use_global_device_ids=true, to_apply=%region_11.12 | all-reduce | flops 7684 | bytes 61472 | tf_op jit(solution)/shard_map/psum | solution.py:97
  554.1 2.9 subtract_divide_fusion.3
  557.0 6.4 fusion.27
  564.4 10.8 %fusion.7 = f32[512,3840]{1,0:T(8,128)S(1)} fusion(pred[512,3840]{1,0:T(32,128)(4,1)S(1)} %get-tuple-element.115, bf16[512,3840]{1,0:T(8,128)(2,1)S(1)} %bitcast.148, f32[512,3840]{1,0:T(8,128)} %get-tuple-element.243, f32[512,3840]{1,0:T(8,128)S(1)} %fusion.27, f32[512]{0:T(512)S(1)} %get-tuple-element.206, f32[48,3840]{1,0:T(8,128)S(1)} %fusion.28, ...), kind=kOutput, calls=%fused_computation.11 | convolution fusion | flops 58982400 | bytes 29528064 | tf_op jit(solution)/shard_map/dot_general | solution.py:83
  575.3 3.2 copy-done.1
  578.4 6.5 fusion.8
  587.4 2.5 divide_bitcast_fusion.1
  596.0 3.5 collective-permute-start.55
  601.0 2.4 collective-permute-start.56
  607.1 3.5 collective-permute-start.59
  616.7 3.5 collective-permute-start.63
  626.6 3.5 collective-permute-start.67
  631.7 39.5 %psum.93 = f32[2]{0:T(128)S(1)} all-reduce(f32[2]{0:T(128)S(1)} %get-tuple-element.106), channel_id=1, replica_groups=mesh['lat'=4,'lon'=8] {'lat','lon'}, use_global_device_ids=true, to_apply=%region_13.14 | all-reduce | flops 2 | bytes 16 | tf_op jit(solution)/shard_map/psum | solution.py:93
  671.2 6.0 fusion.204
  678.1 41.4 %all-reduce = (f32[2,3840]{1,0:T(2,128)S(1)}, f32[2,2]{1,0:T(2,128)S(1)}) all-reduce(f32[2,3840]{1,0:T(2,128)S(1)} %fusion.204, f32[2,2]{1,0:T(2,128)S(1)} %convolution_bitcast_fusion.1), channel_id=1, replica_groups=mesh['lat'=4,'lon'=8] {'lat','lon'}, use_global_device_ids=true, to_apply=%region_15.16 | all-reduce | flops 7684 | bytes 61472 | tf_op jit(solution)/shard_map/psum | solution.py:97
  722.6 2.6 subtract_divide_fusion.1
  (242 shorter events, 106.2 us)
Async XLA Ops:
  1.3 80.5 %collective-permute-start = (f32[1,128]{1,0:T(1,128)S(1)}, f32[1,128]{1,0:T(1,128)S(1)}, u32[]{:S(2)}, u32[]{:S(2)}) collective-permute-start(f32[1,128]{1,0:T(1,128)S(1)} %get-tuple-element.203), channel_id=1, source_target_pairs={{0,8},{8,16},{16,24},{24,0},{1,9},{9,17},{17,25},{25,1},{2,10},{10... | collective-permute-start | bytes 1544 | tf_op jit(solution)/shard_map/ppermute | solution.py:23
  4.3 77.6 %collective-permute-start.1 = (f32[1,128]{1,0:T(1,128)S(1)}, f32[1,128]{1,0:T(1,128)S(1)}, u32[]{:S(2)}, u32[]{:S(2)}) collective-permute-start(f32[1,128]{1,0:T(1,128)S(1)} %get-tuple-element.204), channel_id=1, source_target_pairs={{8,0},{16,8},{24,16},{0,24},{9,1},{17,9},{25,17},{1,25},{10,2},{18... | collective-permute-start | bytes 1544 | tf_op jit(solution)/shard_map/ppermute | solution.py:24
  78.7 8.2 %collective-permute-start.4 = (f32[2,1,128]{2,0,1:T(2,128)S(1)}, f32[2,1,128]{2,0,1:T(2,128)S(1)}, u32[]{:S(2)}, u32[]{:S(2)}) collective-permute-start(f32[2,1,128]{2,0,1:T(2,128)S(1)} %get-tuple-element.199), channel_id=1, source_target_pairs={{0,8},{8,16},{16,24},{24,0},{1,9},{9,17},{17,25},{25,1},{2,10},{10... | collective-permute-start | bytes 3080 | tf_op jit(solution)/shard_map/ppermute | solution.py:23
  79.4 7.6 %collective-permute-start.5 = (f32[2,1,128]{2,0,1:T(2,128)S(1)}, f32[2,1,128]{2,0,1:T(2,128)S(1)}, u32[]{:S(2)}, u32[]{:S(2)}) collective-permute-start(f32[2,1,128]{2,0,1:T(2,128)S(1)} %get-tuple-element.200), channel_id=1, source_target_pairs={{8,0},{16,8},{24,16},{0,24},{9,1},{17,9},{25,17},{1,25},{10,2},{18... | collective-permute-start | bytes 3080 | tf_op jit(solution)/shard_map/ppermute | solution.py:24
  81.9 4.8 collective-permute-start.2
  81.9 4.9 collective-permute-start.3
  87.1 4.9 collective-permute-start.6
  87.1 4.8 collective-permute-start.7
  92.1 4.5 collective-permute-start.8
  92.2 4.5 collective-permute-start.9
  96.7 4.9 collective-permute-start.10
  96.7 4.9 collective-permute-start.11
  101.7 4.5 collective-permute-start.12
  104.7 3.6 collective-permute-start.13
  108.4 4.9 collective-permute-start.14
  108.4 4.9 collective-permute-start.15
  113.4 4.5 collective-permute-start.16
  114.4 3.6 collective-permute-start.17
  118.0 4.9 collective-permute-start.18
  118.0 4.9 collective-permute-start.19
  251.7 4.5 collective-permute-start.20
  254.0 3.6 collective-permute-start.21
  257.7 4.9 collective-permute-start.22
  257.7 4.9 collective-permute-start.23
  262.7 4.5 collective-permute-start.24
  265.1 3.6 collective-permute-start.25
  268.7 4.9 collective-permute-start.26
  268.7 4.9 collective-permute-start.27
  273.7 4.5 collective-permute-start.28
  274.8 3.6 collective-permute-start.29
  278.4 4.9 collective-permute-start.30
  278.4 4.9 collective-permute-start.31
  283.4 4.5 collective-permute-start.32
  284.6 3.6 collective-permute-start.33
  288.3 4.9 collective-permute-start.34
  288.3 4.9 collective-permute-start.35
  421.7 4.5 collective-permute-start.36
  424.0 3.6 collective-permute-start.37
  427.6 4.9 collective-permute-start.38
  427.7 4.9 collective-permute-start.39
  432.6 4.5 collective-permute-start.40
  435.1 3.6 collective-permute-start.41
  438.7 4.9 collective-permute-start.42
  438.7 4.9 collective-permute-start.43
  443.7 4.5 collective-permute-start.44
  444.9 3.6 collective-permute-start.45
  448.6 4.9 collective-permute-start.46
  448.6 4.9 collective-permute-start.47
  453.6 4.5 collective-permute-start.48
  454.6 3.6 collective-permute-start.49
  458.3 4.9 collective-permute-start.50
  458.3 4.9 collective-permute-start.51
  590.0 4.5 collective-permute-start.52
  596.0 4.9 collective-permute-start.54
  596.0 4.9 collective-permute-start.55
  601.0 4.5 collective-permute-start.56
  607.1 4.9 collective-permute-start.58
  607.1 4.9 collective-permute-start.59
  612.1 4.5 collective-permute-start.60
  616.7 4.9 collective-permute-start.62
  616.7 4.9 collective-permute-start.63
  621.7 4.5 collective-permute-start.64
  626.6 4.9 collective-permute-start.66
  626.6 4.9 collective-permute-start.67
  (13 other events, 74.9 us)
where the time goes:
time: 732 us; the launch traced here: 726 us
  blocking collectives  341 us (47%)
  matrix products  132 us (18%)
  starting transfers between devices  112 us (15%)
  waiting for transfers between devices  57.5 us (8%)
  local copies, waits for them, and re-layouts  38 us (5%)
  other arithmetic  24.1 us (3%)
  between operations  22.1 us (3%)
    psum x4, blocking collectives, shards(): lax.psum((jnp.dot(weighted, resid, precision=HIGH), jnp.dot(weighted, uni...  167 us
    psum x4, blocking collectives, shards(): sums = lax.psum(jnp.sum(weight * fresh * fresh, axis=1), ('lat', 'lon'))  158 us
    ppermute x34, starting transfers between devices, with_halo(): after = lax.ppermute(first, axis, down)  83.2 us
    dot_general x4, matrix products, shards(): others = recon - jnp.dot(pair_u.T, pair_v, precision=HIGH)  46.8 us
    ppermute x34, waiting for transfers between devices, with_halo(): before = lax.ppermute(last, axis, up)  45.2 us
    ppermute x34, starting transfers between devices, with_halo(): before = lax.ppermute(last, axis, up)  28.7 us
    dot_general x4, matrix products, shards(): proj = jnp.dot(resid, pair_v.T, precision=HIGH).T  26.1 us
    dot_general x3, matrix products, shards(): recon = others + jnp.dot(unit.T, new_v, precision=HIGH)  24.4 us
  transfers between devices with their start and end apart: 68, of which 48 were waited for; matrix products, arithmetic and copies ran while one was open for 7% of the time, Pallas kernels for 0%

commit v1 on v0

--- a/solution.py
+++ b/solution.py
@@ -13,17 +13,59 @@
 HIGH = lax.Precision.HIGHEST
 
 
-def with_halo(x, sides, width):
-    for axis, dim in sides:
-        count, length = (lax.axis_size(axis), x.shape[dim])
+def pairing(lat_map, lon_map):
+    nlat, nlon = (lax.axis_size("lat"), lax.axis_size("lon"))
+    return [(i * nlon + j, lat_map(i) * nlon + lon_map(j)) for i in range(nlat) for j in range(nlon)]
+
+
+def swap(x, lat_bits, lon_bits):
+    return lax.ppermute(x, ("lat", "lon"), pairing(lambda i: i ^ lat_bits, lambda j: j ^ lon_bits))
+
+
+def sum_all(x):
+    nlat, nlon = (lax.axis_size("lat"), lax.axis_size("lon"))
+    if nlat & (nlat - 1) or nlon & (nlon - 1):
+        return lax.psum(x, ("lat", "lon"))
+    if nlon > 1:
+        x = x + swap(x, 0, 1)
+    for size, first, on_lat in ((nlat, 1, True), (nlon, 2, False)):
+        bit = first
+        while bit < size:
+            bits = lambda b: (b, 0) if on_lat else (0, b)
+            if 2 * bit < size:
+                near, far, both = (swap(x, *bits(b)) for b in (bit, 2 * bit, 3 * bit))
+                x = (x + near) + (far + both)
+                bit *= 4
+            else:
+                x = x + swap(x, *bits(bit))
+                bit *= 2
+    return x
+
+
+def lat_halo(x, dim, depth):
+    count, length = (lax.axis_size("lat"), x.shape[dim])
+    last = lax.slice_in_dim(x, length - depth, length, axis=dim)
+    first = lax.slice_in_dim(x, 0, depth, axis=dim)
+    if count % 2:
         up = [(i, (i + 1) % count) for i in range(count)]
-        down = [(j, i) for i, j in up]
-        last = lax.slice_in_dim(x, length - width, length, axis=dim)
-        first = lax.slice_in_dim(x, 0, width, axis=dim)
-        before = lax.ppermute(last, axis, up)
-        after = lax.ppermute(first, axis, down)
-        x = jnp.concatenate([before, x, after], axis=dim)
-    return x
+        before = lax.ppermute(last, "lat", up)
+        after = lax.ppermute(first, "lat", [(j, i) for i, j in up])
+        return jnp.concatenate([before, x, after], axis=dim)
+    odd = lax.axis_index("lat") % 2 == 1
+    out_a, out_b = (jnp.where(odd, first, last), jnp.where(odd, last, first))
+    same = lambda j: j
+    got_a = lax.ppermute(out_a, ("lat", "lon"), pairing(lambda i: i ^ 1, same))
+    got_b = lax.ppermute(out_b, ("lat", "lon"), pairing(lambda i: (i + 1 if i % 2 else i - 1) % count, same))
+    before, after = (jnp.where(odd, got_a, got_b), jnp.where(odd, got_b, got_a))
+    return jnp.concatenate([before, x, after], axis=dim)
+
+
+def lon_halo(x, dim, depth):
+    count, length = (lax.axis_size("lon"), x.shape[dim])
+    up = [(i, (i + 1) % count) for i in range(count)]
+    before = lax.ppermute(lax.slice_in_dim(x, length - depth, length, axis=dim), "lon", up)
+    after = lax.ppermute(lax.slice_in_dim(x, 0, depth, axis=dim), "lon", [(j, i) for i, j in up])
+    return jnp.concatenate([before, x, after], axis=dim)
 
 
 def latitude_cos(rows, nrows):
@@ -64,8 +106,8 @@
     weight = jnp.broadcast_to(cosl[:, None], (polar_coordinate, zonal_coordinate)).reshape(-1)
     coast = ocean_binary_mask.astype(jnp.float32)
     coast_flat = coast.reshape(-1)
-    depth = 1
-    coast_pad = with_halo(coast, (("lat", 0), ("lon", 1)), depth)
+    depth = SWEEPS
+    coast_pad = lon_halo(lat_halo(coast, 0, depth), 1, depth)
     pad_rows = row_start - depth + jnp.arange(polar_coordinate + 2 * depth)
     inside = ((pad_rows >= 0) & (pad_rows < nlat)).astype(jnp.float32)
     coast_pad = coast_pad * inside[:, None]
@@ -86,18 +128,22 @@
         proj = jnp.dot(resid, pair_v.T, precision=HIGH).T
         gram = jnp.dot(pair_v, pair_v.T, precision=HIGH)
         fresh = (coast_flat * solve_pair(gram, proj)).reshape(2, polar_coordinate, zonal_coordinate)
-        for sweep_index in range(SWEEPS):
-            padded = with_halo(fresh, (("lat", 1), ("lon", 2)), 1)
-            fresh = sweep(padded, coast_pad, klon_pad)
+        fresh = lon_halo(lat_halo(fresh, 1, depth), 2, depth)
+        for cut in range(SWEEPS):
+            inner = slice(cut, -cut) if cut else slice(None)
+            fresh = sweep(fresh, coast_pad[inner, inner], klon_pad[inner])
         fresh = fresh.reshape(2, -1)
-        sums = lax.psum(jnp.sum(weight * fresh * fresh, axis=1), ("lat", "lon"))
-        scale = jnp.sqrt(sums / total + EPS)
+        weighted = fresh * weight
+        raw_days = jnp.dot(weighted, resid, precision=HIGH)
+        raw_gram = jnp.dot(weighted, fresh.T, precision=HIGH)
+        packed = jnp.concatenate([raw_days.reshape(-1), jnp.pad(raw_gram.reshape(-1), (0, 124))]).reshape(-1, 128)
+        packed = sum_all(packed).reshape(-1)
+        raw_days = packed[: 2 * calendar_dates].reshape(2, calendar_dates)
+        raw_gram = packed[2 * calendar_dates : 2 * calendar_dates + 4].reshape(2, 2)
+        scale = jnp.sqrt(jnp.diagonal(raw_gram) / total + EPS)
         unit = fresh / scale[:, None]
-        weighted = unit * weight
-        proj_days, gram_u = lax.psum(
-            (jnp.dot(weighted, resid, precision=HIGH), jnp.dot(weighted, unit.T, precision=HIGH)),
-            ("lat", "lon"),
-        )
+        proj_days = raw_days / scale[:, None]
+        gram_u = raw_gram / (scale[:, None] * scale[None, :])
         new_v = solve_pair(gram_u, proj_days)
         recon = others + jnp.dot(unit.T, new_v, precision=HIGH)
         modes_now = modes_now.at[low : low + 2].set(unit)

time: 732 us -> 379 us (0.52)
  blocking collectives: 341 us -> 16 us
  starting transfers between devices: 112 us -> 64.6 us
  local copies, waits for them, and re-layouts: 38 us -> 56.6 us
  matrix products: 132 us -> 144 us
  waiting for transfers between devices: 57.5 us -> 47.3 us
    psum x8 -> x0, blocking collectives: 325 us -> none  [the longest x4 167 us: shards(): lax.psum((jnp.dot(weighted, resid, precision=HIGH), jnp.dot(weighted, uni...]
    ppermute x68 -> x48, starting transfers between devices: 112 us -> 64.6 us  [the longest x28 32.3 us: swap(): lax.ppermute(x, ('lat', 'lon'), pairing(lambda i: i ^ lat_bits, lambda j:...]
    slice x34 -> x13, local copies, waits for them, and re-layouts: 1.34 us -> 16.2 us  [the longest x8 15.8 us: shards(): raw_gram = packed[2 * calendar_dates:2 * calendar_dates + 4].reshape(2, 2)]
    dot_general x4, matrix products: 46.8 us -> 58.8 us  [shards(): others = recon - jnp.dot(pair_u.T, pair_v, precision=HIGH)]
    ppermute x68 -> x48, waiting for transfers between devices: 57.5 us -> 47.3 us  [the longest x28 33.5 us: swap(): lax.ppermute(x, ('lat', 'lon'), pairing(lambda i: i ^ lat_bits, lambda j:...]
  transfers between devices with their start and end apart: 68 -> 48, of which waited for: 48 -> 35; matrix products, arithmetic and copies ran while one was open for 7% -> 14% of each run, Pallas kernels for 0% -> 0%
where the time goes in v1:
time: 379 us; the launch traced here: 380 us
  matrix products  144 us (38%)
  starting transfers between devices  64.6 us (17%)
  local copies, waits for them, and re-layouts  56.6 us (15%)
  waiting for transfers between devices  47.3 us (12%)
  other arithmetic  29.1 us (8%)
  between operations  22.6 us (6%)
  blocking collectives  16 us (4%)
    dot_general x4, matrix products, shards(): others = recon - jnp.dot(pair_u.T, pair_v, precision=HIGH)  58.8 us
    ppermute x28, waiting for transfers between devices, swap(): lax.ppermute(x, ('lat', 'lon'), pairing(lambda i: i ^ lat_bits, lambda j:...  33.5 us
    ppermute x28, starting transfers between devices, swap(): lax.ppermute(x, ('lat', 'lon'), pairing(lambda i: i ^ lat_bits, lambda j:...  32.3 us
    dot_general x4, matrix products, shards(): proj = jnp.dot(resid, pair_v.T, precision=HIGH).T  26.1 us
    dot_general x4, matrix products, shards(): raw_days = jnp.dot(weighted, resid, precision=HIGH)  24.4 us
    dot_general x3, matrix products, shards(): recon = others + jnp.dot(unit.T, new_v, precision=HIGH)  24.4 us
    unnamed x23, local copies, waits for them, and re-layouts  18.8 us
    ppermute x5, starting transfers between devices, lon_halo(): lax.ppermute(lax.slice_in_dim(x, 0, depth, axis=dim), 'lon', [(j, i) for...  17.6 us
  transfers between devices with their start and end apart: 48, of which 35 were waited for; matrix products, arithmetic and copies ran while one was open for 14% of the time, Pallas kernels for 0%

profile of v1, /device:TPU:0, one launch (start us, length us, event | category | flops | bytes accessed | tf_op | source)
XLA Modules:
  0.0 380.4 jit_solution(3410929182620277699)
XLA Ops:
  1.3 3.9 %collective-permute-start.5 = (f32[4,128]{1,0:T(4,128)S(1)}, f32[4,128]{1,0:T(4,128)S(1)}, u32[]{:S(2)}, u32[]{:S(2)}) collective-permute-start(f32[4,128]{1,0:T(4,128)S(1)} %get-tuple-element.156), channel_id=1, source_target_pairs={{0,24},{1,25},{2,26},{3,27},{4,28},{5,29},{6,30},{7,31},{8,16},{9,... | collective-permute-start | bytes 6152 | tf_op jit(solution)/shard_map/ppermute | solution.py:58
  7.9 16.0 %all-gather = f32[8,480,48]{1,2,0:T(8,128)S(1)} all-gather(f32[1,480,48]{1,2,0:T(8,128)} %bitcast.198), channel_id=1, replica_groups=mesh['lat'=4,'lon'=8] {'lon'}, dimensions={0}, use_global_device_ids=true | all-gather | bytes 829440 | tf_op jit(solution)/shard_map/all_gather | solution.py:118
  26.9 4.0 %copy.60 = s32[480,8,4,128]{3,1,2,0:T(8,128)} copy(s32[480,8,4,128]{3,2,1,0:T(4,128)S(1)} %bitcast.185) | data formatting | bytes 15728640
  30.9 9.3 %copy.39 = s32[512,3840]{1,0:T(8,128)} copy(s32[512,3840]{0,1:T(8,128)} %bitcast.186) | data formatting | bytes 15728640 | tf_op jit(solution)/shard_map/shift_right_arithmetic | solution.py:78
  40.1 8.4 %fusion.203 = f32[512,3840]{1,0:T(8,128)} fusion(f32[3840,48]{0,1:T(8,128)S(1)} %reshape.483, f32[6,8,4,128]{3,2,1,0:T(4,128)S(1)} %bitcast.191), kind=kOutput, calls=%fused_computation.393 | convolution fusion | flops 1132462080 | bytes 8699904 | tf_op jit(solution)/shard_map/dot_general | solution.py:120
  48.5 14.9 %fusion.1 = (f32[512,3840]{1,0:T(8,128)S(1)}, pred[512,3840]{1,0:T(32,128)(4,1)S(1)}, f32[512,3840]{1,0:T(8,128)}) fusion(f32[512,3840]{1,0:T(8,128)} %fusion.203, bf16[4,128,3840]{2,1,0:T(8,128)(2,1)S(1)} %copy-done.4, f32[512]{0:T(512)S(1)} %get-tuple-element.157, s32[512,3840]{1,0:T(8,128)} %copy.39, s32[3840]{0:T(1024)S(1)} %shift_right_arithmetic.23, ...), kind=kOutput, calls=%fused_computation.9 | convolution fusion | flops 62914560 | bytes 37408768 | tf_op jit(solution)/shard_map/dot_general | solution.py:125
  63.4 3.1 copy-done
  66.6 6.7 %convolution_bitcast_fusion = f32[2,512]{1,0:T(2,128)S(1)} fusion(f32[512,3840]{1,0:T(8,128)S(1)} %get-tuple-element.98, f32[48,3840]{1,0:T(8,128)S(1)} %bitcast.189), kind=kOutput, calls=%fused_computation.23 | convolution fusion | flops 47185920 | bytes 7899136 | tf_op jit(solution)/shard_map/dot_general | solution.py:128
  76.0 2.7 divide_bitcast_fusion.7
  78.7 1.5 collective-permute-start.1
  81.2 3.5 collective-permute-start.7
  86.6 3.5 collective-permute-start.3
  92.4 6.3 %fusion.191 = f32[2,3840]{1,0:T(2,128)S(1)} fusion(f32[512,3840]{1,0:T(8,128)} %copy-done, f32[2,4,128]{2,0,1:T(2,128)S(1)} %multiply_add_fusion.15, f32[512]{0:T(512)S(1)} %broadcast_bitcast_fusion), kind=kOutput, calls=%fused_computation.339 | convolution fusion | flops 47186944 | bytes 7901184 | tf_op jit(solution)/shard_map/dot_general | solution.py:137
  100.1 2.5 collective-permute-start.11
  105.0 1.5 collective-permute-done.10
  107.0 3.6 collective-permute-start.14
  112.8 2.6 collective-permute-done.13
  115.5 3.3 slice.908
  124.2 2.6 subtract_divide_fusion.7
  126.9 9.0 %convolution_add_fusion.1 = f32[512,3840]{1,0:T(8,128)S(1)} fusion(f32[512,3840]{1,0:T(8,128)} %get-tuple-element.190, f32[1,3840]{1,0:T(1,128)S(1)} %get-tuple-element.107, f32[1,3840]{1,0:T(1,128)S(1)} %get-tuple-element.106, f32[2,4,128]{2,0,1:T(2,128)S(1)} %multiply_add_fusion.15, f32[2]{0:T(128)S(1)} %add_sqrt_fusion.3), kind=kOutput, calls=%fused_computation.21 | convolution fusion | flops 49160704 | bytes 15763464 | tf_op jit(solution)/shard_map/dot_general | solution.py:148
  136.9 22.4 %fusion.3 = (f32[512,3840]{1,0:T(8,128)S(1)}, f32[512,3840]{1,0:T(8,128)}) fusion(pred[512,3840]{1,0:T(32,128)(4,1)S(1)} %get-tuple-element.99, f32[512,3840]{1,0:T(8,128)S(1)} %convolution_add_fusion.1, bf16[4,128,3840]{2,1,0:T(8,128)(2,1)S(1)} %copy-done.5, f32[512]{0:T(512)S(1)} %get-tuple-element.157, f32[48,3840]{1,0:T(8,128)S(1)} %fusion.142, ...), kind=kOutput, calls=%fused_computation.11 | convolution fusion | flops 57016320 | bytes 29528064 | tf_op jit(solution)/shard_map/dot_general | solution.py:125
  159.3 3.1 copy-done.2
  162.4 6.5 %fusion.94 = f32[2,512]{1,0:T(2,128)S(1)} fusion(f32[512,3840]{1,0:T(8,128)S(1)} %get-tuple-element.191, f32[48,3840]{1,0:T(8,128)S(1)} %fusion.142), kind=kOutput, calls=%fused_computation.177 | convolution fusion | flops 47185920 | bytes 7899136 | tf_op jit(solution)/shard_map/dot_general | solution.py:128
  171.6 2.7 divide_bitcast_fusion.5
  174.3 1.6 collective-permute-start.16
  175.8 1.5 collective-permute-start.15
  177.3 1.5 collective-permute-done.16
  179.5 3.5 collective-permute-start.18
  185.2 6.0 %fusion.190 = f32[2,3840]{1,0:T(2,128)S(1)} fusion(f32[512,3840]{1,0:T(8,128)} %copy-done.2, f32[2,4,128]{2,0,1:T(2,128)S(1)} %multiply_add_fusion.14, f32[512]{0:T(512)S(1)} %broadcast_bitcast_fusion), kind=kOutput, calls=%fused_computation.336 | convolution fusion | flops 47186944 | bytes 7901184 | tf_op jit(solution)/shard_map/dot_general | solution.py:137
  192.8 1.5 collective-permute-start.22
  194.3 1.5 collective-permute-start.21
  198.2 1.5 collective-permute-done.20
  199.8 3.5 collective-permute-start.25
  205.6 2.5 collective-permute-done.24
  208.1 3.3 slice.947
  217.0 2.7 subtract_divide_fusion.5
  219.7 9.0 %convolution_add_fusion = f32[512,3840]{1,0:T(8,128)S(1)} fusion(f32[512,3840]{1,0:T(8,128)} %get-tuple-element.192, f32[1,3840]{1,0:T(1,128)S(1)} %get-tuple-element.105, f32[1,3840]{1,0:T(1,128)S(1)} %get-tuple-element.104, f32[2,4,128]{2,0,1:T(2,128)S(1)} %multiply_add_fusion.14, f32[2]{0:T(128)S(1)} %add_sqrt_fusion.2), kind=kOutput, calls=%fused_computation.19 | convolution fusion | flops 49160704 | bytes 15763464 | tf_op jit(solution)/shard_map/dot_general | solution.py:148
  229.8 10.7 %fusion.5 = (f32[512,3840]{1,0:T(8,128)S(1)}, f32[512,3840]{1,0:T(8,128)}) fusion(pred[512,3840]{1,0:T(32,128)(4,1)S(1)} %get-tuple-element.99, f32[512,3840]{1,0:T(8,128)S(1)} %convolution_add_fusion, bf16[4,128,3840]{2,1,0:T(8,128)(2,1)S(1)} %copy-done.6, f32[512]{0:T(512)S(1)} %get-tuple-element.157, f32[48,3840]{1,0:T(8,128)S(1)} %fusion.141, ...), kind=kOutput, calls=%fused_computation.13 | convolution fusion | flops 57016320 | bytes 29528064 | tf_op jit(solution)/shard_map/dot_general | solution.py:125
  240.5 3.1 copy-done.3
  243.5 6.5 %fusion.89 = f32[2,512]{1,0:T(2,128)S(1)} fusion(f32[512,3840]{1,0:T(8,128)S(1)} %get-tuple-element.193, f32[48,3840]{1,0:T(8,128)S(1)} %fusion.141), kind=kOutput, calls=%fused_computation.172 | convolution fusion | flops 47185920 | bytes 7899136 | tf_op jit(solution)/shard_map/dot_general | solution.py:128
  252.7 2.7 divide_bitcast_fusion.3
  257.4 2.5 collective-permute-done.27
  260.1 3.5 collective-permute-start.29
  265.8 6.0 %fusion.189 = f32[2,3840]{1,0:T(2,128)S(1)} fusion(f32[512,3840]{1,0:T(8,128)} %copy-done.3, f32[2,4,128]{2,0,1:T(2,128)S(1)} %multiply_add_fusion.13, f32[512]{0:T(512)S(1)} %broadcast_bitcast_fusion), kind=kOutput, calls=%fused_computation.333 | convolution fusion | flops 47186944 | bytes 7901184 | tf_op jit(solution)/shard_map/dot_general | solution.py:137
  273.4 2.1 collective-permute-start.33
  279.9 3.5 collective-permute-start.36
  285.8 2.5 collective-permute-done.35
  288.3 3.3 slice.986
  297.1 3.0 subtract_divide_fusion.3
  300.1 6.4 %fusion.139 = f32[512,3840]{1,0:T(8,128)S(1)} fusion(f32[1,3840]{1,0:T(1,128)S(1)} %get-tuple-element.103, f32[1,3840]{1,0:T(1,128)S(1)} %get-tuple-element.102, f32[2,4,128]{2,0,1:T(2,128)S(1)} %multiply_add_fusion.13, f32[2]{0:T(128)S(1)} %add_sqrt_fusion.1), kind=kOutput, calls=%fused_computation.258 | convolution fusion | flops 47194624 | bytes 7899144 | tf_op jit(solution)/shard_map/dot_general | solution.py:148
  307.6 10.8 %fusion.7 = f32[512,3840]{1,0:T(8,128)S(1)} fusion(pred[512,3840]{1,0:T(32,128)(4,1)S(1)} %get-tuple-element.99, bf16[512,3840]{1,0:T(8,128)(2,1)S(1)} %bitcast.184, f32[512,3840]{1,0:T(8,128)} %get-tuple-element.194, f32[512,3840]{1,0:T(8,128)S(1)} %fusion.139, f32[512]{0:T(512)S(1)} %get-tuple-element.157, f32[48,3840]{1,0:T(8,128)S(1)} %fusion.140, ...), kind=kOutput, calls=%fused_computation.15 | convolution fusion | flops 58982400 | bytes 29528064 | tf_op jit(solution)/shard_map/dot_general | solution.py:125
  318.4 3.1 copy-done.1
  321.6 6.5 %fusion.84 = f32[2,512]{1,0:T(2,128)S(1)} fusion(f32[512,3840]{1,0:T(8,128)S(1)} %fusion.7, f32[48,3840]{1,0:T(8,128)S(1)} %fusion.140), kind=kOutput, calls=%fused_computation.167 | convolution fusion | flops 47185920 | bytes 7899136 | tf_op jit(solution)/shard_map/dot_general | solution.py:128
  330.7 2.6 divide_bitcast_fusion.1
  333.3 1.6 collective-permute-start.38
  336.4 1.5 collective-permute-done.38
  338.6 3.5 collective-permute-start.40
  344.3 6.2 %fusion.188 = f32[2,3840]{1,0:T(2,128)S(1)} fusion(f32[512,3840]{1,0:T(8,128)} %copy-done.1, f32[2,4,128]{2,0,1:T(2,128)S(1)} %multiply_add_fusion.12, f32[512]{0:T(512)S(1)} %broadcast_bitcast_fusion), kind=kOutput, calls=%fused_computation.330 | convolution fusion | flops 47186944 | bytes 7901184 | tf_op jit(solution)/shard_map/dot_general | solution.py:137
  353.6 1.5 collective-permute-start.43
  357.5 1.5 collective-permute-done.42
  359.0 3.5 collective-permute-start.47
  364.9 2.5 collective-permute-done.46
  367.4 3.3 slice.1025
  376.8 2.6 subtract_divide_fusion.1
  (217 shorter events, 68.3 us)
Async XLA Ops:
  1.3 79.7 %collective-permute-start.5 = (f32[4,128]{1,0:T(4,128)S(1)}, f32[4,128]{1,0:T(4,128)S(1)}, u32[]{:S(2)}, u32[]{:S(2)}) collective-permute-start(f32[4,128]{1,0:T(4,128)S(1)} %get-tuple-element.156), channel_id=1, source_target_pairs={{0,24},{1,25},{2,26},{3,27},{4,28},{5,29},{6,30},{7,31},{8,16},{9,... | collective-permute-start | bytes 6152 | tf_op jit(solution)/shard_map/ppermute | solution.py:58
  5.2 75.8 %collective-permute-start.4 = (f32[4,128]{1,0:T(4,128)S(1)}, f32[4,128]{1,0:T(4,128)S(1)}, u32[]{:S(2)}, u32[]{:S(2)}) collective-permute-start(f32[4,128]{1,0:T(4,128)S(1)} %get-tuple-element.156), channel_id=1, source_target_pairs={{0,8},{1,9},{2,10},{3,11},{4,12},{5,13},{6,14},{7,15},{8,0},{9,1},... | collective-permute-start | bytes 6152 | tf_op jit(solution)/shard_map/ppermute | solution.py:57
  30.9 9.3 %copy-start.8 = (f32[48,4,128]{2,1,0:T(4,128)S(1)}, f32[48,4,128]{2,1,0:T(4,128)}, u32[]{:S(2)}) copy-start(f32[48,4,128]{2,1,0:T(4,128)} %param.24) | copy-start | bytes 294916
  40.1 8.4 %copy-start.4 = (bf16[4,128,3840]{2,1,0:T(8,128)(2,1)S(1)}, bf16[4,128,3840]{2,1,0:T(8,128)(2,1)}, u32[]{:S(2)}) copy-start(bf16[4,128,3840]{2,1,0:T(8,128)(2,1)} %param.21) | copy-start | bytes 11796484
  63.4 3.1 copy-start
  78.7 7.7 %collective-permute-start.1 = (f32[2,4,128]{2,0,1:T(2,128)S(1)}, f32[2,4,128]{2,0,1:T(2,128)S(1)}, u32[]{:S(2)}, u32[]{:S(2)}) collective-permute-start(f32[2,4,128]{2,0,1:T(2,128)S(1)} %maximum_multiply_fusion.1), channel_id=1, source_target_pairs={{0,24},{1,25},{2,26},{3,27},{4,28},{5,29},{6,30},{7,31},{8,16},{9,... | collective-permute-start | bytes 12296 | tf_op jit(solution)/shard_map/ppermute | solution.py:58
  80.2 6.2 %collective-permute-start = (f32[2,4,128]{2,0,1:T(2,128)S(1)}, f32[2,4,128]{2,0,1:T(2,128)S(1)}, u32[]{:S(2)}, u32[]{:S(2)}) collective-permute-start(f32[2,4,128]{2,0,1:T(2,128)S(1)} %maximum_multiply_fusion.1), channel_id=1, source_target_pairs={{0,8},{1,9},{2,10},{3,11},{4,12},{5,13},{6,14},{7,15},{8,0},{9,1},... | collective-permute-start | bytes 12296 | tf_op jit(solution)/shard_map/ppermute | solution.py:57
  81.2 4.9 %collective-permute-start.6 = (f32[12,4]{1,0:T(8,128)S(1)}, f32[12,4]{1,0:T(8,128)S(1)}, u32[]{:S(2)}, u32[]{:S(2)}) collective-permute-start(f32[12,4]{1,0:T(8,128)S(1)} %get-tuple-element.142), channel_id=1, source_target_pairs={{0,1},{1,2},{2,3},{3,4},{4,5},{5,6},{6,7},{7,0},{8,9},{9,10},{10,1... | collective-permute-start | bytes 584 | tf_op jit(solution)/shard_map/ppermute | solution.py:66
  81.2 4.9 %collective-permute-start.7 = (f32[12,4]{1,0:T(8,128)S(1)}, f32[12,4]{1,0:T(8,128)S(1)}, u32[]{:S(2)}, u32[]{:S(2)}) collective-permute-start(f32[12,4]{1,0:T(8,128)S(1)} %get-tuple-element.143), channel_id=1, source_target_pairs={{1,0},{2,1},{3,2},{4,3},{5,4},{6,5},{7,6},{0,7},{9,8},{10,9},{11,1... | collective-permute-start | bytes 584 | tf_op jit(solution)/shard_map/ppermute | solution.py:67
  86.5 4.9 %collective-permute-start.2 = (f32[2,12,4]{2,0,1:T(2,128)S(1)}, f32[2,12,4]{2,0,1:T(2,128)S(1)}, u32[]{:S(2)}, u32[]{:S(2)}) collective-permute-start(f32[2,12,4]{2,0,1:T(2,128)S(1)} %get-tuple-element.134), channel_id=1, source_target_pairs={{0,1},{1,2},{2,3},{3,4},{4,5},{5,6},{6,7},{7,0},{8,9},{9,10},{10,1... | collective-permute-start | bytes 1160 | tf_op jit(solution)/shard_map/ppermute | solution.py:66
  86.6 4.9 %collective-permute-start.3 = (f32[2,12,4]{2,0,1:T(2,128)S(1)}, f32[2,12,4]{2,0,1:T(2,128)S(1)}, u32[]{:S(2)}, u32[]{:S(2)}) collective-permute-start(f32[2,12,4]{2,0,1:T(2,128)S(1)} %get-tuple-element.135), channel_id=1, source_target_pairs={{1,0},{2,1},{3,2},{4,3},{5,4},{6,5},{7,6},{0,7},{9,8},{10,9},{11,1... | collective-permute-start | bytes 1160 | tf_op jit(solution)/shard_map/ppermute | solution.py:67
  98.8 1.3 collective-permute-start.8
  100.1 4.9 %collective-permute-start.11 = (f32[61,128]{1,0:T(8,128)S(1)}, f32[61,128]{1,0:T(8,128)S(1)}, u32[]{:S(2)}, u32[]{:S(2)}) collective-permute-start(f32[61,128]{1,0:T(8,128)S(1)} %fusion.238), channel_id=1, source_target_pairs={{0,24},{1,25},{2,26},{3,27},{4,28},{5,29},{6,30},{7,31},{8,16},{9,... | collective-permute-start | bytes 93704 | tf_op jit(solution)/shard_map/ppermute | solution.py:22
  102.6 3.9 %collective-permute-start.10 = (f32[61,128]{1,0:T(8,128)S(1)}, f32[61,128]{1,0:T(8,128)S(1)}, u32[]{:S(2)}, u32[]{:S(2)}) collective-permute-start(f32[61,128]{1,0:T(8,128)S(1)} %fusion.238), channel_id=1, source_target_pairs={{0,16},{1,17},{2,18},{3,19},{4,20},{5,21},{6,22},{7,23},{8,24},{9,... | collective-permute-start | bytes 93704 | tf_op jit(solution)/shard_map/ppermute | solution.py:22
  103.1 3.9 %collective-permute-start.9 = (f32[61,128]{1,0:T(8,128)S(1)}, f32[61,128]{1,0:T(8,128)S(1)}, u32[]{:S(2)}, u32[]{:S(2)}) collective-permute-start(f32[61,128]{1,0:T(8,128)S(1)} %fusion.238), channel_id=1, source_target_pairs={{0,8},{1,9},{2,10},{3,11},{4,12},{5,13},{6,14},{7,15},{8,0},{9,1},... | collective-permute-start | bytes 93704 | tf_op jit(solution)/shard_map/ppermute | solution.py:22
  107.0 5.8 %collective-permute-start.14 = (f32[61,128]{1,0:T(8,128)S(1)}, f32[61,128]{1,0:T(8,128)S(1)}, u32[]{:S(2)}, u32[]{:S(2)}) collective-permute-start(f32[61,128]{1,0:T(8,128)S(1)} %add_add_fusion.7), channel_id=1, source_target_pairs={{0,6},{1,7},{2,4},{3,5},{4,2},{5,3},{6,0},{7,1},{8,14},{9,15},{10,... | collective-permute-start | bytes 93704 | tf_op jit(solution)/shard_map/ppermute | solution.py:22
  110.6 4.8 %collective-permute-start.13 = (f32[61,128]{1,0:T(8,128)S(1)}, f32[61,128]{1,0:T(8,128)S(1)}, u32[]{:S(2)}, u32[]{:S(2)}) collective-permute-start(f32[61,128]{1,0:T(8,128)S(1)} %add_add_fusion.7), channel_id=1, source_target_pairs={{0,4},{1,5},{2,6},{3,7},{4,0},{5,1},{6,2},{7,3},{8,12},{9,13},{10,... | collective-permute-start | bytes 93704 | tf_op jit(solution)/shard_map/ppermute | solution.py:22
  110.6 4.8 %collective-permute-start.12 = (f32[61,128]{1,0:T(8,128)S(1)}, f32[61,128]{1,0:T(8,128)S(1)}, u32[]{:S(2)}, u32[]{:S(2)}) collective-permute-start(f32[61,128]{1,0:T(8,128)S(1)} %add_add_fusion.7), channel_id=1, source_target_pairs={{0,2},{1,3},{2,0},{3,1},{4,6},{5,7},{6,4},{7,5},{8,10},{9,11},{10,... | collective-permute-start | bytes 93704 | tf_op jit(solution)/shard_map/ppermute | solution.py:22
  126.9 10.1 %copy-start.5 = (bf16[4,128,3840]{2,1,0:T(8,128)(2,1)S(1)}, bf16[4,128,3840]{2,1,0:T(8,128)(2,1)}, u32[]{:S(2)}) copy-start(bf16[4,128,3840]{2,1,0:T(8,128)(2,1)} %param.21) | copy-start | bytes 11796484
  159.3 3.1 copy-start.2
  174.3 4.6 %collective-permute-start.16 = (f32[2,4,128]{2,0,1:T(2,128)S(1)}, f32[2,4,128]{2,0,1:T(2,128)S(1)}, u32[]{:S(2)}, u32[]{:S(2)}) collective-permute-start(f32[2,4,128]{2,0,1:T(2,128)S(1)} %maximum_multiply_fusion.2), channel_id=1, source_target_pairs={{0,24},{1,25},{2,26},{3,27},{4,28},{5,29},{6,30},{7,31},{8,16},{9,... | collective-permute-start | bytes 12296 | tf_op jit(solution)/shard_map/ppermute | solution.py:58
  175.8 3.6 collective-permute-start.15
  179.5 5.0 %collective-permute-start.17 = (f32[2,12,4]{2,0,1:T(2,128)S(1)}, f32[2,12,4]{2,0,1:T(2,128)S(1)}, u32[]{:S(2)}, u32[]{:S(2)}) collective-permute-start(f32[2,12,4]{2,0,1:T(2,128)S(1)} %get-tuple-element.132), channel_id=1, source_target_pairs={{0,1},{1,2},{2,3},{3,4},{4,5},{5,6},{6,7},{7,0},{8,9},{9,10},{10,1... | collective-permute-start | bytes 1160 | tf_op jit(solution)/shard_map/ppermute | solution.py:66
  179.5 5.0 %collective-permute-start.18 = (f32[2,12,4]{2,0,1:T(2,128)S(1)}, f32[2,12,4]{2,0,1:T(2,128)S(1)}, u32[]{:S(2)}, u32[]{:S(2)}) collective-permute-start(f32[2,12,4]{2,0,1:T(2,128)S(1)} %get-tuple-element.133), channel_id=1, source_target_pairs={{1,0},{2,1},{3,2},{4,3},{5,4},{6,5},{7,6},{0,7},{9,8},{10,9},{11,1... | collective-permute-start | bytes 1160 | tf_op jit(solution)/shard_map/ppermute | solution.py:67
  191.5 1.3 collective-permute-start.19
  192.8 4.9 %collective-permute-start.22 = (f32[61,128]{1,0:T(8,128)S(1)}, f32[61,128]{1,0:T(8,128)S(1)}, u32[]{:S(2)}, u32[]{:S(2)}) collective-permute-start(f32[61,128]{1,0:T(8,128)S(1)} %fusion.237), channel_id=1, source_target_pairs={{0,24},{1,25},{2,26},{3,27},{4,28},{5,29},{6,30},{7,31},{8,16},{9,... | collective-permute-start | bytes 93704 | tf_op jit(solution)/shard_map/ppermute | solution.py:22
  194.3 3.9 %collective-permute-start.21 = (f32[61,128]{1,0:T(8,128)S(1)}, f32[61,128]{1,0:T(8,128)S(1)}, u32[]{:S(2)}, u32[]{:S(2)}) collective-permute-start(f32[61,128]{1,0:T(8,128)S(1)} %fusion.237), channel_id=1, source_target_pairs={{0,16},{1,17},{2,18},{3,19},{4,20},{5,21},{6,22},{7,23},{8,24},{9,... | collective-permute-start | bytes 93704 | tf_op jit(solution)/shard_map/ppermute | solution.py:22
  195.8 3.9 %collective-permute-start.20 = (f32[61,128]{1,0:T(8,128)S(1)}, f32[61,128]{1,0:T(8,128)S(1)}, u32[]{:S(2)}, u32[]{:S(2)}) collective-permute-start(f32[61,128]{1,0:T(8,128)S(1)} %fusion.237), channel_id=1, source_target_pairs={{0,8},{1,9},{2,10},{3,11},{4,12},{5,13},{6,14},{7,15},{8,0},{9,1},... | collective-permute-start | bytes 93704 | tf_op jit(solution)/shard_map/ppermute | solution.py:22
  199.8 5.9 %collective-permute-start.25 = (f32[61,128]{1,0:T(8,128)S(1)}, f32[61,128]{1,0:T(8,128)S(1)}, u32[]{:S(2)}, u32[]{:S(2)}) collective-permute-start(f32[61,128]{1,0:T(8,128)S(1)} %add_add_fusion.5), channel_id=1, source_target_pairs={{0,6},{1,7},{2,4},{3,5},{4,2},{5,3},{6,0},{7,1},{8,14},{9,15},{10,... | collective-permute-start | bytes 93704 | tf_op jit(solution)/shard_map/ppermute | solution.py:22
  203.3 4.8 %collective-permute-start.24 = (f32[61,128]{1,0:T(8,128)S(1)}, f32[61,128]{1,0:T(8,128)S(1)}, u32[]{:S(2)}, u32[]{:S(2)}) collective-permute-start(f32[61,128]{1,0:T(8,128)S(1)} %add_add_fusion.5), channel_id=1, source_target_pairs={{0,4},{1,5},{2,6},{3,7},{4,0},{5,1},{6,2},{7,3},{8,12},{9,13},{10,... | collective-permute-start | bytes 93704 | tf_op jit(solution)/shard_map/ppermute | solution.py:22
  203.3 4.8 %collective-permute-start.23 = (f32[61,128]{1,0:T(8,128)S(1)}, f32[61,128]{1,0:T(8,128)S(1)}, u32[]{:S(2)}, u32[]{:S(2)}) collective-permute-start(f32[61,128]{1,0:T(8,128)S(1)} %add_add_fusion.5), channel_id=1, source_target_pairs={{0,2},{1,3},{2,0},{3,1},{4,6},{5,7},{6,4},{7,5},{8,10},{9,11},{10,... | collective-permute-start | bytes 93704 | tf_op jit(solution)/shard_map/ppermute | solution.py:22
  219.7 10.1 %copy-start.6 = (bf16[4,128,3840]{2,1,0:T(8,128)(2,1)S(1)}, bf16[4,128,3840]{2,1,0:T(8,128)(2,1)}, u32[]{:S(2)}) copy-start(bf16[4,128,3840]{2,1,0:T(8,128)(2,1)} %param.21) | copy-start | bytes 11796484
  240.5 3.1 copy-start.3
  255.4 4.6 %collective-permute-start.27 = (f32[2,4,128]{2,0,1:T(2,128)S(1)}, f32[2,4,128]{2,0,1:T(2,128)S(1)}, u32[]{:S(2)}, u32[]{:S(2)}) collective-permute-start(f32[2,4,128]{2,0,1:T(2,128)S(1)} %maximum_multiply_fusion.3), channel_id=1, source_target_pairs={{0,24},{1,25},{2,26},{3,27},{4,28},{5,29},{6,30},{7,31},{8,16},{9,... | collective-permute-start | bytes 12296 | tf_op jit(solution)/shard_map/ppermute | solution.py:58
  256.4 3.6 collective-permute-start.26
  260.1 5.0 %collective-permute-start.28 = (f32[2,12,4]{2,0,1:T(2,128)S(1)}, f32[2,12,4]{2,0,1:T(2,128)S(1)}, u32[]{:S(2)}, u32[]{:S(2)}) collective-permute-start(f32[2,12,4]{2,0,1:T(2,128)S(1)} %get-tuple-element.130), channel_id=1, source_target_pairs={{0,1},{1,2},{2,3},{3,4},{4,5},{5,6},{6,7},{7,0},{8,9},{9,10},{10,1... | collective-permute-start | bytes 1160 | tf_op jit(solution)/shard_map/ppermute | solution.py:66
  260.1 5.0 %collective-permute-start.29 = (f32[2,12,4]{2,0,1:T(2,128)S(1)}, f32[2,12,4]{2,0,1:T(2,128)S(1)}, u32[]{:S(2)}, u32[]{:S(2)}) collective-permute-start(f32[2,12,4]{2,0,1:T(2,128)S(1)} %get-tuple-element.131), channel_id=1, source_target_pairs={{1,0},{2,1},{3,2},{4,3},{5,4},{6,5},{7,6},{0,7},{9,8},{10,9},{11,1... | collective-permute-start | bytes 1160 | tf_op jit(solution)/shard_map/ppermute | solution.py:67
  272.1 1.3 collective-permute-start.30
  273.4 5.0 %collective-permute-start.33 = (f32[61,128]{1,0:T(8,128)S(1)}, f32[61,128]{1,0:T(8,128)S(1)}, u32[]{:S(2)}, u32[]{:S(2)}) collective-permute-start(f32[61,128]{1,0:T(8,128)S(1)} %fusion.236), channel_id=1, source_target_pairs={{0,24},{1,25},{2,26},{3,27},{4,28},{5,29},{6,30},{7,31},{8,16},{9,... | collective-permute-start | bytes 93704 | tf_op jit(solution)/shard_map/ppermute | solution.py:22
  275.5 3.9 %collective-permute-start.32 = (f32[61,128]{1,0:T(8,128)S(1)}, f32[61,128]{1,0:T(8,128)S(1)}, u32[]{:S(2)}, u32[]{:S(2)}) collective-permute-start(f32[61,128]{1,0:T(8,128)S(1)} %fusion.236), channel_id=1, source_target_pairs={{0,16},{1,17},{2,18},{3,19},{4,20},{5,21},{6,22},{7,23},{8,24},{9,... | collective-permute-start | bytes 93704 | tf_op jit(solution)/shard_map/ppermute | solution.py:22
  276.0 3.9 %collective-permute-start.31 = (f32[61,128]{1,0:T(8,128)S(1)}, f32[61,128]{1,0:T(8,128)S(1)}, u32[]{:S(2)}, u32[]{:S(2)}) collective-permute-start(f32[61,128]{1,0:T(8,128)S(1)} %fusion.236), channel_id=1, source_target_pairs={{0,8},{1,9},{2,10},{3,11},{4,12},{5,13},{6,14},{7,15},{8,0},{9,1},... | collective-permute-start | bytes 93704 | tf_op jit(solution)/shard_map/ppermute | solution.py:22
  279.9 5.9 %collective-permute-start.36 = (f32[61,128]{1,0:T(8,128)S(1)}, f32[61,128]{1,0:T(8,128)S(1)}, u32[]{:S(2)}, u32[]{:S(2)}) collective-permute-start(f32[61,128]{1,0:T(8,128)S(1)} %add_add_fusion.3), channel_id=1, source_target_pairs={{0,6},{1,7},{2,4},{3,5},{4,2},{5,3},{6,0},{7,1},{8,14},{9,15},{10,... | collective-permute-start | bytes 93704 | tf_op jit(solution)/shard_map/ppermute | solution.py:22
  283.4 4.8 %collective-permute-start.35 = (f32[61,128]{1,0:T(8,128)S(1)}, f32[61,128]{1,0:T(8,128)S(1)}, u32[]{:S(2)}, u32[]{:S(2)}) collective-permute-start(f32[61,128]{1,0:T(8,128)S(1)} %add_add_fusion.3), channel_id=1, source_target_pairs={{0,4},{1,5},{2,6},{3,7},{4,0},{5,1},{6,2},{7,3},{8,12},{9,13},{10,... | collective-permute-start | bytes 93704 | tf_op jit(solution)/shard_map/ppermute | solution.py:22
  283.4 4.8 %collective-permute-start.34 = (f32[61,128]{1,0:T(8,128)S(1)}, f32[61,128]{1,0:T(8,128)S(1)}, u32[]{:S(2)}, u32[]{:S(2)}) collective-permute-start(f32[61,128]{1,0:T(8,128)S(1)} %add_add_fusion.3), channel_id=1, source_target_pairs={{0,2},{1,3},{2,0},{3,1},{4,6},{5,7},{6,4},{7,5},{8,10},{9,11},{10,... | collective-permute-start | bytes 93704 | tf_op jit(solution)/shard_map/ppermute | solution.py:22
  297.1 10.5 %copy-start.7 = (bf16[4,128,3840]{2,1,0:T(8,128)(2,1)S(1)}, bf16[4,128,3840]{2,1,0:T(8,128)(2,1)}, u32[]{:S(2)}) copy-start(bf16[4,128,3840]{2,1,0:T(8,128)(2,1)} %param.21) | copy-start | bytes 11796484
  318.4 3.1 copy-start.1
  333.3 4.6 %collective-permute-start.38 = (f32[2,4,128]{2,0,1:T(2,128)S(1)}, f32[2,4,128]{2,0,1:T(2,128)S(1)}, u32[]{:S(2)}, u32[]{:S(2)}) collective-permute-start(f32[2,4,128]{2,0,1:T(2,128)S(1)} %maximum_multiply_fusion.4), channel_id=1, source_target_pairs={{0,24},{1,25},{2,26},{3,27},{4,28},{5,29},{6,30},{7,31},{8,16},{9,... | collective-permute-start | bytes 12296 | tf_op jit(solution)/shard_map/ppermute | solution.py:58
  334.9 3.6 collective-permute-start.37
  338.6 5.0 %collective-permute-start.39 = (f32[2,12,4]{2,0,1:T(2,128)S(1)}, f32[2,12,4]{2,0,1:T(2,128)S(1)}, u32[]{:S(2)}, u32[]{:S(2)}) collective-permute-start(f32[2,12,4]{2,0,1:T(2,128)S(1)} %get-tuple-element.128), channel_id=1, source_target_pairs={{0,1},{1,2},{2,3},{3,4},{4,5},{5,6},{6,7},{7,0},{8,9},{9,10},{10,1... | collective-permute-start | bytes 1160 | tf_op jit(solution)/shard_map/ppermute | solution.py:66
  338.6 5.0 %collective-permute-start.40 = (f32[2,12,4]{2,0,1:T(2,128)S(1)}, f32[2,12,4]{2,0,1:T(2,128)S(1)}, u32[]{:S(2)}, u32[]{:S(2)}) collective-permute-start(f32[2,12,4]{2,0,1:T(2,128)S(1)} %get-tuple-element.129), channel_id=1, source_target_pairs={{1,0},{2,1},{3,2},{4,3},{5,4},{6,5},{7,6},{0,7},{9,8},{10,9},{11,1... | collective-permute-start | bytes 1160 | tf_op jit(solution)/shard_map/ppermute | solution.py:67
  350.8 1.3 collective-permute-start.41
  352.1 4.9 %collective-permute-start.44 = (f32[61,128]{1,0:T(8,128)S(1)}, f32[61,128]{1,0:T(8,128)S(1)}, u32[]{:S(2)}, u32[]{:S(2)}) collective-permute-start(f32[61,128]{1,0:T(8,128)S(1)} %fusion.235), channel_id=1, source_target_pairs={{0,24},{1,25},{2,26},{3,27},{4,28},{5,29},{6,30},{7,31},{8,16},{9,... | collective-permute-start | bytes 93704 | tf_op jit(solution)/shard_map/ppermute | solution.py:22
  353.6 3.9 %collective-permute-start.43 = (f32[61,128]{1,0:T(8,128)S(1)}, f32[61,128]{1,0:T(8,128)S(1)}, u32[]{:S(2)}, u32[]{:S(2)}) collective-permute-start(f32[61,128]{1,0:T(8,128)S(1)} %fusion.235), channel_id=1, source_target_pairs={{0,16},{1,17},{2,18},{3,19},{4,20},{5,21},{6,22},{7,23},{8,24},{9,... | collective-permute-start | bytes 93704 | tf_op jit(solution)/shard_map/ppermute | solution.py:22
  355.1 3.9 %collective-permute-start.42 = (f32[61,128]{1,0:T(8,128)S(1)}, f32[61,128]{1,0:T(8,128)S(1)}, u32[]{:S(2)}, u32[]{:S(2)}) collective-permute-start(f32[61,128]{1,0:T(8,128)S(1)} %fusion.235), channel_id=1, source_target_pairs={{0,8},{1,9},{2,10},{3,11},{4,12},{5,13},{6,14},{7,15},{8,0},{9,1},... | collective-permute-start | bytes 93704 | tf_op jit(solution)/shard_map/ppermute | solution.py:22
  359.0 5.9 %collective-permute-start.47 = (f32[61,128]{1,0:T(8,128)S(1)}, f32[61,128]{1,0:T(8,128)S(1)}, u32[]{:S(2)}, u32[]{:S(2)}) collective-permute-start(f32[61,128]{1,0:T(8,128)S(1)} %add_add_fusion.1), channel_id=1, source_target_pairs={{0,6},{1,7},{2,4},{3,5},{4,2},{5,3},{6,0},{7,1},{8,14},{9,15},{10,... | collective-permute-start | bytes 93704 | tf_op jit(solution)/shard_map/ppermute | solution.py:22
  362.6 4.8 %collective-permute-start.46 = (f32[61,128]{1,0:T(8,128)S(1)}, f32[61,128]{1,0:T(8,128)S(1)}, u32[]{:S(2)}, u32[]{:S(2)}) collective-permute-start(f32[61,128]{1,0:T(8,128)S(1)} %add_add_fusion.1), channel_id=1, source_target_pairs={{0,4},{1,5},{2,6},{3,7},{4,0},{5,1},{6,2},{7,3},{8,12},{9,13},{10,... | collective-permute-start | bytes 93704 | tf_op jit(solution)/shard_map/ppermute | solution.py:22
  362.6 4.8 %collective-permute-start.45 = (f32[61,128]{1,0:T(8,128)S(1)}, f32[61,128]{1,0:T(8,128)S(1)}, u32[]{:S(2)}, u32[]{:S(2)}) collective-permute-start(f32[61,128]{1,0:T(8,128)S(1)} %add_add_fusion.1), channel_id=1, source_target_pairs={{0,2},{1,3},{2,0},{3,1},{4,6},{5,7},{6,4},{7,5},{8,10},{9,11},{10,... | collective-permute-start | bytes 93704 | tf_op jit(solution)/shard_map/ppermute | solution.py:22

commit v2 on v1

v2 whole, which is shorter than its diff:
```python
import functools

import jax
import jax.numpy as jnp
from jax import lax
from jax.experimental import pallas as pl
from jax.experimental.pallas import tpu as pltpu
from jax.sharding import PartitionSpec as P

STEPS = 4
SWEEPS = 4
PAIRS = 2 * STEPS
BITS = 15
LANES = 128

KLAT = 0.2
KLON = 0.05
EPS = 1e-06
F32 = jnp.float32
BF16 = jnp.bfloat16
VMEM = pl.BlockSpec(memory_space=pltpu.VMEM)
SMEM = pl.BlockSpec(memory_space=pltpu.SMEM)
NT = (((1,), (1,)), ((), ()))


def pairing(lat_map, lon_map):
    nlat, nlon = (lax.axis_size("lat"), lax.axis_size("lon"))
    return [(i * nlon + j, lat_map(i) * nlon + lon_map(j)) for i in range(nlat) for j in range(nlon)]


def swap(x, lat_bits, lon_bits):
    return lax.ppermute(x, ("lat", "lon"), pairing(lambda i: i ^ lat_bits, lambda j: j ^ lon_bits))


def sum_all(x):
    nlat, nlon = (lax.axis_size("lat"), lax.axis_size("lon"))
    if nlat & (nlat - 1) or nlon & (nlon - 1):
        return lax.psum(x, ("lat", "lon"))
    if nlon > 1:
        x = x + swap(x, 0, 1)
    for size, first, on_lat in ((nlat, 1, True), (nlon, 2, False)):
        bit = first
        while bit < size:
            bits = lambda b: (b, 0) if on_lat else (0, b)
            if 2 * bit < size:
                near, far, both = (swap(x, *bits(b)) for b in (bit, 2 * bit, 3 * bit))
                x = (x + near) + (far + both)
                bit *= 4
            else:
                x = x + swap(x, *bits(bit))
                bit *= 2
    return x


def lat_partners(x):
    count = lax.axis_size("lat")
    same = lambda j: j
    got_a = lax.ppermute(x, ("lat", "lon"), pairing(lambda i: i ^ 1, same))
    got_b = lax.ppermute(x, ("lat", "lon"), pairing(lambda i: (i + 1 if i % 2 else i - 1) % count, same))
    return got_a, got_b


def lon_ring(to_west, to_east):
    count = lax.axis_size("lon")
    up = [(i, (i + 1) % count) for i in range(count)]
    return lax.ppermute(to_east, "lon", up), lax.ppermute(to_west, "lon", [(j, i) for i, j in up])


def split(x):
    high = x.astype(BF16)
    return high, (x - high.astype(F32)).astype(BF16)


def solve_pair(g00, g01, g10, g11, right0, right1):
    determ = g00 * g11 - g01 * g10
    return (g11 * right0 - g01 * right1) / determ, (g00 * right1 - g10 * right0) / determ


def total_of(x):
    return jnp.sum(x, axis=1, keepdims=True)


def lane_ids(shape):
    return lax.broadcasted_iota(jnp.int32, shape, 1)


def to_block(field, rows, reach):
    n, own = (field.shape[0], rows * LANES)
    halo = field[:, own:]
    lane = lane_ids((n, LANES))
    parts = []
    for r in range(rows):
        east = pltpu.roll(halo, (LANES - rows * reach - reach * r) % LANES, 1)
        west = pltpu.roll(halo, (LANES - reach - reach * r) % LANES, 1)
        edge = jnp.where(lane < LANES // 2, east, west)
        parts.append(jnp.concatenate([field[:, r * LANES : (r + 1) * LANES], edge], axis=1))
    return jnp.concatenate(parts, axis=0)


def from_block(block, rows, reach):
    n = block.shape[0] // rows
    lane = lane_ids((n, LANES))
    halo = jnp.zeros((n, LANES), F32)
    own = []
    for r in range(rows):
        part = block[r * n : (r + 1) * n]
        own.append(part[:, :LANES])
        edge = part[:, LANES:]
        east = pltpu.roll(edge, (rows * reach + reach * r) % LANES, 1)
        west = pltpu.roll(edge, (reach * r + reach) % LANES, 1)
        first = reach * r
        halo = jnp.where((lane >= first) & (lane < first + reach), west, halo)
        first = rows * reach + reach * r
        halo = jnp.where((lane >= first) & (lane < first + reach), east, halo)
    return jnp.concatenate(own + [halo], axis=1)


def unpack_words(words, spread_ref, bit_ref):
    top = ((words >> 8) << 8).astype(F32).astype(BF16)
    bottom = (words & 255).astype(F32).astype(BF16)
    spread = spread_ref[...]
    each = jnp.dot(jnp.concatenate([top, bottom], axis=1), spread, preferred_element_type=F32).astype(jnp.int32)
    return jnp.where((each & bit_ref[...]) == 0, 1.0, 0.0).astype(BF16)


def fill_spread(spread_ref, bit_ref):
    days = spread_ref.shape[1]
    word = lax.broadcasted_iota(jnp.int32, (LANES, days), 0)
    rest = lane_ids((LANES, days)) - BITS * word
    hit = jnp.where((rest >= 0) & (rest < BITS), 1.0, 0.0).astype(BF16)
    spread_ref[:LANES] = hit
    spread_ref[LANES:] = hit
    word = jnp.where((rest >= 0) & (rest < BITS), rest, 0)
    bit_ref[...] = jnp.left_shift(1, jnp.sum(word, axis=0, keepdims=True))


def own_flags_kernel(words_ref, coast_ref, x_ref, m_ref, a_ref, spread_ref, bit_ref):
    @pl.when(pl.program_id(0) == 0)
    def _():
        fill_spread(spread_ref, bit_ref)

    coast = coast_ref[...]
    ocean = coast.astype(F32).astype(BF16)
    days = spread_ref.shape[1]
    for g in range(words_ref.shape[1] // LANES):
        words = words_ref[:, g * LANES : (g + 1) * LANES] * coast
        given = unpack_words(words, spread_ref, bit_ref)
        at = slice(g * days, (g + 1) * days)
        m_ref[:, at] = given
        a_ref[:, at] = x_ref[:, at] * given * ocean


def halo_flags_kernel(words_ref, coast_ref, m_ref, spread_ref, bit_ref):
    fill_spread(spread_ref, bit_ref)
    coast = coast_ref[...]
    days = spread_ref.shape[1]
    for g in range(words_ref.shape[1] // LANES):
        words = words_ref[:, g * LANES : (g + 1) * LANES] * coast
        m_ref[:, g * days : (g + 1) * days] = unpack_words(words, spread_ref, bit_ref)


def given_kernel(rows, reach, v_ref, a_ref, xv_ref, west_ref, east_ref):
    high, low = split(v_ref[:PAIRS])
    both = lax.dot_general(jnp.concatenate([high, low], axis=0), a_ref[...], NT, preferred_element_type=F32)
    xv = both[:PAIRS] + both[PAIRS:]
    xv_ref[...] = xv
    lane = lane_ids((PAIRS, LANES))
    west = jnp.zeros((PAIRS, LANES), F32)
    east = west
    for r in range(rows):
        part = xv[:, r * LANES : (r + 1) * LANES]
        first = rows * reach + reach * r
        west = jnp.where((lane >= first) & (lane < first + reach), pltpu.roll(part, first % LANES, 1), west)
        first = reach * r
        east = jnp.where((lane >= first) & (lane < first + reach), pltpu.roll(part, (first + reach) % LANES, 1), east)
    west_ref[...] = west
    east_ref[...] = east


def fields_kernel(step, rows, reach, total, chunk, *refs):
    m_ref, mh_ref, v_ref, u_ref, coast_ref, xv_ref, xw_ref, xe_ref = refs[:8]
    refs = refs[8:]
    older = refs[: 2 * max(step - 1, 0)]
    refs = refs[len(older) :]
    if step:
        sum_ref, block_ref = refs[:2]
        w_ref, vn_ref, un_ref, vs, us = refs[2:]
    else:
        w_ref, vs, us = refs
    days = v_ref.shape[1]
    low = 2 * step
    vs[...] = v_ref[...]
    us[...] = u_ref[...]
    for q in range(step - 1):
        vs[2 * q : 2 * q + 2] = older[2 * q][...]
        us[2 * q : 2 * q + 2] = older[2 * q + 1][...]
    if step:
        vn, un = new_pair(rows, reach, total, sum_ref, block_ref)
        vn_ref[...] = vn
        un_ref[...] = un
        vs[low - 2 : low] = vn
        us[low - 2 : low] = un
    modes = vs.shape[0]
    acc = accH = None
    for first in range(0, days, chunk):
        at = slice(first, first + chunk)
        v = vs[:, at]
        parts = []
        for j in (low, low + 1):
            parts.append(v * v[j : j + 1])
        high, lower = split(jnp.concatenate(parts, axis=0))
        left = jnp.concatenate([high, lower], axis=0)
        own = lax.dot_general(left, m_ref[:, at], NT, preferred_element_type=F32)
        halo = lax.dot_general(left, mh_ref[:, at], NT, preferred_element_type=F32)
        acc = own if acc is None else acc + own
        accH = halo if accH is None else accH + halo
    masked = jnp.concatenate([acc[: 2 * modes] + acc[2 * modes :], accH[: 2 * modes] + accH[2 * modes :]], axis=1)
    lane = lane_ids((PAIRS, LANES))
    xh = jnp.where(lane < LANES // 2, xw_ref[...], xe_ref[...])
    xv = jnp.concatenate([xv_ref[...], xh], axis=1)
    u = us[...]
    proj = [
        xv[low + j : low + j + 1] - jnp.sum(u * masked[j * modes : (j + 1) * modes], axis=0, keepdims=True)
        for j in range(2)
    ]
    v0, v1 = (vs[low : low + 1], vs[low + 1 : low + 2])
    h00, h01, h11 = (total_of(v0 * v0), total_of(v0 * v1), total_of(v1 * v1))
    add0, add1 = solve_pair(h00, h01, h01, h11, proj[0], proj[1])
    coast = coast_ref[...]
    fresh = coast * jnp.concatenate([u[low : low + 1] + add0, u[low + 1 : low + 2] + add1], axis=0)
    count = 2 * rows
    w_ref[:count] = to_block(fresh, rows, reach)
    if step == 0:
        w_ref[count:] = to_block(jnp.concatenate([coast, coast], axis=0), rows, reach)


def new_pair(rows, reach, total, sum_ref, block_ref):
    days = sum_ref.shape[1] - LANES
    gram = sum_ref[:, days:]
    g00, g01, g11 = (gram[0:1, 0:1], gram[0:1, 1:2], gram[1:2, 1:2])
    n0, n1 = (jnp.sqrt(g00 / total + EPS), jnp.sqrt(g11 / total + EPS))
    first, second = solve_pair(
        g00 / (n0 * n0),
        g01 / (n0 * n1),
        g01 / (n0 * n1),
        g11 / (n1 * n1),
        sum_ref[0:1, :days] / n0,
        sum_ref[1:2, :days] / n1,
    )
    field = from_block(block_ref[...], rows, reach)
    unit = jnp.concatenate([field[0:1] / n0, field[1:2] / n1], axis=0)
    return jnp.concatenate([first, second], axis=0), unit


def sums_kernel(step, rows, chunk, *refs):
    m_ref, a_ref, v_ref, u_ref, place_ref, klon_ref, cosl_ref, w_ref, ga_ref, gb_ref = refs[:10]
    refs = refs[10:]
    if step:
        cw_ref, ca_ref, cb_ref = refs[:3]
        refs = refs[3:]
    older = refs[: 2 * step]
    sum_ref, block_ref, vs, us = refs[2 * step :]
    days = v_ref.shape[1]
    low = 2 * step
    own = rows * LANES
    vs[...] = v_ref[...]
    us[...] = u_ref[:, :own]
    for q in range(step):
        vs[2 * q : 2 * q + 2] = older[2 * q][...]
        us[2 * q : 2 * q + 2] = older[2 * q + 1][:, :own]
    count = 2 * rows
    row0, nlat, odd = (place_ref[0], place_ref[1], place_ref[2])

    def assemble(mid, a, b):
        is_odd = odd == 1
        return jnp.concatenate([jnp.where(is_odd, a, b), mid, jnp.where(is_odd, b, a)], axis=0)

    w = assemble(w_ref[:count], ga_ref[:count], gb_ref[:count])
    if step:
        coast = assemble(cw_ref[count:], ca_ref[count:], cb_ref[count:])
    else:
        coast = assemble(w_ref[count:], ga_ref[count:], gb_ref[count:])
    tall = 3 * count
    row = row0 - rows + lax.broadcasted_iota(jnp.int32, (tall, 2 * LANES), 0) // 2
    coast = jnp.where((row >= 0) & (row < nlat), coast, 0.0)
    north = lambda z: pltpu.roll(z, 2, 0)
    south = lambda z: pltpu.roll(z, tall - 2, 0)
    west = lambda z: pltpu.roll(z, 1, 1)
    east = lambda z: pltpu.roll(z, 2 * LANES - 1, 1)
    cn, cs, cw, ce = (north(coast), south(coast), west(coast), east(coast))
    klon = klon_ref[...]
    for _ in range(SWEEPS):
        flux = KLAT * (cn * (north(w) - w) + cs * (south(w) - w)) + klon * (cw * (west(w) - w) + ce * (east(w) - w))
        w = w + coast * flux
    block = w[count : 2 * count]
    block_ref[...] = block
    cells = lambda z: jnp.concatenate([z[2 * r : 2 * r + 2, :LANES] for r in range(rows)], axis=1)
    fresh = cells(block)
    weighted = cells(block * cosl_ref[...])
    u = us[...]
    modes = u.shape[0]
    high, lower = split(jnp.concatenate([u * weighted[0:1], u * weighted[1:2]], axis=0))
    left = jnp.concatenate([high, lower], axis=0)
    high, lower = split(weighted)
    left_a = jnp.concatenate([high, lower], axis=0)
    lane = lane_ids((1, LANES))
    for j in range(2):
        gram = [total_of(weighted[j : j + 1] * fresh[i : i + 1]) for i in range(2)]
        sum_ref[j : j + 1, days:] = jnp.where(lane == 0, gram[0], jnp.where(lane == 1, gram[1], 0.0))
    old = [[total_of(weighted[j : j + 1] * u[low + i : low + i + 1]) for i in range(2)] for j in range(2)]
    for first in range(0, days, chunk):
        at = slice(first, first + chunk)
        masked = jnp.dot(left, m_ref[:, at], preferred_element_type=F32)
        given = jnp.dot(left_a, a_ref[:, at], preferred_element_type=F32)
        v = vs[:, at]
        for j in range(2):
            part = masked[j * modes : (j + 1) * modes] + masked[(2 + j) * modes : (3 + j) * modes]
            sum_ref[j : j + 1, at] = (
                given[j : j + 1]
                + given[2 + j : 3 + j]
                - jnp.sum(v * part, axis=0, keepdims=True)
                + old[j][0] * v[low : low + 1]
                + old[j][1] * v[low + 1 : low + 2]
            )


def last_kernel(rows, reach, total, sum_ref, block_ref, vn_ref, un_ref):
    vn, un = new_pair(rows, reach, total, sum_ref, block_ref)
    vn_ref[...] = vn
    un_ref[...] = un


def call(kernel, name, outs, scratch, args, smem=(), mib=24):
    return pl.pallas_call(
        kernel,
        out_shape=[jax.ShapeDtypeStruct(s, t) for s, t in outs],
        in_specs=[SMEM if i in smem else VMEM for i in range(len(args))],
        out_specs=[VMEM for _ in outs],
        scratch_shapes=[pltpu.VMEM(s, t) for s, t in scratch],
        compiler_params=pltpu.CompilerParams(vmem_limit_bytes=mib * 2**20),
        name=name,
    )(*args)


def latitude_cos(rows, nrows):
    degree = -60.0 + 120.0 * (rows.astype(F32) + 0.5) / nrows
    return jnp.cos(degree * (jnp.pi / 180.0))


def shards(sea_heat_deviations, missing_date_bitmask, ocean_binary_mask, mode_maps, mode_series):
    rows, columns, days = sea_heat_deviations.shape
    modes, words = (mode_maps.shape[0], missing_date_bitmask.shape[2])
    nlat = rows * lax.axis_size("lat")
    total = float(modes * nlat * columns * lax.axis_size("lon"))
    own, reach = (rows * columns, SWEEPS * STEPS)
    sides = 2 * rows * reach
    cells = own + sides
    assert columns == LANES and sides == LANES and rows == SWEEPS and days == BITS * words
    chunk = days // 5
    row0 = lax.axis_index("lat") * rows
    place = jnp.stack([row0, jnp.int32(nlat), lax.axis_index("lat") % 2]).astype(jnp.int32)
    tall = row0 - rows + jnp.arange(6 * rows) // 2
    cos_tall = latitude_cos(tall, nlat)[:, None]
    klon = jnp.broadcast_to(KLON / (cos_tall * cos_tall), (6 * rows, 2 * LANES))
    cosl = jnp.broadcast_to(cos_tall[2 * rows : 4 * rows], (2 * rows, 2 * LANES))

    fields = jnp.concatenate([mode_maps, ocean_binary_mask.astype(F32)[None]], axis=0)
    from_west, from_east = lon_ring(
        fields[:, :, :reach].reshape(modes + 1, -1), fields[:, :, columns - reach :].reshape(modes + 1, -1)
    )
    words_west, words_east = lon_ring(
        missing_date_bitmask[:, :reach].reshape(-1, words), missing_date_bitmask[:, columns - reach :].reshape(-1, words)
    )
    v = lax.all_gather(mode_series, "lon", axis=1, tiled=True)

    words_per = words // LANES
    spread = [pltpu.VMEM((2 * LANES, days // words_per), BF16), pltpu.VMEM((1, days // words_per), jnp.int32)]
    tile = LANES
    m, a = pl.pallas_call(
        own_flags_kernel,
        grid=(own // tile,),
        out_shape=[jax.ShapeDtypeStruct((own, days), BF16)] * 2,
        in_specs=[
            pl.BlockSpec((tile, words), lambda i: (i, 0)),
            pl.BlockSpec((tile, 1), lambda i: (i, 0)),
            pl.BlockSpec((tile, days), lambda i: (i, 0)),
        ],
        out_specs=[pl.BlockSpec((tile, days), lambda i: (i, 0))] * 2,
        scratch_shapes=spread,
        compiler_params=pltpu.CompilerParams(vmem_limit_bytes=24 * 2**20),
        name="own_flags",
    )(
        missing_date_bitmask.reshape(own, words),
        ocean_binary_mask.reshape(own, 1),
        sea_heat_deviations.reshape(own, days),
    )
    all_fields = jnp.concatenate([fields.reshape(modes + 1, own), from_west, from_east], axis=1)
    u, coast = (all_fields[:modes], all_fields[modes:])
    (m_halo,) = call(
        halo_flags_kernel,
        "halo_flags",
        [((sides, days), BF16)],
        [((2 * LANES, days // words_per), BF16), ((1, days // words_per), jnp.int32)],
        [jnp.concatenate([words_west, words_east], axis=0), coast[0, own:].astype(jnp.int32).reshape(sides, 1)],
    )
    xv, to_west, to_east = call(
        functools.partial(given_kernel, rows, reach),
        "given",
        [((PAIRS, own), F32), ((PAIRS, LANES), F32), ((PAIRS, LANES), F32)],
        [],
        [v, a],
    )
    xv_west, xv_east = lon_ring(to_west, to_east)

    count = 2 * rows
    news = []
    summed = block = None
    coasts = ()
    for step in range(STEPS):
        wide = 2 * count if step == 0 else count
        outs = [((wide, 2 * LANES), F32)]
        extra = []
        if step:
            outs += [((2, days), F32), ((2, cells), F32)]
            extra = [*news, summed, block]
        got = call(
            functools.partial(fields_kernel, step, rows, reach, total, chunk),
            f"fields_{step}",
            outs,
            [((modes, days), F32), ((modes, cells), F32)],
            [m, m_halo, v, u, coast, xv, xv_west, xv_east, *extra],
        )
        fresh = got[0]
        news += got[1:]
        got_a, got_b = lat_partners(fresh)
        partial_sums, block = call(
            functools.partial(sums_kernel, step, rows, chunk),
            f"sums_{step}",
            [((2, days + LANES), F32), ((count, 2 * LANES), F32)],
            [((modes, days), F32), ((modes, own), F32)],
            [m, a, v, u, place, klon, cosl, fresh, got_a, got_b, *coasts, *news],
            smem=(4,),
        )
        if step == 0:
            coasts = (fresh, got_a, got_b)
        summed = sum_all(partial_sums)
    news += call(
        functools.partial(last_kernel, rows, reach, total),
        "last",
        [((2, days), F32), ((2, cells), F32)],
        [],
        [summed, block],
    )
    share = mode_series.shape[1]
    new_v = jnp.concatenate(news[0::2], axis=0)
    new_u = jnp.concatenate([z[:, :own] for z in news[1::2]], axis=0).reshape(PAIRS, rows, columns)
    own_days = lax.dynamic_slice_in_dim(new_v, lax.axis_index("lon") * share, share, 1)
    return (
        jnp.concatenate([new_u, mode_maps[PAIRS:]], axis=0),
        jnp.concatenate([own_days, mode_series[PAIRS:]], axis=0),
    )


def solution(mesh):
    in_specs = (
        P("lat", "lon", None),
        P("lat", "lon", None),
        P("lat", "lon"),
        P(None, "lat", "lon"),
        P(None, "lon"),
    )
    out_specs = (P(None, "lat", "lon"), P(None, "lon"))
    return jax.shard_map(shards, mesh=mesh, in_specs=in_specs, out_specs=out_specs, check_vma=False)
```

time: 379 us -> 154 us (0.41)
  matrix products: 144 us -> 0 us
  local copies, waits for them, and re-layouts: 56.6 us -> 9.88 us
  other arithmetic: 29.1 us -> 2.27 us
  Pallas kernels: 0 us -> 23.1 us
  between operations: 22.6 us -> 1.05 us
  starting transfers between devices: 64.6 us -> 52.8 us
    dot_general x24 -> x0, matrix products: 144 us -> none  [the longest x4 58.8 us: shards(): others = recon - jnp.dot(pair_u.T, pair_v, precision=HIGH)]
    pallas_call x0 -> x12, Pallas kernels: none -> 23.1 us  [the longest x11 20.2 us: call(): pl.pallas_call(kernel, out_shape=[jax.ShapeDtypeStruct(s, t) for s, t in...]
    slice x29 -> x11, local copies, waits for them, and re-layouts: 22.2 us -> 0.31 us  [the longest x1 0.1 us: shards(): fields[:, :, columns - reach:].reshape(modes + 1, -1)]
    div x13 -> x1, other arithmetic: 14.1 us -> 0.05 us  [shards(): klon = jnp.broadcast_to(KLON / (cos_tall * cos_tall), (6 * rows, 2 * LANES))]
    ppermute x20 -> x14, starting transfers between devices: 32.3 us -> 20.6 us  [the longest x3 9.45 us: lon_ring(): lax.ppermute(to_west, 'lon', [(j, i) for i, j in up])]
    another operation x4 -> x1, other arithmetic: 10.7 us -> 0.08 us  [shards(): jnp.stack([row0, jnp.int32(nlat), lax.axis_index('lat') % 2])]
    shift_right_arithmetic x4 -> x0, local copies, waits for them, and re-layouts: 10.5 us -> none  [unpack_days(): flags = jnp.right_shift(words[..., None], shifts) & 1]
    unnamed x23 -> x20, local copies, waits for them, and re-layouts: 18.8 us -> 8.53 us
  transfers between devices with their start and end apart: 48 -> 42, of which waited for: 35 -> 34; matrix products, arithmetic and copies ran while one was open for 14% -> 1% of each run, Pallas kernels for 0% -> 1%
where the time goes in v2:
time: 154 us
  starting transfers between devices  52.8 us (34%)
  waiting for transfers between devices  47.5 us (31%)
  Pallas kernels  23.1 us (15%)
  blocking collectives  17.6 us (11%)
  local copies, waits for them, and re-layouts  9.88 us (6%)
  other arithmetic  2.27 us (1%)
    ppermute x28, starting transfers between devices, swap(): lax.ppermute(x, ('lat', 'lon'), pairing(lambda i: i ^ lat_bits, lambda j:...  32.3 us
    ppermute x28, waiting for transfers between devices, swap(): lax.ppermute(x, ('lat', 'lon'), pairing(lambda i: i ^ lat_bits, lambda j:...  32.1 us
    pallas_call x11, Pallas kernels, call(): pl.pallas_call(kernel, out_shape=[jax.ShapeDtypeStruct(s, t) for s, t in...  20.2 us
    all_gather x1, blocking collectives, shards(): v = lax.all_gather(mode_series, 'lon', axis=1, tiled=True)  17.6 us
    ppermute x3, starting transfers between devices, lon_ring(): lax.ppermute(to_west, 'lon', [(j, i) for i, j in up])  9.45 us
    ppermute x4, waiting for transfers between devices, lat_partners(): lax.ppermute(x, ('lat', 'lon'), pairing(lambda i: (i + 1 if i % 2 else i...  8.75 us
    unnamed x20, local copies, waits for them, and re-layouts  8.53 us
    ppermute x4, starting transfers between devices, lat_partners(): lax.ppermute(x, ('lat', 'lon'), pairing(lambda i: (i + 1 if i % 2 else i...  5.38 us
  transfers between devices with their start and end apart: 42, of which 34 were waited for; matrix products, arithmetic and copies ran while one was open for 1% of the time, Pallas kernels for 1%

profile of v2, /device:TPU:0, one launch (start us, length us, event | category | flops | bytes accessed | tf_op | source)
XLA Modules:
  0.0 154.2 jit_solution(16231251817114684019)
XLA Ops:
  0.6 17.6 %all-gather = f32[8,480,48]{1,2,0:T(8,128)S(1)} all-gather(f32[1,480,48]{1,2,0:T(8,128)} %bitcast.40), channel_id=1, replica_groups=mesh['lat'=4,'lon'=8] {'lon'}, dimensions={0}, use_global_device_ids=true | all-gather | bytes 829440 | tf_op jit(solution)/shard_map/all_gather | solution.py:374
  19.3 2.1 %copy-done.4 = bf16[4,128,3840]{2,1,0:T(8,128)(2,1)S(1)} copy-done((bf16[4,128,3840]{2,1,0:T(8,128)(2,1)S(1)}, bf16[4,128,3840]{2,1,0:T(8,128)(2,1)}, u32[]{:S(2)}) %copy-start.4) | copy-done | bytes 3932184
  21.4 2.9 %own_flags.1 = (bf16[512,3840]{1,0:T(8,128)(2,1)S(1)}, bf16[512,3840]{1,0:T(8,128)(2,1)S(1)}) custom-call(s32[512,256]{1,0:T(8,128)S(1)} %bitcast.36, s32[512,1]{1,0:T(8,128)S(1)} %copy.18.coast_ref, bf16[512,3840]{1,0:T(8,128)(2,1)S(1)} %bitcast.35), custom_call_target="tpu_custom_call" | custom-call | tf_op jit(solution)/shard_map/own_flags/pallas_call | solution.py:379
  24.3 1.9 %copy-done = bf16[512,3840]{1,0:T(8,128)(2,1)} copy-done((bf16[512,3840]{1,0:T(8,128)(2,1)}, bf16[512,3840]{1,0:T(8,128)(2,1)S(1)}, u32[]{:S(2)}) %copy-start) | copy-done | bytes 3932184
  26.2 1.2 given.1
  27.4 1.9 %copy-done.2 = bf16[512,3840]{1,0:T(8,128)(2,1)} copy-done((bf16[512,3840]{1,0:T(8,128)(2,1)}, bf16[512,3840]{1,0:T(8,128)(2,1)S(1)}, u32[]{:S(2)}) %copy-start.2) | copy-done | bytes 3932184
  29.7 3.2 %collective-permute-start.5 = (f32[8,128]{1,0:T(8,128)S(1)}, f32[8,128]{1,0:T(8,128)S(1)}, u32[]{:S(2)}, u32[]{:S(2)}) collective-permute-start(f32[8,128]{1,0:T(8,128)S(1)} %get-tuple-element.30), channel_id=1, source_target_pairs={{1,0},{2,1},{3,2},{4,3},{5,4},{6,5},{7,6},{0,7},{9,8},{10,9},{11,1... | collective-permute-start | bytes 12296 | tf_op jit(solution)/shard_map/ppermute | solution.py:66
  33.5 3.6 %collective-permute-start.3 = (f32[49,64]{1,0:T(8,128)S(1)}, f32[49,64]{1,0:T(8,128)S(1)}, u32[]{:S(2)}, u32[]{:S(2)}) collective-permute-start(f32[49,64]{1,0:T(8,128)S(1)} %copy.22), channel_id=1, source_target_pairs={{1,0},{2,1},{3,2},{4,3},{5,4},{6,5},{7,6},{0,7},{9,8},{10,9},{11,1... | collective-permute-start | bytes 37640 | tf_op jit(solution)/shard_map/ppermute | solution.py:66
  37.3 1.1 collective-permute-done.2
  38.4 2.7 %collective-permute-start.1 = (s32[64,256]{1,0:T(8,128)S(1)}, s32[64,256]{1,0:T(8,128)S(1)}, u32[]{:S(2)}, u32[]{:S(2)}) collective-permute-start(s32[64,256]{1,0:T(8,128)S(1)} %bitcast.43), channel_id=1, source_target_pairs={{1,0},{2,1},{3,2},{4,3},{5,4},{6,5},{7,6},{0,7},{9,8},{10,9},{11,1... | collective-permute-start | bytes 196616 | tf_op jit(solution)/shard_map/ppermute | solution.py:66
  41.4 1.2 collective-permute-done
  43.8 2.1 %copy-done.1 = bf16[512,3840]{1,0:T(8,128)(2,1)S(1)} copy-done((bf16[512,3840]{1,0:T(8,128)(2,1)S(1)}, bf16[512,3840]{1,0:T(8,128)(2,1)}, u32[]{:S(2)}) %copy-start.1) | copy-done | bytes 3932184
  45.9 1.7 %fields_0.1.refs_7_.refs_10_ = f32[16,256]{1,0:T(8,128)S(1)} custom-call(bf16[512,3840]{1,0:T(8,128)(2,1)S(1)} %copy-done.1, bf16[128,3840]{1,0:T(8,128)(2,1)S(1)} %halo_flags.1.refs_1_, f32[48,3840]{1,0:T(8,128)S(1)} %bitcast.27, f32[48,640]{1,0:T(8,128)S(1)} %slice.61.refs_3_, f32[1,640]{1,0:T(1,128)S(1)} %pad_maximum_fusion.4.refs_4_, ...), custom_call_target="tpu_custom_call" | custom-call | tf_op jit(solution)/shard_map/fields_0/pallas_call | solution.py:334
  47.6 1.6 %collective-permute-start.6 = (f32[16,256]{1,0:T(8,128)S(1)}, f32[16,256]{1,0:T(8,128)S(1)}, u32[]{:S(2)}, u32[]{:S(2)}) collective-permute-start(f32[16,256]{1,0:T(8,128)S(1)} %fields_0.1.refs_7_.refs_10_), channel_id=1, source_target_pairs={{0,8},{1,9},{2,10},{3,11},{4,12},{5,13},{6,14},{7,15},{8,0},{9,1},... | collective-permute-start | bytes 49160 | tf_op jit(solution)/shard_map/ppermute | solution.py:58
  49.2 1.5 collective-permute-start.7
  51.4 2.4 %collective-permute-done.7.refs_9_.refs_12_ = f32[16,256]{1,0:T(8,128)S(1)} collective-permute-done((f32[16,256]{1,0:T(8,128)S(1)}, f32[16,256]{1,0:T(8,128)S(1)}, u32[]{:S(2)}, u32[]{:S(2)}) %collective-permute-start.7) | collective-permute-done | bytes 16416 | tf_op jit(solution)/shard_map/ppermute | solution.py:59
  54.0 2.4 %sums_0.1 = (f32[2,3968]{1,0:T(2,128)S(1)}, f32[8,256]{1,0:T(8,128)S(1)}) custom-call(bf16[512,3840]{1,0:T(8,128)(2,1)S(1)} %copy-done.1, bf16[512,3840]{1,0:T(8,128)(2,1)S(1)} %copy-done.3, f32[48,3840]{1,0:T(8,128)S(1)} %bitcast.28, f32[48,640]{1,0:T(8,128)S(1)} %slice.61.refs_3_, s32[3]{0:T(128)S(1)} %pad_add_fusion.1.refs_4_, ...), custom_call_target="tpu_custom_call" | custom-call | tf_op jit(solution)/shard_map/sums_0/pallas_call | solution.py:334
  56.5 1.2 collective-permute-done.8
  57.7 1.6 %collective-permute-start.10 = (f32[2,3968]{1,0:T(2,128)S(1)}, f32[2,3968]{1,0:T(2,128)S(1)}, u32[]{:S(2)}, u32[]{:S(2)}) collective-permute-start(f32[2,3968]{1,0:T(2,128)S(1)} %add.126), channel_id=1, source_target_pairs={{0,16},{1,17},{2,18},{3,19},{4,20},{5,21},{6,22},{7,23},{8,24},{9,... | collective-permute-start | bytes 95240 | tf_op jit(solution)/shard_map/ppermute | solution.py:32
  59.7 1.5 collective-permute-start.9
  61.6 2.4 %collective-permute-done.11 = f32[2,3968]{1,0:T(2,128)S(1)} collective-permute-done((f32[2,3968]{1,0:T(2,128)S(1)}, f32[2,3968]{1,0:T(2,128)S(1)}, u32[]{:S(2)}, u32[]{:S(2)}) %collective-permute-start.11) | collective-permute-done | bytes 31776 | tf_op jit(solution)/shard_map/ppermute | solution.py:32
  64.2 2.7 %collective-permute-start.13 = (f32[2,3968]{1,0:T(2,128)S(1)}, f32[2,3968]{1,0:T(2,128)S(1)}, u32[]{:S(2)}, u32[]{:S(2)}) collective-permute-start(f32[2,3968]{1,0:T(2,128)S(1)} %add_add_fusion.7), channel_id=1, source_target_pairs={{0,4},{1,5},{2,6},{3,7},{4,0},{5,1},{6,2},{7,3},{8,12},{9,13},{10,... | collective-permute-start | bytes 95240 | tf_op jit(solution)/shard_map/ppermute | solution.py:32
  66.9 1.6 %collective-permute-start.14 = (f32[2,3968]{1,0:T(2,128)S(1)}, f32[2,3968]{1,0:T(2,128)S(1)}, u32[]{:S(2)}, u32[]{:S(2)}) collective-permute-start(f32[2,3968]{1,0:T(2,128)S(1)} %add_add_fusion.7), channel_id=1, source_target_pairs={{0,6},{1,7},{2,4},{3,5},{4,2},{5,3},{6,0},{7,1},{8,14},{9,15},{10,... | collective-permute-start | bytes 95240 | tf_op jit(solution)/shard_map/ppermute | solution.py:32
  69.0 3.6 %collective-permute-done.14 = f32[2,3968]{1,0:T(2,128)S(1)} collective-permute-done((f32[2,3968]{1,0:T(2,128)S(1)}, f32[2,3968]{1,0:T(2,128)S(1)}, u32[]{:S(2)}, u32[]{:S(2)}) %collective-permute-start.14) | collective-permute-done | bytes 31776 | tf_op jit(solution)/shard_map/ppermute | solution.py:32
  72.7 2.1 %fields_1.1 = (f32[8,256]{1,0:T(8,128)S(1)}, f32[2,3840]{1,0:T(2,128)S(1)}, f32[2,640]{1,0:T(2,128)S(1)}) custom-call(bf16[512,3840]{1,0:T(8,128)(2,1)S(1)} %copy-done.1, bf16[128,3840]{1,0:T(8,128)(2,1)S(1)} %halo_flags.1.refs_1_, f32[48,3840]{1,0:T(8,128)S(1)} %bitcast.29, f32[48,640]{1,0:T(8,128)S(1)} %slice.61.refs_3_, ...), custom_call_target="tpu_custom_call" | custom-call | tf_op jit(solution)/shard_map/fields_1/pallas_call | solution.py:334
  74.8 1.1 collective-permute-start.15
  75.9 1.5 collective-permute-start.16
  77.3 1.1 collective-permute-done.15.refs_8_
  78.4 2.0 %collective-permute-done.16.refs_9_ = f32[8,256]{1,0:T(8,128)S(1)} collective-permute-done((f32[8,256]{1,0:T(8,128)S(1)}, f32[8,256]{1,0:T(8,128)S(1)}, u32[]{:S(2)}, u32[]{:S(2)}) %collective-permute-start.16) | collective-permute-done | bytes 8224 | tf_op jit(solution)/shard_map/ppermute | solution.py:59
  80.4 2.4 %sums_1.1 = (f32[2,3968]{1,0:T(2,128)S(1)}, f32[8,256]{1,0:T(8,128)S(1)}) custom-call(bf16[512,3840]{1,0:T(8,128)(2,1)S(1)} %copy-done.1, bf16[512,3840]{1,0:T(8,128)(2,1)S(1)} %copy-done.3, f32[48,3840]{1,0:T(8,128)S(1)} %bitcast.30, f32[48,640]{1,0:T(8,128)S(1)} %slice.61.refs_3_, s32[3]{0:T(128)S(1)} %pad_add_fusion.1.refs_4_, ...), custom_call_target="tpu_custom_call" | custom-call | tf_op jit(solution)/shard_map/sums_1/pallas_call | solution.py:334
  82.9 1.2 collective-permute-done.17
  84.1 1.0 collective-permute-start.18
  85.1 1.1 collective-permute-start.19
  86.2 1.4 collective-permute-start.20
  89.0 2.0 %collective-permute-done.20 = f32[2,3968]{1,0:T(2,128)S(1)} collective-permute-done((f32[2,3968]{1,0:T(2,128)S(1)}, f32[2,3968]{1,0:T(2,128)S(1)}, u32[]{:S(2)}, u32[]{:S(2)}) %collective-permute-start.20) | collective-permute-done | bytes 31776 | tf_op jit(solution)/shard_map/ppermute | solution.py:32
  91.1 2.1 %collective-permute-start.22 = (f32[2,3968]{1,0:T(2,128)S(1)}, f32[2,3968]{1,0:T(2,128)S(1)}, u32[]{:S(2)}, u32[]{:S(2)}) collective-permute-start(f32[2,3968]{1,0:T(2,128)S(1)} %add_add_fusion.5), channel_id=1, source_target_pairs={{0,4},{1,5},{2,6},{3,7},{4,0},{5,1},{6,2},{7,3},{8,12},{9,13},{10,... | collective-permute-start | bytes 95240 | tf_op jit(solution)/shard_map/ppermute | solution.py:32
  93.3 2.2 %collective-permute-start.23 = (f32[2,3968]{1,0:T(2,128)S(1)}, f32[2,3968]{1,0:T(2,128)S(1)}, u32[]{:S(2)}, u32[]{:S(2)}) collective-permute-start(f32[2,3968]{1,0:T(2,128)S(1)} %add_add_fusion.5), channel_id=1, source_target_pairs={{0,6},{1,7},{2,4},{3,5},{4,2},{5,3},{6,0},{7,1},{8,14},{9,15},{10,... | collective-permute-start | bytes 95240 | tf_op jit(solution)/shard_map/ppermute | solution.py:32
  96.3 2.7 %collective-permute-done.23 = f32[2,3968]{1,0:T(2,128)S(1)} collective-permute-done((f32[2,3968]{1,0:T(2,128)S(1)}, f32[2,3968]{1,0:T(2,128)S(1)}, u32[]{:S(2)}, u32[]{:S(2)}) %collective-permute-start.23) | collective-permute-done | bytes 31776 | tf_op jit(solution)/shard_map/ppermute | solution.py:32
  99.0 2.1 %fields_2.1 = (f32[8,256]{1,0:T(8,128)S(1)}, f32[2,3840]{1,0:T(2,128)S(1)}, f32[2,640]{1,0:T(2,128)S(1)}) custom-call(bf16[512,3840]{1,0:T(8,128)(2,1)S(1)} %copy-done.1, bf16[128,3840]{1,0:T(8,128)(2,1)S(1)} %halo_flags.1.refs_1_, f32[48,3840]{1,0:T(8,128)S(1)} %bitcast.31, f32[48,640]{1,0:T(8,128)S(1)} %slice.61.refs_3_, ...), custom_call_target="tpu_custom_call" | custom-call | tf_op jit(solution)/shard_map/fields_2/pallas_call | solution.py:334
  101.1 1.5 collective-permute-start.24
  103.5 1.3 collective-permute-done.24.refs_8_
  104.8 2.4 %collective-permute-done.25.refs_9_ = f32[8,256]{1,0:T(8,128)S(1)} collective-permute-done((f32[8,256]{1,0:T(8,128)S(1)}, f32[8,256]{1,0:T(8,128)S(1)}, u32[]{:S(2)}, u32[]{:S(2)}) %collective-permute-start.25) | collective-permute-done | bytes 8224 | tf_op jit(solution)/shard_map/ppermute | solution.py:59
  107.2 2.4 %sums_2.1 = (f32[2,3968]{1,0:T(2,128)S(1)}, f32[8,256]{1,0:T(8,128)S(1)}) custom-call(bf16[512,3840]{1,0:T(8,128)(2,1)S(1)} %copy-done.1, bf16[512,3840]{1,0:T(8,128)(2,1)S(1)} %copy-done.3, f32[48,3840]{1,0:T(8,128)S(1)} %bitcast.32, f32[48,640]{1,0:T(8,128)S(1)} %slice.61.refs_3_, s32[3]{0:T(128)S(1)} %pad_add_fusion.1.refs_4_, ...), custom_call_target="tpu_custom_call" | custom-call | tf_op jit(solution)/shard_map/sums_2/pallas_call | solution.py:334
  109.7 1.2 collective-permute-done.26
  111.5 0.9 collective-permute-start.28
  112.4 2.0 %collective-permute-start.29 = (f32[2,3968]{1,0:T(2,128)S(1)}, f32[2,3968]{1,0:T(2,128)S(1)}, u32[]{:S(2)}, u32[]{:S(2)}) collective-permute-start(f32[2,3968]{1,0:T(2,128)S(1)} %add.140), channel_id=1, source_target_pairs={{0,24},{1,25},{2,26},{3,27},{4,28},{5,29},{6,30},{7,31},{8,16},{9,... | collective-permute-start | bytes 95240 | tf_op jit(solution)/shard_map/ppermute | solution.py:32
  115.4 1.8 %collective-permute-done.29 = f32[2,3968]{1,0:T(2,128)S(1)} collective-permute-done((f32[2,3968]{1,0:T(2,128)S(1)}, f32[2,3968]{1,0:T(2,128)S(1)}, u32[]{:S(2)}, u32[]{:S(2)}) %collective-permute-start.29) | collective-permute-done | bytes 31776 | tf_op jit(solution)/shard_map/ppermute | solution.py:32
  117.3 2.7 %collective-permute-start.31 = (f32[2,3968]{1,0:T(2,128)S(1)}, f32[2,3968]{1,0:T(2,128)S(1)}, u32[]{:S(2)}, u32[]{:S(2)}) collective-permute-start(f32[2,3968]{1,0:T(2,128)S(1)} %add_add_fusion.3), channel_id=1, source_target_pairs={{0,4},{1,5},{2,6},{3,7},{4,0},{5,1},{6,2},{7,3},{8,12},{9,13},{10,... | collective-permute-start | bytes 95240 | tf_op jit(solution)/shard_map/ppermute | solution.py:32
  120.1 1.6 %collective-permute-start.32 = (f32[2,3968]{1,0:T(2,128)S(1)}, f32[2,3968]{1,0:T(2,128)S(1)}, u32[]{:S(2)}, u32[]{:S(2)}) collective-permute-start(f32[2,3968]{1,0:T(2,128)S(1)} %add_add_fusion.3), channel_id=1, source_target_pairs={{0,6},{1,7},{2,4},{3,5},{4,2},{5,3},{6,0},{7,1},{8,14},{9,15},{10,... | collective-permute-start | bytes 95240 | tf_op jit(solution)/shard_map/ppermute | solution.py:32
  122.2 3.6 %collective-permute-done.32 = f32[2,3968]{1,0:T(2,128)S(1)} collective-permute-done((f32[2,3968]{1,0:T(2,128)S(1)}, f32[2,3968]{1,0:T(2,128)S(1)}, u32[]{:S(2)}, u32[]{:S(2)}) %collective-permute-start.32) | collective-permute-done | bytes 31776 | tf_op jit(solution)/shard_map/ppermute | solution.py:32
  125.8 2.3 %fields_3.1 = (f32[8,256]{1,0:T(8,128)S(1)}, f32[2,3840]{1,0:T(2,128)S(1)}, f32[2,640]{1,0:T(2,128)S(1)}) custom-call(bf16[512,3840]{1,0:T(8,128)(2,1)S(1)} %copy-done.1, bf16[128,3840]{1,0:T(8,128)(2,1)S(1)} %halo_flags.1.refs_1_, f32[48,3840]{1,0:T(8,128)S(1)} %bitcast.33, f32[48,640]{1,0:T(8,128)S(1)} %slice.61.refs_3_, ...), custom_call_target="tpu_custom_call" | custom-call | tf_op jit(solution)/shard_map/fields_3/pallas_call | solution.py:334
  128.2 1.1 collective-permute-start.33
  129.3 1.5 collective-permute-start.34
  130.8 1.1 collective-permute-done.33.refs_8_
  131.8 2.0 %collective-permute-done.34.refs_9_ = f32[8,256]{1,0:T(8,128)S(1)} collective-permute-done((f32[8,256]{1,0:T(8,128)S(1)}, f32[8,256]{1,0:T(8,128)S(1)}, u32[]{:S(2)}, u32[]{:S(2)}) %collective-permute-start.34) | collective-permute-done | bytes 8224 | tf_op jit(solution)/shard_map/ppermute | solution.py:59
  133.8 2.4 %sums_3.1 = (f32[2,3968]{1,0:T(2,128)S(1)}, f32[8,256]{1,0:T(8,128)S(1)}) custom-call(bf16[512,3840]{1,0:T(8,128)(2,1)S(1)} %copy-done.1, bf16[512,3840]{1,0:T(8,128)(2,1)S(1)} %copy-done.3, f32[48,3840]{1,0:T(8,128)S(1)} %bitcast.34, f32[48,640]{1,0:T(8,128)S(1)} %slice.61.refs_3_, s32[3]{0:T(128)S(1)} %pad_add_fusion.1.refs_4_, ...), custom_call_target="tpu_custom_call" | custom-call | tf_op jit(solution)/shard_map/sums_3/pallas_call | solution.py:334
  136.3 1.2 collective-permute-done.35
  137.5 1.0 collective-permute-start.36
  138.5 1.1 collective-permute-start.37
  139.7 1.4 collective-permute-start.38
  142.4 2.0 %collective-permute-done.38 = f32[2,3968]{1,0:T(2,128)S(1)} collective-permute-done((f32[2,3968]{1,0:T(2,128)S(1)}, f32[2,3968]{1,0:T(2,128)S(1)}, u32[]{:S(2)}, u32[]{:S(2)}) %collective-permute-start.38) | collective-permute-done | bytes 31776 | tf_op jit(solution)/shard_map/ppermute | solution.py:32
  144.6 2.1 %collective-permute-start.40 = (f32[2,3968]{1,0:T(2,128)S(1)}, f32[2,3968]{1,0:T(2,128)S(1)}, u32[]{:S(2)}, u32[]{:S(2)}) collective-permute-start(f32[2,3968]{1,0:T(2,128)S(1)} %add_add_fusion.1), channel_id=1, source_target_pairs={{0,4},{1,5},{2,6},{3,7},{4,0},{5,1},{6,2},{7,3},{8,12},{9,13},{10,... | collective-permute-start | bytes 95240 | tf_op jit(solution)/shard_map/ppermute | solution.py:32
  146.7 2.2 %collective-permute-start.41 = (f32[2,3968]{1,0:T(2,128)S(1)}, f32[2,3968]{1,0:T(2,128)S(1)}, u32[]{:S(2)}, u32[]{:S(2)}) collective-permute-start(f32[2,3968]{1,0:T(2,128)S(1)} %add_add_fusion.1), channel_id=1, source_target_pairs={{0,6},{1,7},{2,4},{3,5},{4,2},{5,3},{6,0},{7,1},{8,14},{9,15},{10,... | collective-permute-start | bytes 95240 | tf_op jit(solution)/shard_map/ppermute | solution.py:32
  149.7 2.7 %collective-permute-done.41 = f32[2,3968]{1,0:T(2,128)S(1)} collective-permute-done((f32[2,3968]{1,0:T(2,128)S(1)}, f32[2,3968]{1,0:T(2,128)S(1)}, u32[]{:S(2)}, u32[]{:S(2)}) %collective-permute-start.41) | collective-permute-done | bytes 31776 | tf_op jit(solution)/shard_map/ppermute | solution.py:32
  (97 shorter events, 15.6 us)
Async XLA Ops:
  0.6 18.5 %copy-start.8 = (s32[4,128]{1,0:T(4,128)S(1)}, s32[4,128]{1,0:T(4,128)}, u32[]{:S(2)}) copy-start(s32[4,128]{1,0:T(4,128)} %param.7) | copy-start | bytes 6148
  0.6 18.7 %copy-start.5 = (s32[4,128,256]{2,1,0:T(8,128)S(1)}, s32[4,128,256]{2,1,0:T(8,128)}, u32[]{:S(2)}) copy-start(s32[4,128,256]{2,1,0:T(8,128)} %param.6) | copy-start | bytes 1572868
  19.3 2.1 %copy-start.4 = (bf16[4,128,3840]{2,1,0:T(8,128)(2,1)S(1)}, bf16[4,128,3840]{2,1,0:T(8,128)(2,1)}, u32[]{:S(2)}) copy-start(bf16[4,128,3840]{2,1,0:T(8,128)(2,1)} %param.5) | copy-start | bytes 11796484
  21.4 11.5 %copy-start.6 = (f32[48,4,128]{2,1,0:T(4,128)S(1)}, f32[48,4,128]{2,1,0:T(4,128)}, u32[]{:S(2)}) copy-start(f32[48,4,128]{2,1,0:T(4,128)} %param.8) | copy-start | bytes 294916
  24.3 1.9 %copy-start = (bf16[512,3840]{1,0:T(8,128)(2,1)}, bf16[512,3840]{1,0:T(8,128)(2,1)S(1)}, u32[]{:S(2)}) copy-start(bf16[512,3840]{1,0:T(8,128)(2,1)S(1)} %get-tuple-element.26.refs_0_) | copy-start | bytes 11796484
  27.4 2.0 %copy-start.2 = (bf16[512,3840]{1,0:T(8,128)(2,1)}, bf16[512,3840]{1,0:T(8,128)(2,1)S(1)}, u32[]{:S(2)}) copy-start(bf16[512,3840]{1,0:T(8,128)(2,1)S(1)} %get-tuple-element.27.a_ref.refs_1_) | copy-start | bytes 11796484
  29.4 14.4 %collective-permute-start.4 = (f32[8,128]{1,0:T(8,128)S(1)}, f32[8,128]{1,0:T(8,128)S(1)}, u32[]{:S(2)}, u32[]{:S(2)}) collective-permute-start(f32[8,128]{1,0:T(8,128)S(1)} %get-tuple-element.29), channel_id=1, source_target_pairs={{0,1},{1,2},{2,3},{3,4},{4,5},{5,6},{6,7},{7,0},{8,9},{9,10},{10,1... | collective-permute-start | bytes 12296 | tf_op jit(solution)/shard_map/ppermute | solution.py:66
  29.7 14.0 %collective-permute-start.5 = (f32[8,128]{1,0:T(8,128)S(1)}, f32[8,128]{1,0:T(8,128)S(1)}, u32[]{:S(2)}, u32[]{:S(2)}) collective-permute-start(f32[8,128]{1,0:T(8,128)S(1)} %get-tuple-element.30), channel_id=1, source_target_pairs={{1,0},{2,1},{3,2},{4,3},{5,4},{6,5},{7,6},{0,7},{9,8},{10,9},{11,1... | collective-permute-start | bytes 12296 | tf_op jit(solution)/shard_map/ppermute | solution.py:66
  33.2 5.1 %collective-permute-start.2 = (f32[49,64]{1,0:T(8,128)S(1)}, f32[49,64]{1,0:T(8,128)S(1)}, u32[]{:S(2)}, u32[]{:S(2)}) collective-permute-start(f32[49,64]{1,0:T(8,128)S(1)} %copy.20), channel_id=1, source_target_pairs={{0,1},{1,2},{2,3},{3,4},{4,5},{5,6},{6,7},{7,0},{8,9},{9,10},{10,1... | collective-permute-start | bytes 37640 | tf_op jit(solution)/shard_map/ppermute | solution.py:66
  33.5 7.6 %collective-permute-start.3 = (f32[49,64]{1,0:T(8,128)S(1)}, f32[49,64]{1,0:T(8,128)S(1)}, u32[]{:S(2)}, u32[]{:S(2)}) collective-permute-start(f32[49,64]{1,0:T(8,128)S(1)} %copy.22), channel_id=1, source_target_pairs={{1,0},{2,1},{3,2},{4,3},{5,4},{6,5},{7,6},{0,7},{9,8},{10,9},{11,1... | collective-permute-start | bytes 37640 | tf_op jit(solution)/shard_map/ppermute | solution.py:66
  37.1 5.5 %collective-permute-start = (s32[64,256]{1,0:T(8,128)S(1)}, s32[64,256]{1,0:T(8,128)S(1)}, u32[]{:S(2)}, u32[]{:S(2)}) collective-permute-start(s32[64,256]{1,0:T(8,128)S(1)} %bitcast.44), channel_id=1, source_target_pairs={{0,1},{1,2},{2,3},{3,4},{4,5},{5,6},{6,7},{7,0},{8,9},{9,10},{10,1... | collective-permute-start | bytes 196616 | tf_op jit(solution)/shard_map/ppermute | solution.py:66
  38.4 4.6 %collective-permute-start.1 = (s32[64,256]{1,0:T(8,128)S(1)}, s32[64,256]{1,0:T(8,128)S(1)}, u32[]{:S(2)}, u32[]{:S(2)}) collective-permute-start(s32[64,256]{1,0:T(8,128)S(1)} %bitcast.43), channel_id=1, source_target_pairs={{1,0},{2,1},{3,2},{4,3},{5,4},{6,5},{7,6},{0,7},{9,8},{10,9},{11,1... | collective-permute-start | bytes 196616 | tf_op jit(solution)/shard_map/ppermute | solution.py:66
  43.8 2.1 %copy-start.1 = (bf16[512,3840]{1,0:T(8,128)(2,1)S(1)}, bf16[512,3840]{1,0:T(8,128)(2,1)}, u32[]{:S(2)}) copy-start(bf16[512,3840]{1,0:T(8,128)(2,1)} %copy-done) | copy-start | bytes 11796484
  45.9 8.1 %copy-start.3 = (bf16[512,3840]{1,0:T(8,128)(2,1)S(1)}, bf16[512,3840]{1,0:T(8,128)(2,1)}, u32[]{:S(2)}) copy-start(bf16[512,3840]{1,0:T(8,128)(2,1)} %copy-done.2) | copy-start | bytes 11796484
  47.6 3.8 %collective-permute-start.6 = (f32[16,256]{1,0:T(8,128)S(1)}, f32[16,256]{1,0:T(8,128)S(1)}, u32[]{:S(2)}, u32[]{:S(2)}) collective-permute-start(f32[16,256]{1,0:T(8,128)S(1)} %fields_0.1.refs_7_.refs_10_), channel_id=1, source_target_pairs={{0,8},{1,9},{2,10},{3,11},{4,12},{5,13},{6,14},{7,15},{8,0},{9,1},... | collective-permute-start | bytes 49160 | tf_op jit(solution)/shard_map/ppermute | solution.py:58
  49.2 4.6 %collective-permute-start.7 = (f32[16,256]{1,0:T(8,128)S(1)}, f32[16,256]{1,0:T(8,128)S(1)}, u32[]{:S(2)}, u32[]{:S(2)}) collective-permute-start(f32[16,256]{1,0:T(8,128)S(1)} %fields_0.1.refs_7_.refs_10_), channel_id=1, source_target_pairs={{0,24},{1,25},{2,26},{3,27},{4,28},{5,29},{6,30},{7,31},{8,16},{9,... | collective-permute-start | bytes 49160 | tf_op jit(solution)/shard_map/ppermute | solution.py:59
  56.4 1.3 collective-permute-start.8
  57.7 4.0 %collective-permute-start.10 = (f32[2,3968]{1,0:T(2,128)S(1)}, f32[2,3968]{1,0:T(2,128)S(1)}, u32[]{:S(2)}, u32[]{:S(2)}) collective-permute-start(f32[2,3968]{1,0:T(2,128)S(1)} %add.126), channel_id=1, source_target_pairs={{0,16},{1,17},{2,18},{3,19},{4,20},{5,21},{6,22},{7,23},{8,24},{9,... | collective-permute-start | bytes 95240 | tf_op jit(solution)/shard_map/ppermute | solution.py:32
  59.3 4.8 %collective-permute-start.11 = (f32[2,3968]{1,0:T(2,128)S(1)}, f32[2,3968]{1,0:T(2,128)S(1)}, u32[]{:S(2)}, u32[]{:S(2)}) collective-permute-start(f32[2,3968]{1,0:T(2,128)S(1)} %add.126), channel_id=1, source_target_pairs={{0,24},{1,25},{2,26},{3,27},{4,28},{5,29},{6,30},{7,31},{8,16},{9,... | collective-permute-start | bytes 95240 | tf_op jit(solution)/shard_map/ppermute | solution.py:32
  59.7 4.3 %collective-permute-start.9 = (f32[2,3968]{1,0:T(2,128)S(1)}, f32[2,3968]{1,0:T(2,128)S(1)}, u32[]{:S(2)}, u32[]{:S(2)}) collective-permute-start(f32[2,3968]{1,0:T(2,128)S(1)} %add.126), channel_id=1, source_target_pairs={{0,8},{1,9},{2,10},{3,11},{4,12},{5,13},{6,14},{7,15},{8,0},{9,1},... | collective-permute-start | bytes 95240 | tf_op jit(solution)/shard_map/ppermute | solution.py:32
  64.1 4.5 %collective-permute-start.12 = (f32[2,3968]{1,0:T(2,128)S(1)}, f32[2,3968]{1,0:T(2,128)S(1)}, u32[]{:S(2)}, u32[]{:S(2)}) collective-permute-start(f32[2,3968]{1,0:T(2,128)S(1)} %add_add_fusion.7), channel_id=1, source_target_pairs={{0,2},{1,3},{2,0},{3,1},{4,6},{5,7},{6,4},{7,5},{8,10},{9,11},{10,... | collective-permute-start | bytes 95240 | tf_op jit(solution)/shard_map/ppermute | solution.py:32
  64.2 4.9 %collective-permute-start.13 = (f32[2,3968]{1,0:T(2,128)S(1)}, f32[2,3968]{1,0:T(2,128)S(1)}, u32[]{:S(2)}, u32[]{:S(2)}) collective-permute-start(f32[2,3968]{1,0:T(2,128)S(1)} %add_add_fusion.7), channel_id=1, source_target_pairs={{0,4},{1,5},{2,6},{3,7},{4,0},{5,1},{6,2},{7,3},{8,12},{9,13},{10,... | collective-permute-start | bytes 95240 | tf_op jit(solution)/shard_map/ppermute | solution.py:32
  66.9 5.7 %collective-permute-start.14 = (f32[2,3968]{1,0:T(2,128)S(1)}, f32[2,3968]{1,0:T(2,128)S(1)}, u32[]{:S(2)}, u32[]{:S(2)}) collective-permute-start(f32[2,3968]{1,0:T(2,128)S(1)} %add_add_fusion.7), channel_id=1, source_target_pairs={{0,6},{1,7},{2,4},{3,5},{4,2},{5,3},{6,0},{7,1},{8,14},{9,15},{10,... | collective-permute-start | bytes 95240 | tf_op jit(solution)/shard_map/ppermute | solution.py:32
  74.8 3.7 %collective-permute-start.15 = (f32[8,256]{1,0:T(8,128)S(1)}, f32[8,256]{1,0:T(8,128)S(1)}, u32[]{:S(2)}, u32[]{:S(2)}) collective-permute-start(f32[8,256]{1,0:T(8,128)S(1)} %get-tuple-element.35.refs_7_), channel_id=1, source_target_pairs={{0,8},{1,9},{2,10},{3,11},{4,12},{5,13},{6,14},{7,15},{8,0},{9,1},... | collective-permute-start | bytes 24584 | tf_op jit(solution)/shard_map/ppermute | solution.py:58
  75.9 4.5 %collective-permute-start.16 = (f32[8,256]{1,0:T(8,128)S(1)}, f32[8,256]{1,0:T(8,128)S(1)}, u32[]{:S(2)}, u32[]{:S(2)}) collective-permute-start(f32[8,256]{1,0:T(8,128)S(1)} %get-tuple-element.35.refs_7_), channel_id=1, source_target_pairs={{0,24},{1,25},{2,26},{3,27},{4,28},{5,29},{6,30},{7,31},{8,16},{9,... | collective-permute-start | bytes 24584 | tf_op jit(solution)/shard_map/ppermute | solution.py:59
  82.8 1.3 collective-permute-start.17
  84.1 4.0 %collective-permute-start.18 = (f32[2,3968]{1,0:T(2,128)S(1)}, f32[2,3968]{1,0:T(2,128)S(1)}, u32[]{:S(2)}, u32[]{:S(2)}) collective-permute-start(f32[2,3968]{1,0:T(2,128)S(1)} %add.133), channel_id=1, source_target_pairs={{0,8},{1,9},{2,10},{3,11},{4,12},{5,13},{6,14},{7,15},{8,0},{9,1},... | collective-permute-start | bytes 95240 | tf_op jit(solution)/shard_map/ppermute | solution.py:32
  85.1 3.9 %collective-permute-start.19 = (f32[2,3968]{1,0:T(2,128)S(1)}, f32[2,3968]{1,0:T(2,128)S(1)}, u32[]{:S(2)}, u32[]{:S(2)}) collective-permute-start(f32[2,3968]{1,0:T(2,128)S(1)} %add.133), channel_id=1, source_target_pairs={{0,16},{1,17},{2,18},{3,19},{4,20},{5,21},{6,22},{7,23},{8,24},{9,... | collective-permute-start | bytes 95240 | tf_op jit(solution)/shard_map/ppermute | solution.py:32
  86.2 4.8 %collective-permute-start.20 = (f32[2,3968]{1,0:T(2,128)S(1)}, f32[2,3968]{1,0:T(2,128)S(1)}, u32[]{:S(2)}, u32[]{:S(2)}) collective-permute-start(f32[2,3968]{1,0:T(2,128)S(1)} %add.133), channel_id=1, source_target_pairs={{0,24},{1,25},{2,26},{3,27},{4,28},{5,29},{6,30},{7,31},{8,16},{9,... | collective-permute-start | bytes 95240 | tf_op jit(solution)/shard_map/ppermute | solution.py:32
  91.1 4.5 %collective-permute-start.21 = (f32[2,3968]{1,0:T(2,128)S(1)}, f32[2,3968]{1,0:T(2,128)S(1)}, u32[]{:S(2)}, u32[]{:S(2)}) collective-permute-start(f32[2,3968]{1,0:T(2,128)S(1)} %add_add_fusion.5), channel_id=1, source_target_pairs={{0,2},{1,3},{2,0},{3,1},{4,6},{5,7},{6,4},{7,5},{8,10},{9,11},{10,... | collective-permute-start | bytes 95240 | tf_op jit(solution)/shard_map/ppermute | solution.py:32
  91.1 5.1 %collective-permute-start.22 = (f32[2,3968]{1,0:T(2,128)S(1)}, f32[2,3968]{1,0:T(2,128)S(1)}, u32[]{:S(2)}, u32[]{:S(2)}) collective-permute-start(f32[2,3968]{1,0:T(2,128)S(1)} %add_add_fusion.5), channel_id=1, source_target_pairs={{0,4},{1,5},{2,6},{3,7},{4,0},{5,1},{6,2},{7,3},{8,12},{9,13},{10,... | collective-permute-start | bytes 95240 | tf_op jit(solution)/shard_map/ppermute | solution.py:32
  93.3 5.7 %collective-permute-start.23 = (f32[2,3968]{1,0:T(2,128)S(1)}, f32[2,3968]{1,0:T(2,128)S(1)}, u32[]{:S(2)}, u32[]{:S(2)}) collective-permute-start(f32[2,3968]{1,0:T(2,128)S(1)} %add_add_fusion.5), channel_id=1, source_target_pairs={{0,6},{1,7},{2,4},{3,5},{4,2},{5,3},{6,0},{7,1},{8,14},{9,15},{10,... | collective-permute-start | bytes 95240 | tf_op jit(solution)/shard_map/ppermute | solution.py:32
  101.1 3.7 %collective-permute-start.24 = (f32[8,256]{1,0:T(8,128)S(1)}, f32[8,256]{1,0:T(8,128)S(1)}, u32[]{:S(2)}, u32[]{:S(2)}) collective-permute-start(f32[8,256]{1,0:T(8,128)S(1)} %get-tuple-element.40.refs_7_), channel_id=1, source_target_pairs={{0,8},{1,9},{2,10},{3,11},{4,12},{5,13},{6,14},{7,15},{8,0},{9,1},... | collective-permute-start | bytes 24584 | tf_op jit(solution)/shard_map/ppermute | solution.py:58
  102.6 4.5 %collective-permute-start.25 = (f32[8,256]{1,0:T(8,128)S(1)}, f32[8,256]{1,0:T(8,128)S(1)}, u32[]{:S(2)}, u32[]{:S(2)}) collective-permute-start(f32[8,256]{1,0:T(8,128)S(1)} %get-tuple-element.40.refs_7_), channel_id=1, source_target_pairs={{0,24},{1,25},{2,26},{3,27},{4,28},{5,29},{6,30},{7,31},{8,16},{9,... | collective-permute-start | bytes 24584 | tf_op jit(solution)/shard_map/ppermute | solution.py:59
  109.6 1.3 collective-permute-start.26
  110.9 4.0 %collective-permute-start.27 = (f32[2,3968]{1,0:T(2,128)S(1)}, f32[2,3968]{1,0:T(2,128)S(1)}, u32[]{:S(2)}, u32[]{:S(2)}) collective-permute-start(f32[2,3968]{1,0:T(2,128)S(1)} %add.140), channel_id=1, source_target_pairs={{0,8},{1,9},{2,10},{3,11},{4,12},{5,13},{6,14},{7,15},{8,0},{9,1},... | collective-permute-start | bytes 95240 | tf_op jit(solution)/shard_map/ppermute | solution.py:32
  111.5 3.9 %collective-permute-start.28 = (f32[2,3968]{1,0:T(2,128)S(1)}, f32[2,3968]{1,0:T(2,128)S(1)}, u32[]{:S(2)}, u32[]{:S(2)}) collective-permute-start(f32[2,3968]{1,0:T(2,128)S(1)} %add.140), channel_id=1, source_target_pairs={{0,16},{1,17},{2,18},{3,19},{4,20},{5,21},{6,22},{7,23},{8,24},{9,... | collective-permute-start | bytes 95240 | tf_op jit(solution)/shard_map/ppermute | solution.py:32
  112.4 4.8 %collective-permute-start.29 = (f32[2,3968]{1,0:T(2,128)S(1)}, f32[2,3968]{1,0:T(2,128)S(1)}, u32[]{:S(2)}, u32[]{:S(2)}) collective-permute-start(f32[2,3968]{1,0:T(2,128)S(1)} %add.140), channel_id=1, source_target_pairs={{0,24},{1,25},{2,26},{3,27},{4,28},{5,29},{6,30},{7,31},{8,16},{9,... | collective-permute-start | bytes 95240 | tf_op jit(solution)/shard_map/ppermute | solution.py:32
  117.3 4.5 %collective-permute-start.30 = (f32[2,3968]{1,0:T(2,128)S(1)}, f32[2,3968]{1,0:T(2,128)S(1)}, u32[]{:S(2)}, u32[]{:S(2)}) collective-permute-start(f32[2,3968]{1,0:T(2,128)S(1)} %add_add_fusion.3), channel_id=1, source_target_pairs={{0,2},{1,3},{2,0},{3,1},{4,6},{5,7},{6,4},{7,5},{8,10},{9,11},{10,... | collective-permute-start | bytes 95240 | tf_op jit(solution)/shard_map/ppermute | solution.py:32
  117.3 4.9 %collective-permute-start.31 = (f32[2,3968]{1,0:T(2,128)S(1)}, f32[2,3968]{1,0:T(2,128)S(1)}, u32[]{:S(2)}, u32[]{:S(2)}) collective-permute-start(f32[2,3968]{1,0:T(2,128)S(1)} %add_add_fusion.3), channel_id=1, source_target_pairs={{0,4},{1,5},{2,6},{3,7},{4,0},{5,1},{6,2},{7,3},{8,12},{9,13},{10,... | collective-permute-start | bytes 95240 | tf_op jit(solution)/shard_map/ppermute | solution.py:32
  120.1 5.7 %collective-permute-start.32 = (f32[2,3968]{1,0:T(2,128)S(1)}, f32[2,3968]{1,0:T(2,128)S(1)}, u32[]{:S(2)}, u32[]{:S(2)}) collective-permute-start(f32[2,3968]{1,0:T(2,128)S(1)} %add_add_fusion.3), channel_id=1, source_target_pairs={{0,6},{1,7},{2,4},{3,5},{4,2},{5,3},{6,0},{7,1},{8,14},{9,15},{10,... | collective-permute-start | bytes 95240 | tf_op jit(solution)/shard_map/ppermute | solution.py:32
  128.2 3.7 %collective-permute-start.33 = (f32[8,256]{1,0:T(8,128)S(1)}, f32[8,256]{1,0:T(8,128)S(1)}, u32[]{:S(2)}, u32[]{:S(2)}) collective-permute-start(f32[8,256]{1,0:T(8,128)S(1)} %get-tuple-element.44.refs_7_), channel_id=1, source_target_pairs={{0,8},{1,9},{2,10},{3,11},{4,12},{5,13},{6,14},{7,15},{8,0},{9,1},... | collective-permute-start | bytes 24584 | tf_op jit(solution)/shard_map/ppermute | solution.py:58
  129.3 4.5 %collective-permute-start.34 = (f32[8,256]{1,0:T(8,128)S(1)}, f32[8,256]{1,0:T(8,128)S(1)}, u32[]{:S(2)}, u32[]{:S(2)}) collective-permute-start(f32[8,256]{1,0:T(8,128)S(1)} %get-tuple-element.44.refs_7_), channel_id=1, source_target_pairs={{0,24},{1,25},{2,26},{3,27},{4,28},{5,29},{6,30},{7,31},{8,16},{9,... | collective-permute-start | bytes 24584 | tf_op jit(solution)/shard_map/ppermute | solution.py:59
  133.8 15.1 %copy-start.7 = (f32[48,480]{1,0:T(8,128)S(1)}, f32[48,480]{1,0:T(8,128)}, u32[]{:S(2)}) copy-start(f32[48,480]{1,0:T(8,128)} %param.9) | copy-start | bytes 276484
  136.2 1.3 collective-permute-start.35
  137.5 4.0 %collective-permute-start.36 = (f32[2,3968]{1,0:T(2,128)S(1)}, f32[2,3968]{1,0:T(2,128)S(1)}, u32[]{:S(2)}, u32[]{:S(2)}) collective-permute-start(f32[2,3968]{1,0:T(2,128)S(1)} %add.147), channel_id=1, source_target_pairs={{0,8},{1,9},{2,10},{3,11},{4,12},{5,13},{6,14},{7,15},{8,0},{9,1},... | collective-permute-start | bytes 95240 | tf_op jit(solution)/shard_map/ppermute | solution.py:32
  138.5 3.9 %collective-permute-start.37 = (f32[2,3968]{1,0:T(2,128)S(1)}, f32[2,3968]{1,0:T(2,128)S(1)}, u32[]{:S(2)}, u32[]{:S(2)}) collective-permute-start(f32[2,3968]{1,0:T(2,128)S(1)} %add.147), channel_id=1, source_target_pairs={{0,16},{1,17},{2,18},{3,19},{4,20},{5,21},{6,22},{7,23},{8,24},{9,... | collective-permute-start | bytes 95240 | tf_op jit(solution)/shard_map/ppermute | solution.py:32
  139.7 4.8 %collective-permute-start.38 = (f32[2,3968]{1,0:T(2,128)S(1)}, f32[2,3968]{1,0:T(2,128)S(1)}, u32[]{:S(2)}, u32[]{:S(2)}) collective-permute-start(f32[2,3968]{1,0:T(2,128)S(1)} %add.147), channel_id=1, source_target_pairs={{0,24},{1,25},{2,26},{3,27},{4,28},{5,29},{6,30},{7,31},{8,16},{9,... | collective-permute-start | bytes 95240 | tf_op jit(solution)/shard_map/ppermute | solution.py:32
  144.5 4.5 %collective-permute-start.39 = (f32[2,3968]{1,0:T(2,128)S(1)}, f32[2,3968]{1,0:T(2,128)S(1)}, u32[]{:S(2)}, u32[]{:S(2)}) collective-permute-start(f32[2,3968]{1,0:T(2,128)S(1)} %add_add_fusion.1), channel_id=1, source_target_pairs={{0,2},{1,3},{2,0},{3,1},{4,6},{5,7},{6,4},{7,5},{8,10},{9,11},{10,... | collective-permute-start | bytes 95240 | tf_op jit(solution)/shard_map/ppermute | solution.py:32
  144.6 5.1 %collective-permute-start.40 = (f32[2,3968]{1,0:T(2,128)S(1)}, f32[2,3968]{1,0:T(2,128)S(1)}, u32[]{:S(2)}, u32[]{:S(2)}) collective-permute-start(f32[2,3968]{1,0:T(2,128)S(1)} %add_add_fusion.1), channel_id=1, source_target_pairs={{0,4},{1,5},{2,6},{3,7},{4,0},{5,1},{6,2},{7,3},{8,12},{9,13},{10,... | collective-permute-start | bytes 95240 | tf_op jit(solution)/shard_map/ppermute | solution.py:32
  146.7 5.7 %collective-permute-start.41 = (f32[2,3968]{1,0:T(2,128)S(1)}, f32[2,3968]{1,0:T(2,128)S(1)}, u32[]{:S(2)}, u32[]{:S(2)}) collective-permute-start(f32[2,3968]{1,0:T(2,128)S(1)} %add_add_fusion.1), channel_id=1, source_target_pairs={{0,6},{1,7},{2,4},{3,5},{4,2},{5,3},{6,0},{7,1},{8,14},{9,15},{10,... | collective-permute-start | bytes 95240 | tf_op jit(solution)/shard_map/ppermute | solution.py:32

commit v3 on v2

--- a/solution.py
+++ b/solution.py
@@ -36,12 +36,13 @@
     nlat, nlon = (lax.axis_size("lat"), lax.axis_size("lon"))
     if nlat & (nlat - 1) or nlon & (nlon - 1):
         return lax.psum(x, ("lat", "lon"))
-    if nlon > 1:
-        x = x + swap(x, 0, 1)
+    core = 1 if nlon > 1 else 0
+    if core:
+        x = x + swap(x, 0, core)
     for size, first, on_lat in ((nlat, 1, True), (nlon, 2, False)):
         bit = first
         while bit < size:
-            bits = lambda b: (b, 0) if on_lat else (0, b)
+            bits = lambda b: (b, core) if on_lat else (0, b | core)
             if 2 * bit < size:
                 near, far, both = (swap(x, *bits(b)) for b in (bit, 2 * bit, 3 * bit))
                 x = (x + near) + (far + both)
@@ -134,13 +135,18 @@
     bit_ref[...] = jnp.left_shift(1, jnp.sum(word, axis=0, keepdims=True))
 
 
+def as_column(row):
+    return jnp.transpose(jnp.broadcast_to(row, (8, LANES)))[:, :1]
+
+
 def own_flags_kernel(words_ref, coast_ref, x_ref, m_ref, a_ref, spread_ref, bit_ref):
     @pl.when(pl.program_id(0) == 0)
     def _():
         fill_spread(spread_ref, bit_ref)
 
-    coast = coast_ref[...]
-    ocean = coast.astype(F32).astype(BF16)
+    coast = as_column(coast_ref[pl.ds(pl.program_id(0), 1), :].astype(F32))
+    ocean = coast.astype(BF16)
+    coast = coast.astype(jnp.int32)
     days = spread_ref.shape[1]
     for g in range(words_ref.shape[1] // LANES):
         words = words_ref[:, g * LANES : (g + 1) * LANES] * coast
@@ -150,36 +156,80 @@
         a_ref[:, at] = x_ref[:, at] * given * ocean
 
 
-def halo_flags_kernel(words_ref, coast_ref, m_ref, spread_ref, bit_ref):
+def edges(pieces, reach):
+    rows = len(pieces)
+    shape = pieces[0].shape
+    lane = lane_ids(shape)
+    west = jnp.zeros(shape, F32)
+    east = west
+    for r, part in enumerate(pieces):
+        first = rows * reach + reach * r
+        west = jnp.where((lane >= first) & (lane < first + reach), pltpu.roll(part, first % LANES, 1), west)
+        first = reach * r
+        east = jnp.where((lane >= first) & (lane < first + reach), pltpu.roll(part, (first + reach) % LANES, 1), east)
+    return west, east
+
+
+def prep_kernel(reach, maps_ref, coast_ref, words_ref, u_ref, row_ref, west_ref, east_ref):
+    modes, rows = maps_ref.shape[:2]
+    coast = coast_ref[...].astype(F32)
+    pieces = []
+    for r in range(rows):
+        at = slice(r * LANES, (r + 1) * LANES)
+        u = maps_ref[:, r, :]
+        u_ref[:, at] = u
+        row_ref[:, at] = coast[r : r + 1]
+        pieces.append(jnp.concatenate([u, jnp.broadcast_to(coast[r : r + 1], (8, LANES))], axis=0))
+    west, east = edges(pieces, reach)
+    base = modes + 8
+    west_ref[:base] = west
+    east_ref[:base] = east
+    for g in range(words_ref.shape[2] // LANES):
+        for r in range(rows):
+            at = slice(base + reach * (rows * g + r), base + reach * (rows * g + r + 1))
+            west_ref[at] = words_ref[r, :reach, g * LANES : (g + 1) * LANES].astype(F32)
+            east_ref[at] = words_ref[r, LANES - reach :, g * LANES : (g + 1) * LANES].astype(F32)
+
+
+def halo_flags_kernel(modes, west_ref, east_ref, m_ref, u_ref, row_ref, spread_ref, bit_ref):
     fill_spread(spread_ref, bit_ref)
-    coast = coast_ref[...]
+    base = modes + 8
+    lane = lane_ids((base, LANES))
+    fields = jnp.where(lane < LANES // 2, west_ref[:base], east_ref[:base])
+    u_ref[...] = fields[:modes]
+    row_ref[...] = fields[modes : modes + 1]
+    coast = as_column(fields[modes : modes + 1]).astype(jnp.int32)
     days = spread_ref.shape[1]
-    for g in range(words_ref.shape[1] // LANES):
-        words = words_ref[:, g * LANES : (g + 1) * LANES] * coast
+    half = LANES // 2
+    for g in range(m_ref.shape[1] // days):
+        at = slice(base + half * g, base + half * (g + 1))
+        words = jnp.concatenate([west_ref[at], east_ref[at]], axis=0).astype(jnp.int32) * coast
         m_ref[:, g * days : (g + 1) * days] = unpack_words(words, spread_ref, bit_ref)
 
 
-def given_kernel(rows, reach, v_ref, a_ref, xv_ref, west_ref, east_ref):
+def given_kernel(rows, reach, *refs):
+    a_ref, place_ref = refs[:2]
+    pieces = [ref[...] for ref in refs[2:-4]]
+    v_ref, xv_ref, west_ref, east_ref = refs[-4:]
+    here = place_ref[3]
+    bit = 1
+    while bit < len(pieces):
+        turn = (here // bit) % 2 == 1
+        pieces = [jnp.where(turn, pieces[i ^ bit], pieces[i]) for i in range(len(pieces))]
+        bit *= 2
+    share = pieces[0].shape[1]
+    for i, piece in enumerate(pieces):
+        v_ref[:, i * share : (i + 1) * share] = piece
     high, low = split(v_ref[:PAIRS])
     both = lax.dot_general(jnp.concatenate([high, low], axis=0), a_ref[...], NT, preferred_element_type=F32)
     xv = both[:PAIRS] + both[PAIRS:]
     xv_ref[...] = xv
-    lane = lane_ids((PAIRS, LANES))
-    west = jnp.zeros((PAIRS, LANES), F32)
-    east = west
-    for r in range(rows):
-        part = xv[:, r * LANES : (r + 1) * LANES]
-        first = rows * reach + reach * r
-        west = jnp.where((lane >= first) & (lane < first + reach), pltpu.roll(part, first % LANES, 1), west)
-        first = reach * r
-        east = jnp.where((lane >= first) & (lane < first + reach), pltpu.roll(part, (first + reach) % LANES, 1), east)
-    west_ref[...] = west
-    east_ref[...] = east
+    west_ref[...], east_ref[...] = edges([xv[:, r * LANES : (r + 1) * LANES] for r in range(rows)], reach)
 
 
 def fields_kernel(step, rows, reach, total, chunk, *refs):
-    m_ref, mh_ref, v_ref, u_ref, coast_ref, xv_ref, xw_ref, xe_ref = refs[:8]
-    refs = refs[8:]
+    m_ref, mh_ref, v_ref, u_ref, uh_ref, coast_ref, coasth_ref, xv_ref, xw_ref, xe_ref = refs[:10]
+    refs = refs[10:]
     older = refs[: 2 * max(step - 1, 0)]
     refs = refs[len(older) :]
     if step:
@@ -189,8 +239,10 @@
         w_ref, vs, us = refs
     days = v_ref.shape[1]
     low = 2 * step
+    own = rows * LANES
     vs[...] = v_ref[...]
-    us[...] = u_ref[...]
+    us[:, :own] = u_ref[...]
+    us[:, own:] = uh_ref[...]
     for q in range(step - 1):
         vs[2 * q : 2 * q + 2] = older[2 * q][...]
         us[2 * q : 2 * q + 2] = older[2 * q + 1][...]
@@ -201,7 +253,7 @@
         vs[low - 2 : low] = vn
         us[low - 2 : low] = un
     modes = vs.shape[0]
-    acc = accH = None
+    acc = acc_h = None
     for first in range(0, days, chunk):
         at = slice(first, first + chunk)
         v = vs[:, at]
@@ -210,11 +262,11 @@
             parts.append(v * v[j : j + 1])
         high, lower = split(jnp.concatenate(parts, axis=0))
         left = jnp.concatenate([high, lower], axis=0)
-        own = lax.dot_general(left, m_ref[:, at], NT, preferred_element_type=F32)
-        halo = lax.dot_general(left, mh_ref[:, at], NT, preferred_element_type=F32)
-        acc = own if acc is None else acc + own
-        accH = halo if accH is None else accH + halo
-    masked = jnp.concatenate([acc[: 2 * modes] + acc[2 * modes :], accH[: 2 * modes] + accH[2 * modes :]], axis=1)
+        mid = lax.dot_general(left, m_ref[:, at], NT, preferred_element_type=F32)
+        edge = lax.dot_general(left, mh_ref[:, at], NT, preferred_element_type=F32)
+        acc = mid if acc is None else acc + mid
+        acc_h = edge if acc_h is None else acc_h + edge
+    masked = jnp.concatenate([acc[: 2 * modes] + acc[2 * modes :], acc_h[: 2 * modes] + acc_h[2 * modes :]], axis=1)
     lane = lane_ids((PAIRS, LANES))
     xh = jnp.where(lane < LANES // 2, xw_ref[...], xe_ref[...])
     xv = jnp.concatenate([xv_ref[...], xh], axis=1)
@@ -226,7 +278,7 @@
     v0, v1 = (vs[low : low + 1], vs[low + 1 : low + 2])
     h00, h01, h11 = (total_of(v0 * v0), total_of(v0 * v1), total_of(v1 * v1))
     add0, add1 = solve_pair(h00, h01, h01, h11, proj[0], proj[1])
-    coast = coast_ref[...]
+    coast = jnp.concatenate([coast_ref[...], coasth_ref[...]], axis=1)
     fresh = coast * jnp.concatenate([u[low : low + 1] + add0, u[low + 1 : low + 2] + add1], axis=0)
     count = 2 * rows
     w_ref[:count] = to_block(fresh, rows, reach)
@@ -264,7 +316,7 @@
     low = 2 * step
     own = rows * LANES
     vs[...] = v_ref[...]
-    us[...] = u_ref[:, :own]
+    us[...] = u_ref[...]
     for q in range(step):
         vs[2 * q : 2 * q + 2] = older[2 * q][...]
         us[2 * q : 2 * q + 2] = older[2 * q + 1][:, :own]
@@ -330,7 +382,8 @@
     un_ref[...] = un
 
 
-def call(kernel, name, outs, scratch, args, smem=(), mib=24):
+def call(kernel, name, outs, scratch, args, smem=(), mib=24, flops=0):
+    moved = sum(z.size * z.dtype.itemsize for z in args)
     return pl.pallas_call(
         kernel,
         out_shape=[jax.ShapeDtypeStruct(s, t) for s, t in outs],
@@ -338,6 +391,7 @@
         out_specs=[VMEM for _ in outs],
         scratch_shapes=[pltpu.VMEM(s, t) for s, t in scratch],
         compiler_params=pltpu.CompilerParams(vmem_limit_bytes=mib * 2**20),
+        cost_estimate=pl.CostEstimate(flops=flops, bytes_accessed=moved, transcendentals=0),
         name=name,
     )(*args)
 
@@ -358,57 +412,63 @@
     assert columns == LANES and sides == LANES and rows == SWEEPS and days == BITS * words
     chunk = days // 5
     row0 = lax.axis_index("lat") * rows
-    place = jnp.stack([row0, jnp.int32(nlat), lax.axis_index("lat") % 2]).astype(jnp.int32)
+    here = lax.axis_index("lon")
+    place = jnp.stack([row0, jnp.int32(nlat), lax.axis_index("lat") % 2, here]).astype(jnp.int32)
     tall = row0 - rows + jnp.arange(6 * rows) // 2
     cos_tall = latitude_cos(tall, nlat)[:, None]
     klon = jnp.broadcast_to(KLON / (cos_tall * cos_tall), (6 * rows, 2 * LANES))
     cosl = jnp.broadcast_to(cos_tall[2 * rows : 4 * rows], (2 * rows, 2 * LANES))
 
-    fields = jnp.concatenate([mode_maps, ocean_binary_mask.astype(F32)[None]], axis=0)
-    from_west, from_east = lon_ring(
-        fields[:, :, :reach].reshape(modes + 1, -1), fields[:, :, columns - reach :].reshape(modes + 1, -1)
-    )
-    words_west, words_east = lon_ring(
-        missing_date_bitmask[:, :reach].reshape(-1, words), missing_date_bitmask[:, columns - reach :].reshape(-1, words)
-    )
-    v = lax.all_gather(mode_series, "lon", axis=1, tiled=True)
+    tall_edge = modes + 8 + rows * reach * (words // LANES)
+    u, coast, to_west, to_east = call(
+        functools.partial(prep_kernel, reach),
+        "prep",
+        [((modes, own), F32), ((1, own), F32), ((tall_edge, LANES), F32), ((tall_edge, LANES), F32)],
+        [],
+        [mode_maps, ocean_binary_mask, missing_date_bitmask],
+    )
+    from_west, from_east = lon_ring(to_west, to_east)
+    nlon = lax.axis_size("lon")
+    if nlon == 8:
+        pieces = [mode_series] + [swap(mode_series, 0, b) for b in (2, 4, 6)]
+        pieces = [z for piece in pieces for z in (piece, swap(piece, 0, 1))]
+    else:
+        pieces = [lax.all_gather(mode_series, "lon", axis=1, tiled=True)]
 
     words_per = words // LANES
-    spread = [pltpu.VMEM((2 * LANES, days // words_per), BF16), pltpu.VMEM((1, days // words_per), jnp.int32)]
-    tile = LANES
+    flags_scratch = [((2 * LANES, days // words_per), BF16), ((1, days // words_per), jnp.int32)]
+    x = pltpu.with_memory_space_constraint(sea_heat_deviations.reshape(own, days), pltpu.HBM)
     m, a = pl.pallas_call(
         own_flags_kernel,
-        grid=(own // tile,),
+        grid=(rows,),
         out_shape=[jax.ShapeDtypeStruct((own, days), BF16)] * 2,
         in_specs=[
-            pl.BlockSpec((tile, words), lambda i: (i, 0)),
-            pl.BlockSpec((tile, 1), lambda i: (i, 0)),
-            pl.BlockSpec((tile, days), lambda i: (i, 0)),
+            pl.BlockSpec((LANES, words), lambda i: (i, 0)),
+            pl.BlockSpec((rows, LANES), lambda i: (0, 0)),
+            pl.BlockSpec((LANES, days), lambda i: (i, 0)),
         ],
-        out_specs=[pl.BlockSpec((tile, days), lambda i: (i, 0))] * 2,
-        scratch_shapes=spread,
+        out_specs=[pl.BlockSpec((LANES, days), lambda i: (i, 0))] * 2,
+        scratch_shapes=[pltpu.VMEM(s, t) for s, t in flags_scratch],
         compiler_params=pltpu.CompilerParams(vmem_limit_bytes=24 * 2**20),
+        cost_estimate=pl.CostEstimate(flops=4 * LANES * own * days, bytes_accessed=6 * own * days, transcendentals=0),
         name="own_flags",
-    )(
-        missing_date_bitmask.reshape(own, words),
-        ocean_binary_mask.reshape(own, 1),
-        sea_heat_deviations.reshape(own, days),
-    )
-    all_fields = jnp.concatenate([fields.reshape(modes + 1, own), from_west, from_east], axis=1)
-    u, coast = (all_fields[:modes], all_fields[modes:])
-    (m_halo,) = call(
-        halo_flags_kernel,
+    )(missing_date_bitmask.reshape(own, words), ocean_binary_mask, x)
+    m_halo, u_halo, coast_halo = call(
+        functools.partial(halo_flags_kernel, modes),
         "halo_flags",
-        [((sides, days), BF16)],
-        [((2 * LANES, days // words_per), BF16), ((1, days // words_per), jnp.int32)],
-        [jnp.concatenate([words_west, words_east], axis=0), coast[0, own:].astype(jnp.int32).reshape(sides, 1)],
-    )
-    xv, to_west, to_east = call(
+        [((sides, days), BF16), ((modes, sides), F32), ((1, sides), F32)],
+        flags_scratch,
+        [from_west, from_east],
+        flops=4 * LANES * sides * days,
+    )
+    v, xv, to_west, to_east = call(
         functools.partial(given_kernel, rows, reach),
         "given",
-        [((PAIRS, own), F32), ((PAIRS, LANES), F32), ((PAIRS, LANES), F32)],
+        [((modes, days), F32), ((PAIRS, own), F32), ((PAIRS, LANES), F32), ((PAIRS, LANES), F32)],
         [],
-        [v, a],
+        [a, place, *pieces],
+        smem=(1,),
+        flops=4 * PAIRS * own * days,
     )
     xv_west, xv_east = lon_ring(to_west, to_east)
 
@@ -428,7 +488,8 @@
             f"fields_{step}",
             outs,
             [((modes, days), F32), ((modes, cells), F32)],
-            [m, m_halo, v, u, coast, xv, xv_west, xv_east, *extra],
+            [m, m_halo, v, u, u_halo, coast, coast_halo, xv, xv_west, xv_east, *extra],
+            flops=8 * modes * cells * days,
         )
         fresh = got[0]
         news += got[1:]
@@ -440,6 +501,7 @@
             [((modes, days), F32), ((modes, own), F32)],
             [m, a, v, u, place, klon, cosl, fresh, got_a, got_b, *coasts, *news],
             smem=(4,),
+            flops=8 * modes * own * days,
         )
         if step == 0:
             coasts = (fresh, got_a, got_b)

time: 154 us -> 133 us (0.86)
  blocking collectives: 17.6 us -> 0 us
  local copies, waits for them, and re-layouts: 9.88 us -> 4.58 us
  Pallas kernels: 23.1 us -> 26 us
  starting transfers between devices: 52.8 us -> 51 us
    all_gather x1 -> x0, blocking collectives: 17.6 us -> none  [shards(): v = lax.all_gather(mode_series, 'lon', axis=1, tiled=True)]
    unnamed x20 -> x12, local copies, waits for them, and re-layouts: 8.53 us -> 4.34 us
    ppermute x3 -> x2, starting transfers between devices: 9.45 us -> 5.99 us  [lon_ring(): lax.ppermute(to_west, 'lon', [(j, i) for i, j in up])]
    ppermute x28 -> x35, waiting for transfers between devices: 32.1 us -> 29.8 us  [swap(): lax.ppermute(x, ('lat', 'lon'), pairing(lambda i: i ^ lat_bits, lambda j:...]
    ppermute x28 -> x35, starting transfers between devices: 32.3 us -> 34.4 us  [swap(): lax.ppermute(x, ('lat', 'lon'), pairing(lambda i: i ^ lat_bits, lambda j:...]
    pallas_call x1, Pallas kernels: 2.9 us -> 4.94 us  [shards(): pl.pallas_call(own_flags_kernel, grid=(rows,), out_shape=[jax.ShapeDtypeS...]
    ppermute x3 -> x2, waiting for transfers between devices: 2.29 us -> 3.5 us  [lon_ring(): lax.ppermute(to_east, 'lon', up)]
    pallas_call x11 -> x12, Pallas kernels: 20.2 us -> 21.1 us  [call(): pl.pallas_call(kernel, out_shape=[jax.ShapeDtypeStruct(s, t) for s, t in...]
  transfers between devices with their start and end apart: 42 -> 47, of which waited for: 34 -> 35; matrix products, arithmetic and copies ran while one was open for 1% -> 0% of each run, Pallas kernels for 1% -> 6%
where the time goes in v3:
time: 133 us
  starting transfers between devices  51 us (38%)
  waiting for transfers between devices  48 us (36%)
  Pallas kernels  26 us (20%)
  local copies, waits for them, and re-layouts  4.58 us (3%)
  other arithmetic  1.91 us (1%)
    ppermute x35, starting transfers between devices, swap(): lax.ppermute(x, ('lat', 'lon'), pairing(lambda i: i ^ lat_bits, lambda j:...  34.4 us
    ppermute x35, waiting for transfers between devices, swap(): lax.ppermute(x, ('lat', 'lon'), pairing(lambda i: i ^ lat_bits, lambda j:...  29.8 us
    pallas_call x12, Pallas kernels, call(): pl.pallas_call(kernel, out_shape=[jax.ShapeDtypeStruct(s, t) for s, t in...  21.1 us
    ppermute x4, waiting for transfers between devices, lat_partners(): lax.ppermute(x, ('lat', 'lon'), pairing(lambda i: (i + 1 if i % 2 else i...  9.6 us
    ppermute x4, starting transfers between devices, lat_partners(): got_a = lax.ppermute(x, ('lat', 'lon'), pairing(lambda i: i ^ 1, same))  6.14 us
    ppermute x2, starting transfers between devices, lon_ring(): lax.ppermute(to_west, 'lon', [(j, i) for i, j in up])  5.99 us
    pallas_call x1, Pallas kernels, shards(): pl.pallas_call(own_flags_kernel, grid=(rows,), out_shape=[jax.ShapeDtypeS...  4.94 us
    ppermute x4, waiting for transfers between devices, lat_partners(): got_a = lax.ppermute(x, ('lat', 'lon'), pairing(lambda i: i ^ 1, same))  4.66 us
  transfers between devices with their start and end apart: 47, of which 35 were waited for; matrix products, arithmetic and copies ran while one was open for 0% of the time, Pallas kernels for 6%

profile of v3, /device:TPU:0, one launch (start us, length us, event | category | flops | bytes accessed | tf_op | source)
XLA Modules:
  0.0 132.5 jit_solution(12984612840157407319)
XLA Ops:
  0.6 3.1 %collective-permute-start.3 = (f32[48,480]{1,0:T(8,128)}, f32[48,480]{1,0:T(8,128)S(1)}, u32[]{:S(2)}, u32[]{:S(2)}) collective-permute-start(f32[48,480]{1,0:T(8,128)} %refs_2_.1), channel_id=1, source_target_pairs={{0,2},{1,3},{2,0},{3,1},{4,6},{5,7},{6,4},{7,5},{8,10},{9,11},{10,... | collective-permute-start | bytes 276488 | tf_op jit(solution)/shard_map/ppermute | solution.py:32
  3.7 2.6 %collective-permute-start.5 = (f32[48,480]{1,0:T(8,128)}, f32[48,480]{1,0:T(8,128)S(1)}, u32[]{:S(2)}, u32[]{:S(2)}) collective-permute-start(f32[48,480]{1,0:T(8,128)} %refs_2_.1), channel_id=1, source_target_pairs={{0,4},{1,5},{2,6},{3,7},{4,0},{5,1},{6,2},{7,3},{8,12},{9,13},{10,... | collective-permute-start | bytes 276488 | tf_op jit(solution)/shard_map/ppermute | solution.py:32
  6.3 1.0 copy-done
  7.4 0.9 copy-done.2
  8.3 0.7 copy-done.4
  9.8 3.5 %collective-permute-start.1 = (f32[184,128]{1,0:T(8,128)S(1)}, f32[184,128]{1,0:T(8,128)S(1)}, u32[]{:S(2)}, u32[]{:S(2)}) collective-permute-start(f32[184,128]{1,0:T(8,128)S(1)} %get-tuple-element.36), channel_id=1, source_target_pairs={{1,0},{2,1},{3,2},{4,3},{5,4},{6,5},{7,6},{0,7},{9,8},{10,9},{11,1... | collective-permute-start | bytes 282632 | tf_op jit(solution)/shard_map/ppermute | solution.py:67
  13.2 1.2 collective-permute-done.5.refs_6_
  15.1 1.0 copy-done.1
  16.1 0.7 copy-done.5
  16.8 4.9 %own_flags.1 = (bf16[512,3840]{1,0:T(8,128)(2,1)S(1)}, bf16[512,3840]{1,0:T(8,128)(2,1)S(1)}) custom-call(s32[512,256]{1,0:T(8,128)S(1)} %bitcast.7, s32[4,128]{1,0:T(4,128)S(1)} %copy-done.5, bf16[512,3840]{1,0:T(8,128)(2,1)} %bitcast.8), custom_call_target="tpu_custom_call" | custom-call | flops 1006632960 | bytes 11796480 | tf_op jit(solution)/shard_map/own_flags/pallas_call | solution.py:441
  21.8 1.8 %given.1 = (f32[48,3840]{1,0:T(8,128)S(1)}, f32[8,512]{1,0:T(8,128)S(1)}, f32[8,128]{1,0:T(8,128)S(1)}, f32[8,128]{1,0:T(8,128)S(1)}) custom-call(bf16[512,3840]{1,0:T(8,128)(2,1)S(1)} %get-tuple-element.38.refs_0_.refs_1_, s32[4]{0:T(128)S(1)} %pad_add_fusion.refs_1_.refs_4_, f32[48,480]{1,0:T(8,128)S(1)} %copy-done.3, ...), custom_call_target="tpu_custom_call" | custom-call | flops 62914560 | bytes 4669456 | tf_op jit(solution)/shard_map/given/pallas_call | solution.py:387
  23.6 2.5 %collective-permute-start.10 = (f32[8,128]{1,0:T(8,128)S(1)}, f32[8,128]{1,0:T(8,128)S(1)}, u32[]{:S(2)}, u32[]{:S(2)}) collective-permute-start(f32[8,128]{1,0:T(8,128)S(1)} %get-tuple-element.46), channel_id=1, source_target_pairs={{1,0},{2,1},{3,2},{4,3},{5,4},{6,5},{7,6},{0,7},{9,8},{10,9},{11,1... | collective-permute-start | bytes 12296 | tf_op jit(solution)/shard_map/ppermute | solution.py:67
  26.1 0.8 halo_flags.1
  27.4 3.5 %collective-permute-done.9.refs_8_ = f32[8,128]{1,0:T(8,128)S(1)} collective-permute-done((f32[8,128]{1,0:T(8,128)S(1)}, f32[8,128]{1,0:T(8,128)S(1)}, u32[]{:S(2)}, u32[]{:S(2)}) %collective-permute-start.9) | collective-permute-done | bytes 4128 | tf_op jit(solution)/shard_map/ppermute | solution.py:67
  30.9 1.8 %fields_0.1.refs_7_.refs_10_ = f32[16,256]{1,0:T(8,128)S(1)} custom-call(bf16[512,3840]{1,0:T(8,128)(2,1)S(1)} %get-tuple-element.34.refs_0_, bf16[128,3840]{1,0:T(8,128)(2,1)S(1)} %get-tuple-element.37.refs_1_, f32[48,3840]{1,0:T(8,128)S(1)} %get-tuple-element.39.refs_2_, f32[48,512]{1,0:T(8,128)S(1)} %get-tuple-element.40.refs_3_, ...), custom_call_target="tpu_custom_call" | custom-call | flops 943718400 | bytes 5802496 | tf_op jit(solution)/shard_map/fields_0/pallas_call | solution.py:387
  32.7 1.6 %collective-permute-start.11 = (f32[16,256]{1,0:T(8,128)S(1)}, f32[16,256]{1,0:T(8,128)S(1)}, u32[]{:S(2)}, u32[]{:S(2)}) collective-permute-start(f32[16,256]{1,0:T(8,128)S(1)} %fields_0.1.refs_7_.refs_10_), channel_id=1, source_target_pairs={{0,8},{1,9},{2,10},{3,11},{4,12},{5,13},{6,14},{7,15},{8,0},{9,1},... | collective-permute-start | bytes 49160 | tf_op jit(solution)/shard_map/ppermute | solution.py:59
  34.3 1.5 %collective-permute-start.12 = (f32[16,256]{1,0:T(8,128)S(1)}, f32[16,256]{1,0:T(8,128)S(1)}, u32[]{:S(2)}, u32[]{:S(2)}) collective-permute-start(f32[16,256]{1,0:T(8,128)S(1)} %fields_0.1.refs_7_.refs_10_), channel_id=1, source_target_pairs={{0,24},{1,25},{2,26},{3,27},{4,28},{5,29},{6,30},{7,31},{8,16},{9,... | collective-permute-start | bytes 49160 | tf_op jit(solution)/shard_map/ppermute | solution.py:60
  35.9 0.6 collective-permute-done.11.refs_8_.refs_11_
  36.5 2.4 %collective-permute-done.12.refs_9_.refs_12_ = f32[16,256]{1,0:T(8,128)S(1)} collective-permute-done((f32[16,256]{1,0:T(8,128)S(1)}, f32[16,256]{1,0:T(8,128)S(1)}, u32[]{:S(2)}, u32[]{:S(2)}) %collective-permute-start.12) | collective-permute-done | bytes 16416 | tf_op jit(solution)/shard_map/ppermute | solution.py:60
  39.0 2.4 %sums_0.1 = (f32[2,3968]{1,0:T(2,128)S(1)}, f32[8,256]{1,0:T(8,128)S(1)}) custom-call(bf16[512,3840]{1,0:T(8,128)(2,1)S(1)} %get-tuple-element.34.refs_0_, bf16[512,3840]{1,0:T(8,128)(2,1)S(1)} %get-tuple-element.38.refs_0_.refs_1_, f32[48,3840]{1,0:T(8,128)S(1)} %get-tuple-element.39.refs_2_, f32[48,512]{1,0:T(8,128)S(1)} %get-tuple-element.40.refs_3_, ...), custom_call_target="tpu_custom_call" | custom-call | flops 754974720 | bytes 8781840 | tf_op jit(solution)/shard_map/sums_0/pallas_call | solution.py:387
  41.5 1.2 collective-permute-done.13
  43.1 1.5 %collective-permute-start.15 = (f32[2,3968]{1,0:T(2,128)S(1)}, f32[2,3968]{1,0:T(2,128)S(1)}, u32[]{:S(2)}, u32[]{:S(2)}) collective-permute-start(f32[2,3968]{1,0:T(2,128)S(1)} %add.126), channel_id=1, source_target_pairs={{0,17},{1,16},{2,19},{3,18},{4,21},{5,20},{6,23},{7,22},{8,25},{9,... | collective-permute-start | bytes 95240 | tf_op jit(solution)/shard_map/ppermute | solution.py:32
  44.6 1.2 collective-permute-start.16
  46.4 2.4 %collective-permute-done.16 = f32[2,3968]{1,0:T(2,128)S(1)} collective-permute-done((f32[2,3968]{1,0:T(2,128)S(1)}, f32[2,3968]{1,0:T(2,128)S(1)}, u32[]{:S(2)}, u32[]{:S(2)}) %collective-permute-start.16) | collective-permute-done | bytes 31776 | tf_op jit(solution)/shard_map/ppermute | solution.py:32
  48.9 1.5 %collective-permute-start.18 = (f32[2,3968]{1,0:T(2,128)S(1)}, f32[2,3968]{1,0:T(2,128)S(1)}, u32[]{:S(2)}, u32[]{:S(2)}) collective-permute-start(f32[2,3968]{1,0:T(2,128)S(1)} %add_add_fusion.7), channel_id=1, source_target_pairs={{0,5},{1,4},{2,7},{3,6},{4,1},{5,0},{6,3},{7,2},{8,13},{9,12},{10,... | collective-permute-start | bytes 95240 | tf_op jit(solution)/shard_map/ppermute | solution.py:32
  50.4 2.4 %collective-permute-start.19 = (f32[2,3968]{1,0:T(2,128)S(1)}, f32[2,3968]{1,0:T(2,128)S(1)}, u32[]{:S(2)}, u32[]{:S(2)}) collective-permute-start(f32[2,3968]{1,0:T(2,128)S(1)} %add_add_fusion.7), channel_id=1, source_target_pairs={{0,7},{1,6},{2,5},{3,4},{4,3},{5,2},{6,1},{7,0},{8,15},{9,14},{10,... | collective-permute-start | bytes 95240 | tf_op jit(solution)/shard_map/ppermute | solution.py:32
  53.2 2.3 %collective-permute-done.19 = f32[2,3968]{1,0:T(2,128)S(1)} collective-permute-done((f32[2,3968]{1,0:T(2,128)S(1)}, f32[2,3968]{1,0:T(2,128)S(1)}, u32[]{:S(2)}, u32[]{:S(2)}) %collective-permute-start.19) | collective-permute-done | bytes 31776 | tf_op jit(solution)/shard_map/ppermute | solution.py:32
  55.6 2.1 %fields_1.1 = (f32[8,256]{1,0:T(8,128)S(1)}, f32[2,3840]{1,0:T(2,128)S(1)}, f32[2,640]{1,0:T(2,128)S(1)}) custom-call(bf16[512,3840]{1,0:T(8,128)(2,1)S(1)} %get-tuple-element.34.refs_0_, bf16[128,3840]{1,0:T(8,128)(2,1)S(1)} %get-tuple-element.37.refs_1_, f32[48,3840]{1,0:T(8,128)S(1)} %get-tuple-element.39.refs_2_, ...), custom_call_target="tpu_custom_call" | custom-call | flops 943718400 | bytes 5842432 | tf_op jit(solution)/shard_map/fields_1/pallas_call | solution.py:387
  57.7 1.5 %collective-permute-start.20 = (f32[8,256]{1,0:T(8,128)S(1)}, f32[8,256]{1,0:T(8,128)S(1)}, u32[]{:S(2)}, u32[]{:S(2)}) collective-permute-start(f32[8,256]{1,0:T(8,128)S(1)} %get-tuple-element.51.refs_7_), channel_id=1, source_target_pairs={{0,8},{1,9},{2,10},{3,11},{4,12},{5,13},{6,14},{7,15},{8,0},{9,1},... | collective-permute-start | bytes 24584 | tf_op jit(solution)/shard_map/ppermute | solution.py:59
  59.7 1.7 %collective-permute-done.20.refs_8_ = f32[8,256]{1,0:T(8,128)S(1)} collective-permute-done((f32[8,256]{1,0:T(8,128)S(1)}, f32[8,256]{1,0:T(8,128)S(1)}, u32[]{:S(2)}, u32[]{:S(2)}) %collective-permute-start.20) | collective-permute-done | bytes 8224 | tf_op jit(solution)/shard_map/ppermute | solution.py:59
  61.4 2.4 %collective-permute-done.21.refs_9_ = f32[8,256]{1,0:T(8,128)S(1)} collective-permute-done((f32[8,256]{1,0:T(8,128)S(1)}, f32[8,256]{1,0:T(8,128)S(1)}, u32[]{:S(2)}, u32[]{:S(2)}) %collective-permute-start.21) | collective-permute-done | bytes 8224 | tf_op jit(solution)/shard_map/ppermute | solution.py:60
  63.8 2.4 %sums_1.1 = (f32[2,3968]{1,0:T(2,128)S(1)}, f32[8,256]{1,0:T(8,128)S(1)}) custom-call(bf16[512,3840]{1,0:T(8,128)(2,1)S(1)} %get-tuple-element.34.refs_0_, bf16[512,3840]{1,0:T(8,128)(2,1)S(1)} %get-tuple-element.38.refs_0_.refs_1_, f32[48,3840]{1,0:T(8,128)S(1)} %get-tuple-element.39.refs_2_, f32[48,512]{1,0:T(8,128)S(1)} %get-tuple-element.40.refs_3_, ...), custom_call_target="tpu_custom_call" | custom-call | flops 754974720 | bytes 8842256 | tf_op jit(solution)/shard_map/sums_1/pallas_call | solution.py:387
  66.3 1.2 collective-permute-done.22
  68.3 2.2 %collective-permute-start.25 = (f32[2,3968]{1,0:T(2,128)S(1)}, f32[2,3968]{1,0:T(2,128)S(1)}, u32[]{:S(2)}, u32[]{:S(2)}) collective-permute-start(f32[2,3968]{1,0:T(2,128)S(1)} %add.133), channel_id=1, source_target_pairs={{0,25},{1,24},{2,27},{3,26},{4,29},{5,28},{6,31},{7,30},{8,17},{9,... | collective-permute-start | bytes 95240 | tf_op jit(solution)/shard_map/ppermute | solution.py:32
  71.2 1.4 %collective-permute-done.25 = f32[2,3968]{1,0:T(2,128)S(1)} collective-permute-done((f32[2,3968]{1,0:T(2,128)S(1)}, f32[2,3968]{1,0:T(2,128)S(1)}, u32[]{:S(2)}, u32[]{:S(2)}) %collective-permute-start.25) | collective-permute-done | bytes 31776 | tf_op jit(solution)/shard_map/ppermute | solution.py:32
  72.6 2.9 %collective-permute-start.27 = (f32[2,3968]{1,0:T(2,128)S(1)}, f32[2,3968]{1,0:T(2,128)S(1)}, u32[]{:S(2)}, u32[]{:S(2)}) collective-permute-start(f32[2,3968]{1,0:T(2,128)S(1)} %add_add_fusion.5), channel_id=1, source_target_pairs={{0,5},{1,4},{2,7},{3,6},{4,1},{5,0},{6,3},{7,2},{8,13},{9,12},{10,... | collective-permute-start | bytes 95240 | tf_op jit(solution)/shard_map/ppermute | solution.py:32
  75.5 1.0 collective-permute-start.28
  77.1 3.5 %collective-permute-done.28 = f32[2,3968]{1,0:T(2,128)S(1)} collective-permute-done((f32[2,3968]{1,0:T(2,128)S(1)}, f32[2,3968]{1,0:T(2,128)S(1)}, u32[]{:S(2)}, u32[]{:S(2)}) %collective-permute-start.28) | collective-permute-done | bytes 31776 | tf_op jit(solution)/shard_map/ppermute | solution.py:32
  80.7 2.1 %fields_2.1 = (f32[8,256]{1,0:T(8,128)S(1)}, f32[2,3840]{1,0:T(2,128)S(1)}, f32[2,640]{1,0:T(2,128)S(1)}) custom-call(bf16[512,3840]{1,0:T(8,128)(2,1)S(1)} %get-tuple-element.34.refs_0_, bf16[128,3840]{1,0:T(8,128)(2,1)S(1)} %get-tuple-element.37.refs_1_, f32[48,3840]{1,0:T(8,128)S(1)} %get-tuple-element.39.refs_2_, ...), custom_call_target="tpu_custom_call" | custom-call | flops 943718400 | bytes 5878272 | tf_op jit(solution)/shard_map/fields_2/pallas_call | solution.py:387
  82.8 1.5 %collective-permute-start.29 = (f32[8,256]{1,0:T(8,128)S(1)}, f32[8,256]{1,0:T(8,128)S(1)}, u32[]{:S(2)}, u32[]{:S(2)}) collective-permute-start(f32[8,256]{1,0:T(8,128)S(1)} %get-tuple-element.56.refs_7_), channel_id=1, source_target_pairs={{0,8},{1,9},{2,10},{3,11},{4,12},{5,13},{6,14},{7,15},{8,0},{9,1},... | collective-permute-start | bytes 24584 | tf_op jit(solution)/shard_map/ppermute | solution.py:59
  84.3 1.5 %collective-permute-start.30 = (f32[8,256]{1,0:T(8,128)S(1)}, f32[8,256]{1,0:T(8,128)S(1)}, u32[]{:S(2)}, u32[]{:S(2)}) collective-permute-start(f32[8,256]{1,0:T(8,128)S(1)} %get-tuple-element.56.refs_7_), channel_id=1, source_target_pairs={{0,24},{1,25},{2,26},{3,27},{4,28},{5,29},{6,30},{7,31},{8,16},{9,... | collective-permute-start | bytes 24584 | tf_op jit(solution)/shard_map/ppermute | solution.py:60
  85.8 0.7 collective-permute-done.29.refs_8_
  86.5 2.4 %collective-permute-done.30.refs_9_ = f32[8,256]{1,0:T(8,128)S(1)} collective-permute-done((f32[8,256]{1,0:T(8,128)S(1)}, f32[8,256]{1,0:T(8,128)S(1)}, u32[]{:S(2)}, u32[]{:S(2)}) %collective-permute-start.30) | collective-permute-done | bytes 8224 | tf_op jit(solution)/shard_map/ppermute | solution.py:60
  88.9 2.4 %sums_2.1 = (f32[2,3968]{1,0:T(2,128)S(1)}, f32[8,256]{1,0:T(8,128)S(1)}) custom-call(bf16[512,3840]{1,0:T(8,128)(2,1)S(1)} %get-tuple-element.34.refs_0_, bf16[512,3840]{1,0:T(8,128)(2,1)S(1)} %get-tuple-element.38.refs_0_.refs_1_, f32[48,3840]{1,0:T(8,128)S(1)} %get-tuple-element.39.refs_2_, f32[48,512]{1,0:T(8,128)S(1)} %get-tuple-element.40.refs_3_, ...), custom_call_target="tpu_custom_call" | custom-call | flops 754974720 | bytes 8878096 | tf_op jit(solution)/shard_map/sums_2/pallas_call | solution.py:387
  91.4 1.2 collective-permute-done.31
  92.9 1.5 %collective-permute-start.33 = (f32[2,3968]{1,0:T(2,128)S(1)}, f32[2,3968]{1,0:T(2,128)S(1)}, u32[]{:S(2)}, u32[]{:S(2)}) collective-permute-start(f32[2,3968]{1,0:T(2,128)S(1)} %add.140), channel_id=1, source_target_pairs={{0,17},{1,16},{2,19},{3,18},{4,21},{5,20},{6,23},{7,22},{8,25},{9,... | collective-permute-start | bytes 95240 | tf_op jit(solution)/shard_map/ppermute | solution.py:32
  94.4 1.2 collective-permute-start.34
  96.3 2.4 %collective-permute-done.34 = f32[2,3968]{1,0:T(2,128)S(1)} collective-permute-done((f32[2,3968]{1,0:T(2,128)S(1)}, f32[2,3968]{1,0:T(2,128)S(1)}, u32[]{:S(2)}, u32[]{:S(2)}) %collective-permute-start.34) | collective-permute-done | bytes 31776 | tf_op jit(solution)/shard_map/ppermute | solution.py:32
  98.7 1.5 %collective-permute-start.36 = (f32[2,3968]{1,0:T(2,128)S(1)}, f32[2,3968]{1,0:T(2,128)S(1)}, u32[]{:S(2)}, u32[]{:S(2)}) collective-permute-start(f32[2,3968]{1,0:T(2,128)S(1)} %add_add_fusion.3), channel_id=1, source_target_pairs={{0,5},{1,4},{2,7},{3,6},{4,1},{5,0},{6,3},{7,2},{8,13},{9,12},{10,... | collective-permute-start | bytes 95240 | tf_op jit(solution)/shard_map/ppermute | solution.py:32
  100.2 2.4 %collective-permute-start.37 = (f32[2,3968]{1,0:T(2,128)S(1)}, f32[2,3968]{1,0:T(2,128)S(1)}, u32[]{:S(2)}, u32[]{:S(2)}) collective-permute-start(f32[2,3968]{1,0:T(2,128)S(1)} %add_add_fusion.3), channel_id=1, source_target_pairs={{0,7},{1,6},{2,5},{3,4},{4,3},{5,2},{6,1},{7,0},{8,15},{9,14},{10,... | collective-permute-start | bytes 95240 | tf_op jit(solution)/shard_map/ppermute | solution.py:32
  103.0 2.3 %collective-permute-done.37 = f32[2,3968]{1,0:T(2,128)S(1)} collective-permute-done((f32[2,3968]{1,0:T(2,128)S(1)}, f32[2,3968]{1,0:T(2,128)S(1)}, u32[]{:S(2)}, u32[]{:S(2)}) %collective-permute-start.37) | collective-permute-done | bytes 31776 | tf_op jit(solution)/shard_map/ppermute | solution.py:32
  105.4 2.3 %fields_3.1 = (f32[8,256]{1,0:T(8,128)S(1)}, f32[2,3840]{1,0:T(2,128)S(1)}, f32[2,640]{1,0:T(2,128)S(1)}) custom-call(bf16[512,3840]{1,0:T(8,128)(2,1)S(1)} %get-tuple-element.34.refs_0_, bf16[128,3840]{1,0:T(8,128)(2,1)S(1)} %get-tuple-element.37.refs_1_, f32[48,3840]{1,0:T(8,128)S(1)} %get-tuple-element.39.refs_2_, ...), custom_call_target="tpu_custom_call" | custom-call | flops 943718400 | bytes 5914112 | tf_op jit(solution)/shard_map/fields_3/pallas_call | solution.py:387
  107.7 1.5 %collective-permute-start.38 = (f32[8,256]{1,0:T(8,128)S(1)}, f32[8,256]{1,0:T(8,128)S(1)}, u32[]{:S(2)}, u32[]{:S(2)}) collective-permute-start(f32[8,256]{1,0:T(8,128)S(1)} %get-tuple-element.60.refs_7_), channel_id=1, source_target_pairs={{0,8},{1,9},{2,10},{3,11},{4,12},{5,13},{6,14},{7,15},{8,0},{9,1},... | collective-permute-start | bytes 24584 | tf_op jit(solution)/shard_map/ppermute | solution.py:59
  109.7 1.7 %collective-permute-done.38.refs_8_ = f32[8,256]{1,0:T(8,128)S(1)} collective-permute-done((f32[8,256]{1,0:T(8,128)S(1)}, f32[8,256]{1,0:T(8,128)S(1)}, u32[]{:S(2)}, u32[]{:S(2)}) %collective-permute-start.38) | collective-permute-done | bytes 8224 | tf_op jit(solution)/shard_map/ppermute | solution.py:59
  111.4 2.4 %collective-permute-done.39.refs_9_ = f32[8,256]{1,0:T(8,128)S(1)} collective-permute-done((f32[8,256]{1,0:T(8,128)S(1)}, f32[8,256]{1,0:T(8,128)S(1)}, u32[]{:S(2)}, u32[]{:S(2)}) %collective-permute-start.39) | collective-permute-done | bytes 8224 | tf_op jit(solution)/shard_map/ppermute | solution.py:60
  113.8 2.4 %sums_3.1 = (f32[2,3968]{1,0:T(2,128)S(1)}, f32[8,256]{1,0:T(8,128)S(1)}) custom-call(bf16[512,3840]{1,0:T(8,128)(2,1)S(1)} %get-tuple-element.34.refs_0_, bf16[512,3840]{1,0:T(8,128)(2,1)S(1)} %get-tuple-element.38.refs_0_.refs_1_, f32[48,3840]{1,0:T(8,128)S(1)} %get-tuple-element.39.refs_2_, f32[48,512]{1,0:T(8,128)S(1)} %get-tuple-element.40.refs_3_, ...), custom_call_target="tpu_custom_call" | custom-call | flops 754974720 | bytes 8913936 | tf_op jit(solution)/shard_map/sums_3/pallas_call | solution.py:387
  116.3 1.2 collective-permute-done.40
  118.3 2.2 %collective-permute-start.43 = (f32[2,3968]{1,0:T(2,128)S(1)}, f32[2,3968]{1,0:T(2,128)S(1)}, u32[]{:S(2)}, u32[]{:S(2)}) collective-permute-start(f32[2,3968]{1,0:T(2,128)S(1)} %add.147), channel_id=1, source_target_pairs={{0,25},{1,24},{2,27},{3,26},{4,29},{5,28},{6,31},{7,30},{8,17},{9,... | collective-permute-start | bytes 95240 | tf_op jit(solution)/shard_map/ppermute | solution.py:32
  121.2 1.4 %collective-permute-done.43 = f32[2,3968]{1,0:T(2,128)S(1)} collective-permute-done((f32[2,3968]{1,0:T(2,128)S(1)}, f32[2,3968]{1,0:T(2,128)S(1)}, u32[]{:S(2)}, u32[]{:S(2)}) %collective-permute-start.43) | collective-permute-done | bytes 31776 | tf_op jit(solution)/shard_map/ppermute | solution.py:32
  122.7 2.9 %collective-permute-start.45 = (f32[2,3968]{1,0:T(2,128)S(1)}, f32[2,3968]{1,0:T(2,128)S(1)}, u32[]{:S(2)}, u32[]{:S(2)}) collective-permute-start(f32[2,3968]{1,0:T(2,128)S(1)} %add_add_fusion.1), channel_id=1, source_target_pairs={{0,5},{1,4},{2,7},{3,6},{4,1},{5,0},{6,3},{7,2},{8,13},{9,12},{10,... | collective-permute-start | bytes 95240 | tf_op jit(solution)/shard_map/ppermute | solution.py:32
  125.6 1.0 collective-permute-start.46
  127.1 3.5 %collective-permute-done.46 = f32[2,3968]{1,0:T(2,128)S(1)} collective-permute-done((f32[2,3968]{1,0:T(2,128)S(1)}, f32[2,3968]{1,0:T(2,128)S(1)}, u32[]{:S(2)}, u32[]{:S(2)}) %collective-permute-start.46) | collective-permute-done | bytes 31776 | tf_op jit(solution)/shard_map/ppermute | solution.py:32
  131.2 0.6 pad_maximum_fusion.1
  131.8 0.7 pad_maximum_fusion
  (85 shorter events, 11.4 us)
Async XLA Ops:
  0.6 9.1 %collective-permute-start.3 = (f32[48,480]{1,0:T(8,128)}, f32[48,480]{1,0:T(8,128)S(1)}, u32[]{:S(2)}, u32[]{:S(2)}) collective-permute-start(f32[48,480]{1,0:T(8,128)} %refs_2_.1), channel_id=1, source_target_pairs={{0,2},{1,3},{2,0},{3,1},{4,6},{5,7},{6,4},{7,5},{8,10},{9,11},{10,... | collective-permute-start | bytes 276488 | tf_op jit(solution)/shard_map/ppermute | solution.py:32
  3.7 10.8 %collective-permute-start.5 = (f32[48,480]{1,0:T(8,128)}, f32[48,480]{1,0:T(8,128)S(1)}, u32[]{:S(2)}, u32[]{:S(2)}) collective-permute-start(f32[48,480]{1,0:T(8,128)} %refs_2_.1), channel_id=1, source_target_pairs={{0,4},{1,5},{2,6},{3,7},{4,0},{5,1},{6,2},{7,3},{8,12},{9,13},{10,... | collective-permute-start | bytes 276488 | tf_op jit(solution)/shard_map/ppermute | solution.py:32
  6.3 8.2 %collective-permute-start.7 = (f32[48,480]{1,0:T(8,128)}, f32[48,480]{1,0:T(8,128)S(1)}, u32[]{:S(2)}, u32[]{:S(2)}) collective-permute-start(f32[48,480]{1,0:T(8,128)} %refs_2_.1), channel_id=1, source_target_pairs={{0,6},{1,7},{2,4},{3,5},{4,2},{5,3},{6,0},{7,1},{8,14},{9,15},{10,... | collective-permute-start | bytes 276488 | tf_op jit(solution)/shard_map/ppermute | solution.py:32
  6.3 8.7 %collective-permute-start.2 = (f32[48,480]{1,0:T(8,128)}, f32[48,480]{1,0:T(8,128)S(1)}, u32[]{:S(2)}, u32[]{:S(2)}) collective-permute-start(f32[48,480]{1,0:T(8,128)} %refs_2_.1), channel_id=1, source_target_pairs={{0,1},{1,0},{2,3},{3,2},{4,5},{5,4},{6,7},{7,6},{8,9},{9,8},{10,11... | collective-permute-start | bytes 276488 | tf_op jit(solution)/shard_map/ppermute | solution.py:32
  6.3 1.0 copy-start
  7.4 0.9 copy-start.2
  8.3 0.7 copy-start.4
  8.9 12.8 %copy-start.3 = (f32[48,480]{1,0:T(8,128)S(1)}, f32[48,480]{1,0:T(8,128)}, u32[]{:S(2)}) copy-start(f32[48,480]{1,0:T(8,128)} %refs_2_.1) | copy-start | bytes 276484
  9.1 17.0 %collective-permute-start = (f32[184,128]{1,0:T(8,128)S(1)}, f32[184,128]{1,0:T(8,128)S(1)}, u32[]{:S(2)}, u32[]{:S(2)}) collective-permute-start(f32[184,128]{1,0:T(8,128)S(1)} %get-tuple-element.35), channel_id=1, source_target_pairs={{0,1},{1,2},{2,3},{3,4},{4,5},{5,6},{6,7},{7,0},{8,9},{9,10},{10,1... | collective-permute-start | bytes 282632 | tf_op jit(solution)/shard_map/ppermute | solution.py:67
  9.8 16.3 %collective-permute-start.1 = (f32[184,128]{1,0:T(8,128)S(1)}, f32[184,128]{1,0:T(8,128)S(1)}, u32[]{:S(2)}, u32[]{:S(2)}) collective-permute-start(f32[184,128]{1,0:T(8,128)S(1)} %get-tuple-element.36), channel_id=1, source_target_pairs={{1,0},{2,1},{3,2},{4,3},{5,4},{6,5},{7,6},{0,7},{9,8},{10,9},{11,1... | collective-permute-start | bytes 282632 | tf_op jit(solution)/shard_map/ppermute | solution.py:67
  14.5 7.3 %collective-permute-start.4 = (f32[48,480]{1,0:T(8,128)S(1)}, f32[48,480]{1,0:T(8,128)S(1)}, u32[]{:S(2)}, u32[]{:S(2)}) collective-permute-start(f32[48,480]{1,0:T(8,128)S(1)} %collective-permute-done.3.refs_4_), channel_id=1, source_target_pairs={{0,1},{1,0},{2,3},{3,2},{4,5},{5,4},{6,7},{7,6},{8,9},{9,8},{10,11... | collective-permute-start | bytes 276488 | tf_op jit(solution)/shard_map/ppermute | solution.py:32
  14.5 7.3 %collective-permute-start.6 = (f32[48,480]{1,0:T(8,128)S(1)}, f32[48,480]{1,0:T(8,128)S(1)}, u32[]{:S(2)}, u32[]{:S(2)}) collective-permute-start(f32[48,480]{1,0:T(8,128)S(1)} %collective-permute-done.5.refs_6_), channel_id=1, source_target_pairs={{0,1},{1,0},{2,3},{3,2},{4,5},{5,4},{6,7},{7,6},{8,9},{9,8},{10,11... | collective-permute-start | bytes 276488 | tf_op jit(solution)/shard_map/ppermute | solution.py:32
  15.0 6.8 %collective-permute-start.8 = (f32[48,480]{1,0:T(8,128)S(1)}, f32[48,480]{1,0:T(8,128)S(1)}, u32[]{:S(2)}, u32[]{:S(2)}) collective-permute-start(f32[48,480]{1,0:T(8,128)S(1)} %collective-permute-done.7.refs_8_), channel_id=1, source_target_pairs={{0,1},{1,0},{2,3},{3,2},{4,5},{5,4},{6,7},{7,6},{8,9},{9,8},{10,11... | collective-permute-start | bytes 276488 | tf_op jit(solution)/shard_map/ppermute | solution.py:32
  15.1 1.0 copy-start.1
  16.1 0.7 copy-start.5
  23.6 3.9 %collective-permute-start.10 = (f32[8,128]{1,0:T(8,128)S(1)}, f32[8,128]{1,0:T(8,128)S(1)}, u32[]{:S(2)}, u32[]{:S(2)}) collective-permute-start(f32[8,128]{1,0:T(8,128)S(1)} %get-tuple-element.46), channel_id=1, source_target_pairs={{1,0},{2,1},{3,2},{4,3},{5,4},{6,5},{7,6},{0,7},{9,8},{10,9},{11,1... | collective-permute-start | bytes 12296 | tf_op jit(solution)/shard_map/ppermute | solution.py:67
  26.1 4.8 %collective-permute-start.9 = (f32[8,128]{1,0:T(8,128)S(1)}, f32[8,128]{1,0:T(8,128)S(1)}, u32[]{:S(2)}, u32[]{:S(2)}) collective-permute-start(f32[8,128]{1,0:T(8,128)S(1)} %get-tuple-element.45), channel_id=1, source_target_pairs={{0,1},{1,2},{2,3},{3,4},{4,5},{5,6},{6,7},{7,0},{8,9},{9,10},{10,1... | collective-permute-start | bytes 12296 | tf_op jit(solution)/shard_map/ppermute | solution.py:67
  32.7 3.8 %collective-permute-start.11 = (f32[16,256]{1,0:T(8,128)S(1)}, f32[16,256]{1,0:T(8,128)S(1)}, u32[]{:S(2)}, u32[]{:S(2)}) collective-permute-start(f32[16,256]{1,0:T(8,128)S(1)} %fields_0.1.refs_7_.refs_10_), channel_id=1, source_target_pairs={{0,8},{1,9},{2,10},{3,11},{4,12},{5,13},{6,14},{7,15},{8,0},{9,1},... | collective-permute-start | bytes 49160 | tf_op jit(solution)/shard_map/ppermute | solution.py:59
  34.3 4.6 %collective-permute-start.12 = (f32[16,256]{1,0:T(8,128)S(1)}, f32[16,256]{1,0:T(8,128)S(1)}, u32[]{:S(2)}, u32[]{:S(2)}) collective-permute-start(f32[16,256]{1,0:T(8,128)S(1)} %fields_0.1.refs_7_.refs_10_), channel_id=1, source_target_pairs={{0,24},{1,25},{2,26},{3,27},{4,28},{5,29},{6,30},{7,31},{8,16},{9,... | collective-permute-start | bytes 49160 | tf_op jit(solution)/shard_map/ppermute | solution.py:60
  41.5 1.3 collective-permute-start.13
  42.7 3.4 %collective-permute-start.14 = (f32[2,3968]{1,0:T(2,128)S(1)}, f32[2,3968]{1,0:T(2,128)S(1)}, u32[]{:S(2)}, u32[]{:S(2)}) collective-permute-start(f32[2,3968]{1,0:T(2,128)S(1)} %add.126), channel_id=1, source_target_pairs={{0,9},{1,8},{2,11},{3,10},{4,13},{5,12},{6,15},{7,14},{8,1},{9,0},... | collective-permute-start | bytes 95240 | tf_op jit(solution)/shard_map/ppermute | solution.py:32
  43.1 3.3 %collective-permute-start.15 = (f32[2,3968]{1,0:T(2,128)S(1)}, f32[2,3968]{1,0:T(2,128)S(1)}, u32[]{:S(2)}, u32[]{:S(2)}) collective-permute-start(f32[2,3968]{1,0:T(2,128)S(1)} %add.126), channel_id=1, source_target_pairs={{0,17},{1,16},{2,19},{3,18},{4,21},{5,20},{6,23},{7,22},{8,25},{9,... | collective-permute-start | bytes 95240 | tf_op jit(solution)/shard_map/ppermute | solution.py:32
  44.6 4.2 %collective-permute-start.16 = (f32[2,3968]{1,0:T(2,128)S(1)}, f32[2,3968]{1,0:T(2,128)S(1)}, u32[]{:S(2)}, u32[]{:S(2)}) collective-permute-start(f32[2,3968]{1,0:T(2,128)S(1)} %add.126), channel_id=1, source_target_pairs={{0,25},{1,24},{2,27},{3,26},{4,29},{5,28},{6,31},{7,30},{8,17},{9,... | collective-permute-start | bytes 95240 | tf_op jit(solution)/shard_map/ppermute | solution.py:32
  48.8 3.9 %collective-permute-start.17 = (f32[2,3968]{1,0:T(2,128)S(1)}, f32[2,3968]{1,0:T(2,128)S(1)}, u32[]{:S(2)}, u32[]{:S(2)}) collective-permute-start(f32[2,3968]{1,0:T(2,128)S(1)} %add_add_fusion.7), channel_id=1, source_target_pairs={{0,3},{1,2},{2,1},{3,0},{4,7},{5,6},{6,5},{7,4},{8,11},{9,10},{10,... | collective-permute-start | bytes 95240 | tf_op jit(solution)/shard_map/ppermute | solution.py:32
  48.9 4.3 %collective-permute-start.18 = (f32[2,3968]{1,0:T(2,128)S(1)}, f32[2,3968]{1,0:T(2,128)S(1)}, u32[]{:S(2)}, u32[]{:S(2)}) collective-permute-start(f32[2,3968]{1,0:T(2,128)S(1)} %add_add_fusion.7), channel_id=1, source_target_pairs={{0,5},{1,4},{2,7},{3,6},{4,1},{5,0},{6,3},{7,2},{8,13},{9,12},{10,... | collective-permute-start | bytes 95240 | tf_op jit(solution)/shard_map/ppermute | solution.py:32
  50.4 5.1 %collective-permute-start.19 = (f32[2,3968]{1,0:T(2,128)S(1)}, f32[2,3968]{1,0:T(2,128)S(1)}, u32[]{:S(2)}, u32[]{:S(2)}) collective-permute-start(f32[2,3968]{1,0:T(2,128)S(1)} %add_add_fusion.7), channel_id=1, source_target_pairs={{0,7},{1,6},{2,5},{3,4},{4,3},{5,2},{6,1},{7,0},{8,15},{9,14},{10,... | collective-permute-start | bytes 95240 | tf_op jit(solution)/shard_map/ppermute | solution.py:32
  57.7 3.7 %collective-permute-start.20 = (f32[8,256]{1,0:T(8,128)S(1)}, f32[8,256]{1,0:T(8,128)S(1)}, u32[]{:S(2)}, u32[]{:S(2)}) collective-permute-start(f32[8,256]{1,0:T(8,128)S(1)} %get-tuple-element.51.refs_7_), channel_id=1, source_target_pairs={{0,8},{1,9},{2,10},{3,11},{4,12},{5,13},{6,14},{7,15},{8,0},{9,1},... | collective-permute-start | bytes 24584 | tf_op jit(solution)/shard_map/ppermute | solution.py:59
  59.2 4.5 %collective-permute-start.21 = (f32[8,256]{1,0:T(8,128)S(1)}, f32[8,256]{1,0:T(8,128)S(1)}, u32[]{:S(2)}, u32[]{:S(2)}) collective-permute-start(f32[8,256]{1,0:T(8,128)S(1)} %get-tuple-element.51.refs_7_), channel_id=1, source_target_pairs={{0,24},{1,25},{2,26},{3,27},{4,28},{5,29},{6,30},{7,31},{8,16},{9,... | collective-permute-start | bytes 24584 | tf_op jit(solution)/shard_map/ppermute | solution.py:60
  66.2 1.3 collective-permute-start.22
  67.5 3.4 %collective-permute-start.23 = (f32[2,3968]{1,0:T(2,128)S(1)}, f32[2,3968]{1,0:T(2,128)S(1)}, u32[]{:S(2)}, u32[]{:S(2)}) collective-permute-start(f32[2,3968]{1,0:T(2,128)S(1)} %add.133), channel_id=1, source_target_pairs={{0,9},{1,8},{2,11},{3,10},{4,13},{5,12},{6,15},{7,14},{8,1},{9,0},... | collective-permute-start | bytes 95240 | tf_op jit(solution)/shard_map/ppermute | solution.py:32
  67.8 3.3 %collective-permute-start.24 = (f32[2,3968]{1,0:T(2,128)S(1)}, f32[2,3968]{1,0:T(2,128)S(1)}, u32[]{:S(2)}, u32[]{:S(2)}) collective-permute-start(f32[2,3968]{1,0:T(2,128)S(1)} %add.133), channel_id=1, source_target_pairs={{0,17},{1,16},{2,19},{3,18},{4,21},{5,20},{6,23},{7,22},{8,25},{9,... | collective-permute-start | bytes 95240 | tf_op jit(solution)/shard_map/ppermute | solution.py:32
  68.3 4.2 %collective-permute-start.25 = (f32[2,3968]{1,0:T(2,128)S(1)}, f32[2,3968]{1,0:T(2,128)S(1)}, u32[]{:S(2)}, u32[]{:S(2)}) collective-permute-start(f32[2,3968]{1,0:T(2,128)S(1)} %add.133), channel_id=1, source_target_pairs={{0,25},{1,24},{2,27},{3,26},{4,29},{5,28},{6,31},{7,30},{8,17},{9,... | collective-permute-start | bytes 95240 | tf_op jit(solution)/shard_map/ppermute | solution.py:32
  72.5 3.9 %collective-permute-start.26 = (f32[2,3968]{1,0:T(2,128)S(1)}, f32[2,3968]{1,0:T(2,128)S(1)}, u32[]{:S(2)}, u32[]{:S(2)}) collective-permute-start(f32[2,3968]{1,0:T(2,128)S(1)} %add_add_fusion.5), channel_id=1, source_target_pairs={{0,3},{1,2},{2,1},{3,0},{4,7},{5,6},{6,5},{7,4},{8,11},{9,10},{10,... | collective-permute-start | bytes 95240 | tf_op jit(solution)/shard_map/ppermute | solution.py:32
  72.6 4.5 %collective-permute-start.27 = (f32[2,3968]{1,0:T(2,128)S(1)}, f32[2,3968]{1,0:T(2,128)S(1)}, u32[]{:S(2)}, u32[]{:S(2)}) collective-permute-start(f32[2,3968]{1,0:T(2,128)S(1)} %add_add_fusion.5), channel_id=1, source_target_pairs={{0,5},{1,4},{2,7},{3,6},{4,1},{5,0},{6,3},{7,2},{8,13},{9,12},{10,... | collective-permute-start | bytes 95240 | tf_op jit(solution)/shard_map/ppermute | solution.py:32
  75.5 5.1 %collective-permute-start.28 = (f32[2,3968]{1,0:T(2,128)S(1)}, f32[2,3968]{1,0:T(2,128)S(1)}, u32[]{:S(2)}, u32[]{:S(2)}) collective-permute-start(f32[2,3968]{1,0:T(2,128)S(1)} %add_add_fusion.5), channel_id=1, source_target_pairs={{0,7},{1,6},{2,5},{3,4},{4,3},{5,2},{6,1},{7,0},{8,15},{9,14},{10,... | collective-permute-start | bytes 95240 | tf_op jit(solution)/shard_map/ppermute | solution.py:32
  82.8 3.7 %collective-permute-start.29 = (f32[8,256]{1,0:T(8,128)S(1)}, f32[8,256]{1,0:T(8,128)S(1)}, u32[]{:S(2)}, u32[]{:S(2)}) collective-permute-start(f32[8,256]{1,0:T(8,128)S(1)} %get-tuple-element.56.refs_7_), channel_id=1, source_target_pairs={{0,8},{1,9},{2,10},{3,11},{4,12},{5,13},{6,14},{7,15},{8,0},{9,1},... | collective-permute-start | bytes 24584 | tf_op jit(solution)/shard_map/ppermute | solution.py:59
  84.3 4.5 %collective-permute-start.30 = (f32[8,256]{1,0:T(8,128)S(1)}, f32[8,256]{1,0:T(8,128)S(1)}, u32[]{:S(2)}, u32[]{:S(2)}) collective-permute-start(f32[8,256]{1,0:T(8,128)S(1)} %get-tuple-element.56.refs_7_), channel_id=1, source_target_pairs={{0,24},{1,25},{2,26},{3,27},{4,28},{5,29},{6,30},{7,31},{8,16},{9,... | collective-permute-start | bytes 24584 | tf_op jit(solution)/shard_map/ppermute | solution.py:60
  91.3 1.3 collective-permute-start.31
  92.6 3.4 %collective-permute-start.32 = (f32[2,3968]{1,0:T(2,128)S(1)}, f32[2,3968]{1,0:T(2,128)S(1)}, u32[]{:S(2)}, u32[]{:S(2)}) collective-permute-start(f32[2,3968]{1,0:T(2,128)S(1)} %add.140), channel_id=1, source_target_pairs={{0,9},{1,8},{2,11},{3,10},{4,13},{5,12},{6,15},{7,14},{8,1},{9,0},... | collective-permute-start | bytes 95240 | tf_op jit(solution)/shard_map/ppermute | solution.py:32
  92.9 3.3 %collective-permute-start.33 = (f32[2,3968]{1,0:T(2,128)S(1)}, f32[2,3968]{1,0:T(2,128)S(1)}, u32[]{:S(2)}, u32[]{:S(2)}) collective-permute-start(f32[2,3968]{1,0:T(2,128)S(1)} %add.140), channel_id=1, source_target_pairs={{0,17},{1,16},{2,19},{3,18},{4,21},{5,20},{6,23},{7,22},{8,25},{9,... | collective-permute-start | bytes 95240 | tf_op jit(solution)/shard_map/ppermute | solution.py:32
  94.4 4.2 %collective-permute-start.34 = (f32[2,3968]{1,0:T(2,128)S(1)}, f32[2,3968]{1,0:T(2,128)S(1)}, u32[]{:S(2)}, u32[]{:S(2)}) collective-permute-start(f32[2,3968]{1,0:T(2,128)S(1)} %add.140), channel_id=1, source_target_pairs={{0,25},{1,24},{2,27},{3,26},{4,29},{5,28},{6,31},{7,30},{8,17},{9,... | collective-permute-start | bytes 95240 | tf_op jit(solution)/shard_map/ppermute | solution.py:32
  98.7 3.9 %collective-permute-start.35 = (f32[2,3968]{1,0:T(2,128)S(1)}, f32[2,3968]{1,0:T(2,128)S(1)}, u32[]{:S(2)}, u32[]{:S(2)}) collective-permute-start(f32[2,3968]{1,0:T(2,128)S(1)} %add_add_fusion.3), channel_id=1, source_target_pairs={{0,3},{1,2},{2,1},{3,0},{4,7},{5,6},{6,5},{7,4},{8,11},{9,10},{10,... | collective-permute-start | bytes 95240 | tf_op jit(solution)/shard_map/ppermute | solution.py:32
  98.7 4.3 %collective-permute-start.36 = (f32[2,3968]{1,0:T(2,128)S(1)}, f32[2,3968]{1,0:T(2,128)S(1)}, u32[]{:S(2)}, u32[]{:S(2)}) collective-permute-start(f32[2,3968]{1,0:T(2,128)S(1)} %add_add_fusion.3), channel_id=1, source_target_pairs={{0,5},{1,4},{2,7},{3,6},{4,1},{5,0},{6,3},{7,2},{8,13},{9,12},{10,... | collective-permute-start | bytes 95240 | tf_op jit(solution)/shard_map/ppermute | solution.py:32
  100.2 5.1 %collective-permute-start.37 = (f32[2,3968]{1,0:T(2,128)S(1)}, f32[2,3968]{1,0:T(2,128)S(1)}, u32[]{:S(2)}, u32[]{:S(2)}) collective-permute-start(f32[2,3968]{1,0:T(2,128)S(1)} %add_add_fusion.3), channel_id=1, source_target_pairs={{0,7},{1,6},{2,5},{3,4},{4,3},{5,2},{6,1},{7,0},{8,15},{9,14},{10,... | collective-permute-start | bytes 95240 | tf_op jit(solution)/shard_map/ppermute | solution.py:32
  107.7 3.7 %collective-permute-start.38 = (f32[8,256]{1,0:T(8,128)S(1)}, f32[8,256]{1,0:T(8,128)S(1)}, u32[]{:S(2)}, u32[]{:S(2)}) collective-permute-start(f32[8,256]{1,0:T(8,128)S(1)} %get-tuple-element.60.refs_7_), channel_id=1, source_target_pairs={{0,8},{1,9},{2,10},{3,11},{4,12},{5,13},{6,14},{7,15},{8,0},{9,1},... | collective-permute-start | bytes 24584 | tf_op jit(solution)/shard_map/ppermute | solution.py:59
  109.3 4.5 %collective-permute-start.39 = (f32[8,256]{1,0:T(8,128)S(1)}, f32[8,256]{1,0:T(8,128)S(1)}, u32[]{:S(2)}, u32[]{:S(2)}) collective-permute-start(f32[8,256]{1,0:T(8,128)S(1)} %get-tuple-element.60.refs_7_), channel_id=1, source_target_pairs={{0,24},{1,25},{2,26},{3,27},{4,28},{5,29},{6,30},{7,31},{8,16},{9,... | collective-permute-start | bytes 24584 | tf_op jit(solution)/shard_map/ppermute | solution.py:60
  113.8 18.0 %slice-start = ((f32[48,4,128]{2,1,0:T(4,128)}), f32[40,4,128]{2,1,0:T(4,128)S(1)}, s32[]{:S(2)}) async-start(f32[48,4,128]{2,1,0:T(4,128)} %maps_ref.1), calls=%async_computation | async-start | bytes 163840 | tf_op jit(solution)/shard_map/slice | solution.py:521
  116.2 1.3 collective-permute-start.40
  117.5 3.4 %collective-permute-start.41 = (f32[2,3968]{1,0:T(2,128)S(1)}, f32[2,3968]{1,0:T(2,128)S(1)}, u32[]{:S(2)}, u32[]{:S(2)}) collective-permute-start(f32[2,3968]{1,0:T(2,128)S(1)} %add.147), channel_id=1, source_target_pairs={{0,9},{1,8},{2,11},{3,10},{4,13},{5,12},{6,15},{7,14},{8,1},{9,0},... | collective-permute-start | bytes 95240 | tf_op jit(solution)/shard_map/ppermute | solution.py:32
  117.9 3.3 %collective-permute-start.42 = (f32[2,3968]{1,0:T(2,128)S(1)}, f32[2,3968]{1,0:T(2,128)S(1)}, u32[]{:S(2)}, u32[]{:S(2)}) collective-permute-start(f32[2,3968]{1,0:T(2,128)S(1)} %add.147), channel_id=1, source_target_pairs={{0,17},{1,16},{2,19},{3,18},{4,21},{5,20},{6,23},{7,22},{8,25},{9,... | collective-permute-start | bytes 95240 | tf_op jit(solution)/shard_map/ppermute | solution.py:32
  118.3 4.2 %collective-permute-start.43 = (f32[2,3968]{1,0:T(2,128)S(1)}, f32[2,3968]{1,0:T(2,128)S(1)}, u32[]{:S(2)}, u32[]{:S(2)}) collective-permute-start(f32[2,3968]{1,0:T(2,128)S(1)} %add.147), channel_id=1, source_target_pairs={{0,25},{1,24},{2,27},{3,26},{4,29},{5,28},{6,31},{7,30},{8,17},{9,... | collective-permute-start | bytes 95240 | tf_op jit(solution)/shard_map/ppermute | solution.py:32
  122.6 4.0 %collective-permute-start.44 = (f32[2,3968]{1,0:T(2,128)S(1)}, f32[2,3968]{1,0:T(2,128)S(1)}, u32[]{:S(2)}, u32[]{:S(2)}) collective-permute-start(f32[2,3968]{1,0:T(2,128)S(1)} %add_add_fusion.1), channel_id=1, source_target_pairs={{0,3},{1,2},{2,1},{3,0},{4,7},{5,6},{6,5},{7,4},{8,11},{9,10},{10,... | collective-permute-start | bytes 95240 | tf_op jit(solution)/shard_map/ppermute | solution.py:32
  122.7 4.5 %collective-permute-start.45 = (f32[2,3968]{1,0:T(2,128)S(1)}, f32[2,3968]{1,0:T(2,128)S(1)}, u32[]{:S(2)}, u32[]{:S(2)}) collective-permute-start(f32[2,3968]{1,0:T(2,128)S(1)} %add_add_fusion.1), channel_id=1, source_target_pairs={{0,5},{1,4},{2,7},{3,6},{4,1},{5,0},{6,3},{7,2},{8,13},{9,12},{10,... | collective-permute-start | bytes 95240 | tf_op jit(solution)/shard_map/ppermute | solution.py:32
  125.6 5.1 %collective-permute-start.46 = (f32[2,3968]{1,0:T(2,128)S(1)}, f32[2,3968]{1,0:T(2,128)S(1)}, u32[]{:S(2)}, u32[]{:S(2)}) collective-permute-start(f32[2,3968]{1,0:T(2,128)S(1)} %add_add_fusion.1), channel_id=1, source_target_pairs={{0,7},{1,6},{2,5},{3,4},{4,3},{5,2},{6,1},{7,0},{8,15},{9,14},{10,... | collective-permute-start | bytes 95240 | tf_op jit(solution)/shard_map/ppermute | solution.py:32

commit v4 on v3

--- a/solution.py
+++ b/solution.py
@@ -139,21 +139,31 @@
     return jnp.transpose(jnp.broadcast_to(row, (8, LANES)))[:, :1]
 
 
-def own_flags_kernel(words_ref, coast_ref, x_ref, m_ref, a_ref, spread_ref, bit_ref):
-    @pl.when(pl.program_id(0) == 0)
-    def _():
-        fill_spread(spread_ref, bit_ref)
-
-    coast = as_column(coast_ref[pl.ds(pl.program_id(0), 1), :].astype(F32))
-    ocean = coast.astype(BF16)
-    coast = coast.astype(jnp.int32)
+def own_flags_kernel(words_hbm, coast_hbm, x_hbm, m_ref, a_ref, words_ref, coast_ref, x_ref, spread_ref, bit_ref, sems):
+    rows = coast_ref.shape[0]
+    loads = [pltpu.make_async_copy(words_hbm, words_ref, sems.at[0]), pltpu.make_async_copy(coast_hbm, coast_ref, sems.at[1])]
+    for r in range(rows):
+        at = pl.ds(r * LANES, LANES)
+        loads.append(pltpu.make_async_copy(x_hbm.at[at], x_ref.at[at], sems.at[2 + r]))
+    for load in loads:
+        load.start()
+    fill_spread(spread_ref, bit_ref)
+    loads[0].wait()
+    loads[1].wait()
     days = spread_ref.shape[1]
-    for g in range(words_ref.shape[1] // LANES):
-        words = words_ref[:, g * LANES : (g + 1) * LANES] * coast
-        given = unpack_words(words, spread_ref, bit_ref)
-        at = slice(g * days, (g + 1) * days)
-        m_ref[:, at] = given
-        a_ref[:, at] = x_ref[:, at] * given * ocean
+    coasts = jnp.transpose(jnp.concatenate([coast_ref[...].astype(F32)] * (8 // rows), axis=0))
+    for r in range(rows):
+        coast = coasts[:, r : r + 1]
+        ocean = coast.astype(BF16)
+        coast = coast.astype(jnp.int32)
+        loads[2 + r].wait()
+        cell = slice(r * LANES, (r + 1) * LANES)
+        for g in range(words_ref.shape[1] // LANES):
+            words = words_ref[cell, g * LANES : (g + 1) * LANES] * coast
+            given = unpack_words(words, spread_ref, bit_ref)
+            at = slice(g * days, (g + 1) * days)
+            m_ref[cell, at] = given
+            a_ref[cell, at] = x_ref[cell, at] * given * ocean
 
 
 def edges(pieces, reach):
@@ -170,7 +180,17 @@
     return west, east
 
 
-def prep_kernel(reach, maps_ref, coast_ref, words_ref, u_ref, row_ref, west_ref, east_ref):
+def prep_kernel(reach, maps_hbm, coast_hbm, words_hbm, u_ref, row_ref, west_ref, east_ref, maps_ref, coast_ref, first_ref, last_ref, sems):
+    loads = [
+        pltpu.make_async_copy(maps_hbm, maps_ref, sems.at[0]),
+        pltpu.make_async_copy(coast_hbm, coast_ref, sems.at[1]),
+        pltpu.make_async_copy(words_hbm.at[:, pl.ds(0, reach)], first_ref, sems.at[2]),
+        pltpu.make_async_copy(words_hbm.at[:, pl.ds(LANES - reach, reach)], last_ref, sems.at[3]),
+    ]
+    for load in loads:
+        load.start()
+    for load in loads:
+        load.wait()
     modes, rows = maps_ref.shape[:2]
     coast = coast_ref[...].astype(F32)
     pieces = []
@@ -184,11 +204,11 @@
     base = modes + 8
     west_ref[:base] = west
     east_ref[:base] = east
-    for g in range(words_ref.shape[2] // LANES):
+    for g in range(first_ref.shape[2] // LANES):
         for r in range(rows):
             at = slice(base + reach * (rows * g + r), base + reach * (rows * g + r + 1))
-            west_ref[at] = words_ref[r, :reach, g * LANES : (g + 1) * LANES].astype(F32)
-            east_ref[at] = words_ref[r, LANES - reach :, g * LANES : (g + 1) * LANES].astype(F32)
+            west_ref[at] = first_ref[r, :, g * LANES : (g + 1) * LANES].astype(F32)
+            east_ref[at] = last_ref[r, :, g * LANES : (g + 1) * LANES].astype(F32)
 
 
 def halo_flags_kernel(modes, west_ref, east_ref, m_ref, u_ref, row_ref, spread_ref, bit_ref):
@@ -382,14 +402,18 @@
     un_ref[...] = un
 
 
-def call(kernel, name, outs, scratch, args, smem=(), mib=24, flops=0):
+def call(kernel, name, outs, scratch, args, smem=(), mib=24, flops=0, loads=0):
     moved = sum(z.size * z.dtype.itemsize for z in args)
+    place = VMEM
+    if loads:
+        place = pl.BlockSpec(memory_space=pl.ANY)
+        args = [pltpu.with_memory_space_constraint(z, pltpu.HBM) for z in args]
     return pl.pallas_call(
         kernel,
         out_shape=[jax.ShapeDtypeStruct(s, t) for s, t in outs],
-        in_specs=[SMEM if i in smem else VMEM for i in range(len(args))],
+        in_specs=[SMEM if i in smem else place for i in range(len(args))],
         out_specs=[VMEM for _ in outs],
-        scratch_shapes=[pltpu.VMEM(s, t) for s, t in scratch],
+        scratch_shapes=[pltpu.VMEM(s, t) for s, t in scratch] + ([pltpu.SemaphoreType.DMA((loads,))] if loads else []),
         compiler_params=pltpu.CompilerParams(vmem_limit_bytes=mib * 2**20),
         cost_estimate=pl.CostEstimate(flops=flops, bytes_accessed=moved, transcendentals=0),
         name=name,
@@ -424,35 +448,29 @@
         functools.partial(prep_kernel, reach),
         "prep",
         [((modes, own), F32), ((1, own), F32), ((tall_edge, LANES), F32), ((tall_edge, LANES), F32)],
-        [],
+        [(mode_maps.shape, F32), ((rows, LANES), jnp.int32)] + [((rows, reach, words), jnp.int32)] * 2,
         [mode_maps, ocean_binary_mask, missing_date_bitmask],
+        loads=4,
     )
     from_west, from_east = lon_ring(to_west, to_east)
+    words_per = words // LANES
+    flags_scratch = [((2 * LANES, days // words_per), BF16), ((1, days // words_per), jnp.int32)]
+    m, a = call(
+        own_flags_kernel,
+        "own_flags",
+        [((own, days), BF16)] * 2,
+        [((own, words), jnp.int32), ((rows, LANES), jnp.int32), ((own, days), BF16), *flags_scratch],
+        [missing_date_bitmask.reshape(own, words), ocean_binary_mask, sea_heat_deviations.reshape(own, days)],
+        flops=4 * LANES * own * days,
+        loads=2 + rows,
+    )
     nlon = lax.axis_size("lon")
     if nlon == 8:
-        pieces = [mode_series] + [swap(mode_series, 0, b) for b in (2, 4, 6)]
-        pieces = [z for piece in pieces for z in (piece, swap(piece, 0, 1))]
+        pieces = [swap(mode_series, 0, b) for b in (2, 4, 6)]
+        *pieces, m, a = lax.optimization_barrier((*pieces, m, a))
+        pieces = [z for piece in [mode_series, *pieces] for z in (piece, swap(piece, 0, 1))]
     else:
         pieces = [lax.all_gather(mode_series, "lon", axis=1, tiled=True)]
-
-    words_per = words // LANES
-    flags_scratch = [((2 * LANES, days // words_per), BF16), ((1, days // words_per), jnp.int32)]
-    x = pltpu.with_memory_space_constraint(sea_heat_deviations.reshape(own, days), pltpu.HBM)
-    m, a = pl.pallas_call(
-        own_flags_kernel,
-        grid=(rows,),
-        out_shape=[jax.ShapeDtypeStruct((own, days), BF16)] * 2,
-        in_specs=[
-            pl.BlockSpec((LANES, words), lambda i: (i, 0)),
-            pl.BlockSpec((rows, LANES), lambda i: (0, 0)),
-            pl.BlockSpec((LANES, days), lambda i: (i, 0)),
-        ],
-        out_specs=[pl.BlockSpec((LANES, days), lambda i: (i, 0))] * 2,
-        scratch_shapes=[pltpu.VMEM(s, t) for s, t in flags_scratch],
-        compiler_params=pltpu.CompilerParams(vmem_limit_bytes=24 * 2**20),
-        cost_estimate=pl.CostEstimate(flops=4 * LANES * own * days, bytes_accessed=6 * own * days, transcendentals=0),
-        name="own_flags",
-    )(missing_date_bitmask.reshape(own, words), ocean_binary_mask, x)
     m_halo, u_halo, coast_halo = call(
         functools.partial(halo_flags_kernel, modes),
         "halo_flags",

time: 133 us -> 127 us (0.955)
  local copies, waits for them, and re-layouts: 4.58 us -> 0.24 us
    pallas_call x12 -> x13, Pallas kernels: 21.1 us -> 26.1 us  [call(): pl.pallas_call(kernel, out_shape=[jax.ShapeDtypeStruct(s, t) for s, t in...]
    pallas_call x1 -> x0, Pallas kernels: 4.94 us -> none  [shards(): pl.pallas_call(own_flags_kernel, grid=(rows,), out_shape=[jax.ShapeDtypeS...]
    unnamed x12 -> x2, local copies, waits for them, and re-layouts: 4.34 us -> 0.01 us
  transfers between devices with their start and end apart: 47 -> 47, of which waited for: 35 -> 37; matrix products, arithmetic and copies ran while one was open for 0% -> 0% of each run, Pallas kernels for 6% -> 6%
where the time goes in v4:
time: 127 us
  starting transfers between devices  49.9 us (39%)
  waiting for transfers between devices  48 us (38%)
  Pallas kernels  26.1 us (21%)
  other arithmetic  1.91 us (2%)
    ppermute x35, starting transfers between devices, swap(): lax.ppermute(x, ('lat', 'lon'), pairing(lambda i: i ^ lat_bits, lambda j:...  34.4 us
    ppermute x35, waiting for transfers between devices, swap(): lax.ppermute(x, ('lat', 'lon'), pairing(lambda i: i ^ lat_bits, lambda j:...  29.8 us
    pallas_call x13, Pallas kernels, call(): pl.pallas_call(kernel, out_shape=[jax.ShapeDtypeStruct(s, t) for s, t in...  26.1 us
    ppermute x4, waiting for transfers between devices, lat_partners(): lax.ppermute(x, ('lat', 'lon'), pairing(lambda i: (i + 1 if i % 2 else i...  9.55 us
    ppermute x4, starting transfers between devices, lat_partners(): got_a = lax.ppermute(x, ('lat', 'lon'), pairing(lambda i: i ^ 1, same))  6.1 us
    ppermute x2, starting transfers between devices, lon_ring(): lax.ppermute(to_west, 'lon', [(j, i) for i, j in up])  4.9 us
    ppermute x4, waiting for transfers between devices, lat_partners(): got_a = lax.ppermute(x, ('lat', 'lon'), pairing(lambda i: i ^ 1, same))  4.7 us
    ppermute x4, starting transfers between devices, lat_partners(): lax.ppermute(x, ('lat', 'lon'), pairing(lambda i: (i + 1 if i % 2 else i...  3.91 us
  transfers between devices with their start and end apart: 47, of which 37 were waited for; matrix products, arithmetic and copies ran while one was open for 0% of the time, Pallas kernels for 6%

profile of v4, /device:TPU:0, one launch (start us, length us, event | category | flops | bytes accessed | tf_op | source)
XLA Modules:
  0.0 127.1 jit_solution(12249056987148645389)
XLA Ops:
  0.6 3.1 %collective-permute-start = (f32[48,480]{1,0:T(8,128)}, f32[48,480]{1,0:T(8,128)S(1)}, u32[]{:S(2)}, u32[]{:S(2)}) collective-permute-start(f32[48,480]{1,0:T(8,128)} %refs_2_.1), channel_id=1, source_target_pairs={{0,2},{1,3},{2,0},{3,1},{4,6},{5,7},{6,4},{7,5},{8,10},{9,11},{10,... | collective-permute-start | bytes 276488 | tf_op jit(solution)/shard_map/ppermute | solution.py:32
  3.7 2.6 %collective-permute-start.1 = (f32[48,480]{1,0:T(8,128)}, f32[48,480]{1,0:T(8,128)S(1)}, u32[]{:S(2)}, u32[]{:S(2)}) collective-permute-start(f32[48,480]{1,0:T(8,128)} %refs_2_.1), channel_id=1, source_target_pairs={{0,4},{1,5},{2,6},{3,7},{4,0},{5,1},{6,2},{7,3},{8,12},{9,13},{10,... | collective-permute-start | bytes 276488 | tf_op jit(solution)/shard_map/ppermute | solution.py:32
  6.3 1.1 prep.1
  7.4 0.6 collective-permute-start.3
  8.1 4.1 %own_flags.1 = (bf16[512,3840]{1,0:T(8,128)(2,1)S(1)}, bf16[512,3840]{1,0:T(8,128)(2,1)S(1)}) custom-call(s32[512,256]{1,0:T(8,128)} %bitcast.8, s32[4,128]{1,0:T(4,128)} %coast_hbm.3, bf16[512,3840]{1,0:T(8,128)(2,1)} %bitcast.7), custom_call_target="tpu_custom_call" | custom-call | flops 1006632960 | bytes 4458496 | tf_op jit(solution)/shard_map/own_flags/pallas_call | solution.py:411
  12.1 3.5 %collective-permute-start.4 = (f32[184,128]{1,0:T(8,128)S(1)}, f32[184,128]{1,0:T(8,128)S(1)}, u32[]{:S(2)}, u32[]{:S(2)}) collective-permute-start(f32[184,128]{1,0:T(8,128)S(1)} %get-tuple-element.43), channel_id=1, source_target_pairs={{1,0},{2,1},{3,2},{4,3},{5,4},{6,5},{7,6},{0,7},{9,8},{10,9},{11,1... | collective-permute-start | bytes 282632 | tf_op jit(solution)/shard_map/ppermute | solution.py:67
  15.7 0.5 collective-permute-start.7
  16.3 0.6 collective-permute-done.6.refs_5_
  17.5 1.8 %given.1 = (f32[48,3840]{1,0:T(8,128)S(1)}, f32[8,512]{1,0:T(8,128)S(1)}, f32[8,128]{1,0:T(8,128)S(1)}, f32[8,128]{1,0:T(8,128)S(1)}) custom-call(bf16[512,3840]{1,0:T(8,128)(2,1)S(1)} %get-tuple-element.45.refs_0_.refs_1_, s32[4]{0:T(128)S(1)} %pad_add_fusion.refs_1_.refs_4_, f32[48,480]{1,0:T(8,128)S(1)} %copy-done, ...), custom_call_target="tpu_custom_call" | custom-call | flops 62914560 | bytes 4669456 | tf_op jit(solution)/shard_map/given/pallas_call | solution.py:411
  19.3 1.4 %collective-permute-start.10 = (f32[8,128]{1,0:T(8,128)S(1)}, f32[8,128]{1,0:T(8,128)S(1)}, u32[]{:S(2)}, u32[]{:S(2)}) collective-permute-start(f32[8,128]{1,0:T(8,128)S(1)} %get-tuple-element.56), channel_id=1, source_target_pairs={{1,0},{2,1},{3,2},{4,3},{5,4},{6,5},{7,6},{0,7},{9,8},{10,9},{11,1... | collective-permute-start | bytes 12296 | tf_op jit(solution)/shard_map/ppermute | solution.py:67
  20.7 0.8 halo_flags.1
  22.0 3.5 %collective-permute-done.9.refs_8_ = f32[8,128]{1,0:T(8,128)S(1)} collective-permute-done((f32[8,128]{1,0:T(8,128)S(1)}, f32[8,128]{1,0:T(8,128)S(1)}, u32[]{:S(2)}, u32[]{:S(2)}) %collective-permute-start.9) | collective-permute-done | bytes 4128 | tf_op jit(solution)/shard_map/ppermute | solution.py:67
  25.5 1.8 %fields_0.1.refs_7_.refs_10_ = f32[16,256]{1,0:T(8,128)S(1)} custom-call(bf16[512,3840]{1,0:T(8,128)(2,1)S(1)} %get-tuple-element.41.refs_0_, bf16[128,3840]{1,0:T(8,128)(2,1)S(1)} %get-tuple-element.44.refs_1_, f32[48,3840]{1,0:T(8,128)S(1)} %get-tuple-element.49.refs_2_, f32[48,512]{1,0:T(8,128)S(1)} %get-tuple-element.50.refs_3_, ...), custom_call_target="tpu_custom_call" | custom-call | flops 943718400 | bytes 5802496 | tf_op jit(solution)/shard_map/fields_0/pallas_call | solution.py:411
  27.3 1.6 %collective-permute-start.11 = (f32[16,256]{1,0:T(8,128)S(1)}, f32[16,256]{1,0:T(8,128)S(1)}, u32[]{:S(2)}, u32[]{:S(2)}) collective-permute-start(f32[16,256]{1,0:T(8,128)S(1)} %fields_0.1.refs_7_.refs_10_), channel_id=1, source_target_pairs={{0,8},{1,9},{2,10},{3,11},{4,12},{5,13},{6,14},{7,15},{8,0},{9,1},... | collective-permute-start | bytes 49160 | tf_op jit(solution)/shard_map/ppermute | solution.py:59
  28.8 1.5 %collective-permute-start.12 = (f32[16,256]{1,0:T(8,128)S(1)}, f32[16,256]{1,0:T(8,128)S(1)}, u32[]{:S(2)}, u32[]{:S(2)}) collective-permute-start(f32[16,256]{1,0:T(8,128)S(1)} %fields_0.1.refs_7_.refs_10_), channel_id=1, source_target_pairs={{0,24},{1,25},{2,26},{3,27},{4,28},{5,29},{6,30},{7,31},{8,16},{9,... | collective-permute-start | bytes 49160 | tf_op jit(solution)/shard_map/ppermute | solution.py:60
  30.4 0.6 collective-permute-done.11.refs_8_.refs_11_
  31.1 2.4 %collective-permute-done.12.refs_9_.refs_12_ = f32[16,256]{1,0:T(8,128)S(1)} collective-permute-done((f32[16,256]{1,0:T(8,128)S(1)}, f32[16,256]{1,0:T(8,128)S(1)}, u32[]{:S(2)}, u32[]{:S(2)}) %collective-permute-start.12) | collective-permute-done | bytes 16416 | tf_op jit(solution)/shard_map/ppermute | solution.py:60
  33.6 2.4 %sums_0.1 = (f32[2,3968]{1,0:T(2,128)S(1)}, f32[8,256]{1,0:T(8,128)S(1)}) custom-call(bf16[512,3840]{1,0:T(8,128)(2,1)S(1)} %get-tuple-element.41.refs_0_, bf16[512,3840]{1,0:T(8,128)(2,1)S(1)} %get-tuple-element.45.refs_0_.refs_1_, f32[48,3840]{1,0:T(8,128)S(1)} %get-tuple-element.49.refs_2_, f32[48,512]{1,0:T(8,128)S(1)} %get-tuple-element.50.refs_3_, ...), custom_call_target="tpu_custom_call" | custom-call | flops 754974720 | bytes 8781840 | tf_op jit(solution)/shard_map/sums_0/pallas_call | solution.py:411
  36.1 1.2 collective-permute-done.13
  37.7 1.5 %collective-permute-start.15 = (f32[2,3968]{1,0:T(2,128)S(1)}, f32[2,3968]{1,0:T(2,128)S(1)}, u32[]{:S(2)}, u32[]{:S(2)}) collective-permute-start(f32[2,3968]{1,0:T(2,128)S(1)} %add.126), channel_id=1, source_target_pairs={{0,17},{1,16},{2,19},{3,18},{4,21},{5,20},{6,23},{7,22},{8,25},{9,... | collective-permute-start | bytes 95240 | tf_op jit(solution)/shard_map/ppermute | solution.py:32
  39.1 1.2 collective-permute-start.16
  41.0 2.4 %collective-permute-done.16 = f32[2,3968]{1,0:T(2,128)S(1)} collective-permute-done((f32[2,3968]{1,0:T(2,128)S(1)}, f32[2,3968]{1,0:T(2,128)S(1)}, u32[]{:S(2)}, u32[]{:S(2)}) %collective-permute-start.16) | collective-permute-done | bytes 31776 | tf_op jit(solution)/shard_map/ppermute | solution.py:32
  43.5 0.7 collective-permute-start.18
  44.2 3.2 %collective-permute-start.19 = (f32[2,3968]{1,0:T(2,128)S(1)}, f32[2,3968]{1,0:T(2,128)S(1)}, u32[]{:S(2)}, u32[]{:S(2)}) collective-permute-start(f32[2,3968]{1,0:T(2,128)S(1)} %add_add_fusion.7), channel_id=1, source_target_pairs={{0,7},{1,6},{2,5},{3,4},{4,3},{5,2},{6,1},{7,0},{8,15},{9,14},{10,... | collective-permute-start | bytes 95240 | tf_op jit(solution)/shard_map/ppermute | solution.py:32
  47.8 1.8 %collective-permute-done.19 = f32[2,3968]{1,0:T(2,128)S(1)} collective-permute-done((f32[2,3968]{1,0:T(2,128)S(1)}, f32[2,3968]{1,0:T(2,128)S(1)}, u32[]{:S(2)}, u32[]{:S(2)}) %collective-permute-start.19) | collective-permute-done | bytes 31776 | tf_op jit(solution)/shard_map/ppermute | solution.py:32
  49.6 2.1 %fields_1.1 = (f32[8,256]{1,0:T(8,128)S(1)}, f32[2,3840]{1,0:T(2,128)S(1)}, f32[2,640]{1,0:T(2,128)S(1)}) custom-call(bf16[512,3840]{1,0:T(8,128)(2,1)S(1)} %get-tuple-element.41.refs_0_, bf16[128,3840]{1,0:T(8,128)(2,1)S(1)} %get-tuple-element.44.refs_1_, f32[48,3840]{1,0:T(8,128)S(1)} %get-tuple-element.49.refs_2_, ...), custom_call_target="tpu_custom_call" | custom-call | flops 943718400 | bytes 5842432 | tf_op jit(solution)/shard_map/fields_1/pallas_call | solution.py:411
  51.7 1.5 %collective-permute-start.20 = (f32[8,256]{1,0:T(8,128)S(1)}, f32[8,256]{1,0:T(8,128)S(1)}, u32[]{:S(2)}, u32[]{:S(2)}) collective-permute-start(f32[8,256]{1,0:T(8,128)S(1)} %get-tuple-element.61.refs_7_), channel_id=1, source_target_pairs={{0,8},{1,9},{2,10},{3,11},{4,12},{5,13},{6,14},{7,15},{8,0},{9,1},... | collective-permute-start | bytes 24584 | tf_op jit(solution)/shard_map/ppermute | solution.py:59
  53.2 0.5 collective-permute-start.21
  53.7 1.7 %collective-permute-done.20.refs_8_ = f32[8,256]{1,0:T(8,128)S(1)} collective-permute-done((f32[8,256]{1,0:T(8,128)S(1)}, f32[8,256]{1,0:T(8,128)S(1)}, u32[]{:S(2)}, u32[]{:S(2)}) %collective-permute-start.20) | collective-permute-done | bytes 8224 | tf_op jit(solution)/shard_map/ppermute | solution.py:59
  55.4 2.4 %collective-permute-done.21.refs_9_ = f32[8,256]{1,0:T(8,128)S(1)} collective-permute-done((f32[8,256]{1,0:T(8,128)S(1)}, f32[8,256]{1,0:T(8,128)S(1)}, u32[]{:S(2)}, u32[]{:S(2)}) %collective-permute-start.21) | collective-permute-done | bytes 8224 | tf_op jit(solution)/shard_map/ppermute | solution.py:60
  57.8 2.4 %sums_1.1 = (f32[2,3968]{1,0:T(2,128)S(1)}, f32[8,256]{1,0:T(8,128)S(1)}) custom-call(bf16[512,3840]{1,0:T(8,128)(2,1)S(1)} %get-tuple-element.41.refs_0_, bf16[512,3840]{1,0:T(8,128)(2,1)S(1)} %get-tuple-element.45.refs_0_.refs_1_, f32[48,3840]{1,0:T(8,128)S(1)} %get-tuple-element.49.refs_2_, f32[48,512]{1,0:T(8,128)S(1)} %get-tuple-element.50.refs_3_, ...), custom_call_target="tpu_custom_call" | custom-call | flops 754974720 | bytes 8842256 | tf_op jit(solution)/shard_map/sums_1/pallas_call | solution.py:411
  60.2 1.2 collective-permute-done.22
  62.3 2.2 %collective-permute-start.25 = (f32[2,3968]{1,0:T(2,128)S(1)}, f32[2,3968]{1,0:T(2,128)S(1)}, u32[]{:S(2)}, u32[]{:S(2)}) collective-permute-start(f32[2,3968]{1,0:T(2,128)S(1)} %add.133), channel_id=1, source_target_pairs={{0,25},{1,24},{2,27},{3,26},{4,29},{5,28},{6,31},{7,30},{8,17},{9,... | collective-permute-start | bytes 95240 | tf_op jit(solution)/shard_map/ppermute | solution.py:32
  65.2 1.3 %collective-permute-done.25 = f32[2,3968]{1,0:T(2,128)S(1)} collective-permute-done((f32[2,3968]{1,0:T(2,128)S(1)}, f32[2,3968]{1,0:T(2,128)S(1)}, u32[]{:S(2)}, u32[]{:S(2)}) %collective-permute-start.25) | collective-permute-done | bytes 31776 | tf_op jit(solution)/shard_map/ppermute | solution.py:32
  66.6 3.4 %collective-permute-start.27 = (f32[2,3968]{1,0:T(2,128)S(1)}, f32[2,3968]{1,0:T(2,128)S(1)}, u32[]{:S(2)}, u32[]{:S(2)}) collective-permute-start(f32[2,3968]{1,0:T(2,128)S(1)} %add_add_fusion.5), channel_id=1, source_target_pairs={{0,5},{1,4},{2,7},{3,6},{4,1},{5,0},{6,3},{7,2},{8,13},{9,12},{10,... | collective-permute-start | bytes 95240 | tf_op jit(solution)/shard_map/ppermute | solution.py:32
  70.5 1.3 collective-permute-done.27
  71.7 3.4 %collective-permute-done.28 = f32[2,3968]{1,0:T(2,128)S(1)} collective-permute-done((f32[2,3968]{1,0:T(2,128)S(1)}, f32[2,3968]{1,0:T(2,128)S(1)}, u32[]{:S(2)}, u32[]{:S(2)}) %collective-permute-start.28) | collective-permute-done | bytes 31776 | tf_op jit(solution)/shard_map/ppermute | solution.py:32
  75.2 2.1 %fields_2.1 = (f32[8,256]{1,0:T(8,128)S(1)}, f32[2,3840]{1,0:T(2,128)S(1)}, f32[2,640]{1,0:T(2,128)S(1)}) custom-call(bf16[512,3840]{1,0:T(8,128)(2,1)S(1)} %get-tuple-element.41.refs_0_, bf16[128,3840]{1,0:T(8,128)(2,1)S(1)} %get-tuple-element.44.refs_1_, f32[48,3840]{1,0:T(8,128)S(1)} %get-tuple-element.49.refs_2_, ...), custom_call_target="tpu_custom_call" | custom-call | flops 943718400 | bytes 5878272 | tf_op jit(solution)/shard_map/fields_2/pallas_call | solution.py:411
  77.3 1.5 %collective-permute-start.29 = (f32[8,256]{1,0:T(8,128)S(1)}, f32[8,256]{1,0:T(8,128)S(1)}, u32[]{:S(2)}, u32[]{:S(2)}) collective-permute-start(f32[8,256]{1,0:T(8,128)S(1)} %get-tuple-element.66.refs_7_), channel_id=1, source_target_pairs={{0,8},{1,9},{2,10},{3,11},{4,12},{5,13},{6,14},{7,15},{8,0},{9,1},... | collective-permute-start | bytes 24584 | tf_op jit(solution)/shard_map/ppermute | solution.py:59
  78.8 1.5 %collective-permute-start.30 = (f32[8,256]{1,0:T(8,128)S(1)}, f32[8,256]{1,0:T(8,128)S(1)}, u32[]{:S(2)}, u32[]{:S(2)}) collective-permute-start(f32[8,256]{1,0:T(8,128)S(1)} %get-tuple-element.66.refs_7_), channel_id=1, source_target_pairs={{0,24},{1,25},{2,26},{3,27},{4,28},{5,29},{6,30},{7,31},{8,16},{9,... | collective-permute-start | bytes 24584 | tf_op jit(solution)/shard_map/ppermute | solution.py:60
  80.3 0.7 collective-permute-done.29.refs_8_
  81.0 2.4 %collective-permute-done.30.refs_9_ = f32[8,256]{1,0:T(8,128)S(1)} collective-permute-done((f32[8,256]{1,0:T(8,128)S(1)}, f32[8,256]{1,0:T(8,128)S(1)}, u32[]{:S(2)}, u32[]{:S(2)}) %collective-permute-start.30) | collective-permute-done | bytes 8224 | tf_op jit(solution)/shard_map/ppermute | solution.py:60
  83.4 2.4 %sums_2.1 = (f32[2,3968]{1,0:T(2,128)S(1)}, f32[8,256]{1,0:T(8,128)S(1)}) custom-call(bf16[512,3840]{1,0:T(8,128)(2,1)S(1)} %get-tuple-element.41.refs_0_, bf16[512,3840]{1,0:T(8,128)(2,1)S(1)} %get-tuple-element.45.refs_0_.refs_1_, f32[48,3840]{1,0:T(8,128)S(1)} %get-tuple-element.49.refs_2_, f32[48,512]{1,0:T(8,128)S(1)} %get-tuple-element.50.refs_3_, ...), custom_call_target="tpu_custom_call" | custom-call | flops 754974720 | bytes 8878096 | tf_op jit(solution)/shard_map/sums_2/pallas_call | solution.py:411
  85.9 1.2 collective-permute-done.31
  87.5 1.5 %collective-permute-start.33 = (f32[2,3968]{1,0:T(2,128)S(1)}, f32[2,3968]{1,0:T(2,128)S(1)}, u32[]{:S(2)}, u32[]{:S(2)}) collective-permute-start(f32[2,3968]{1,0:T(2,128)S(1)} %add.140), channel_id=1, source_target_pairs={{0,17},{1,16},{2,19},{3,18},{4,21},{5,20},{6,23},{7,22},{8,25},{9,... | collective-permute-start | bytes 95240 | tf_op jit(solution)/shard_map/ppermute | solution.py:32
  88.9 1.2 collective-permute-start.34
  90.8 2.4 %collective-permute-done.34 = f32[2,3968]{1,0:T(2,128)S(1)} collective-permute-done((f32[2,3968]{1,0:T(2,128)S(1)}, f32[2,3968]{1,0:T(2,128)S(1)}, u32[]{:S(2)}, u32[]{:S(2)}) %collective-permute-start.34) | collective-permute-done | bytes 31776 | tf_op jit(solution)/shard_map/ppermute | solution.py:32
  93.3 1.3 %collective-permute-start.36 = (f32[2,3968]{1,0:T(2,128)S(1)}, f32[2,3968]{1,0:T(2,128)S(1)}, u32[]{:S(2)}, u32[]{:S(2)}) collective-permute-start(f32[2,3968]{1,0:T(2,128)S(1)} %add_add_fusion.3), channel_id=1, source_target_pairs={{0,5},{1,4},{2,7},{3,6},{4,1},{5,0},{6,3},{7,2},{8,13},{9,12},{10,... | collective-permute-start | bytes 95240 | tf_op jit(solution)/shard_map/ppermute | solution.py:32
  94.6 2.6 %collective-permute-start.37 = (f32[2,3968]{1,0:T(2,128)S(1)}, f32[2,3968]{1,0:T(2,128)S(1)}, u32[]{:S(2)}, u32[]{:S(2)}) collective-permute-start(f32[2,3968]{1,0:T(2,128)S(1)} %add_add_fusion.3), channel_id=1, source_target_pairs={{0,7},{1,6},{2,5},{3,4},{4,3},{5,2},{6,1},{7,0},{8,15},{9,14},{10,... | collective-permute-start | bytes 95240 | tf_op jit(solution)/shard_map/ppermute | solution.py:32
  97.6 2.1 %collective-permute-done.37 = f32[2,3968]{1,0:T(2,128)S(1)} collective-permute-done((f32[2,3968]{1,0:T(2,128)S(1)}, f32[2,3968]{1,0:T(2,128)S(1)}, u32[]{:S(2)}, u32[]{:S(2)}) %collective-permute-start.37) | collective-permute-done | bytes 31776 | tf_op jit(solution)/shard_map/ppermute | solution.py:32
  99.8 2.3 %fields_3.1 = (f32[8,256]{1,0:T(8,128)S(1)}, f32[2,3840]{1,0:T(2,128)S(1)}, f32[2,640]{1,0:T(2,128)S(1)}) custom-call(bf16[512,3840]{1,0:T(8,128)(2,1)S(1)} %get-tuple-element.41.refs_0_, bf16[128,3840]{1,0:T(8,128)(2,1)S(1)} %get-tuple-element.44.refs_1_, f32[48,3840]{1,0:T(8,128)S(1)} %get-tuple-element.49.refs_2_, ...), custom_call_target="tpu_custom_call" | custom-call | flops 943718400 | bytes 5914112 | tf_op jit(solution)/shard_map/fields_3/pallas_call | solution.py:411
  102.1 1.5 %collective-permute-start.38 = (f32[8,256]{1,0:T(8,128)S(1)}, f32[8,256]{1,0:T(8,128)S(1)}, u32[]{:S(2)}, u32[]{:S(2)}) collective-permute-start(f32[8,256]{1,0:T(8,128)S(1)} %get-tuple-element.70.refs_7_), channel_id=1, source_target_pairs={{0,8},{1,9},{2,10},{3,11},{4,12},{5,13},{6,14},{7,15},{8,0},{9,1},... | collective-permute-start | bytes 24584 | tf_op jit(solution)/shard_map/ppermute | solution.py:59
  104.1 1.7 %collective-permute-done.38.refs_8_ = f32[8,256]{1,0:T(8,128)S(1)} collective-permute-done((f32[8,256]{1,0:T(8,128)S(1)}, f32[8,256]{1,0:T(8,128)S(1)}, u32[]{:S(2)}, u32[]{:S(2)}) %collective-permute-start.38) | collective-permute-done | bytes 8224 | tf_op jit(solution)/shard_map/ppermute | solution.py:59
  105.8 2.4 %collective-permute-done.39.refs_9_ = f32[8,256]{1,0:T(8,128)S(1)} collective-permute-done((f32[8,256]{1,0:T(8,128)S(1)}, f32[8,256]{1,0:T(8,128)S(1)}, u32[]{:S(2)}, u32[]{:S(2)}) %collective-permute-start.39) | collective-permute-done | bytes 8224 | tf_op jit(solution)/shard_map/ppermute | solution.py:60
  108.2 2.4 %sums_3.1 = (f32[2,3968]{1,0:T(2,128)S(1)}, f32[8,256]{1,0:T(8,128)S(1)}) custom-call(bf16[512,3840]{1,0:T(8,128)(2,1)S(1)} %get-tuple-element.41.refs_0_, bf16[512,3840]{1,0:T(8,128)(2,1)S(1)} %get-tuple-element.45.refs_0_.refs_1_, f32[48,3840]{1,0:T(8,128)S(1)} %get-tuple-element.49.refs_2_, f32[48,512]{1,0:T(8,128)S(1)} %get-tuple-element.50.refs_3_, ...), custom_call_target="tpu_custom_call" | custom-call | flops 754974720 | bytes 8913936 | tf_op jit(solution)/shard_map/sums_3/pallas_call | solution.py:411
  110.7 1.2 collective-permute-done.40
  112.7 2.2 %collective-permute-start.43 = (f32[2,3968]{1,0:T(2,128)S(1)}, f32[2,3968]{1,0:T(2,128)S(1)}, u32[]{:S(2)}, u32[]{:S(2)}) collective-permute-start(f32[2,3968]{1,0:T(2,128)S(1)} %add.147), channel_id=1, source_target_pairs={{0,25},{1,24},{2,27},{3,26},{4,29},{5,28},{6,31},{7,30},{8,17},{9,... | collective-permute-start | bytes 95240 | tf_op jit(solution)/shard_map/ppermute | solution.py:32
  115.6 1.3 %collective-permute-done.43 = f32[2,3968]{1,0:T(2,128)S(1)} collective-permute-done((f32[2,3968]{1,0:T(2,128)S(1)}, f32[2,3968]{1,0:T(2,128)S(1)}, u32[]{:S(2)}, u32[]{:S(2)}) %collective-permute-start.43) | collective-permute-done | bytes 31776 | tf_op jit(solution)/shard_map/ppermute | solution.py:32
  117.0 3.1 %collective-permute-start.45 = (f32[2,3968]{1,0:T(2,128)S(1)}, f32[2,3968]{1,0:T(2,128)S(1)}, u32[]{:S(2)}, u32[]{:S(2)}) collective-permute-start(f32[2,3968]{1,0:T(2,128)S(1)} %add_add_fusion.1), channel_id=1, source_target_pairs={{0,5},{1,4},{2,7},{3,6},{4,1},{5,0},{6,3},{7,2},{8,13},{9,12},{10,... | collective-permute-start | bytes 95240 | tf_op jit(solution)/shard_map/ppermute | solution.py:32
  120.1 0.8 collective-permute-start.46
  120.9 0.8 collective-permute-done.45
  121.7 3.5 %collective-permute-done.46 = f32[2,3968]{1,0:T(2,128)S(1)} collective-permute-done((f32[2,3968]{1,0:T(2,128)S(1)}, f32[2,3968]{1,0:T(2,128)S(1)}, u32[]{:S(2)}, u32[]{:S(2)}) %collective-permute-start.46) | collective-permute-done | bytes 31776 | tf_op jit(solution)/shard_map/ppermute | solution.py:32
  125.7 0.6 pad_maximum_fusion.1
  126.4 0.7 pad_maximum_fusion
  (75 shorter events, 9.5 us)
Async XLA Ops:
  0.6 16.8 %copy-start = (f32[48,480]{1,0:T(8,128)S(1)}, f32[48,480]{1,0:T(8,128)}, u32[]{:S(2)}) copy-start(f32[48,480]{1,0:T(8,128)} %refs_2_.1) | copy-start | bytes 276484
  0.6 11.5 %collective-permute-start = (f32[48,480]{1,0:T(8,128)}, f32[48,480]{1,0:T(8,128)S(1)}, u32[]{:S(2)}, u32[]{:S(2)}) collective-permute-start(f32[48,480]{1,0:T(8,128)} %refs_2_.1), channel_id=1, source_target_pairs={{0,2},{1,3},{2,0},{3,1},{4,6},{5,7},{6,4},{7,5},{8,10},{9,11},{10,... | collective-permute-start | bytes 276488 | tf_op jit(solution)/shard_map/ppermute | solution.py:32
  3.7 11.9 %collective-permute-start.1 = (f32[48,480]{1,0:T(8,128)}, f32[48,480]{1,0:T(8,128)S(1)}, u32[]{:S(2)}, u32[]{:S(2)}) collective-permute-start(f32[48,480]{1,0:T(8,128)} %refs_2_.1), channel_id=1, source_target_pairs={{0,4},{1,5},{2,6},{3,7},{4,0},{5,1},{6,2},{7,3},{8,12},{9,13},{10,... | collective-permute-start | bytes 276488 | tf_op jit(solution)/shard_map/ppermute | solution.py:32
  6.3 9.3 %collective-permute-start.2 = (f32[48,480]{1,0:T(8,128)}, f32[48,480]{1,0:T(8,128)S(1)}, u32[]{:S(2)}, u32[]{:S(2)}) collective-permute-start(f32[48,480]{1,0:T(8,128)} %refs_2_.1), channel_id=1, source_target_pairs={{0,6},{1,7},{2,4},{3,5},{4,2},{5,3},{6,0},{7,1},{8,14},{9,15},{10,... | collective-permute-start | bytes 276488 | tf_op jit(solution)/shard_map/ppermute | solution.py:32
  6.3 9.8 %collective-permute-start.5 = (f32[48,480]{1,0:T(8,128)}, f32[48,480]{1,0:T(8,128)S(1)}, u32[]{:S(2)}, u32[]{:S(2)}) collective-permute-start(f32[48,480]{1,0:T(8,128)} %refs_2_.1), channel_id=1, source_target_pairs={{0,1},{1,0},{2,3},{3,2},{4,5},{5,4},{6,7},{7,6},{8,9},{9,8},{10,11... | collective-permute-start | bytes 276488 | tf_op jit(solution)/shard_map/ppermute | solution.py:32
  7.4 13.2 %collective-permute-start.3 = (f32[184,128]{1,0:T(8,128)S(1)}, f32[184,128]{1,0:T(8,128)S(1)}, u32[]{:S(2)}, u32[]{:S(2)}) collective-permute-start(f32[184,128]{1,0:T(8,128)S(1)} %get-tuple-element.42), channel_id=1, source_target_pairs={{0,1},{1,2},{2,3},{3,4},{4,5},{5,6},{6,7},{7,0},{8,9},{9,10},{10,1... | collective-permute-start | bytes 282632 | tf_op jit(solution)/shard_map/ppermute | solution.py:67
  12.1 8.5 %collective-permute-start.4 = (f32[184,128]{1,0:T(8,128)S(1)}, f32[184,128]{1,0:T(8,128)S(1)}, u32[]{:S(2)}, u32[]{:S(2)}) collective-permute-start(f32[184,128]{1,0:T(8,128)S(1)} %get-tuple-element.43), channel_id=1, source_target_pairs={{1,0},{2,1},{3,2},{4,3},{5,4},{6,5},{7,6},{0,7},{9,8},{10,9},{11,1... | collective-permute-start | bytes 282632 | tf_op jit(solution)/shard_map/ppermute | solution.py:67
  15.6 1.3 %collective-permute-start.6 = (f32[48,480]{1,0:T(8,128)S(1)}, f32[48,480]{1,0:T(8,128)S(1)}, u32[]{:S(2)}, u32[]{:S(2)}) collective-permute-start(f32[48,480]{1,0:T(8,128)S(1)} %collective-permute-done.refs_4_), channel_id=1, source_target_pairs={{0,1},{1,0},{2,3},{3,2},{4,5},{5,4},{6,7},{7,6},{8,9},{9,8},{10,11... | collective-permute-start | bytes 276488 | tf_op jit(solution)/shard_map/ppermute | solution.py:32
  15.7 1.4 %collective-permute-start.7 = (f32[48,480]{1,0:T(8,128)S(1)}, f32[48,480]{1,0:T(8,128)S(1)}, u32[]{:S(2)}, u32[]{:S(2)}) collective-permute-start(f32[48,480]{1,0:T(8,128)S(1)} %collective-permute-done.1.refs_6_), channel_id=1, source_target_pairs={{0,1},{1,0},{2,3},{3,2},{4,5},{5,4},{6,7},{7,6},{8,9},{9,8},{10,11... | collective-permute-start | bytes 276488 | tf_op jit(solution)/shard_map/ppermute | solution.py:32
  16.2 1.3 %collective-permute-start.8 = (f32[48,480]{1,0:T(8,128)S(1)}, f32[48,480]{1,0:T(8,128)S(1)}, u32[]{:S(2)}, u32[]{:S(2)}) collective-permute-start(f32[48,480]{1,0:T(8,128)S(1)} %collective-permute-done.2.refs_8_), channel_id=1, source_target_pairs={{0,1},{1,0},{2,3},{3,2},{4,5},{5,4},{6,7},{7,6},{8,9},{9,8},{10,11... | collective-permute-start | bytes 276488 | tf_op jit(solution)/shard_map/ppermute | solution.py:32
  19.3 2.7 %collective-permute-start.10 = (f32[8,128]{1,0:T(8,128)S(1)}, f32[8,128]{1,0:T(8,128)S(1)}, u32[]{:S(2)}, u32[]{:S(2)}) collective-permute-start(f32[8,128]{1,0:T(8,128)S(1)} %get-tuple-element.56), channel_id=1, source_target_pairs={{1,0},{2,1},{3,2},{4,3},{5,4},{6,5},{7,6},{0,7},{9,8},{10,9},{11,1... | collective-permute-start | bytes 12296 | tf_op jit(solution)/shard_map/ppermute | solution.py:67
  20.7 4.8 %collective-permute-start.9 = (f32[8,128]{1,0:T(8,128)S(1)}, f32[8,128]{1,0:T(8,128)S(1)}, u32[]{:S(2)}, u32[]{:S(2)}) collective-permute-start(f32[8,128]{1,0:T(8,128)S(1)} %get-tuple-element.55), channel_id=1, source_target_pairs={{0,1},{1,2},{2,3},{3,4},{4,5},{5,6},{6,7},{7,0},{8,9},{9,10},{10,1... | collective-permute-start | bytes 12296 | tf_op jit(solution)/shard_map/ppermute | solution.py:67
  27.3 3.8 %collective-permute-start.11 = (f32[16,256]{1,0:T(8,128)S(1)}, f32[16,256]{1,0:T(8,128)S(1)}, u32[]{:S(2)}, u32[]{:S(2)}) collective-permute-start(f32[16,256]{1,0:T(8,128)S(1)} %fields_0.1.refs_7_.refs_10_), channel_id=1, source_target_pairs={{0,8},{1,9},{2,10},{3,11},{4,12},{5,13},{6,14},{7,15},{8,0},{9,1},... | collective-permute-start | bytes 49160 | tf_op jit(solution)/shard_map/ppermute | solution.py:59
  28.8 4.6 %collective-permute-start.12 = (f32[16,256]{1,0:T(8,128)S(1)}, f32[16,256]{1,0:T(8,128)S(1)}, u32[]{:S(2)}, u32[]{:S(2)}) collective-permute-start(f32[16,256]{1,0:T(8,128)S(1)} %fields_0.1.refs_7_.refs_10_), channel_id=1, source_target_pairs={{0,24},{1,25},{2,26},{3,27},{4,28},{5,29},{6,30},{7,31},{8,16},{9,... | collective-permute-start | bytes 49160 | tf_op jit(solution)/shard_map/ppermute | solution.py:60
  36.0 1.3 collective-permute-start.13
  37.3 3.4 %collective-permute-start.14 = (f32[2,3968]{1,0:T(2,128)S(1)}, f32[2,3968]{1,0:T(2,128)S(1)}, u32[]{:S(2)}, u32[]{:S(2)}) collective-permute-start(f32[2,3968]{1,0:T(2,128)S(1)} %add.126), channel_id=1, source_target_pairs={{0,9},{1,8},{2,11},{3,10},{4,13},{5,12},{6,15},{7,14},{8,1},{9,0},... | collective-permute-start | bytes 95240 | tf_op jit(solution)/shard_map/ppermute | solution.py:32
  37.7 3.3 %collective-permute-start.15 = (f32[2,3968]{1,0:T(2,128)S(1)}, f32[2,3968]{1,0:T(2,128)S(1)}, u32[]{:S(2)}, u32[]{:S(2)}) collective-permute-start(f32[2,3968]{1,0:T(2,128)S(1)} %add.126), channel_id=1, source_target_pairs={{0,17},{1,16},{2,19},{3,18},{4,21},{5,20},{6,23},{7,22},{8,25},{9,... | collective-permute-start | bytes 95240 | tf_op jit(solution)/shard_map/ppermute | solution.py:32
  39.1 4.2 %collective-permute-start.16 = (f32[2,3968]{1,0:T(2,128)S(1)}, f32[2,3968]{1,0:T(2,128)S(1)}, u32[]{:S(2)}, u32[]{:S(2)}) collective-permute-start(f32[2,3968]{1,0:T(2,128)S(1)} %add.126), channel_id=1, source_target_pairs={{0,25},{1,24},{2,27},{3,26},{4,29},{5,28},{6,31},{7,30},{8,17},{9,... | collective-permute-start | bytes 95240 | tf_op jit(solution)/shard_map/ppermute | solution.py:32
  43.4 3.9 %collective-permute-start.17 = (f32[2,3968]{1,0:T(2,128)S(1)}, f32[2,3968]{1,0:T(2,128)S(1)}, u32[]{:S(2)}, u32[]{:S(2)}) collective-permute-start(f32[2,3968]{1,0:T(2,128)S(1)} %add_add_fusion.7), channel_id=1, source_target_pairs={{0,3},{1,2},{2,1},{3,0},{4,7},{5,6},{6,5},{7,4},{8,11},{9,10},{10,... | collective-permute-start | bytes 95240 | tf_op jit(solution)/shard_map/ppermute | solution.py:32
  43.5 4.3 %collective-permute-start.18 = (f32[2,3968]{1,0:T(2,128)S(1)}, f32[2,3968]{1,0:T(2,128)S(1)}, u32[]{:S(2)}, u32[]{:S(2)}) collective-permute-start(f32[2,3968]{1,0:T(2,128)S(1)} %add_add_fusion.7), channel_id=1, source_target_pairs={{0,5},{1,4},{2,7},{3,6},{4,1},{5,0},{6,3},{7,2},{8,13},{9,12},{10,... | collective-permute-start | bytes 95240 | tf_op jit(solution)/shard_map/ppermute | solution.py:32
  44.2 5.4 %collective-permute-start.19 = (f32[2,3968]{1,0:T(2,128)S(1)}, f32[2,3968]{1,0:T(2,128)S(1)}, u32[]{:S(2)}, u32[]{:S(2)}) collective-permute-start(f32[2,3968]{1,0:T(2,128)S(1)} %add_add_fusion.7), channel_id=1, source_target_pairs={{0,7},{1,6},{2,5},{3,4},{4,3},{5,2},{6,1},{7,0},{8,15},{9,14},{10,... | collective-permute-start | bytes 95240 | tf_op jit(solution)/shard_map/ppermute | solution.py:32
  51.7 3.7 %collective-permute-start.20 = (f32[8,256]{1,0:T(8,128)S(1)}, f32[8,256]{1,0:T(8,128)S(1)}, u32[]{:S(2)}, u32[]{:S(2)}) collective-permute-start(f32[8,256]{1,0:T(8,128)S(1)} %get-tuple-element.61.refs_7_), channel_id=1, source_target_pairs={{0,8},{1,9},{2,10},{3,11},{4,12},{5,13},{6,14},{7,15},{8,0},{9,1},... | collective-permute-start | bytes 24584 | tf_op jit(solution)/shard_map/ppermute | solution.py:59
  53.2 4.5 %collective-permute-start.21 = (f32[8,256]{1,0:T(8,128)S(1)}, f32[8,256]{1,0:T(8,128)S(1)}, u32[]{:S(2)}, u32[]{:S(2)}) collective-permute-start(f32[8,256]{1,0:T(8,128)S(1)} %get-tuple-element.61.refs_7_), channel_id=1, source_target_pairs={{0,24},{1,25},{2,26},{3,27},{4,28},{5,29},{6,30},{7,31},{8,16},{9,... | collective-permute-start | bytes 24584 | tf_op jit(solution)/shard_map/ppermute | solution.py:60
  60.2 1.3 collective-permute-start.22
  61.5 3.4 %collective-permute-start.23 = (f32[2,3968]{1,0:T(2,128)S(1)}, f32[2,3968]{1,0:T(2,128)S(1)}, u32[]{:S(2)}, u32[]{:S(2)}) collective-permute-start(f32[2,3968]{1,0:T(2,128)S(1)} %add.133), channel_id=1, source_target_pairs={{0,9},{1,8},{2,11},{3,10},{4,13},{5,12},{6,15},{7,14},{8,1},{9,0},... | collective-permute-start | bytes 95240 | tf_op jit(solution)/shard_map/ppermute | solution.py:32
  61.8 3.3 %collective-permute-start.24 = (f32[2,3968]{1,0:T(2,128)S(1)}, f32[2,3968]{1,0:T(2,128)S(1)}, u32[]{:S(2)}, u32[]{:S(2)}) collective-permute-start(f32[2,3968]{1,0:T(2,128)S(1)} %add.133), channel_id=1, source_target_pairs={{0,17},{1,16},{2,19},{3,18},{4,21},{5,20},{6,23},{7,22},{8,25},{9,... | collective-permute-start | bytes 95240 | tf_op jit(solution)/shard_map/ppermute | solution.py:32
  62.3 4.2 %collective-permute-start.25 = (f32[2,3968]{1,0:T(2,128)S(1)}, f32[2,3968]{1,0:T(2,128)S(1)}, u32[]{:S(2)}, u32[]{:S(2)}) collective-permute-start(f32[2,3968]{1,0:T(2,128)S(1)} %add.133), channel_id=1, source_target_pairs={{0,25},{1,24},{2,27},{3,26},{4,29},{5,28},{6,31},{7,30},{8,17},{9,... | collective-permute-start | bytes 95240 | tf_op jit(solution)/shard_map/ppermute | solution.py:32
  66.5 3.9 %collective-permute-start.26 = (f32[2,3968]{1,0:T(2,128)S(1)}, f32[2,3968]{1,0:T(2,128)S(1)}, u32[]{:S(2)}, u32[]{:S(2)}) collective-permute-start(f32[2,3968]{1,0:T(2,128)S(1)} %add_add_fusion.5), channel_id=1, source_target_pairs={{0,3},{1,2},{2,1},{3,0},{4,7},{5,6},{6,5},{7,4},{8,11},{9,10},{10,... | collective-permute-start | bytes 95240 | tf_op jit(solution)/shard_map/ppermute | solution.py:32
  66.6 5.1 %collective-permute-start.27 = (f32[2,3968]{1,0:T(2,128)S(1)}, f32[2,3968]{1,0:T(2,128)S(1)}, u32[]{:S(2)}, u32[]{:S(2)}) collective-permute-start(f32[2,3968]{1,0:T(2,128)S(1)} %add_add_fusion.5), channel_id=1, source_target_pairs={{0,5},{1,4},{2,7},{3,6},{4,1},{5,0},{6,3},{7,2},{8,13},{9,12},{10,... | collective-permute-start | bytes 95240 | tf_op jit(solution)/shard_map/ppermute | solution.py:32
  70.1 5.1 %collective-permute-start.28 = (f32[2,3968]{1,0:T(2,128)S(1)}, f32[2,3968]{1,0:T(2,128)S(1)}, u32[]{:S(2)}, u32[]{:S(2)}) collective-permute-start(f32[2,3968]{1,0:T(2,128)S(1)} %add_add_fusion.5), channel_id=1, source_target_pairs={{0,7},{1,6},{2,5},{3,4},{4,3},{5,2},{6,1},{7,0},{8,15},{9,14},{10,... | collective-permute-start | bytes 95240 | tf_op jit(solution)/shard_map/ppermute | solution.py:32
  77.3 3.7 %collective-permute-start.29 = (f32[8,256]{1,0:T(8,128)S(1)}, f32[8,256]{1,0:T(8,128)S(1)}, u32[]{:S(2)}, u32[]{:S(2)}) collective-permute-start(f32[8,256]{1,0:T(8,128)S(1)} %get-tuple-element.66.refs_7_), channel_id=1, source_target_pairs={{0,8},{1,9},{2,10},{3,11},{4,12},{5,13},{6,14},{7,15},{8,0},{9,1},... | collective-permute-start | bytes 24584 | tf_op jit(solution)/shard_map/ppermute | solution.py:59
  78.8 4.5 %collective-permute-start.30 = (f32[8,256]{1,0:T(8,128)S(1)}, f32[8,256]{1,0:T(8,128)S(1)}, u32[]{:S(2)}, u32[]{:S(2)}) collective-permute-start(f32[8,256]{1,0:T(8,128)S(1)} %get-tuple-element.66.refs_7_), channel_id=1, source_target_pairs={{0,24},{1,25},{2,26},{3,27},{4,28},{5,29},{6,30},{7,31},{8,16},{9,... | collective-permute-start | bytes 24584 | tf_op jit(solution)/shard_map/ppermute | solution.py:60
  85.8 1.3 collective-permute-start.31
  87.1 3.4 %collective-permute-start.32 = (f32[2,3968]{1,0:T(2,128)S(1)}, f32[2,3968]{1,0:T(2,128)S(1)}, u32[]{:S(2)}, u32[]{:S(2)}) collective-permute-start(f32[2,3968]{1,0:T(2,128)S(1)} %add.140), channel_id=1, source_target_pairs={{0,9},{1,8},{2,11},{3,10},{4,13},{5,12},{6,15},{7,14},{8,1},{9,0},... | collective-permute-start | bytes 95240 | tf_op jit(solution)/shard_map/ppermute | solution.py:32
  87.5 3.3 %collective-permute-start.33 = (f32[2,3968]{1,0:T(2,128)S(1)}, f32[2,3968]{1,0:T(2,128)S(1)}, u32[]{:S(2)}, u32[]{:S(2)}) collective-permute-start(f32[2,3968]{1,0:T(2,128)S(1)} %add.140), channel_id=1, source_target_pairs={{0,17},{1,16},{2,19},{3,18},{4,21},{5,20},{6,23},{7,22},{8,25},{9,... | collective-permute-start | bytes 95240 | tf_op jit(solution)/shard_map/ppermute | solution.py:32
  88.9 4.2 %collective-permute-start.34 = (f32[2,3968]{1,0:T(2,128)S(1)}, f32[2,3968]{1,0:T(2,128)S(1)}, u32[]{:S(2)}, u32[]{:S(2)}) collective-permute-start(f32[2,3968]{1,0:T(2,128)S(1)} %add.140), channel_id=1, source_target_pairs={{0,25},{1,24},{2,27},{3,26},{4,29},{5,28},{6,31},{7,30},{8,17},{9,... | collective-permute-start | bytes 95240 | tf_op jit(solution)/shard_map/ppermute | solution.py:32
  93.2 3.9 %collective-permute-start.35 = (f32[2,3968]{1,0:T(2,128)S(1)}, f32[2,3968]{1,0:T(2,128)S(1)}, u32[]{:S(2)}, u32[]{:S(2)}) collective-permute-start(f32[2,3968]{1,0:T(2,128)S(1)} %add_add_fusion.3), channel_id=1, source_target_pairs={{0,3},{1,2},{2,1},{3,0},{4,7},{5,6},{6,5},{7,4},{8,11},{9,10},{10,... | collective-permute-start | bytes 95240 | tf_op jit(solution)/shard_map/ppermute | solution.py:32
  93.3 4.3 %collective-permute-start.36 = (f32[2,3968]{1,0:T(2,128)S(1)}, f32[2,3968]{1,0:T(2,128)S(1)}, u32[]{:S(2)}, u32[]{:S(2)}) collective-permute-start(f32[2,3968]{1,0:T(2,128)S(1)} %add_add_fusion.3), channel_id=1, source_target_pairs={{0,5},{1,4},{2,7},{3,6},{4,1},{5,0},{6,3},{7,2},{8,13},{9,12},{10,... | collective-permute-start | bytes 95240 | tf_op jit(solution)/shard_map/ppermute | solution.py:32
  94.6 5.1 %collective-permute-start.37 = (f32[2,3968]{1,0:T(2,128)S(1)}, f32[2,3968]{1,0:T(2,128)S(1)}, u32[]{:S(2)}, u32[]{:S(2)}) collective-permute-start(f32[2,3968]{1,0:T(2,128)S(1)} %add_add_fusion.3), channel_id=1, source_target_pairs={{0,7},{1,6},{2,5},{3,4},{4,3},{5,2},{6,1},{7,0},{8,15},{9,14},{10,... | collective-permute-start | bytes 95240 | tf_op jit(solution)/shard_map/ppermute | solution.py:32
  102.1 3.7 %collective-permute-start.38 = (f32[8,256]{1,0:T(8,128)S(1)}, f32[8,256]{1,0:T(8,128)S(1)}, u32[]{:S(2)}, u32[]{:S(2)}) collective-permute-start(f32[8,256]{1,0:T(8,128)S(1)} %get-tuple-element.70.refs_7_), channel_id=1, source_target_pairs={{0,8},{1,9},{2,10},{3,11},{4,12},{5,13},{6,14},{7,15},{8,0},{9,1},... | collective-permute-start | bytes 24584 | tf_op jit(solution)/shard_map/ppermute | solution.py:59
  103.6 4.5 %collective-permute-start.39 = (f32[8,256]{1,0:T(8,128)S(1)}, f32[8,256]{1,0:T(8,128)S(1)}, u32[]{:S(2)}, u32[]{:S(2)}) collective-permute-start(f32[8,256]{1,0:T(8,128)S(1)} %get-tuple-element.70.refs_7_), channel_id=1, source_target_pairs={{0,24},{1,25},{2,26},{3,27},{4,28},{5,29},{6,30},{7,31},{8,16},{9,... | collective-permute-start | bytes 24584 | tf_op jit(solution)/shard_map/ppermute | solution.py:60
  108.2 18.2 %slice-start = ((f32[48,4,128]{2,1,0:T(4,128)}), f32[40,4,128]{2,1,0:T(4,128)S(1)}, s32[]{:S(2)}) async-start(f32[48,4,128]{2,1,0:T(4,128)} %maps_hbm.1), calls=%async_computation | async-start | bytes 163840 | tf_op jit(solution)/shard_map/slice | solution.py:539
  110.6 1.3 collective-permute-start.40
  111.9 3.4 %collective-permute-start.41 = (f32[2,3968]{1,0:T(2,128)S(1)}, f32[2,3968]{1,0:T(2,128)S(1)}, u32[]{:S(2)}, u32[]{:S(2)}) collective-permute-start(f32[2,3968]{1,0:T(2,128)S(1)} %add.147), channel_id=1, source_target_pairs={{0,9},{1,8},{2,11},{3,10},{4,13},{5,12},{6,15},{7,14},{8,1},{9,0},... | collective-permute-start | bytes 95240 | tf_op jit(solution)/shard_map/ppermute | solution.py:32
  112.2 3.3 %collective-permute-start.42 = (f32[2,3968]{1,0:T(2,128)S(1)}, f32[2,3968]{1,0:T(2,128)S(1)}, u32[]{:S(2)}, u32[]{:S(2)}) collective-permute-start(f32[2,3968]{1,0:T(2,128)S(1)} %add.147), channel_id=1, source_target_pairs={{0,17},{1,16},{2,19},{3,18},{4,21},{5,20},{6,23},{7,22},{8,25},{9,... | collective-permute-start | bytes 95240 | tf_op jit(solution)/shard_map/ppermute | solution.py:32
  112.7 4.2 %collective-permute-start.43 = (f32[2,3968]{1,0:T(2,128)S(1)}, f32[2,3968]{1,0:T(2,128)S(1)}, u32[]{:S(2)}, u32[]{:S(2)}) collective-permute-start(f32[2,3968]{1,0:T(2,128)S(1)} %add.147), channel_id=1, source_target_pairs={{0,25},{1,24},{2,27},{3,26},{4,29},{5,28},{6,31},{7,30},{8,17},{9,... | collective-permute-start | bytes 95240 | tf_op jit(solution)/shard_map/ppermute | solution.py:32
  117.0 4.0 %collective-permute-start.44 = (f32[2,3968]{1,0:T(2,128)S(1)}, f32[2,3968]{1,0:T(2,128)S(1)}, u32[]{:S(2)}, u32[]{:S(2)}) collective-permute-start(f32[2,3968]{1,0:T(2,128)S(1)} %add_add_fusion.1), channel_id=1, source_target_pairs={{0,3},{1,2},{2,1},{3,0},{4,7},{5,6},{6,5},{7,4},{8,11},{9,10},{10,... | collective-permute-start | bytes 95240 | tf_op jit(solution)/shard_map/ppermute | solution.py:32
  117.0 4.7 %collective-permute-start.45 = (f32[2,3968]{1,0:T(2,128)S(1)}, f32[2,3968]{1,0:T(2,128)S(1)}, u32[]{:S(2)}, u32[]{:S(2)}) collective-permute-start(f32[2,3968]{1,0:T(2,128)S(1)} %add_add_fusion.1), channel_id=1, source_target_pairs={{0,5},{1,4},{2,7},{3,6},{4,1},{5,0},{6,3},{7,2},{8,13},{9,12},{10,... | collective-permute-start | bytes 95240 | tf_op jit(solution)/shard_map/ppermute | solution.py:32
  120.1 5.1 %collective-permute-start.46 = (f32[2,3968]{1,0:T(2,128)S(1)}, f32[2,3968]{1,0:T(2,128)S(1)}, u32[]{:S(2)}, u32[]{:S(2)}) collective-permute-start(f32[2,3968]{1,0:T(2,128)S(1)} %add_add_fusion.1), channel_id=1, source_target_pairs={{0,7},{1,6},{2,5},{3,4},{4,3},{5,2},{6,1},{7,0},{8,15},{9,14},{10,... | collective-permute-start | bytes 95240 | tf_op jit(solution)/shard_map/ppermute | solution.py:32

commit v5 on v4

--- a/solution.py
+++ b/solution.py
@@ -61,10 +61,11 @@
     return got_a, got_b
 
 
-def lon_ring(to_west, to_east):
+def lon_partners(near, far):
     count = lax.axis_size("lon")
-    up = [(i, (i + 1) % count) for i in range(count)]
-    return lax.ppermute(to_east, "lon", up), lax.ppermute(to_west, "lon", [(j, i) for i, j in up])
+    same = lambda i: i
+    got_far = lax.ppermute(far, ("lat", "lon"), pairing(same, lambda j: (j + 1 if j % 2 else j - 1) % count))
+    return swap(near, 0, 1), got_far
 
 
 def split(x):
@@ -139,19 +140,27 @@
     return jnp.transpose(jnp.broadcast_to(row, (8, LANES)))[:, :1]
 
 
-def own_flags_kernel(words_hbm, coast_hbm, x_hbm, m_ref, a_ref, words_ref, coast_ref, x_ref, spread_ref, bit_ref, sems):
+def own_flags_kernel(reach, *refs):
+    words_hbm, coast_hbm, x_hbm, maps_hbm = refs[:4]
+    m_ref, a_ref, u_ref, row_ref, west_ref, east_ref = refs[4:10]
+    words_ref, coast_ref, x_ref, maps_ref, spread_ref, bit_ref, sems = refs[10:]
     rows = coast_ref.shape[0]
-    loads = [pltpu.make_async_copy(words_hbm, words_ref, sems.at[0]), pltpu.make_async_copy(coast_hbm, coast_ref, sems.at[1])]
+    loads = [
+        pltpu.make_async_copy(words_hbm, words_ref, sems.at[0]),
+        pltpu.make_async_copy(coast_hbm, coast_ref, sems.at[1]),
+    ]
     for r in range(rows):
         at = pl.ds(r * LANES, LANES)
         loads.append(pltpu.make_async_copy(x_hbm.at[at], x_ref.at[at], sems.at[2 + r]))
+    loads.append(pltpu.make_async_copy(maps_hbm, maps_ref, sems.at[2 + rows]))
     for load in loads:
         load.start()
     fill_spread(spread_ref, bit_ref)
     loads[0].wait()
     loads[1].wait()
     days = spread_ref.shape[1]
-    coasts = jnp.transpose(jnp.concatenate([coast_ref[...].astype(F32)] * (8 // rows), axis=0))
+    coast_own = coast_ref[...].astype(F32)
+    coasts = jnp.transpose(jnp.concatenate([coast_own] * (8 // rows), axis=0))
     for r in range(rows):
         coast = coasts[:, r : r + 1]
         ocean = coast.astype(BF16)
@@ -164,6 +173,23 @@
             at = slice(g * days, (g + 1) * days)
             m_ref[cell, at] = given
             a_ref[cell, at] = x_ref[cell, at] * given * ocean
+    loads[2 + rows].wait()
+    modes = maps_ref.shape[0]
+    pieces = []
+    for r in range(rows):
+        at = slice(r * LANES, (r + 1) * LANES)
+        u = maps_ref[:, r, :]
+        u_ref[:, at] = u
+        row_ref[:, at] = coast_own[r : r + 1]
+        pieces.append(jnp.concatenate([u, jnp.broadcast_to(coast_own[r : r + 1], (8, LANES))], axis=0))
+    base = modes + 8
+    west_ref[:base], east_ref[:base] = edges(pieces, reach)
+    for g in range(words_ref.shape[1] // LANES):
+        for r in range(rows):
+            at = slice(base + reach * (rows * g + r), base + reach * (rows * g + r + 1))
+            group = slice(g * LANES, (g + 1) * LANES)
+            west_ref[at] = words_ref[r * LANES : r * LANES + reach, group].astype(F32)
+            east_ref[at] = words_ref[(r + 1) * LANES - reach : (r + 1) * LANES, group].astype(F32)
 
 
 def edges(pieces, reach):
@@ -180,57 +206,10 @@
     return west, east
 
 
-def prep_kernel(reach, maps_hbm, coast_hbm, words_hbm, u_ref, row_ref, west_ref, east_ref, maps_ref, coast_ref, first_ref, last_ref, sems):
-    loads = [
-        pltpu.make_async_copy(maps_hbm, maps_ref, sems.at[0]),
-        pltpu.make_async_copy(coast_hbm, coast_ref, sems.at[1]),
-        pltpu.make_async_copy(words_hbm.at[:, pl.ds(0, reach)], first_ref, sems.at[2]),
-        pltpu.make_async_copy(words_hbm.at[:, pl.ds(LANES - reach, reach)], last_ref, sems.at[3]),
-    ]
-    for load in loads:
-        load.start()
-    for load in loads:
-        load.wait()
-    modes, rows = maps_ref.shape[:2]
-    coast = coast_ref[...].astype(F32)
-    pieces = []
-    for r in range(rows):
-        at = slice(r * LANES, (r + 1) * LANES)
-        u = maps_ref[:, r, :]
-        u_ref[:, at] = u
-        row_ref[:, at] = coast[r : r + 1]
-        pieces.append(jnp.concatenate([u, jnp.broadcast_to(coast[r : r + 1], (8, LANES))], axis=0))
-    west, east = edges(pieces, reach)
-    base = modes + 8
-    west_ref[:base] = west
-    east_ref[:base] = east
-    for g in range(first_ref.shape[2] // LANES):
-        for r in range(rows):
-            at = slice(base + reach * (rows * g + r), base + reach * (rows * g + r + 1))
-            west_ref[at] = first_ref[r, :, g * LANES : (g + 1) * LANES].astype(F32)
-            east_ref[at] = last_ref[r, :, g * LANES : (g + 1) * LANES].astype(F32)
-
-
-def halo_flags_kernel(modes, west_ref, east_ref, m_ref, u_ref, row_ref, spread_ref, bit_ref):
-    fill_spread(spread_ref, bit_ref)
-    base = modes + 8
-    lane = lane_ids((base, LANES))
-    fields = jnp.where(lane < LANES // 2, west_ref[:base], east_ref[:base])
-    u_ref[...] = fields[:modes]
-    row_ref[...] = fields[modes : modes + 1]
-    coast = as_column(fields[modes : modes + 1]).astype(jnp.int32)
-    days = spread_ref.shape[1]
-    half = LANES // 2
-    for g in range(m_ref.shape[1] // days):
-        at = slice(base + half * g, base + half * (g + 1))
-        words = jnp.concatenate([west_ref[at], east_ref[at]], axis=0).astype(jnp.int32) * coast
-        m_ref[:, g * days : (g + 1) * days] = unpack_words(words, spread_ref, bit_ref)
-
-
 def given_kernel(rows, reach, *refs):
-    a_ref, place_ref = refs[:2]
-    pieces = [ref[...] for ref in refs[2:-4]]
-    v_ref, xv_ref, west_ref, east_ref = refs[-4:]
+    a_ref, place_ref, ew_ref, ee_ref = refs[:4]
+    pieces = [ref[...] for ref in refs[4:-4]]
+    v_ref, xv_ref, near_ref, far_ref = refs[-4:]
     here = place_ref[3]
     bit = 1
     while bit < len(pieces):
@@ -244,20 +223,78 @@
     both = lax.dot_general(jnp.concatenate([high, low], axis=0), a_ref[...], NT, preferred_element_type=F32)
     xv = both[:PAIRS] + both[PAIRS:]
     xv_ref[...] = xv
-    west_ref[...], east_ref[...] = edges([xv[:, r * LANES : (r + 1) * LANES] for r in range(rows)], reach)
+    west, east = edges([xv[:, r * LANES : (r + 1) * LANES] for r in range(rows)], reach)
+    odd = here % 2 == 1
+    tall = ew_ref.shape[0]
+    near_ref[:tall] = jnp.where(odd, ew_ref[...], ee_ref[...])
+    near_ref[tall:] = jnp.where(odd, west, east)
+    far_ref[:tall] = jnp.where(odd, ee_ref[...], ew_ref[...])
+    far_ref[tall:] = jnp.where(odd, east, west)
+
+
+def masked_products(vs, u, low, chunk, m_ref):
+    modes, days = vs.shape
+    acc = None
+    for first in range(0, days, chunk):
+        at = slice(first, first + chunk)
+        v = vs[:, at]
+        high, lower = split(jnp.concatenate([v * v[j : j + 1] for j in (low, low + 1)], axis=0))
+        left = jnp.concatenate([high, lower], axis=0)
+        part = lax.dot_general(left, m_ref[:, at], NT, preferred_element_type=F32)
+        acc = part if acc is None else acc + part
+    acc = acc[: 2 * modes] + acc[2 * modes :]
+    return jnp.concatenate(
+        [jnp.sum(u * acc[j * modes : (j + 1) * modes], axis=0, keepdims=True) for j in range(2)], axis=0
+    )
+
+
+def own_products_kernel(chunk, m_ref, v_ref, u_ref, base_ref):
+    base_ref[...] = masked_products(v_ref, u_ref[...], 0, chunk, m_ref)
+
+
+def new_fields(pair, u_pair, coast, proj):
+    v0, v1 = (pair[0:1], pair[1:2])
+    h00, h01, h11 = (total_of(v0 * v0), total_of(v0 * v1), total_of(v1 * v1))
+    add0, add1 = solve_pair(h00, h01, h01, h11, proj[0:1], proj[1:2])
+    return coast * (u_pair + jnp.concatenate([add0, add1], axis=0))
+
+
+def first_fields_kernel(rows, reach, chunk, *refs):
+    near_ref, far_ref, place_ref, v_ref, u_ref, row_ref, xv_ref, base_ref = refs[:8]
+    w_ref, m_ref, uh_ref, rowh_ref, xh_ref, spread_ref, bit_ref = refs[8:]
+    fill_spread(spread_ref, bit_ref)
+    odd = place_ref[3] % 2 == 1
+    west = jnp.where(odd, near_ref[...], far_ref[...])
+    east = jnp.where(odd, far_ref[...], near_ref[...])
+    modes = v_ref.shape[0]
+    base = modes + 8
+    lane = lane_ids((base, LANES))
+    fields = jnp.where(lane < LANES // 2, west[:base], east[:base])
+    u_halo = fields[:modes]
+    uh_ref[...] = u_halo
+    rowh_ref[...] = fields[modes : modes + 1]
+    xh = jnp.where(lane[:PAIRS] < LANES // 2, west[-PAIRS:], east[-PAIRS:])
+    xh_ref[...] = xh
+    coast = as_column(fields[modes : modes + 1]).astype(jnp.int32)
+    days = spread_ref.shape[1]
+    half = LANES // 2
+    for g in range(m_ref.shape[1] // days):
+        at = slice(base + half * g, base + half * (g + 1))
+        words = jnp.concatenate([west[at], east[at]], axis=0).astype(jnp.int32) * coast
+        m_ref[:, g * days : (g + 1) * days] = unpack_words(words, spread_ref, bit_ref)
+    halo = xh[:2] - masked_products(v_ref, u_halo, 0, chunk, m_ref)
+    proj = jnp.concatenate([xv_ref[:2] - base_ref[...], halo], axis=1)
+    u_pair = jnp.concatenate([u_ref[:2], u_halo[:2]], axis=1)
+    coast = jnp.concatenate([row_ref[...], fields[modes : modes + 1]], axis=1)
+    count = 2 * rows
+    w_ref[:count] = to_block(new_fields(v_ref[:2], u_pair, coast, proj), rows, reach)
+    w_ref[count:] = to_block(jnp.concatenate([coast, coast], axis=0), rows, reach)
 
 
 def fields_kernel(step, rows, reach, total, chunk, *refs):
-    m_ref, mh_ref, v_ref, u_ref, uh_ref, coast_ref, coasth_ref, xv_ref, xw_ref, xe_ref = refs[:10]
-    refs = refs[10:]
-    older = refs[: 2 * max(step - 1, 0)]
-    refs = refs[len(older) :]
-    if step:
-        sum_ref, block_ref = refs[:2]
-        w_ref, vn_ref, un_ref, vs, us = refs[2:]
-    else:
-        w_ref, vs, us = refs
-    days = v_ref.shape[1]
+    m_ref, mh_ref, v_ref, u_ref, uh_ref, row_ref, rowh_ref, xv_ref, xh_ref = refs[:9]
+    older = refs[9 : 9 + 2 * (step - 1)]
+    sum_ref, block_ref, w_ref, vn_ref, un_ref, vs, us = refs[9 + len(older) :]
     low = 2 * step
     own = rows * LANES
     vs[...] = v_ref[...]
@@ -266,44 +303,16 @@
     for q in range(step - 1):
         vs[2 * q : 2 * q + 2] = older[2 * q][...]
         us[2 * q : 2 * q + 2] = older[2 * q + 1][...]
-    if step:
-        vn, un = new_pair(rows, reach, total, sum_ref, block_ref)
-        vn_ref[...] = vn
-        un_ref[...] = un
-        vs[low - 2 : low] = vn
-        us[low - 2 : low] = un
-    modes = vs.shape[0]
-    acc = acc_h = None
-    for first in range(0, days, chunk):
-        at = slice(first, first + chunk)
-        v = vs[:, at]
-        parts = []
-        for j in (low, low + 1):
-            parts.append(v * v[j : j + 1])
-        high, lower = split(jnp.concatenate(parts, axis=0))
-        left = jnp.concatenate([high, lower], axis=0)
-        mid = lax.dot_general(left, m_ref[:, at], NT, preferred_element_type=F32)
-        edge = lax.dot_general(left, mh_ref[:, at], NT, preferred_element_type=F32)
-        acc = mid if acc is None else acc + mid
-        acc_h = edge if acc_h is None else acc_h + edge
-    masked = jnp.concatenate([acc[: 2 * modes] + acc[2 * modes :], acc_h[: 2 * modes] + acc_h[2 * modes :]], axis=1)
-    lane = lane_ids((PAIRS, LANES))
-    xh = jnp.where(lane < LANES // 2, xw_ref[...], xe_ref[...])
-    xv = jnp.concatenate([xv_ref[...], xh], axis=1)
-    u = us[...]
-    proj = [
-        xv[low + j : low + j + 1] - jnp.sum(u * masked[j * modes : (j + 1) * modes], axis=0, keepdims=True)
-        for j in range(2)
-    ]
-    v0, v1 = (vs[low : low + 1], vs[low + 1 : low + 2])
-    h00, h01, h11 = (total_of(v0 * v0), total_of(v0 * v1), total_of(v1 * v1))
-    add0, add1 = solve_pair(h00, h01, h01, h11, proj[0], proj[1])
-    coast = jnp.concatenate([coast_ref[...], coasth_ref[...]], axis=1)
-    fresh = coast * jnp.concatenate([u[low : low + 1] + add0, u[low + 1 : low + 2] + add1], axis=0)
-    count = 2 * rows
-    w_ref[:count] = to_block(fresh, rows, reach)
-    if step == 0:
-        w_ref[count:] = to_block(jnp.concatenate([coast, coast], axis=0), rows, reach)
+    vn, un = new_pair(rows, reach, total, sum_ref, block_ref)
+    vn_ref[...] = vn
+    un_ref[...] = un
+    vs[low - 2 : low] = vn
+    us[low - 2 : low] = un
+    mid = xv_ref[low : low + 2] - masked_products(vs, us[:, :own], low, chunk, m_ref)
+    edge = xh_ref[low : low + 2] - masked_products(vs, us[:, own:], low, chunk, mh_ref)
+    proj = jnp.concatenate([mid, edge], axis=1)
+    coast = jnp.concatenate([row_ref[...], rowh_ref[...]], axis=1)
+    w_ref[...] = to_block(new_fields(vs[low : low + 2], us[low : low + 2], coast, proj), rows, reach)
 
 
 def new_pair(rows, reach, total, sum_ref, block_ref):
@@ -311,14 +320,12 @@
     gram = sum_ref[:, days:]
     g00, g01, g11 = (gram[0:1, 0:1], gram[0:1, 1:2], gram[1:2, 1:2])
     n0, n1 = (jnp.sqrt(g00 / total + EPS), jnp.sqrt(g11 / total + EPS))
-    first, second = solve_pair(
-        g00 / (n0 * n0),
-        g01 / (n0 * n1),
-        g01 / (n0 * n1),
-        g11 / (n1 * n1),
-        sum_ref[0:1, :days] / n0,
-        sum_ref[1:2, :days] / n1,
-    )
+    g00, g01, g11 = (g00 / (n0 * n0), g01 / (n0 * n1), g11 / (n1 * n1))
+    determ = g00 * g11 - g01 * g01
+    p0, p1 = (sum_ref[0:1, :days], sum_ref[1:2, :days])
+    cross = g01 / determ
+    first = (g11 / determ / n0) * p0 - (cross / n1) * p1
+    second = (g00 / determ / n1) * p1 - (cross / n0) * p0
     field = from_block(block_ref[...], rows, reach)
     unit = jnp.concatenate([field[0:1] / n0, field[1:2] / n1], axis=0)
     return jnp.concatenate([first, second], axis=0), unit
@@ -359,11 +366,12 @@
     south = lambda z: pltpu.roll(z, tall - 2, 0)
     west = lambda z: pltpu.roll(z, 1, 1)
     east = lambda z: pltpu.roll(z, 2 * LANES - 1, 1)
-    cn, cs, cw, ce = (north(coast), south(coast), west(coast), east(coast))
-    klon = klon_ref[...]
+    klon = klon_ref[...] * coast
+    klat = KLAT * coast
+    an, as_, aw, ae = (klat * north(coast), klat * south(coast), klon * west(coast), klon * east(coast))
+    stay = 1.0 - (an + as_ + aw + ae)
     for _ in range(SWEEPS):
-        flux = KLAT * (cn * (north(w) - w) + cs * (south(w) - w)) + klon * (cw * (west(w) - w) + ce * (east(w) - w))
-        w = w + coast * flux
+        w = stay * w + (an * north(w) + as_ * south(w)) + (aw * west(w) + ae * east(w))
     block = w[count : 2 * count]
     block_ref[...] = block
     cells = lambda z: jnp.concatenate([z[2 * r : 2 * r + 2, :LANES] for r in range(rows)], axis=1)
@@ -443,74 +451,76 @@
     klon = jnp.broadcast_to(KLON / (cos_tall * cos_tall), (6 * rows, 2 * LANES))
     cosl = jnp.broadcast_to(cos_tall[2 * rows : 4 * rows], (2 * rows, 2 * LANES))
 
-    tall_edge = modes + 8 + rows * reach * (words // LANES)
-    u, coast, to_west, to_east = call(
-        functools.partial(prep_kernel, reach),
-        "prep",
-        [((modes, own), F32), ((1, own), F32), ((tall_edge, LANES), F32), ((tall_edge, LANES), F32)],
-        [(mode_maps.shape, F32), ((rows, LANES), jnp.int32)] + [((rows, reach, words), jnp.int32)] * 2,
-        [mode_maps, ocean_binary_mask, missing_date_bitmask],
-        loads=4,
-    )
-    from_west, from_east = lon_ring(to_west, to_east)
     words_per = words // LANES
     flags_scratch = [((2 * LANES, days // words_per), BF16), ((1, days // words_per), jnp.int32)]
-    m, a = call(
-        own_flags_kernel,
+    edge = ((modes + 8 + rows * reach * words_per, LANES), F32)
+    m, a, u, row, edge_west, edge_east = call(
+        functools.partial(own_flags_kernel, reach),
         "own_flags",
-        [((own, days), BF16)] * 2,
-        [((own, words), jnp.int32), ((rows, LANES), jnp.int32), ((own, days), BF16), *flags_scratch],
-        [missing_date_bitmask.reshape(own, words), ocean_binary_mask, sea_heat_deviations.reshape(own, days)],
+        [((own, days), BF16), ((own, days), BF16), ((modes, own), F32), ((1, own), F32), edge, edge],
+        [((own, words), jnp.int32), ((rows, LANES), jnp.int32), ((own, days), BF16), (mode_maps.shape, F32), *flags_scratch],
+        [missing_date_bitmask.reshape(own, words), ocean_binary_mask, sea_heat_deviations.reshape(own, days), mode_maps],
         flops=4 * LANES * own * days,
-        loads=2 + rows,
-    )
-    nlon = lax.axis_size("lon")
-    if nlon == 8:
-        pieces = [swap(mode_series, 0, b) for b in (2, 4, 6)]
+        loads=3 + rows,
+    )
+    if lax.axis_size("lon") == 8:
+        pieces = [swap(mode_series, 0, b | 1) for b in (2, 4, 6)]
         *pieces, m, a = lax.optimization_barrier((*pieces, m, a))
-        pieces = [z for piece in [mode_series, *pieces] for z in (piece, swap(piece, 0, 1))]
+        pieces = [z for piece in pieces for z in (swap(piece, 0, 1), piece)]
+        pieces = [mode_series, swap(mode_series, 0, 1), *pieces]
     else:
         pieces = [lax.all_gather(mode_series, "lon", axis=1, tiled=True)]
-    m_halo, u_halo, coast_halo = call(
-        functools.partial(halo_flags_kernel, modes),
-        "halo_flags",
-        [((sides, days), BF16), ((modes, sides), F32), ((1, sides), F32)],
-        flags_scratch,
-        [from_west, from_east],
-        flops=4 * LANES * sides * days,
-    )
-    v, xv, to_west, to_east = call(
+    edge = ((edge[0][0] + PAIRS, LANES), F32)
+    v, xv, near, far = call(
         functools.partial(given_kernel, rows, reach),
         "given",
-        [((modes, days), F32), ((PAIRS, own), F32), ((PAIRS, LANES), F32), ((PAIRS, LANES), F32)],
+        [((modes, days), F32), ((PAIRS, own), F32), edge, edge],
         [],
-        [a, place, *pieces],
+        [a, place, edge_west, edge_east, *pieces],
         smem=(1,),
         flops=4 * PAIRS * own * days,
     )
-    xv_west, xv_east = lon_ring(to_west, to_east)
+    near, far = lon_partners(near, far)
+    (base,) = call(
+        functools.partial(own_products_kernel, chunk),
+        "own_products",
+        [((2, own), F32)],
+        [],
+        [m, v, u],
+        flops=8 * modes * own * days,
+    )
 
     count = 2 * rows
     news = []
     summed = block = None
     coasts = ()
     for step in range(STEPS):
-        wide = 2 * count if step == 0 else count
-        outs = [((wide, 2 * LANES), F32)]
-        extra = []
-        if step:
-            outs += [((2, days), F32), ((2, cells), F32)]
-            extra = [*news, summed, block]
-        got = call(
-            functools.partial(fields_kernel, step, rows, reach, total, chunk),
-            f"fields_{step}",
-            outs,
-            [((modes, days), F32), ((modes, cells), F32)],
-            [m, m_halo, v, u, u_halo, coast, coast_halo, xv, xv_west, xv_east, *extra],
-            flops=8 * modes * cells * days,
-        )
-        fresh = got[0]
-        news += got[1:]
+        if step == 0:
+            fresh, m_halo, u_halo, row_halo, xv_halo = call(
+                functools.partial(first_fields_kernel, rows, reach, chunk),
+                "fields_0",
+                [
+                    ((2 * count, 2 * LANES), F32),
+                    ((sides, days), BF16),
+                    ((modes, sides), F32),
+                    ((1, sides), F32),
+                    ((PAIRS, sides), F32),
+                ],
+                flags_scratch,
+                [near, far, place, v, u, row, xv, base],
+                smem=(2,),
+                flops=8 * modes * sides * days,
+            )
+        else:
+            fresh, *new = call(
+                functools.partial(fields_kernel, step, rows, reach, total, chunk),
+                f"fields_{step}",
+                [((count, 2 * LANES), F32), ((2, days), F32), ((2, cells), F32)],
+                [((modes, days), F32), ((modes, cells), F32)],
+                [m, m_halo, v, u, u_halo, row, row_halo, xv, xv_halo, *news, summed, block],
+                flops=8 * modes * cells * days,
+            )
+            news += new
         got_a, got_b = lat_partners(fresh)
         partial_sums, block = call(
             functools.partial(sums_kernel, step, rows, chunk),

time: 127 us -> 126 us (level)
  starting transfers between devices: 49.9 us -> 47.8 us
    ppermute x35 -> x36, waiting for transfers between devices: 29.8 us -> 33.7 us  [swap(): lax.ppermute(x, ('lat', 'lon'), pairing(lambda i: i ^ lat_bits, lambda j:...]
    ppermute x4 -> x1, starting transfers between devices: 5.46 us -> 2.27 us  [lon_partners(): lax.ppermute(far, ('lat', 'lon'), pairing(same, lambda j: (j + 1 if j % 2...]
    ppermute x4, starting transfers between devices: 3.91 us -> 6.43 us  [lat_partners(): lax.ppermute(x, ('lat', 'lon'), pairing(lambda i: (i + 1 if i % 2 else i...]
    ppermute x4, starting transfers between devices: 6.1 us -> 4.15 us  [lat_partners(): got_a = lax.ppermute(x, ('lat', 'lon'), pairing(lambda i: i ^ 1, same))]
    ppermute x4 -> x1, waiting for transfers between devices: 3.97 us -> 2.15 us  [lon_partners(): lax.ppermute(far, ('lat', 'lon'), pairing(same, lambda j: (j + 1 if j % 2...]
    ppermute x4, waiting for transfers between devices: 9.55 us -> 7.81 us  [lat_partners(): lax.ppermute(x, ('lat', 'lon'), pairing(lambda i: (i + 1 if i % 2 else i...]
    ppermute x35 -> x36, starting transfers between devices: 34.4 us -> 35 us  [swap(): lax.ppermute(x, ('lat', 'lon'), pairing(lambda i: i ^ lat_bits, lambda j:...]
    pallas_call x13 -> x12, Pallas kernels: 26.1 us -> 26 us  [call(): pl.pallas_call(kernel, out_shape=[jax.ShapeDtypeStruct(s, t) for s, t in...]
  transfers between devices with their start and end apart: 47 -> 45, of which waited for: 37 -> 37; matrix products, arithmetic and copies ran while one was open for 0% -> 0% of each run, Pallas kernels for 6% -> 4%
where the time goes in v5:
time: 126 us
  waiting for transfers between devices  48.7 us (39%)
  starting transfers between devices  47.8 us (38%)
  Pallas kernels  26 us (21%)
  other arithmetic  1.91 us (2%)
    ppermute x36, starting transfers between devices, swap(): lax.ppermute(x, ('lat', 'lon'), pairing(lambda i: i ^ lat_bits, lambda j:...  35 us
    ppermute x36, waiting for transfers between devices, swap(): lax.ppermute(x, ('lat', 'lon'), pairing(lambda i: i ^ lat_bits, lambda j:...  33.7 us
    pallas_call x12, Pallas kernels, call(): pl.pallas_call(kernel, out_shape=[jax.ShapeDtypeStruct(s, t) for s, t in...  26 us
    ppermute x4, waiting for transfers between devices, lat_partners(): lax.ppermute(x, ('lat', 'lon'), pairing(lambda i: (i + 1 if i % 2 else i...  7.81 us
    ppermute x4, starting transfers between devices, lat_partners(): lax.ppermute(x, ('lat', 'lon'), pairing(lambda i: (i + 1 if i % 2 else i...  6.43 us
    ppermute x4, waiting for transfers between devices, lat_partners(): got_a = lax.ppermute(x, ('lat', 'lon'), pairing(lambda i: i ^ 1, same))  4.99 us
    ppermute x4, starting transfers between devices, lat_partners(): got_a = lax.ppermute(x, ('lat', 'lon'), pairing(lambda i: i ^ 1, same))  4.15 us
  transfers between devices with their start and end apart: 45, of which 37 were waited for; matrix products, arithmetic and copies ran while one was open for 0% of the time, Pallas kernels for 4%

profile of v5, /device:TPU:0, one launch (start us, length us, event | category | flops | bytes accessed | tf_op | source)
XLA Modules:
  0.0 125.6 jit_solution(10264781370027679887)
XLA Ops:
  0.6 2.5 %collective-permute-start = (f32[48,480]{1,0:T(8,128)}, f32[48,480]{1,0:T(8,128)S(1)}, u32[]{:S(2)}, u32[]{:S(2)}) collective-permute-start(f32[48,480]{1,0:T(8,128)} %refs_4_.1), channel_id=1, source_target_pairs={{0,3},{1,2},{2,1},{3,0},{4,7},{5,6},{6,5},{7,4},{8,11},{9,10},{10,... | collective-permute-start | bytes 276488 | tf_op jit(solution)/shard_map/ppermute | solution.py:32
  3.2 2.9 %collective-permute-start.1 = (f32[48,480]{1,0:T(8,128)}, f32[48,480]{1,0:T(8,128)S(1)}, u32[]{:S(2)}, u32[]{:S(2)}) collective-permute-start(f32[48,480]{1,0:T(8,128)} %refs_4_.1), channel_id=1, source_target_pairs={{0,5},{1,4},{2,7},{3,6},{4,1},{5,0},{6,3},{7,2},{8,13},{9,12},{10,... | collective-permute-start | bytes 276488 | tf_op jit(solution)/shard_map/ppermute | solution.py:32
  6.0 4.2 %own_flags.1 = (bf16[512,3840]{1,0:T(8,128)(2,1)S(1)}, bf16[512,3840]{1,0:T(8,128)(2,1)S(1)}, f32[48,512]{1,0:T(8,128)S(1)}, f32[1,512]{1,0:T(1,128)S(1)}, f32[1...) custom-call(s32[512,256]{1,0:T(8,128)} %bitcast.8, s32[4,128]{1,0:T(4,128)} %refs_1_.1, bf16[512,3840]{1,0:T(8,128)(2,1)} %bitcast.7, ...), custom_call_target="tpu_custom_call" | custom-call | flops 1006632960 | bytes 4556800 | tf_op jit(solution)/shard_map/own_flags/pallas_call | solution.py:419
  10.3 3.4 %collective-permute-done.2.refs_11_ = f32[48,480]{1,0:T(8,128)S(1)} collective-permute-done((f32[48,480]{1,0:T(8,128)}, f32[48,480]{1,0:T(8,128)S(1)}, u32[]{:S(2)}, u32[]{:S(2)}) %collective-permute-start.2) | collective-permute-done | bytes 92192 | tf_op jit(solution)/shard_map/ppermute | solution.py:32
  15.6 1.8 %given.1 = (f32[48,3840]{1,0:T(8,128)S(1)}, f32[8,512]{1,0:T(8,128)S(1)}, f32[192,128]{1,0:T(8,128)S(1)}, f32[192,128]{1,0:T(8,128)S(1)}) custom-call(bf16[512,3840]{1,0:T(8,128)(2,1)S(1)} %get-tuple-element.44.refs_0_.refs_1_, s32[4]{0:T(128)S(1)} %pad_add_fusion.refs_1_.refs_2_.refs_4_, f32[184,128]{1,0:T(8,128)S(1)} %get-tuple-element.45.refs_2_, ...), custom_call_target="tpu_custom_call" | custom-call | flops 62914560 | bytes 4857872 | tf_op jit(solution)/shard_map/given/pallas_call | solution.py:419
  17.8 2.3 %collective-permute-start.8 = (f32[192,128]{1,0:T(8,128)S(1)}, f32[192,128]{1,0:T(8,128)S(1)}, u32[]{:S(2)}, u32[]{:S(2)}) collective-permute-start(f32[192,128]{1,0:T(8,128)S(1)} %get-tuple-element.51), channel_id=1, source_target_pairs={{0,7},{1,2},{2,1},{3,4},{4,3},{5,6},{6,5},{7,0},{8,15},{9,10},{10,... | collective-permute-start | bytes 294920 | tf_op jit(solution)/shard_map/ppermute | solution.py:67
  20.1 1.4 %own_products.1.refs_7_ = f32[2,512]{1,0:T(2,128)S(1)} custom-call(bf16[512,3840]{1,0:T(8,128)(2,1)S(1)} %get-tuple-element.43.m_ref.refs_0_, f32[48,3840]{1,0:T(8,128)S(1)} %get-tuple-element.52.v_ref.refs_3_.refs_2_, f32[48,512]{1,0:T(8,128)S(1)} %get-tuple-element.53.u_ref.refs_4_.refs_3_), custom_call_target="tpu_custom_call" | custom-call | flops 754974720 | bytes 4767744 | tf_op jit(solution)/shard_map/own_products/pallas_call | solution.py:419
  21.6 2.2 %collective-permute-done.8.refs_1_ = f32[192,128]{1,0:T(8,128)S(1)} collective-permute-done((f32[192,128]{1,0:T(8,128)S(1)}, f32[192,128]{1,0:T(8,128)S(1)}, u32[]{:S(2)}, u32[]{:S(2)}) %collective-permute-start.8) | collective-permute-done | bytes 98336 | tf_op jit(solution)/shard_map/ppermute | solution.py:67
  23.8 1.9 %fields_0.1 = (f32[16,256]{1,0:T(8,128)S(1)}, bf16[128,3840]{1,0:T(8,128)(2,1)S(1)}, f32[48,128]{1,0:T(8,128)S(1)}, f32[1,128]{1,0:T(1,128)S(1)}, f32[8,128]{1,0:T(8,128)S(1)}) custom-call(f32[192,128]{1,0:T(8,128)S(1)} %collective-permute-done.7.refs_0_, f32[192,128]{1,0:T(8,128)S(1)} %collective-permute-done.8.refs_1_, ...), custom_call_target="tpu_custom_call" | custom-call | flops 188743680 | bytes 1054736 | tf_op jit(solution)/shard_map/fields_0/pallas_call | solution.py:419
  25.7 2.5 %collective-permute-start.10 = (f32[16,256]{1,0:T(8,128)S(1)}, f32[16,256]{1,0:T(8,128)S(1)}, u32[]{:S(2)}, u32[]{:S(2)}) collective-permute-start(f32[16,256]{1,0:T(8,128)S(1)} %get-tuple-element.60.refs_7_.refs_10_), channel_id=1, source_target_pairs={{0,24},{1,25},{2,26},{3,27},{4,28},{5,29},{6,30},{7,31},{8,16},{9,... | collective-permute-start | bytes 49160 | tf_op jit(solution)/shard_map/ppermute | solution.py:60
  28.9 1.5 %collective-permute-done.10.refs_9_.refs_12_ = f32[16,256]{1,0:T(8,128)S(1)} collective-permute-done((f32[16,256]{1,0:T(8,128)S(1)}, f32[16,256]{1,0:T(8,128)S(1)}, u32[]{:S(2)}, u32[]{:S(2)}) %collective-permute-start.10) | collective-permute-done | bytes 16416 | tf_op jit(solution)/shard_map/ppermute | solution.py:60
  30.4 1.5 %collective-permute-done.9.refs_8_.refs_11_ = f32[16,256]{1,0:T(8,128)S(1)} collective-permute-done((f32[16,256]{1,0:T(8,128)S(1)}, f32[16,256]{1,0:T(8,128)S(1)}, u32[]{:S(2)}, u32[]{:S(2)}) %collective-permute-start.9) | collective-permute-done | bytes 16416 | tf_op jit(solution)/shard_map/ppermute | solution.py:59
  32.1 2.4 %sums_0.1 = (f32[2,3968]{1,0:T(2,128)S(1)}, f32[8,256]{1,0:T(8,128)S(1)}) custom-call(bf16[512,3840]{1,0:T(8,128)(2,1)S(1)} %get-tuple-element.43.m_ref.refs_0_, bf16[512,3840]{1,0:T(8,128)(2,1)S(1)} %get-tuple-element.44.refs_0_.refs_1_, f32[48,3840]{1,0:T(8,128)S(1)} %get-tuple-element.52.v_ref.refs_3_.refs_2_, ...), custom_call_target="tpu_custom_call" | custom-call | flops 754974720 | bytes 8781840 | tf_op jit(solution)/shard_map/sums_0/pallas_call | solution.py:419
  34.6 1.2 collective-permute-done.11
  36.2 0.9 collective-permute-start.13
  37.0 1.8 %collective-permute-start.14 = (f32[2,3968]{1,0:T(2,128)S(1)}, f32[2,3968]{1,0:T(2,128)S(1)}, u32[]{:S(2)}, u32[]{:S(2)}) collective-permute-start(f32[2,3968]{1,0:T(2,128)S(1)} %add.126), channel_id=1, source_target_pairs={{0,25},{1,24},{2,27},{3,26},{4,29},{5,28},{6,31},{7,30},{8,17},{9,... | collective-permute-start | bytes 95240 | tf_op jit(solution)/shard_map/ppermute | solution.py:32
  39.5 1.8 %collective-permute-done.14 = f32[2,3968]{1,0:T(2,128)S(1)} collective-permute-done((f32[2,3968]{1,0:T(2,128)S(1)}, f32[2,3968]{1,0:T(2,128)S(1)}, u32[]{:S(2)}, u32[]{:S(2)}) %collective-permute-start.14) | collective-permute-done | bytes 31776 | tf_op jit(solution)/shard_map/ppermute | solution.py:32
  41.9 1.3 %collective-permute-start.16 = (f32[2,3968]{1,0:T(2,128)S(1)}, f32[2,3968]{1,0:T(2,128)S(1)}, u32[]{:S(2)}, u32[]{:S(2)}) collective-permute-start(f32[2,3968]{1,0:T(2,128)S(1)} %add_add_fusion.7), channel_id=1, source_target_pairs={{0,5},{1,4},{2,7},{3,6},{4,1},{5,0},{6,3},{7,2},{8,13},{9,12},{10,... | collective-permute-start | bytes 95240 | tf_op jit(solution)/shard_map/ppermute | solution.py:32
  43.2 2.1 %collective-permute-start.17 = (f32[2,3968]{1,0:T(2,128)S(1)}, f32[2,3968]{1,0:T(2,128)S(1)}, u32[]{:S(2)}, u32[]{:S(2)}) collective-permute-start(f32[2,3968]{1,0:T(2,128)S(1)} %add_add_fusion.7), channel_id=1, source_target_pairs={{0,7},{1,6},{2,5},{3,4},{4,3},{5,2},{6,1},{7,0},{8,15},{9,14},{10,... | collective-permute-start | bytes 95240 | tf_op jit(solution)/shard_map/ppermute | solution.py:32
  45.3 0.9 collective-permute-done.16
  46.2 2.3 %collective-permute-done.17 = f32[2,3968]{1,0:T(2,128)S(1)} collective-permute-done((f32[2,3968]{1,0:T(2,128)S(1)}, f32[2,3968]{1,0:T(2,128)S(1)}, u32[]{:S(2)}, u32[]{:S(2)}) %collective-permute-start.17) | collective-permute-done | bytes 31776 | tf_op jit(solution)/shard_map/ppermute | solution.py:32
  48.5 2.2 %fields_1.1 = (f32[8,256]{1,0:T(8,128)S(1)}, f32[2,3840]{1,0:T(2,128)S(1)}, f32[2,640]{1,0:T(2,128)S(1)}) custom-call(bf16[512,3840]{1,0:T(8,128)(2,1)S(1)} %get-tuple-element.43.m_ref.refs_0_, bf16[128,3840]{1,0:T(8,128)(2,1)S(1)} %get-tuple-element.56.refs_1_, f32[48,3840]{1,0:T(8,128)S(1)} %get-tuple-element.52.v_ref.refs_3_.refs_2_, ...), custom_call_target="tpu_custom_call" | custom-call | flops 943718400 | bytes 5838336 | tf_op jit(solution)/shard_map/fields_1/pallas_call | solution.py:419
  50.6 1.1 collective-permute-start.18
  51.7 1.5 %collective-permute-start.19 = (f32[8,256]{1,0:T(8,128)S(1)}, f32[8,256]{1,0:T(8,128)S(1)}, u32[]{:S(2)}, u32[]{:S(2)}) collective-permute-start(f32[8,256]{1,0:T(8,128)S(1)} %get-tuple-element.65.refs_7_), channel_id=1, source_target_pairs={{0,24},{1,25},{2,26},{3,27},{4,28},{5,29},{6,30},{7,31},{8,16},{9,... | collective-permute-start | bytes 24584 | tf_op jit(solution)/shard_map/ppermute | solution.py:60
  53.2 1.1 collective-permute-done.18.refs_8_
  54.3 2.0 %collective-permute-done.19.refs_9_ = f32[8,256]{1,0:T(8,128)S(1)} collective-permute-done((f32[8,256]{1,0:T(8,128)S(1)}, f32[8,256]{1,0:T(8,128)S(1)}, u32[]{:S(2)}, u32[]{:S(2)}) %collective-permute-start.19) | collective-permute-done | bytes 8224 | tf_op jit(solution)/shard_map/ppermute | solution.py:60
  56.3 2.4 %sums_1.1 = (f32[2,3968]{1,0:T(2,128)S(1)}, f32[8,256]{1,0:T(8,128)S(1)}) custom-call(bf16[512,3840]{1,0:T(8,128)(2,1)S(1)} %get-tuple-element.43.m_ref.refs_0_, bf16[512,3840]{1,0:T(8,128)(2,1)S(1)} %get-tuple-element.44.refs_0_.refs_1_, f32[48,3840]{1,0:T(8,128)S(1)} %get-tuple-element.52.v_ref.refs_3_.refs_2_, ...), custom_call_target="tpu_custom_call" | custom-call | flops 754974720 | bytes 8842256 | tf_op jit(solution)/shard_map/sums_1/pallas_call | solution.py:419
  58.7 1.2 collective-permute-done.20
  59.9 0.8 collective-permute-start.21
  60.7 1.1 collective-permute-start.22
  61.8 1.2 collective-permute-start.23
  63.3 0.7 collective-permute-done.22
  64.1 1.9 %collective-permute-done.23 = f32[2,3968]{1,0:T(2,128)S(1)} collective-permute-done((f32[2,3968]{1,0:T(2,128)S(1)}, f32[2,3968]{1,0:T(2,128)S(1)}, u32[]{:S(2)}, u32[]{:S(2)}) %collective-permute-start.23) | collective-permute-done | bytes 31776 | tf_op jit(solution)/shard_map/ppermute | solution.py:32
  66.1 2.5 %collective-permute-start.25 = (f32[2,3968]{1,0:T(2,128)S(1)}, f32[2,3968]{1,0:T(2,128)S(1)}, u32[]{:S(2)}, u32[]{:S(2)}) collective-permute-start(f32[2,3968]{1,0:T(2,128)S(1)} %add_add_fusion.5), channel_id=1, source_target_pairs={{0,5},{1,4},{2,7},{3,6},{4,1},{5,0},{6,3},{7,2},{8,13},{9,12},{10,... | collective-permute-start | bytes 95240 | tf_op jit(solution)/shard_map/ppermute | solution.py:32
  68.6 1.4 %collective-permute-start.26 = (f32[2,3968]{1,0:T(2,128)S(1)}, f32[2,3968]{1,0:T(2,128)S(1)}, u32[]{:S(2)}, u32[]{:S(2)}) collective-permute-start(f32[2,3968]{1,0:T(2,128)S(1)} %add_add_fusion.5), channel_id=1, source_target_pairs={{0,7},{1,6},{2,5},{3,4},{4,3},{5,2},{6,1},{7,0},{8,15},{9,14},{10,... | collective-permute-start | bytes 95240 | tf_op jit(solution)/shard_map/ppermute | solution.py:32
  70.4 3.3 %collective-permute-done.26 = f32[2,3968]{1,0:T(2,128)S(1)} collective-permute-done((f32[2,3968]{1,0:T(2,128)S(1)}, f32[2,3968]{1,0:T(2,128)S(1)}, u32[]{:S(2)}, u32[]{:S(2)}) %collective-permute-start.26) | collective-permute-done | bytes 31776 | tf_op jit(solution)/shard_map/ppermute | solution.py:32
  73.7 2.2 %fields_2.1 = (f32[8,256]{1,0:T(8,128)S(1)}, f32[2,3840]{1,0:T(2,128)S(1)}, f32[2,640]{1,0:T(2,128)S(1)}) custom-call(bf16[512,3840]{1,0:T(8,128)(2,1)S(1)} %get-tuple-element.43.m_ref.refs_0_, bf16[128,3840]{1,0:T(8,128)(2,1)S(1)} %get-tuple-element.56.refs_1_, f32[48,3840]{1,0:T(8,128)S(1)} %get-tuple-element.52.v_ref.refs_3_.refs_2_, ...), custom_call_target="tpu_custom_call" | custom-call | flops 943718400 | bytes 5874176 | tf_op jit(solution)/shard_map/fields_2/pallas_call | solution.py:419
  76.0 1.5 %collective-permute-start.27 = (f32[8,256]{1,0:T(8,128)S(1)}, f32[8,256]{1,0:T(8,128)S(1)}, u32[]{:S(2)}, u32[]{:S(2)}) collective-permute-start(f32[8,256]{1,0:T(8,128)S(1)} %get-tuple-element.70.refs_7_), channel_id=1, source_target_pairs={{0,8},{1,9},{2,10},{3,11},{4,12},{5,13},{6,14},{7,15},{8,0},{9,1},... | collective-permute-start | bytes 24584 | tf_op jit(solution)/shard_map/ppermute | solution.py:59
  77.5 0.9 collective-permute-start.28
  78.4 1.3 %collective-permute-done.27.refs_8_ = f32[8,256]{1,0:T(8,128)S(1)} collective-permute-done((f32[8,256]{1,0:T(8,128)S(1)}, f32[8,256]{1,0:T(8,128)S(1)}, u32[]{:S(2)}, u32[]{:S(2)}) %collective-permute-start.27) | collective-permute-done | bytes 8224 | tf_op jit(solution)/shard_map/ppermute | solution.py:59
  79.6 2.4 %collective-permute-done.28.refs_9_ = f32[8,256]{1,0:T(8,128)S(1)} collective-permute-done((f32[8,256]{1,0:T(8,128)S(1)}, f32[8,256]{1,0:T(8,128)S(1)}, u32[]{:S(2)}, u32[]{:S(2)}) %collective-permute-start.28) | collective-permute-done | bytes 8224 | tf_op jit(solution)/shard_map/ppermute | solution.py:60
  82.0 2.4 %sums_2.1 = (f32[2,3968]{1,0:T(2,128)S(1)}, f32[8,256]{1,0:T(8,128)S(1)}) custom-call(bf16[512,3840]{1,0:T(8,128)(2,1)S(1)} %get-tuple-element.43.m_ref.refs_0_, bf16[512,3840]{1,0:T(8,128)(2,1)S(1)} %get-tuple-element.44.refs_0_.refs_1_, f32[48,3840]{1,0:T(8,128)S(1)} %get-tuple-element.52.v_ref.refs_3_.refs_2_, ...), custom_call_target="tpu_custom_call" | custom-call | flops 754974720 | bytes 8878096 | tf_op jit(solution)/shard_map/sums_2/pallas_call | solution.py:419
  84.5 1.2 collective-permute-done.29
  86.1 0.9 collective-permute-start.31
  87.0 1.8 %collective-permute-start.32 = (f32[2,3968]{1,0:T(2,128)S(1)}, f32[2,3968]{1,0:T(2,128)S(1)}, u32[]{:S(2)}, u32[]{:S(2)}) collective-permute-start(f32[2,3968]{1,0:T(2,128)S(1)} %add.140), channel_id=1, source_target_pairs={{0,25},{1,24},{2,27},{3,26},{4,29},{5,28},{6,31},{7,30},{8,17},{9,... | collective-permute-start | bytes 95240 | tf_op jit(solution)/shard_map/ppermute | solution.py:32
  89.4 1.8 %collective-permute-done.32 = f32[2,3968]{1,0:T(2,128)S(1)} collective-permute-done((f32[2,3968]{1,0:T(2,128)S(1)}, f32[2,3968]{1,0:T(2,128)S(1)}, u32[]{:S(2)}, u32[]{:S(2)}) %collective-permute-start.32) | collective-permute-done | bytes 31776 | tf_op jit(solution)/shard_map/ppermute | solution.py:32
  91.3 1.9 %collective-permute-start.34 = (f32[2,3968]{1,0:T(2,128)S(1)}, f32[2,3968]{1,0:T(2,128)S(1)}, u32[]{:S(2)}, u32[]{:S(2)}) collective-permute-start(f32[2,3968]{1,0:T(2,128)S(1)} %add_add_fusion.3), channel_id=1, source_target_pairs={{0,5},{1,4},{2,7},{3,6},{4,1},{5,0},{6,3},{7,2},{8,13},{9,12},{10,... | collective-permute-start | bytes 95240 | tf_op jit(solution)/shard_map/ppermute | solution.py:32
  93.2 2.0 %collective-permute-start.35 = (f32[2,3968]{1,0:T(2,128)S(1)}, f32[2,3968]{1,0:T(2,128)S(1)}, u32[]{:S(2)}, u32[]{:S(2)}) collective-permute-start(f32[2,3968]{1,0:T(2,128)S(1)} %add_add_fusion.3), channel_id=1, source_target_pairs={{0,7},{1,6},{2,5},{3,4},{4,3},{5,2},{6,1},{7,0},{8,15},{9,14},{10,... | collective-permute-start | bytes 95240 | tf_op jit(solution)/shard_map/ppermute | solution.py:32
  95.6 2.7 %collective-permute-done.35 = f32[2,3968]{1,0:T(2,128)S(1)} collective-permute-done((f32[2,3968]{1,0:T(2,128)S(1)}, f32[2,3968]{1,0:T(2,128)S(1)}, u32[]{:S(2)}, u32[]{:S(2)}) %collective-permute-start.35) | collective-permute-done | bytes 31776 | tf_op jit(solution)/shard_map/ppermute | solution.py:32
  98.4 2.2 %fields_3.1 = (f32[8,256]{1,0:T(8,128)S(1)}, f32[2,3840]{1,0:T(2,128)S(1)}, f32[2,640]{1,0:T(2,128)S(1)}) custom-call(bf16[512,3840]{1,0:T(8,128)(2,1)S(1)} %get-tuple-element.43.m_ref.refs_0_, bf16[128,3840]{1,0:T(8,128)(2,1)S(1)} %get-tuple-element.56.refs_1_, f32[48,3840]{1,0:T(8,128)S(1)} %get-tuple-element.52.v_ref.refs_3_.refs_2_, ...), custom_call_target="tpu_custom_call" | custom-call | flops 943718400 | bytes 5910016 | tf_op jit(solution)/shard_map/fields_3/pallas_call | solution.py:419
  100.6 1.1 collective-permute-start.36
  101.7 1.5 %collective-permute-start.37 = (f32[8,256]{1,0:T(8,128)S(1)}, f32[8,256]{1,0:T(8,128)S(1)}, u32[]{:S(2)}, u32[]{:S(2)}) collective-permute-start(f32[8,256]{1,0:T(8,128)S(1)} %get-tuple-element.74.refs_7_), channel_id=1, source_target_pairs={{0,24},{1,25},{2,26},{3,27},{4,28},{5,29},{6,30},{7,31},{8,16},{9,... | collective-permute-start | bytes 24584 | tf_op jit(solution)/shard_map/ppermute | solution.py:60
  103.2 1.1 collective-permute-done.36.refs_8_
  104.3 1.9 %collective-permute-done.37.refs_9_ = f32[8,256]{1,0:T(8,128)S(1)} collective-permute-done((f32[8,256]{1,0:T(8,128)S(1)}, f32[8,256]{1,0:T(8,128)S(1)}, u32[]{:S(2)}, u32[]{:S(2)}) %collective-permute-start.37) | collective-permute-done | bytes 8224 | tf_op jit(solution)/shard_map/ppermute | solution.py:60
  106.2 2.4 %sums_3.1 = (f32[2,3968]{1,0:T(2,128)S(1)}, f32[8,256]{1,0:T(8,128)S(1)}) custom-call(bf16[512,3840]{1,0:T(8,128)(2,1)S(1)} %get-tuple-element.43.m_ref.refs_0_, bf16[512,3840]{1,0:T(8,128)(2,1)S(1)} %get-tuple-element.44.refs_0_.refs_1_, f32[48,3840]{1,0:T(8,128)S(1)} %get-tuple-element.52.v_ref.refs_3_.refs_2_, ...), custom_call_target="tpu_custom_call" | custom-call | flops 754974720 | bytes 8913936 | tf_op jit(solution)/shard_map/sums_3/pallas_call | solution.py:419
  108.7 1.2 collective-permute-done.38
  109.9 0.8 collective-permute-start.39
  110.7 1.1 collective-permute-start.40
  111.8 1.2 collective-permute-start.41
  113.3 0.7 collective-permute-done.40
  114.1 1.9 %collective-permute-done.41 = f32[2,3968]{1,0:T(2,128)S(1)} collective-permute-done((f32[2,3968]{1,0:T(2,128)S(1)}, f32[2,3968]{1,0:T(2,128)S(1)}, u32[]{:S(2)}, u32[]{:S(2)}) %collective-permute-start.41) | collective-permute-done | bytes 31776 | tf_op jit(solution)/shard_map/ppermute | solution.py:32
  116.1 2.5 %collective-permute-start.43 = (f32[2,3968]{1,0:T(2,128)S(1)}, f32[2,3968]{1,0:T(2,128)S(1)}, u32[]{:S(2)}, u32[]{:S(2)}) collective-permute-start(f32[2,3968]{1,0:T(2,128)S(1)} %add_add_fusion.1), channel_id=1, source_target_pairs={{0,5},{1,4},{2,7},{3,6},{4,1},{5,0},{6,3},{7,2},{8,13},{9,12},{10,... | collective-permute-start | bytes 95240 | tf_op jit(solution)/shard_map/ppermute | solution.py:32
  118.6 1.4 %collective-permute-start.44 = (f32[2,3968]{1,0:T(2,128)S(1)}, f32[2,3968]{1,0:T(2,128)S(1)}, u32[]{:S(2)}, u32[]{:S(2)}) collective-permute-start(f32[2,3968]{1,0:T(2,128)S(1)} %add_add_fusion.1), channel_id=1, source_target_pairs={{0,7},{1,6},{2,5},{3,4},{4,3},{5,2},{6,1},{7,0},{8,15},{9,14},{10,... | collective-permute-start | bytes 95240 | tf_op jit(solution)/shard_map/ppermute | solution.py:32
  120.4 3.3 %collective-permute-done.44 = f32[2,3968]{1,0:T(2,128)S(1)} collective-permute-done((f32[2,3968]{1,0:T(2,128)S(1)}, f32[2,3968]{1,0:T(2,128)S(1)}, u32[]{:S(2)}, u32[]{:S(2)}) %collective-permute-start.44) | collective-permute-done | bytes 31776 | tf_op jit(solution)/shard_map/ppermute | solution.py:32
  (70 shorter events, 10.5 us)
Async XLA Ops:
  0.6 15.0 %copy-start = (f32[48,480]{1,0:T(8,128)S(1)}, f32[48,480]{1,0:T(8,128)}, u32[]{:S(2)}) copy-start(f32[48,480]{1,0:T(8,128)} %refs_4_.1) | copy-start | bytes 276484
  0.6 9.6 %collective-permute-start = (f32[48,480]{1,0:T(8,128)}, f32[48,480]{1,0:T(8,128)S(1)}, u32[]{:S(2)}, u32[]{:S(2)}) collective-permute-start(f32[48,480]{1,0:T(8,128)} %refs_4_.1), channel_id=1, source_target_pairs={{0,3},{1,2},{2,1},{3,0},{4,7},{5,6},{6,5},{7,4},{8,11},{9,10},{10,... | collective-permute-start | bytes 276488 | tf_op jit(solution)/shard_map/ppermute | solution.py:32
  3.2 7.1 %collective-permute-start.1 = (f32[48,480]{1,0:T(8,128)}, f32[48,480]{1,0:T(8,128)S(1)}, u32[]{:S(2)}, u32[]{:S(2)}) collective-permute-start(f32[48,480]{1,0:T(8,128)} %refs_4_.1), channel_id=1, source_target_pairs={{0,5},{1,4},{2,7},{3,6},{4,1},{5,0},{6,3},{7,2},{8,13},{9,12},{10,... | collective-permute-start | bytes 276488 | tf_op jit(solution)/shard_map/ppermute | solution.py:32
  6.0 7.6 %collective-permute-start.2 = (f32[48,480]{1,0:T(8,128)}, f32[48,480]{1,0:T(8,128)S(1)}, u32[]{:S(2)}, u32[]{:S(2)}) collective-permute-start(f32[48,480]{1,0:T(8,128)} %refs_4_.1), channel_id=1, source_target_pairs={{0,7},{1,6},{2,5},{3,4},{4,3},{5,2},{6,1},{7,0},{8,15},{9,14},{10,... | collective-permute-start | bytes 276488 | tf_op jit(solution)/shard_map/ppermute | solution.py:32
  6.0 8.7 %collective-permute-start.3 = (f32[48,480]{1,0:T(8,128)}, f32[48,480]{1,0:T(8,128)S(1)}, u32[]{:S(2)}, u32[]{:S(2)}) collective-permute-start(f32[48,480]{1,0:T(8,128)} %refs_4_.1), channel_id=1, source_target_pairs={{0,1},{1,0},{2,3},{3,2},{4,5},{5,4},{6,7},{7,6},{8,9},{9,8},{10,11... | collective-permute-start | bytes 276488 | tf_op jit(solution)/shard_map/ppermute | solution.py:32
  13.7 1.5 %collective-permute-start.4 = (f32[48,480]{1,0:T(8,128)S(1)}, f32[48,480]{1,0:T(8,128)S(1)}, u32[]{:S(2)}, u32[]{:S(2)}) collective-permute-start(f32[48,480]{1,0:T(8,128)S(1)} %collective-permute-done.refs_7_), channel_id=1, source_target_pairs={{0,1},{1,0},{2,3},{3,2},{4,5},{5,4},{6,7},{7,6},{8,9},{9,8},{10,11... | collective-permute-start | bytes 276488 | tf_op jit(solution)/shard_map/ppermute | solution.py:32
  14.2 1.3 %collective-permute-start.5 = (f32[48,480]{1,0:T(8,128)S(1)}, f32[48,480]{1,0:T(8,128)S(1)}, u32[]{:S(2)}, u32[]{:S(2)}) collective-permute-start(f32[48,480]{1,0:T(8,128)S(1)} %collective-permute-done.1.refs_9_), channel_id=1, source_target_pairs={{0,1},{1,0},{2,3},{3,2},{4,5},{5,4},{6,7},{7,6},{8,9},{9,8},{10,11... | collective-permute-start | bytes 276488 | tf_op jit(solution)/shard_map/ppermute | solution.py:32
  14.2 1.5 %collective-permute-start.6 = (f32[48,480]{1,0:T(8,128)S(1)}, f32[48,480]{1,0:T(8,128)S(1)}, u32[]{:S(2)}, u32[]{:S(2)}) collective-permute-start(f32[48,480]{1,0:T(8,128)S(1)} %collective-permute-done.2.refs_11_), channel_id=1, source_target_pairs={{0,1},{1,0},{2,3},{3,2},{4,5},{5,4},{6,7},{7,6},{8,9},{9,8},{10,11... | collective-permute-start | bytes 276488 | tf_op jit(solution)/shard_map/ppermute | solution.py:32
  17.4 4.2 %collective-permute-start.7 = (f32[192,128]{1,0:T(8,128)S(1)}, f32[192,128]{1,0:T(8,128)S(1)}, u32[]{:S(2)}, u32[]{:S(2)}) collective-permute-start(f32[192,128]{1,0:T(8,128)S(1)} %get-tuple-element.50), channel_id=1, source_target_pairs={{0,1},{1,0},{2,3},{3,2},{4,5},{5,4},{6,7},{7,6},{8,9},{9,8},{10,11... | collective-permute-start | bytes 294920 | tf_op jit(solution)/shard_map/ppermute | solution.py:32
  17.8 5.9 %collective-permute-start.8 = (f32[192,128]{1,0:T(8,128)S(1)}, f32[192,128]{1,0:T(8,128)S(1)}, u32[]{:S(2)}, u32[]{:S(2)}) collective-permute-start(f32[192,128]{1,0:T(8,128)S(1)} %get-tuple-element.51), channel_id=1, source_target_pairs={{0,7},{1,2},{2,1},{3,4},{4,3},{5,6},{6,5},{7,0},{8,15},{9,10},{10,... | collective-permute-start | bytes 294920 | tf_op jit(solution)/shard_map/ppermute | solution.py:67
  25.7 4.7 %collective-permute-start.10 = (f32[16,256]{1,0:T(8,128)S(1)}, f32[16,256]{1,0:T(8,128)S(1)}, u32[]{:S(2)}, u32[]{:S(2)}) collective-permute-start(f32[16,256]{1,0:T(8,128)S(1)} %get-tuple-element.60.refs_7_.refs_10_), channel_id=1, source_target_pairs={{0,24},{1,25},{2,26},{3,27},{4,28},{5,29},{6,30},{7,31},{8,16},{9,... | collective-permute-start | bytes 49160 | tf_op jit(solution)/shard_map/ppermute | solution.py:60
  28.2 3.7 %collective-permute-start.9 = (f32[16,256]{1,0:T(8,128)S(1)}, f32[16,256]{1,0:T(8,128)S(1)}, u32[]{:S(2)}, u32[]{:S(2)}) collective-permute-start(f32[16,256]{1,0:T(8,128)S(1)} %get-tuple-element.60.refs_7_.refs_10_), channel_id=1, source_target_pairs={{0,8},{1,9},{2,10},{3,11},{4,12},{5,13},{6,14},{7,15},{8,0},{9,1},... | collective-permute-start | bytes 49160 | tf_op jit(solution)/shard_map/ppermute | solution.py:59
  34.5 1.3 %collective-permute-start.11 = (f32[2,3968]{1,0:T(2,128)S(1)}, f32[2,3968]{1,0:T(2,128)S(1)}, u32[]{:S(2)}, u32[]{:S(2)}) collective-permute-start(f32[2,3968]{1,0:T(2,128)S(1)} %get-tuple-element.61), channel_id=1, source_target_pairs={{0,1},{1,0},{2,3},{3,2},{4,5},{5,4},{6,7},{7,6},{8,9},{9,8},{10,11... | collective-permute-start | bytes 95240 | tf_op jit(solution)/shard_map/ppermute | solution.py:32
  35.8 3.4 %collective-permute-start.12 = (f32[2,3968]{1,0:T(2,128)S(1)}, f32[2,3968]{1,0:T(2,128)S(1)}, u32[]{:S(2)}, u32[]{:S(2)}) collective-permute-start(f32[2,3968]{1,0:T(2,128)S(1)} %add.126), channel_id=1, source_target_pairs={{0,9},{1,8},{2,11},{3,10},{4,13},{5,12},{6,15},{7,14},{8,1},{9,0},... | collective-permute-start | bytes 95240 | tf_op jit(solution)/shard_map/ppermute | solution.py:32
  36.2 3.3 %collective-permute-start.13 = (f32[2,3968]{1,0:T(2,128)S(1)}, f32[2,3968]{1,0:T(2,128)S(1)}, u32[]{:S(2)}, u32[]{:S(2)}) collective-permute-start(f32[2,3968]{1,0:T(2,128)S(1)} %add.126), channel_id=1, source_target_pairs={{0,17},{1,16},{2,19},{3,18},{4,21},{5,20},{6,23},{7,22},{8,25},{9,... | collective-permute-start | bytes 95240 | tf_op jit(solution)/shard_map/ppermute | solution.py:32
  37.0 4.2 %collective-permute-start.14 = (f32[2,3968]{1,0:T(2,128)S(1)}, f32[2,3968]{1,0:T(2,128)S(1)}, u32[]{:S(2)}, u32[]{:S(2)}) collective-permute-start(f32[2,3968]{1,0:T(2,128)S(1)} %add.126), channel_id=1, source_target_pairs={{0,25},{1,24},{2,27},{3,26},{4,29},{5,28},{6,31},{7,30},{8,17},{9,... | collective-permute-start | bytes 95240 | tf_op jit(solution)/shard_map/ppermute | solution.py:32
  41.3 3.9 %collective-permute-start.15 = (f32[2,3968]{1,0:T(2,128)S(1)}, f32[2,3968]{1,0:T(2,128)S(1)}, u32[]{:S(2)}, u32[]{:S(2)}) collective-permute-start(f32[2,3968]{1,0:T(2,128)S(1)} %add_add_fusion.7), channel_id=1, source_target_pairs={{0,3},{1,2},{2,1},{3,0},{4,7},{5,6},{6,5},{7,4},{8,11},{9,10},{10,... | collective-permute-start | bytes 95240 | tf_op jit(solution)/shard_map/ppermute | solution.py:32
  41.9 4.2 %collective-permute-start.16 = (f32[2,3968]{1,0:T(2,128)S(1)}, f32[2,3968]{1,0:T(2,128)S(1)}, u32[]{:S(2)}, u32[]{:S(2)}) collective-permute-start(f32[2,3968]{1,0:T(2,128)S(1)} %add_add_fusion.7), channel_id=1, source_target_pairs={{0,5},{1,4},{2,7},{3,6},{4,1},{5,0},{6,3},{7,2},{8,13},{9,12},{10,... | collective-permute-start | bytes 95240 | tf_op jit(solution)/shard_map/ppermute | solution.py:32
  43.2 5.2 %collective-permute-start.17 = (f32[2,3968]{1,0:T(2,128)S(1)}, f32[2,3968]{1,0:T(2,128)S(1)}, u32[]{:S(2)}, u32[]{:S(2)}) collective-permute-start(f32[2,3968]{1,0:T(2,128)S(1)} %add_add_fusion.7), channel_id=1, source_target_pairs={{0,7},{1,6},{2,5},{3,4},{4,3},{5,2},{6,1},{7,0},{8,15},{9,14},{10,... | collective-permute-start | bytes 95240 | tf_op jit(solution)/shard_map/ppermute | solution.py:32
  50.6 3.7 %collective-permute-start.18 = (f32[8,256]{1,0:T(8,128)S(1)}, f32[8,256]{1,0:T(8,128)S(1)}, u32[]{:S(2)}, u32[]{:S(2)}) collective-permute-start(f32[8,256]{1,0:T(8,128)S(1)} %get-tuple-element.65.refs_7_), channel_id=1, source_target_pairs={{0,8},{1,9},{2,10},{3,11},{4,12},{5,13},{6,14},{7,15},{8,0},{9,1},... | collective-permute-start | bytes 24584 | tf_op jit(solution)/shard_map/ppermute | solution.py:59
  51.7 4.5 %collective-permute-start.19 = (f32[8,256]{1,0:T(8,128)S(1)}, f32[8,256]{1,0:T(8,128)S(1)}, u32[]{:S(2)}, u32[]{:S(2)}) collective-permute-start(f32[8,256]{1,0:T(8,128)S(1)} %get-tuple-element.65.refs_7_), channel_id=1, source_target_pairs={{0,24},{1,25},{2,26},{3,27},{4,28},{5,29},{6,30},{7,31},{8,16},{9,... | collective-permute-start | bytes 24584 | tf_op jit(solution)/shard_map/ppermute | solution.py:60
  58.6 1.3 %collective-permute-start.20 = (f32[2,3968]{1,0:T(2,128)S(1)}, f32[2,3968]{1,0:T(2,128)S(1)}, u32[]{:S(2)}, u32[]{:S(2)}) collective-permute-start(f32[2,3968]{1,0:T(2,128)S(1)} %get-tuple-element.66), channel_id=1, source_target_pairs={{0,1},{1,0},{2,3},{3,2},{4,5},{5,4},{6,7},{7,6},{8,9},{9,8},{10,11... | collective-permute-start | bytes 95240 | tf_op jit(solution)/shard_map/ppermute | solution.py:32
  59.9 3.4 %collective-permute-start.21 = (f32[2,3968]{1,0:T(2,128)S(1)}, f32[2,3968]{1,0:T(2,128)S(1)}, u32[]{:S(2)}, u32[]{:S(2)}) collective-permute-start(f32[2,3968]{1,0:T(2,128)S(1)} %add.133), channel_id=1, source_target_pairs={{0,9},{1,8},{2,11},{3,10},{4,13},{5,12},{6,15},{7,14},{8,1},{9,0},... | collective-permute-start | bytes 95240 | tf_op jit(solution)/shard_map/ppermute | solution.py:32
  60.7 3.3 %collective-permute-start.22 = (f32[2,3968]{1,0:T(2,128)S(1)}, f32[2,3968]{1,0:T(2,128)S(1)}, u32[]{:S(2)}, u32[]{:S(2)}) collective-permute-start(f32[2,3968]{1,0:T(2,128)S(1)} %add.133), channel_id=1, source_target_pairs={{0,17},{1,16},{2,19},{3,18},{4,21},{5,20},{6,23},{7,22},{8,25},{9,... | collective-permute-start | bytes 95240 | tf_op jit(solution)/shard_map/ppermute | solution.py:32
  61.8 4.2 %collective-permute-start.23 = (f32[2,3968]{1,0:T(2,128)S(1)}, f32[2,3968]{1,0:T(2,128)S(1)}, u32[]{:S(2)}, u32[]{:S(2)}) collective-permute-start(f32[2,3968]{1,0:T(2,128)S(1)} %add.133), channel_id=1, source_target_pairs={{0,25},{1,24},{2,27},{3,26},{4,29},{5,28},{6,31},{7,30},{8,17},{9,... | collective-permute-start | bytes 95240 | tf_op jit(solution)/shard_map/ppermute | solution.py:32
  66.0 3.9 %collective-permute-start.24 = (f32[2,3968]{1,0:T(2,128)S(1)}, f32[2,3968]{1,0:T(2,128)S(1)}, u32[]{:S(2)}, u32[]{:S(2)}) collective-permute-start(f32[2,3968]{1,0:T(2,128)S(1)} %add_add_fusion.5), channel_id=1, source_target_pairs={{0,3},{1,2},{2,1},{3,0},{4,7},{5,6},{6,5},{7,4},{8,11},{9,10},{10,... | collective-permute-start | bytes 95240 | tf_op jit(solution)/shard_map/ppermute | solution.py:32
  66.1 4.3 %collective-permute-start.25 = (f32[2,3968]{1,0:T(2,128)S(1)}, f32[2,3968]{1,0:T(2,128)S(1)}, u32[]{:S(2)}, u32[]{:S(2)}) collective-permute-start(f32[2,3968]{1,0:T(2,128)S(1)} %add_add_fusion.5), channel_id=1, source_target_pairs={{0,5},{1,4},{2,7},{3,6},{4,1},{5,0},{6,3},{7,2},{8,13},{9,12},{10,... | collective-permute-start | bytes 95240 | tf_op jit(solution)/shard_map/ppermute | solution.py:32
  68.6 5.1 %collective-permute-start.26 = (f32[2,3968]{1,0:T(2,128)S(1)}, f32[2,3968]{1,0:T(2,128)S(1)}, u32[]{:S(2)}, u32[]{:S(2)}) collective-permute-start(f32[2,3968]{1,0:T(2,128)S(1)} %add_add_fusion.5), channel_id=1, source_target_pairs={{0,7},{1,6},{2,5},{3,4},{4,3},{5,2},{6,1},{7,0},{8,15},{9,14},{10,... | collective-permute-start | bytes 95240 | tf_op jit(solution)/shard_map/ppermute | solution.py:32
  76.0 3.7 %collective-permute-start.27 = (f32[8,256]{1,0:T(8,128)S(1)}, f32[8,256]{1,0:T(8,128)S(1)}, u32[]{:S(2)}, u32[]{:S(2)}) collective-permute-start(f32[8,256]{1,0:T(8,128)S(1)} %get-tuple-element.70.refs_7_), channel_id=1, source_target_pairs={{0,8},{1,9},{2,10},{3,11},{4,12},{5,13},{6,14},{7,15},{8,0},{9,1},... | collective-permute-start | bytes 24584 | tf_op jit(solution)/shard_map/ppermute | solution.py:59
  77.5 4.5 %collective-permute-start.28 = (f32[8,256]{1,0:T(8,128)S(1)}, f32[8,256]{1,0:T(8,128)S(1)}, u32[]{:S(2)}, u32[]{:S(2)}) collective-permute-start(f32[8,256]{1,0:T(8,128)S(1)} %get-tuple-element.70.refs_7_), channel_id=1, source_target_pairs={{0,24},{1,25},{2,26},{3,27},{4,28},{5,29},{6,30},{7,31},{8,16},{9,... | collective-permute-start | bytes 24584 | tf_op jit(solution)/shard_map/ppermute | solution.py:60
  84.4 1.3 %collective-permute-start.29 = (f32[2,3968]{1,0:T(2,128)S(1)}, f32[2,3968]{1,0:T(2,128)S(1)}, u32[]{:S(2)}, u32[]{:S(2)}) collective-permute-start(f32[2,3968]{1,0:T(2,128)S(1)} %get-tuple-element.71), channel_id=1, source_target_pairs={{0,1},{1,0},{2,3},{3,2},{4,5},{5,4},{6,7},{7,6},{8,9},{9,8},{10,11... | collective-permute-start | bytes 95240 | tf_op jit(solution)/shard_map/ppermute | solution.py:32
  85.7 3.4 %collective-permute-start.30 = (f32[2,3968]{1,0:T(2,128)S(1)}, f32[2,3968]{1,0:T(2,128)S(1)}, u32[]{:S(2)}, u32[]{:S(2)}) collective-permute-start(f32[2,3968]{1,0:T(2,128)S(1)} %add.140), channel_id=1, source_target_pairs={{0,9},{1,8},{2,11},{3,10},{4,13},{5,12},{6,15},{7,14},{8,1},{9,0},... | collective-permute-start | bytes 95240 | tf_op jit(solution)/shard_map/ppermute | solution.py:32
  86.1 3.3 %collective-permute-start.31 = (f32[2,3968]{1,0:T(2,128)S(1)}, f32[2,3968]{1,0:T(2,128)S(1)}, u32[]{:S(2)}, u32[]{:S(2)}) collective-permute-start(f32[2,3968]{1,0:T(2,128)S(1)} %add.140), channel_id=1, source_target_pairs={{0,17},{1,16},{2,19},{3,18},{4,21},{5,20},{6,23},{7,22},{8,25},{9,... | collective-permute-start | bytes 95240 | tf_op jit(solution)/shard_map/ppermute | solution.py:32
  87.0 4.2 %collective-permute-start.32 = (f32[2,3968]{1,0:T(2,128)S(1)}, f32[2,3968]{1,0:T(2,128)S(1)}, u32[]{:S(2)}, u32[]{:S(2)}) collective-permute-start(f32[2,3968]{1,0:T(2,128)S(1)} %add.140), channel_id=1, source_target_pairs={{0,25},{1,24},{2,27},{3,26},{4,29},{5,28},{6,31},{7,30},{8,17},{9,... | collective-permute-start | bytes 95240 | tf_op jit(solution)/shard_map/ppermute | solution.py:32
  91.2 3.9 %collective-permute-start.33 = (f32[2,3968]{1,0:T(2,128)S(1)}, f32[2,3968]{1,0:T(2,128)S(1)}, u32[]{:S(2)}, u32[]{:S(2)}) collective-permute-start(f32[2,3968]{1,0:T(2,128)S(1)} %add_add_fusion.3), channel_id=1, source_target_pairs={{0,3},{1,2},{2,1},{3,0},{4,7},{5,6},{6,5},{7,4},{8,11},{9,10},{10,... | collective-permute-start | bytes 95240 | tf_op jit(solution)/shard_map/ppermute | solution.py:32
  91.3 4.3 %collective-permute-start.34 = (f32[2,3968]{1,0:T(2,128)S(1)}, f32[2,3968]{1,0:T(2,128)S(1)}, u32[]{:S(2)}, u32[]{:S(2)}) collective-permute-start(f32[2,3968]{1,0:T(2,128)S(1)} %add_add_fusion.3), channel_id=1, source_target_pairs={{0,5},{1,4},{2,7},{3,6},{4,1},{5,0},{6,3},{7,2},{8,13},{9,12},{10,... | collective-permute-start | bytes 95240 | tf_op jit(solution)/shard_map/ppermute | solution.py:32
  93.2 5.1 %collective-permute-start.35 = (f32[2,3968]{1,0:T(2,128)S(1)}, f32[2,3968]{1,0:T(2,128)S(1)}, u32[]{:S(2)}, u32[]{:S(2)}) collective-permute-start(f32[2,3968]{1,0:T(2,128)S(1)} %add_add_fusion.3), channel_id=1, source_target_pairs={{0,7},{1,6},{2,5},{3,4},{4,3},{5,2},{6,1},{7,0},{8,15},{9,14},{10,... | collective-permute-start | bytes 95240 | tf_op jit(solution)/shard_map/ppermute | solution.py:32
  100.6 3.7 %collective-permute-start.36 = (f32[8,256]{1,0:T(8,128)S(1)}, f32[8,256]{1,0:T(8,128)S(1)}, u32[]{:S(2)}, u32[]{:S(2)}) collective-permute-start(f32[8,256]{1,0:T(8,128)S(1)} %get-tuple-element.74.refs_7_), channel_id=1, source_target_pairs={{0,8},{1,9},{2,10},{3,11},{4,12},{5,13},{6,14},{7,15},{8,0},{9,1},... | collective-permute-start | bytes 24584 | tf_op jit(solution)/shard_map/ppermute | solution.py:59
  101.7 4.5 %collective-permute-start.37 = (f32[8,256]{1,0:T(8,128)S(1)}, f32[8,256]{1,0:T(8,128)S(1)}, u32[]{:S(2)}, u32[]{:S(2)}) collective-permute-start(f32[8,256]{1,0:T(8,128)S(1)} %get-tuple-element.74.refs_7_), channel_id=1, source_target_pairs={{0,24},{1,25},{2,26},{3,27},{4,28},{5,29},{6,30},{7,31},{8,16},{9,... | collective-permute-start | bytes 24584 | tf_op jit(solution)/shard_map/ppermute | solution.py:60
  106.2 18.7 %slice-start = ((f32[48,4,128]{2,1,0:T(4,128)}), f32[40,4,128]{2,1,0:T(4,128)S(1)}, s32[]{:S(2)}) async-start(f32[48,4,128]{2,1,0:T(4,128)} %refs_3_.1), calls=%async_computation | async-start | bytes 163840 | tf_op jit(solution)/shard_map/slice | solution.py:549
  108.6 1.3 %collective-permute-start.38 = (f32[2,3968]{1,0:T(2,128)S(1)}, f32[2,3968]{1,0:T(2,128)S(1)}, u32[]{:S(2)}, u32[]{:S(2)}) collective-permute-start(f32[2,3968]{1,0:T(2,128)S(1)} %get-tuple-element.76), channel_id=1, source_target_pairs={{0,1},{1,0},{2,3},{3,2},{4,5},{5,4},{6,7},{7,6},{8,9},{9,8},{10,11... | collective-permute-start | bytes 95240 | tf_op jit(solution)/shard_map/ppermute | solution.py:32
  109.9 3.4 %collective-permute-start.39 = (f32[2,3968]{1,0:T(2,128)S(1)}, f32[2,3968]{1,0:T(2,128)S(1)}, u32[]{:S(2)}, u32[]{:S(2)}) collective-permute-start(f32[2,3968]{1,0:T(2,128)S(1)} %add.147), channel_id=1, source_target_pairs={{0,9},{1,8},{2,11},{3,10},{4,13},{5,12},{6,15},{7,14},{8,1},{9,0},... | collective-permute-start | bytes 95240 | tf_op jit(solution)/shard_map/ppermute | solution.py:32
  110.7 3.3 %collective-permute-start.40 = (f32[2,3968]{1,0:T(2,128)S(1)}, f32[2,3968]{1,0:T(2,128)S(1)}, u32[]{:S(2)}, u32[]{:S(2)}) collective-permute-start(f32[2,3968]{1,0:T(2,128)S(1)} %add.147), channel_id=1, source_target_pairs={{0,17},{1,16},{2,19},{3,18},{4,21},{5,20},{6,23},{7,22},{8,25},{9,... | collective-permute-start | bytes 95240 | tf_op jit(solution)/shard_map/ppermute | solution.py:32
  111.8 4.2 %collective-permute-start.41 = (f32[2,3968]{1,0:T(2,128)S(1)}, f32[2,3968]{1,0:T(2,128)S(1)}, u32[]{:S(2)}, u32[]{:S(2)}) collective-permute-start(f32[2,3968]{1,0:T(2,128)S(1)} %add.147), channel_id=1, source_target_pairs={{0,25},{1,24},{2,27},{3,26},{4,29},{5,28},{6,31},{7,30},{8,17},{9,... | collective-permute-start | bytes 95240 | tf_op jit(solution)/shard_map/ppermute | solution.py:32
  116.0 4.0 %collective-permute-start.42 = (f32[2,3968]{1,0:T(2,128)S(1)}, f32[2,3968]{1,0:T(2,128)S(1)}, u32[]{:S(2)}, u32[]{:S(2)}) collective-permute-start(f32[2,3968]{1,0:T(2,128)S(1)} %add_add_fusion.1), channel_id=1, source_target_pairs={{0,3},{1,2},{2,1},{3,0},{4,7},{5,6},{6,5},{7,4},{8,11},{9,10},{10,... | collective-permute-start | bytes 95240 | tf_op jit(solution)/shard_map/ppermute | solution.py:32
  116.1 4.3 %collective-permute-start.43 = (f32[2,3968]{1,0:T(2,128)S(1)}, f32[2,3968]{1,0:T(2,128)S(1)}, u32[]{:S(2)}, u32[]{:S(2)}) collective-permute-start(f32[2,3968]{1,0:T(2,128)S(1)} %add_add_fusion.1), channel_id=1, source_target_pairs={{0,5},{1,4},{2,7},{3,6},{4,1},{5,0},{6,3},{7,2},{8,13},{9,12},{10,... | collective-permute-start | bytes 95240 | tf_op jit(solution)/shard_map/ppermute | solution.py:32
  118.6 5.1 %collective-permute-start.44 = (f32[2,3968]{1,0:T(2,128)S(1)}, f32[2,3968]{1,0:T(2,128)S(1)}, u32[]{:S(2)}, u32[]{:S(2)}) collective-permute-start(f32[2,3968]{1,0:T(2,128)S(1)} %add_add_fusion.1), channel_id=1, source_target_pairs={{0,7},{1,6},{2,5},{3,4},{4,3},{5,2},{6,1},{7,0},{8,15},{9,14},{10,... | collective-permute-start | bytes 95240 | tf_op jit(solution)/shard_map/ppermute | solution.py:32

commit v6 on v5

--- a/solution.py
+++ b/solution.py
@@ -141,9 +141,9 @@
 
 
 def own_flags_kernel(reach, *refs):
-    words_hbm, coast_hbm, x_hbm, maps_hbm = refs[:4]
-    m_ref, a_ref, u_ref, row_ref, west_ref, east_ref = refs[4:10]
-    words_ref, coast_ref, x_ref, maps_ref, spread_ref, bit_ref, sems = refs[10:]
+    words_hbm, coast_hbm, x_hbm, maps_hbm, series_hbm, place_ref = refs[:6]
+    m_ref, a_ref, u_ref, row_ref, near_ref, far_ref, maps_out, series_out = refs[6:14]
+    words_ref, coast_ref, x_ref, maps_ref, series_ref, spread_ref, bit_ref, sems = refs[14:]
     rows = coast_ref.shape[0]
     loads = [
         pltpu.make_async_copy(words_hbm, words_ref, sems.at[0]),
@@ -153,6 +153,11 @@
         at = pl.ds(r * LANES, LANES)
         loads.append(pltpu.make_async_copy(x_hbm.at[at], x_ref.at[at], sems.at[2 + r]))
     loads.append(pltpu.make_async_copy(maps_hbm, maps_ref, sems.at[2 + rows]))
+    loads.append(pltpu.make_async_copy(series_hbm, series_ref, sems.at[3 + rows]))
+    stores = [
+        pltpu.make_async_copy(maps_ref, maps_out, sems.at[4 + rows]),
+        pltpu.make_async_copy(series_ref, series_out, sems.at[5 + rows]),
+    ]
     for load in loads:
         load.start()
     fill_spread(spread_ref, bit_ref)
@@ -173,7 +178,9 @@
             at = slice(g * days, (g + 1) * days)
             m_ref[cell, at] = given
             a_ref[cell, at] = x_ref[cell, at] * given * ocean
-    loads[2 + rows].wait()
+    for load, store in zip(loads[-2:], stores, strict=True):
+        load.wait()
+        store.start()
     modes = maps_ref.shape[0]
     pieces = []
     for r in range(rows):
@@ -183,13 +190,20 @@
         row_ref[:, at] = coast_own[r : r + 1]
         pieces.append(jnp.concatenate([u, jnp.broadcast_to(coast_own[r : r + 1], (8, LANES))], axis=0))
     base = modes + 8
-    west_ref[:base], east_ref[:base] = edges(pieces, reach)
+    odd = place_ref[3] % 2 == 1
+    west, east = edges(pieces, reach)
+    near_ref[:base] = jnp.where(odd, west, east)
+    far_ref[:base] = jnp.where(odd, east, west)
     for g in range(words_ref.shape[1] // LANES):
         for r in range(rows):
             at = slice(base + reach * (rows * g + r), base + reach * (rows * g + r + 1))
             group = slice(g * LANES, (g + 1) * LANES)
-            west_ref[at] = words_ref[r * LANES : r * LANES + reach, group].astype(F32)
-            east_ref[at] = words_ref[(r + 1) * LANES - reach : (r + 1) * LANES, group].astype(F32)
+            west = words_ref[r * LANES : r * LANES + reach, group].astype(F32)
+            east = words_ref[(r + 1) * LANES - reach : (r + 1) * LANES, group].astype(F32)
+            near_ref[at] = jnp.where(odd, west, east)
+            far_ref[at] = jnp.where(odd, east, west)
+    for store in stores:
+        store.wait()
 
 
 def edges(pieces, reach):
@@ -207,8 +221,8 @@
 
 
 def given_kernel(rows, reach, *refs):
-    a_ref, place_ref, ew_ref, ee_ref = refs[:4]
-    pieces = [ref[...] for ref in refs[4:-4]]
+    a_ref, place_ref = refs[:2]
+    pieces = [ref[...] for ref in refs[2:-4]]
     v_ref, xv_ref, near_ref, far_ref = refs[-4:]
     here = place_ref[3]
     bit = 1
@@ -225,11 +239,8 @@
     xv_ref[...] = xv
     west, east = edges([xv[:, r * LANES : (r + 1) * LANES] for r in range(rows)], reach)
     odd = here % 2 == 1
-    tall = ew_ref.shape[0]
-    near_ref[:tall] = jnp.where(odd, ew_ref[...], ee_ref[...])
-    near_ref[tall:] = jnp.where(odd, west, east)
-    far_ref[:tall] = jnp.where(odd, ee_ref[...], ew_ref[...])
-    far_ref[tall:] = jnp.where(odd, east, west)
+    near_ref[...] = jnp.where(odd, west, east)
+    far_ref[...] = jnp.where(odd, east, west)
 
 
 def masked_products(vs, u, low, chunk, m_ref):
@@ -248,8 +259,31 @@
     )
 
 
-def own_products_kernel(chunk, m_ref, v_ref, u_ref, base_ref):
-    base_ref[...] = masked_products(v_ref, u_ref[...], 0, chunk, m_ref)
+def first_products_kernel(chunk, *refs):
+    near_ref, far_ref, place_ref, m_ref, v_ref, u_own_ref, row_own_ref = refs[:7]
+    base_ref, mh_ref, u_ref, row_ref, spread_ref, bit_ref = refs[7:]
+    fill_spread(spread_ref, bit_ref)
+    odd = place_ref[3] % 2 == 1
+    west = jnp.where(odd, near_ref[...], far_ref[...])
+    east = jnp.where(odd, far_ref[...], near_ref[...])
+    modes, own = u_own_ref.shape
+    base = modes + 8
+    lane = lane_ids((base, LANES))
+    fields = jnp.where(lane < LANES // 2, west[:base], east[:base])
+    u_own, u_halo, row_halo = (u_own_ref[...], fields[:modes], fields[modes : modes + 1])
+    u_ref[:, :own] = u_own
+    u_ref[:, own:] = u_halo
+    row_ref[:, :own] = row_own_ref[...]
+    row_ref[:, own:] = row_halo
+    coast = as_column(row_halo).astype(jnp.int32)
+    days = spread_ref.shape[1]
+    half = LANES // 2
+    for g in range(mh_ref.shape[1] // days):
+        at = slice(base + half * g, base + half * (g + 1))
+        words = jnp.concatenate([west[at], east[at]], axis=0).astype(jnp.int32) * coast
+        mh_ref[:, g * days : (g + 1) * days] = unpack_words(words, spread_ref, bit_ref)
+    base_ref[:, :own] = masked_products(v_ref, u_own, 0, chunk, m_ref)
+    base_ref[:, own:] = masked_products(v_ref, u_halo, 0, chunk, mh_ref)
 
 
 def new_fields(pair, u_pair, coast, proj):
@@ -259,60 +293,30 @@
     return coast * (u_pair + jnp.concatenate([add0, add1], axis=0))
 
 
-def first_fields_kernel(rows, reach, chunk, *refs):
-    near_ref, far_ref, place_ref, v_ref, u_ref, row_ref, xv_ref, base_ref = refs[:8]
-    w_ref, m_ref, uh_ref, rowh_ref, xh_ref, spread_ref, bit_ref = refs[8:]
-    fill_spread(spread_ref, bit_ref)
+def first_fields_kernel(rows, reach, near_ref, far_ref, place_ref, v_ref, u_ref, row_ref, xv_ref, base_ref, w_ref, xh_ref):
     odd = place_ref[3] % 2 == 1
     west = jnp.where(odd, near_ref[...], far_ref[...])
     east = jnp.where(odd, far_ref[...], near_ref[...])
-    modes = v_ref.shape[0]
-    base = modes + 8
-    lane = lane_ids((base, LANES))
-    fields = jnp.where(lane < LANES // 2, west[:base], east[:base])
-    u_halo = fields[:modes]
-    uh_ref[...] = u_halo
-    rowh_ref[...] = fields[modes : modes + 1]
-    xh = jnp.where(lane[:PAIRS] < LANES // 2, west[-PAIRS:], east[-PAIRS:])
+    xh = jnp.where(lane_ids((PAIRS, LANES)) < LANES // 2, west, east)
     xh_ref[...] = xh
-    coast = as_column(fields[modes : modes + 1]).astype(jnp.int32)
-    days = spread_ref.shape[1]
-    half = LANES // 2
-    for g in range(m_ref.shape[1] // days):
-        at = slice(base + half * g, base + half * (g + 1))
-        words = jnp.concatenate([west[at], east[at]], axis=0).astype(jnp.int32) * coast
-        m_ref[:, g * days : (g + 1) * days] = unpack_words(words, spread_ref, bit_ref)
-    halo = xh[:2] - masked_products(v_ref, u_halo, 0, chunk, m_ref)
-    proj = jnp.concatenate([xv_ref[:2] - base_ref[...], halo], axis=1)
-    u_pair = jnp.concatenate([u_ref[:2], u_halo[:2]], axis=1)
-    coast = jnp.concatenate([row_ref[...], fields[modes : modes + 1]], axis=1)
+    proj = jnp.concatenate([xv_ref[:2], xh[:2]], axis=1) - base_ref[...]
+    coast = row_ref[...]
     count = 2 * rows
-    w_ref[:count] = to_block(new_fields(v_ref[:2], u_pair, coast, proj), rows, reach)
+    w_ref[:count] = to_block(new_fields(v_ref[:2], u_ref[:2], coast, proj), rows, reach)
     w_ref[count:] = to_block(jnp.concatenate([coast, coast], axis=0), rows, reach)
 
 
 def fields_kernel(step, rows, reach, total, chunk, *refs):
-    m_ref, mh_ref, v_ref, u_ref, uh_ref, row_ref, rowh_ref, xv_ref, xh_ref = refs[:9]
-    older = refs[9 : 9 + 2 * (step - 1)]
-    sum_ref, block_ref, w_ref, vn_ref, un_ref, vs, us = refs[9 + len(older) :]
+    m_ref, mh_ref, v_ref, u_ref, row_ref, xv_ref, xh_ref, sum_ref, block_ref, w_ref, vs, us = refs
     low = 2 * step
     own = rows * LANES
     vs[...] = v_ref[...]
-    us[:, :own] = u_ref[...]
-    us[:, own:] = uh_ref[...]
-    for q in range(step - 1):
-        vs[2 * q : 2 * q + 2] = older[2 * q][...]
-        us[2 * q : 2 * q + 2] = older[2 * q + 1][...]
-    vn, un = new_pair(rows, reach, total, sum_ref, block_ref)
-    vn_ref[...] = vn
-    un_ref[...] = un
-    vs[low - 2 : low] = vn
-    us[low - 2 : low] = un
+    us[...] = u_ref[...]
+    vs[low - 2 : low], us[low - 2 : low] = new_pair(rows, reach, total, sum_ref, block_ref)
     mid = xv_ref[low : low + 2] - masked_products(vs, us[:, :own], low, chunk, m_ref)
     edge = xh_ref[low : low + 2] - masked_products(vs, us[:, own:], low, chunk, mh_ref)
     proj = jnp.concatenate([mid, edge], axis=1)
-    coast = jnp.concatenate([row_ref[...], rowh_ref[...]], axis=1)
-    w_ref[...] = to_block(new_fields(vs[low : low + 2], us[low : low + 2], coast, proj), rows, reach)
+    w_ref[...] = to_block(new_fields(vs[low : low + 2], us[low : low + 2], row_ref[...], proj), rows, reach)
 
 
 def new_pair(rows, reach, total, sum_ref, block_ref):
@@ -337,16 +341,10 @@
     if step:
         cw_ref, ca_ref, cb_ref = refs[:3]
         refs = refs[3:]
-    older = refs[: 2 * step]
-    sum_ref, block_ref, vs, us = refs[2 * step :]
+    sum_ref, block_ref = refs
     days = v_ref.shape[1]
     low = 2 * step
     own = rows * LANES
-    vs[...] = v_ref[...]
-    us[...] = u_ref[...]
-    for q in range(step):
-        vs[2 * q : 2 * q + 2] = older[2 * q][...]
-        us[2 * q : 2 * q + 2] = older[2 * q + 1][:, :own]
     count = 2 * rows
     row0, nlat, odd = (place_ref[0], place_ref[1], place_ref[2])
 
@@ -377,7 +375,7 @@
     cells = lambda z: jnp.concatenate([z[2 * r : 2 * r + 2, :LANES] for r in range(rows)], axis=1)
     fresh = cells(block)
     weighted = cells(block * cosl_ref[...])
-    u = us[...]
+    u = u_ref[:, :own]
     modes = u.shape[0]
     high, lower = split(jnp.concatenate([u * weighted[0:1], u * weighted[1:2]], axis=0))
     left = jnp.concatenate([high, lower], axis=0)
@@ -392,7 +390,7 @@
         at = slice(first, first + chunk)
         masked = jnp.dot(left, m_ref[:, at], preferred_element_type=F32)
         given = jnp.dot(left_a, a_ref[:, at], preferred_element_type=F32)
-        v = vs[:, at]
+        v = v_ref[:, at]
         for j in range(2):
             part = masked[j * modes : (j + 1) * modes] + masked[(2 + j) * modes : (3 + j) * modes]
             sum_ref[j : j + 1, at] = (
@@ -404,24 +402,40 @@
             )
 
 
-def last_kernel(rows, reach, total, sum_ref, block_ref, vn_ref, un_ref):
+def last_kernel(rows, reach, total, *refs):
+    v_ref, u_ref, sum_ref, block_ref, place_ref = refs[:5]
+    maps_out, series_out, maps_new, series_new, sems = refs[7:]
+    share = series_new.shape[1]
+    stores = [
+        pltpu.make_async_copy(maps_new, maps_out.at[pl.ds(0, PAIRS)], sems.at[0]),
+        pltpu.make_async_copy(series_new, series_out.at[pl.ds(0, PAIRS)], sems.at[1]),
+    ]
     vn, un = new_pair(rows, reach, total, sum_ref, block_ref)
-    vn_ref[...] = vn
-    un_ref[...] = un
-
-
-def call(kernel, name, outs, scratch, args, smem=(), mib=24, flops=0, loads=0):
+    u = jnp.concatenate([u_ref[: PAIRS - 2], un], axis=0)
+    for r in range(rows):
+        maps_new[:, r, :] = u[:, r * LANES : (r + 1) * LANES]
+    stores[0].start()
+    v = jnp.concatenate([v_ref[: PAIRS - 2], vn], axis=0)
+    mine = v[:, :share]
+    for i in range(1, v.shape[1] // share):
+        mine = jnp.where(place_ref[3] == i, v[:, i * share : (i + 1) * share], mine)
+    series_new[...] = mine
+    stores[1].start()
+    for store in stores:
+        store.wait()
+
+
+def call(kernel, name, outs, scratch, args, smem=(), mib=24, flops=0, copies=0, in_hbm=(), out_hbm=(), aliases={}):
     moved = sum(z.size * z.dtype.itemsize for z in args)
-    place = VMEM
-    if loads:
-        place = pl.BlockSpec(memory_space=pl.ANY)
-        args = [pltpu.with_memory_space_constraint(z, pltpu.HBM) for z in args]
+    hbm = pl.BlockSpec(memory_space=pl.ANY)
+    args = [pltpu.with_memory_space_constraint(z, pltpu.HBM) if i in in_hbm else z for i, z in enumerate(args)]
     return pl.pallas_call(
         kernel,
         out_shape=[jax.ShapeDtypeStruct(s, t) for s, t in outs],
-        in_specs=[SMEM if i in smem else place for i in range(len(args))],
-        out_specs=[VMEM for _ in outs],
-        scratch_shapes=[pltpu.VMEM(s, t) for s, t in scratch] + ([pltpu.SemaphoreType.DMA((loads,))] if loads else []),
+        in_specs=[SMEM if i in smem else hbm if i in in_hbm else VMEM for i in range(len(args))],
+        out_specs=[hbm if i in out_hbm else VMEM for i in range(len(outs))],
+        scratch_shapes=[pltpu.VMEM(s, t) for s, t in scratch] + ([pltpu.SemaphoreType.DMA((copies,))] if copies else []),
+        input_output_aliases=aliases,
         compiler_params=pltpu.CompilerParams(vmem_limit_bytes=mib * 2**20),
         cost_estimate=pl.CostEstimate(flops=flops, bytes_accessed=moved, transcendentals=0),
         name=name,
@@ -454,14 +468,22 @@
     words_per = words // LANES
     flags_scratch = [((2 * LANES, days // words_per), BF16), ((1, days // words_per), jnp.int32)]
     edge = ((modes + 8 + rows * reach * words_per, LANES), F32)
-    m, a, u, row, edge_west, edge_east = call(
+    inputs = [missing_date_bitmask.reshape(own, words), ocean_binary_mask, sea_heat_deviations.reshape(own, days)]
+    inputs += [mode_maps, mode_series]
+    place, klon, cosl = lax.optimization_barrier((place, klon, cosl))
+    m, a, u, row, near, far, maps_out, series_out = call(
         functools.partial(own_flags_kernel, reach),
         "own_flags",
-        [((own, days), BF16), ((own, days), BF16), ((modes, own), F32), ((1, own), F32), edge, edge],
-        [((own, words), jnp.int32), ((rows, LANES), jnp.int32), ((own, days), BF16), (mode_maps.shape, F32), *flags_scratch],
-        [missing_date_bitmask.reshape(own, words), ocean_binary_mask, sea_heat_deviations.reshape(own, days), mode_maps],
+        [((own, days), BF16), ((own, days), BF16), ((modes, own), F32), ((1, own), F32), edge, edge]
+        + [(mode_maps.shape, F32), (mode_series.shape, F32)],
+        [((own, words), jnp.int32), ((rows, LANES), jnp.int32), ((own, days), BF16)]
+        + [(mode_maps.shape, F32), (mode_series.shape, F32), *flags_scratch],
+        [*inputs, place],
+        smem=(5,),
+        in_hbm=range(5),
+        out_hbm=(6, 7),
+        copies=6 + rows,
         flops=4 * LANES * own * days,
-        loads=3 + rows,
     )
     if lax.axis_size("lon") == 8:
         pieces = [swap(mode_series, 0, b | 1) for b in (2, 4, 6)]
@@ -470,84 +492,73 @@
         pieces = [mode_series, swap(mode_series, 0, 1), *pieces]
     else:
         pieces = [lax.all_gather(mode_series, "lon", axis=1, tiled=True)]
-    edge = ((edge[0][0] + PAIRS, LANES), F32)
-    v, xv, near, far = call(
+    near, far = lon_partners(near, far)
+    v, xv, near_xv, far_xv = call(
         functools.partial(given_kernel, rows, reach),
         "given",
-        [((modes, days), F32), ((PAIRS, own), F32), edge, edge],
+        [((modes, days), F32), ((PAIRS, own), F32), ((PAIRS, LANES), F32), ((PAIRS, LANES), F32)],
         [],
-        [a, place, edge_west, edge_east, *pieces],
+        [a, place, *pieces],
         smem=(1,),
         flops=4 * PAIRS * own * days,
     )
-    near, far = lon_partners(near, far)
-    (base,) = call(
-        functools.partial(own_products_kernel, chunk),
-        "own_products",
-        [((2, own), F32)],
-        [],
-        [m, v, u],
-        flops=8 * modes * own * days,
+    near_xv, far_xv = lon_partners(near_xv, far_xv)
+    base, m_halo, u, row = call(
+        functools.partial(first_products_kernel, chunk),
+        "first_products",
+        [((2, cells), F32), ((sides, days), BF16), ((modes, cells), F32), ((1, cells), F32)],
+        flags_scratch,
+        [near, far, place, m, v, u, row],
+        smem=(2,),
+        flops=8 * modes * cells * days,
     )
 
     count = 2 * rows
-    news = []
     summed = block = None
     coasts = ()
     for step in range(STEPS):
         if step == 0:
-            fresh, m_halo, u_halo, row_halo, xv_halo = call(
-                functools.partial(first_fields_kernel, rows, reach, chunk),
+            fresh, xv_halo = call(
+                functools.partial(first_fields_kernel, rows, reach),
                 "fields_0",
-                [
-                    ((2 * count, 2 * LANES), F32),
-                    ((sides, days), BF16),
-                    ((modes, sides), F32),
-                    ((1, sides), F32),
-                    ((PAIRS, sides), F32),
-                ],
-                flags_scratch,
-                [near, far, place, v, u, row, xv, base],
+                [((2 * count, 2 * LANES), F32), ((PAIRS, sides), F32)],
+                [],
+                [near_xv, far_xv, place, v, u, row, xv, base],
                 smem=(2,),
-                flops=8 * modes * sides * days,
             )
         else:
-            fresh, *new = call(
+            fresh, v, u = call(
                 functools.partial(fields_kernel, step, rows, reach, total, chunk),
                 f"fields_{step}",
-                [((count, 2 * LANES), F32), ((2, days), F32), ((2, cells), F32)],
-                [((modes, days), F32), ((modes, cells), F32)],
-                [m, m_halo, v, u, u_halo, row, row_halo, xv, xv_halo, *news, summed, block],
+                [((count, 2 * LANES), F32), ((modes, days), F32), ((modes, cells), F32)],
+                [],
+                [m, m_halo, v, u, row, xv, xv_halo, summed, block],
                 flops=8 * modes * cells * days,
             )
-            news += new
         got_a, got_b = lat_partners(fresh)
         partial_sums, block = call(
             functools.partial(sums_kernel, step, rows, chunk),
             f"sums_{step}",
             [((2, days + LANES), F32), ((count, 2 * LANES), F32)],
-            [((modes, days), F32), ((modes, own), F32)],
-            [m, a, v, u, place, klon, cosl, fresh, got_a, got_b, *coasts, *news],
+            [],
+            [m, a, v, u, place, klon, cosl, fresh, got_a, got_b, *coasts],
             smem=(4,),
             flops=8 * modes * own * days,
         )
         if step == 0:
             coasts = (fresh, got_a, got_b)
         summed = sum_all(partial_sums)
-    news += call(
+    return call(
         functools.partial(last_kernel, rows, reach, total),
         "last",
-        [((2, days), F32), ((2, cells), F32)],
-        [],
-        [summed, block],
-    )
-    share = mode_series.shape[1]
-    new_v = jnp.concatenate(news[0::2], axis=0)
-    new_u = jnp.concatenate([z[:, :own] for z in news[1::2]], axis=0).reshape(PAIRS, rows, columns)
-    own_days = lax.dynamic_slice_in_dim(new_v, lax.axis_index("lon") * share, share, 1)
-    return (
-        jnp.concatenate([new_u, mode_maps[PAIRS:]], axis=0),
-        jnp.concatenate([own_days, mode_series[PAIRS:]], axis=0),
+        [(mode_maps.shape, F32), (mode_series.shape, F32)],
+        [((PAIRS, rows, columns), F32), ((PAIRS, mode_series.shape[1]), F32)],
+        [v, u, summed, block, place, maps_out, series_out],
+        smem=(4,),
+        in_hbm=(5, 6),
+        out_hbm=(0, 1),
+        copies=2,
+        aliases={5: 0, 6: 1},
     )
 
 

time: 126 us -> 121 us (0.960)
  waiting for transfers between devices: 48.7 us -> 40.1 us
  Pallas kernels: 26 us -> 29.3 us
  starting transfers between devices: 47.8 us -> 49.4 us
  other arithmetic: 1.91 us -> 0.44 us
    ppermute x36 -> x37, waiting for transfers between devices: 33.7 us -> 28.6 us  [swap(): lax.ppermute(x, ('lat', 'lon'), pairing(lambda i: i ^ lat_bits, lambda j:...]
    pallas_call x12, Pallas kernels: 26 us -> 29.3 us  [call(): pl.pallas_call(kernel, out_shape=[jax.ShapeDtypeStruct(s, t) for s, t in...]
    ppermute x4, waiting for transfers between devices: 4.99 us -> 3.25 us  [lat_partners(): got_a = lax.ppermute(x, ('lat', 'lon'), pairing(lambda i: i ^ 1, same))]
    ppermute x1 -> x2, waiting for transfers between devices: 2.15 us -> 0.67 us  [lon_partners(): lax.ppermute(far, ('lat', 'lon'), pairing(same, lambda j: (j + 1 if j % 2...]
    concatenate x3 -> x0, other arithmetic: 1.4 us -> none  [the longest x1 0.66 us: shards(): jnp.concatenate([new_u, mode_maps[PAIRS:]], axis=0)]
    ppermute x1 -> x2, starting transfers between devices: 2.27 us -> 3.61 us  [lon_partners(): lax.ppermute(far, ('lat', 'lon'), pairing(same, lambda j: (j + 1 if j % 2...]
    ppermute x36 -> x37, starting transfers between devices: 35 us -> 34.9 us  [swap(): lax.ppermute(x, ('lat', 'lon'), pairing(lambda i: i ^ lat_bits, lambda j:...]
  transfers between devices with their start and end apart: 45 -> 47, of which waited for: 37 -> 33; matrix products, arithmetic and copies ran while one was open for 0% -> 0% of each run, Pallas kernels for 4% -> 8%
where the time goes in v6:
time: 121 us; the launch traced here: 120 us
  starting transfers between devices  49.4 us (41%)
  waiting for transfers between devices  40.1 us (33%)
  Pallas kernels  29.3 us (24%)
    ppermute x37, starting transfers between devices, swap(): lax.ppermute(x, ('lat', 'lon'), pairing(lambda i: i ^ lat_bits, lambda j:...  34.9 us
    pallas_call x12, Pallas kernels, call(): pl.pallas_call(kernel, out_shape=[jax.ShapeDtypeStruct(s, t) for s, t in...  29.3 us
    ppermute x37, waiting for transfers between devices, swap(): lax.ppermute(x, ('lat', 'lon'), pairing(lambda i: i ^ lat_bits, lambda j:...  28.6 us
    ppermute x4, waiting for transfers between devices, lat_partners(): lax.ppermute(x, ('lat', 'lon'), pairing(lambda i: (i + 1 if i % 2 else i...  7.54 us
    ppermute x4, starting transfers between devices, lat_partners(): lax.ppermute(x, ('lat', 'lon'), pairing(lambda i: (i + 1 if i % 2 else i...  6.94 us
    ppermute x4, starting transfers between devices, lat_partners(): got_a = lax.ppermute(x, ('lat', 'lon'), pairing(lambda i: i ^ 1, same))  3.9 us
    ppermute x2, starting transfers between devices, lon_partners(): lax.ppermute(far, ('lat', 'lon'), pairing(same, lambda j: (j + 1 if j % 2...  3.61 us
    ppermute x4, waiting for transfers between devices, lat_partners(): got_a = lax.ppermute(x, ('lat', 'lon'), pairing(lambda i: i ^ 1, same))  3.25 us
  transfers between devices with their start and end apart: 47, of which 33 were waited for; matrix products, arithmetic and copies ran while one was open for 0% of the time, Pallas kernels for 8%

profile of v6, /device:TPU:0, one launch (start us, length us, event | category | flops | bytes accessed | tf_op | source)
XLA Modules:
  0.0 120.4 jit_solution(15513933716843305342)
XLA Ops:
  0.6 4.6 %collective-permute-start.2 = (f32[48,480]{1,0:T(8,128)}, f32[48,480]{1,0:T(8,128)S(1)}, u32[]{:S(2)}, u32[]{:S(2)}) collective-permute-start(f32[48,480]{1,0:T(8,128)} %refs_2_.1), channel_id=1, source_target_pairs={{0,7},{1,6},{2,5},{3,4},{4,3},{5,2},{6,1},{7,0},{8,15},{9,14},{10,... | collective-permute-start | bytes 276488 | tf_op jit(solution)/shard_map/ppermute | solution.py:32
  5.2 0.9 collective-permute-start
  6.5 5.3 %own_flags.1 = (bf16[512,3840]{1,0:T(8,128)(2,1)S(1)}, bf16[512,3840]{1,0:T(8,128)(2,1)S(1)}, f32[48,512]{1,0:T(8,128)S(1)}, f32[1,512]{1,0:T(1,128)S(1)}, f32[1...) custom-call(s32[512,256]{1,0:T(8,128)} %bitcast.6, s32[4,128]{1,0:T(4,128)} %refs_1_.1, ...), custom_call_target="tpu_custom_call" | custom-call | flops 1006632960 | bytes 4648976 | tf_op jit(solution)/shard_map/own_flags/pallas_call | solution.py:432
  11.8 2.9 %collective-permute-done.1.refs_7_ = f32[48,480]{1,0:T(8,128)S(1)} collective-permute-done((f32[48,480]{1,0:T(8,128)}, f32[48,480]{1,0:T(8,128)S(1)}, u32[]{:S(2)}, u32[]{:S(2)}) %collective-permute-start.1) | collective-permute-done | bytes 92192 | tf_op jit(solution)/shard_map/ppermute | solution.py:32
  15.7 2.3 %collective-permute-start.4 = (f32[184,128]{1,0:T(8,128)S(1)}, f32[184,128]{1,0:T(8,128)S(1)}, u32[]{:S(2)}, u32[]{:S(2)}) collective-permute-start(f32[184,128]{1,0:T(8,128)S(1)} %get-tuple-element.50), channel_id=1, source_target_pairs={{0,7},{1,2},{2,1},{3,4},{4,3},{5,6},{6,5},{7,0},{8,15},{9,10},{10,... | collective-permute-start | bytes 282632 | tf_op jit(solution)/shard_map/ppermute | solution.py:67
  18.0 1.8 %given.1 = (f32[48,3840]{1,0:T(8,128)S(1)}, f32[8,512]{1,0:T(8,128)S(1)}, f32[8,128]{1,0:T(8,128)S(1)}, f32[8,128]{1,0:T(8,128)S(1)}) custom-call(bf16[512,3840]{1,0:T(8,128)(2,1)S(1)} %get-tuple-element.51.refs_0_.refs_1_, s32[4]{0:T(128)S(1)} %pad_add_fusion.refs_5_.refs_1_.refs_2_.place_ref.refs_4_, f32[48,480]{1,0:T(8,128)S(1)} %copy-done, ...), custom_call_target="tpu_custom_call" | custom-call | flops 62914560 | bytes 4669456 | tf_op jit(solution)/shard_map/given/pallas_call | solution.py:432
  19.9 1.3 %collective-permute-start.10 = (f32[8,128]{1,0:T(8,128)S(1)}, f32[8,128]{1,0:T(8,128)S(1)}, u32[]{:S(2)}, u32[]{:S(2)}) collective-permute-start(f32[8,128]{1,0:T(8,128)S(1)} %get-tuple-element.63), channel_id=1, source_target_pairs={{0,7},{1,2},{2,1},{3,4},{4,3},{5,6},{6,5},{7,0},{8,15},{9,10},{10,... | collective-permute-start | bytes 12296 | tf_op jit(solution)/shard_map/ppermute | solution.py:67
  21.8 3.0 %first_products.1 = (f32[2,640]{1,0:T(2,128)S(1)}, bf16[128,3840]{1,0:T(8,128)(2,1)S(1)}, f32[48,640]{1,0:T(8,128)S(1)}, f32[1,640]{1,0:T(1,128)S(1)}) custom-call(f32[184,128]{1,0:T(8,128)S(1)} %collective-permute-done.3.refs_0_, f32[184,128]{1,0:T(8,128)S(1)} %collective-permute-done.4.refs_1_, s32[4]{0:T(128)S(1)} %pad_add_fusion.refs_5_.refs_1_.refs_2_.place_ref.refs_4_, ...), custom_call_target="tpu_custom_call" | custom-call | flops 943718400 | bytes 4958224 | tf_op jit(solution)/shard_map/first_products/pallas_call | solution.py:432
  24.9 0.8 fields_0.1
  25.7 2.5 %collective-permute-start.12 = (f32[16,256]{1,0:T(8,128)S(1)}, f32[16,256]{1,0:T(8,128)S(1)}, u32[]{:S(2)}, u32[]{:S(2)}) collective-permute-start(f32[16,256]{1,0:T(8,128)S(1)} %get-tuple-element.68.refs_7_.refs_10_), channel_id=1, source_target_pairs={{0,24},{1,25},{2,26},{3,27},{4,28},{5,29},{6,30},{7,31},{8,16},{9,... | collective-permute-start | bytes 49160 | tf_op jit(solution)/shard_map/ppermute | solution.py:60
  28.8 1.7 %collective-permute-done.12.refs_9_.refs_12_ = f32[16,256]{1,0:T(8,128)S(1)} collective-permute-done((f32[16,256]{1,0:T(8,128)S(1)}, f32[16,256]{1,0:T(8,128)S(1)}, u32[]{:S(2)}, u32[]{:S(2)}) %collective-permute-start.12) | collective-permute-done | bytes 16416 | tf_op jit(solution)/shard_map/ppermute | solution.py:60
  30.5 1.6 %collective-permute-done.11.refs_8_.refs_11_ = f32[16,256]{1,0:T(8,128)S(1)} collective-permute-done((f32[16,256]{1,0:T(8,128)S(1)}, f32[16,256]{1,0:T(8,128)S(1)}, u32[]{:S(2)}, u32[]{:S(2)}) %collective-permute-start.11) | collective-permute-done | bytes 16416 | tf_op jit(solution)/shard_map/ppermute | solution.py:59
  32.0 2.4 %sums_0.1 = (f32[2,3968]{1,0:T(2,128)S(1)}, f32[8,256]{1,0:T(8,128)S(1)}) custom-call(bf16[512,3840]{1,0:T(8,128)(2,1)S(1)} %get-tuple-element.48.refs_3_.refs_0_, bf16[512,3840]{1,0:T(8,128)(2,1)S(1)} %get-tuple-element.51.refs_0_.refs_1_, f32[48,3840]{1,0:T(8,128)S(1)} %get-tuple-element.55.refs_4_.v_ref.refs_2_, ...), custom_call_target="tpu_custom_call" | custom-call | flops 754974720 | bytes 8806416 | tf_op jit(solution)/shard_map/sums_0/pallas_call | solution.py:432
  34.5 1.2 collective-permute-done.13
  36.4 1.0 collective-permute-start.15
  37.5 1.3 %collective-permute-start.14 = (f32[2,3968]{1,0:T(2,128)S(1)}, f32[2,3968]{1,0:T(2,128)S(1)}, u32[]{:S(2)}, u32[]{:S(2)}) collective-permute-start(f32[2,3968]{1,0:T(2,128)S(1)} %add.123), channel_id=1, source_target_pairs={{0,9},{1,8},{2,11},{3,10},{4,13},{5,12},{6,15},{7,14},{8,1},{9,0},... | collective-permute-start | bytes 95240 | tf_op jit(solution)/shard_map/ppermute | solution.py:32
  38.7 1.4 %collective-permute-done.16 = f32[2,3968]{1,0:T(2,128)S(1)} collective-permute-done((f32[2,3968]{1,0:T(2,128)S(1)}, f32[2,3968]{1,0:T(2,128)S(1)}, u32[]{:S(2)}, u32[]{:S(2)}) %collective-permute-start.16) | collective-permute-done | bytes 31776 | tf_op jit(solution)/shard_map/ppermute | solution.py:32
  42.2 2.5 %collective-permute-start.17 = (f32[2,3968]{1,0:T(2,128)S(1)}, f32[2,3968]{1,0:T(2,128)S(1)}, u32[]{:S(2)}, u32[]{:S(2)}) collective-permute-start(f32[2,3968]{1,0:T(2,128)S(1)} %add_add_fusion.7), channel_id=1, source_target_pairs={{0,3},{1,2},{2,1},{3,0},{4,7},{5,6},{6,5},{7,4},{8,11},{9,10},{10,... | collective-permute-start | bytes 95240 | tf_op jit(solution)/shard_map/ppermute | solution.py:32
  44.8 1.4 %collective-permute-done.19 = f32[2,3968]{1,0:T(2,128)S(1)} collective-permute-done((f32[2,3968]{1,0:T(2,128)S(1)}, f32[2,3968]{1,0:T(2,128)S(1)}, u32[]{:S(2)}, u32[]{:S(2)}) %collective-permute-start.19) | collective-permute-done | bytes 31776 | tf_op jit(solution)/shard_map/ppermute | solution.py:32
  46.1 0.9 collective-permute-done.17
  47.0 2.2 %fields_1.1 = (f32[8,256]{1,0:T(8,128)S(1)}, f32[48,3840]{1,0:T(8,128)S(1)}, f32[48,640]{1,0:T(8,128)S(1)}) custom-call(bf16[512,3840]{1,0:T(8,128)(2,1)S(1)} %get-tuple-element.48.refs_3_.refs_0_, bf16[128,3840]{1,0:T(8,128)(2,1)S(1)} %get-tuple-element.58.refs_1_, f32[48,3840]{1,0:T(8,128)S(1)} %get-tuple-element.55.refs_4_.v_ref.refs_2_, ...), custom_call_target="tpu_custom_call" | custom-call | flops 943718400 | bytes 5838336 | tf_op jit(solution)/shard_map/fields_1/pallas_call | solution.py:432
  49.3 1.5 %collective-permute-start.21 = (f32[8,256]{1,0:T(8,128)S(1)}, f32[8,256]{1,0:T(8,128)S(1)}, u32[]{:S(2)}, u32[]{:S(2)}) collective-permute-start(f32[8,256]{1,0:T(8,128)S(1)} %get-tuple-element.73.refs_7_), channel_id=1, source_target_pairs={{0,24},{1,25},{2,26},{3,27},{4,28},{5,29},{6,30},{7,31},{8,16},{9,... | collective-permute-start | bytes 24584 | tf_op jit(solution)/shard_map/ppermute | solution.py:60
  50.7 1.4 %collective-permute-start.20 = (f32[8,256]{1,0:T(8,128)S(1)}, f32[8,256]{1,0:T(8,128)S(1)}, u32[]{:S(2)}, u32[]{:S(2)}) collective-permute-start(f32[8,256]{1,0:T(8,128)S(1)} %get-tuple-element.73.refs_7_), channel_id=1, source_target_pairs={{0,8},{1,9},{2,10},{3,11},{4,12},{5,13},{6,14},{7,15},{8,0},{9,1},... | collective-permute-start | bytes 24584 | tf_op jit(solution)/shard_map/ppermute | solution.py:59
  52.1 1.7 %collective-permute-done.21.refs_9_ = f32[8,256]{1,0:T(8,128)S(1)} collective-permute-done((f32[8,256]{1,0:T(8,128)S(1)}, f32[8,256]{1,0:T(8,128)S(1)}, u32[]{:S(2)}, u32[]{:S(2)}) %collective-permute-start.21) | collective-permute-done | bytes 8224 | tf_op jit(solution)/shard_map/ppermute | solution.py:60
  54.4 2.4 %sums_1.1 = (f32[2,3968]{1,0:T(2,128)S(1)}, f32[8,256]{1,0:T(8,128)S(1)}) custom-call(bf16[512,3840]{1,0:T(8,128)(2,1)S(1)} %get-tuple-element.48.refs_3_.refs_0_, bf16[512,3840]{1,0:T(8,128)(2,1)S(1)} %get-tuple-element.51.refs_0_.refs_1_, f32[48,3840]{1,0:T(8,128)S(1)} %get-tuple-element.71.refs_2_, f32[48,640]{1,0:T(8,128)S(1)} %get-tuple-element.72.refs_3_, ...), custom_call_target="tpu_custom_call" | custom-call | flops 754974720 | bytes 8830992 | tf_op jit(solution)/shard_map/sums_1/pallas_call | solution.py:432
  56.8 1.2 collective-permute-done.22
  58.1 1.3 %collective-permute-start.25 = (f32[2,3968]{1,0:T(2,128)S(1)}, f32[2,3968]{1,0:T(2,128)S(1)}, u32[]{:S(2)}, u32[]{:S(2)}) collective-permute-start(f32[2,3968]{1,0:T(2,128)S(1)} %add.130), channel_id=1, source_target_pairs={{0,25},{1,24},{2,27},{3,26},{4,29},{5,28},{6,31},{7,30},{8,17},{9,... | collective-permute-start | bytes 95240 | tf_op jit(solution)/shard_map/ppermute | solution.py:32
  59.4 1.3 %collective-permute-start.24 = (f32[2,3968]{1,0:T(2,128)S(1)}, f32[2,3968]{1,0:T(2,128)S(1)}, u32[]{:S(2)}, u32[]{:S(2)}) collective-permute-start(f32[2,3968]{1,0:T(2,128)S(1)} %add.130), channel_id=1, source_target_pairs={{0,17},{1,16},{2,19},{3,18},{4,21},{5,20},{6,23},{7,22},{8,25},{9,... | collective-permute-start | bytes 95240 | tf_op jit(solution)/shard_map/ppermute | solution.py:32
  61.1 1.3 %collective-permute-done.25 = f32[2,3968]{1,0:T(2,128)S(1)} collective-permute-done((f32[2,3968]{1,0:T(2,128)S(1)}, f32[2,3968]{1,0:T(2,128)S(1)}, u32[]{:S(2)}, u32[]{:S(2)}) %collective-permute-start.25) | collective-permute-done | bytes 31776 | tf_op jit(solution)/shard_map/ppermute | solution.py:32
  63.2 0.8 collective-permute-done.23
  64.0 1.3 %collective-permute-start.28 = (f32[2,3968]{1,0:T(2,128)S(1)}, f32[2,3968]{1,0:T(2,128)S(1)}, u32[]{:S(2)}, u32[]{:S(2)}) collective-permute-start(f32[2,3968]{1,0:T(2,128)S(1)} %add_add_fusion.5), channel_id=1, source_target_pairs={{0,7},{1,6},{2,5},{3,4},{4,3},{5,2},{6,1},{7,0},{8,15},{9,14},{10,... | collective-permute-start | bytes 95240 | tf_op jit(solution)/shard_map/ppermute | solution.py:32
  65.4 1.0 collective-permute-start.27
  66.4 1.8 %collective-permute-start.26 = (f32[2,3968]{1,0:T(2,128)S(1)}, f32[2,3968]{1,0:T(2,128)S(1)}, u32[]{:S(2)}, u32[]{:S(2)}) collective-permute-start(f32[2,3968]{1,0:T(2,128)S(1)} %add_add_fusion.5), channel_id=1, source_target_pairs={{0,3},{1,2},{2,1},{3,0},{4,7},{5,6},{6,5},{7,4},{8,11},{9,10},{10,... | collective-permute-start | bytes 95240 | tf_op jit(solution)/shard_map/ppermute | solution.py:32
  68.2 1.3 %collective-permute-done.28 = f32[2,3968]{1,0:T(2,128)S(1)} collective-permute-done((f32[2,3968]{1,0:T(2,128)S(1)}, f32[2,3968]{1,0:T(2,128)S(1)}, u32[]{:S(2)}, u32[]{:S(2)}) %collective-permute-start.28) | collective-permute-done | bytes 31776 | tf_op jit(solution)/shard_map/ppermute | solution.py:32
  69.4 1.6 %collective-permute-done.27 = f32[2,3968]{1,0:T(2,128)S(1)} collective-permute-done((f32[2,3968]{1,0:T(2,128)S(1)}, f32[2,3968]{1,0:T(2,128)S(1)}, u32[]{:S(2)}, u32[]{:S(2)}) %collective-permute-start.27) | collective-permute-done | bytes 31776 | tf_op jit(solution)/shard_map/ppermute | solution.py:32
  71.1 2.2 %fields_2.1 = (f32[8,256]{1,0:T(8,128)S(1)}, f32[48,3840]{1,0:T(8,128)S(1)}, f32[48,640]{1,0:T(8,128)S(1)}) custom-call(bf16[512,3840]{1,0:T(8,128)(2,1)S(1)} %get-tuple-element.48.refs_3_.refs_0_, bf16[128,3840]{1,0:T(8,128)(2,1)S(1)} %get-tuple-element.58.refs_1_, f32[48,3840]{1,0:T(8,128)S(1)} %get-tuple-element.71.refs_2_, ...), custom_call_target="tpu_custom_call" | custom-call | flops 943718400 | bytes 5838336 | tf_op jit(solution)/shard_map/fields_2/pallas_call | solution.py:432
  73.3 1.7 %collective-permute-start.30 = (f32[8,256]{1,0:T(8,128)S(1)}, f32[8,256]{1,0:T(8,128)S(1)}, u32[]{:S(2)}, u32[]{:S(2)}) collective-permute-start(f32[8,256]{1,0:T(8,128)S(1)} %get-tuple-element.78.refs_7_), channel_id=1, source_target_pairs={{0,24},{1,25},{2,26},{3,27},{4,28},{5,29},{6,30},{7,31},{8,16},{9,... | collective-permute-start | bytes 24584 | tf_op jit(solution)/shard_map/ppermute | solution.py:60
  75.7 2.2 %collective-permute-done.30.refs_9_ = f32[8,256]{1,0:T(8,128)S(1)} collective-permute-done((f32[8,256]{1,0:T(8,128)S(1)}, f32[8,256]{1,0:T(8,128)S(1)}, u32[]{:S(2)}, u32[]{:S(2)}) %collective-permute-start.30) | collective-permute-done | bytes 8224 | tf_op jit(solution)/shard_map/ppermute | solution.py:60
  78.7 2.4 %sums_2.1 = (f32[2,3968]{1,0:T(2,128)S(1)}, f32[8,256]{1,0:T(8,128)S(1)}) custom-call(bf16[512,3840]{1,0:T(8,128)(2,1)S(1)} %get-tuple-element.48.refs_3_.refs_0_, bf16[512,3840]{1,0:T(8,128)(2,1)S(1)} %get-tuple-element.51.refs_0_.refs_1_, f32[48,3840]{1,0:T(8,128)S(1)} %get-tuple-element.76.refs_2_, f32[48,640]{1,0:T(8,128)S(1)} %get-tuple-element.77.refs_3_, ...), custom_call_target="tpu_custom_call" | custom-call | flops 754974720 | bytes 8830992 | tf_op jit(solution)/shard_map/sums_2/pallas_call | solution.py:432
  81.1 1.2 collective-permute-done.31
  82.3 1.1 collective-permute-start.34
  84.3 1.1 collective-permute-start.32
  85.4 1.3 %collective-permute-done.34 = f32[2,3968]{1,0:T(2,128)S(1)} collective-permute-done((f32[2,3968]{1,0:T(2,128)S(1)}, f32[2,3968]{1,0:T(2,128)S(1)}, u32[]{:S(2)}, u32[]{:S(2)}) %collective-permute-start.34) | collective-permute-done | bytes 31776 | tf_op jit(solution)/shard_map/ppermute | solution.py:32
  86.7 0.9 collective-permute-done.33
  87.6 1.3 %collective-permute-start.37 = (f32[2,3968]{1,0:T(2,128)S(1)}, f32[2,3968]{1,0:T(2,128)S(1)}, u32[]{:S(2)}, u32[]{:S(2)}) collective-permute-start(f32[2,3968]{1,0:T(2,128)S(1)} %add_add_fusion.3), channel_id=1, source_target_pairs={{0,7},{1,6},{2,5},{3,4},{4,3},{5,2},{6,1},{7,0},{8,15},{9,14},{10,... | collective-permute-start | bytes 95240 | tf_op jit(solution)/shard_map/ppermute | solution.py:32
  89.6 2.0 %collective-permute-start.35 = (f32[2,3968]{1,0:T(2,128)S(1)}, f32[2,3968]{1,0:T(2,128)S(1)}, u32[]{:S(2)}, u32[]{:S(2)}) collective-permute-start(f32[2,3968]{1,0:T(2,128)S(1)} %add_add_fusion.3), channel_id=1, source_target_pairs={{0,3},{1,2},{2,1},{3,0},{4,7},{5,6},{6,5},{7,4},{8,11},{9,10},{10,... | collective-permute-start | bytes 95240 | tf_op jit(solution)/shard_map/ppermute | solution.py:32
  91.6 1.3 %collective-permute-done.37 = f32[2,3968]{1,0:T(2,128)S(1)} collective-permute-done((f32[2,3968]{1,0:T(2,128)S(1)}, f32[2,3968]{1,0:T(2,128)S(1)}, u32[]{:S(2)}, u32[]{:S(2)}) %collective-permute-start.37) | collective-permute-done | bytes 31776 | tf_op jit(solution)/shard_map/ppermute | solution.py:32
  92.8 1.6 %collective-permute-done.36 = f32[2,3968]{1,0:T(2,128)S(1)} collective-permute-done((f32[2,3968]{1,0:T(2,128)S(1)}, f32[2,3968]{1,0:T(2,128)S(1)}, u32[]{:S(2)}, u32[]{:S(2)}) %collective-permute-start.36) | collective-permute-done | bytes 31776 | tf_op jit(solution)/shard_map/ppermute | solution.py:32
  94.5 2.2 %fields_3.1 = (f32[8,256]{1,0:T(8,128)S(1)}, f32[48,3840]{1,0:T(8,128)S(1)}, f32[48,640]{1,0:T(8,128)S(1)}) custom-call(bf16[512,3840]{1,0:T(8,128)(2,1)S(1)} %get-tuple-element.48.refs_3_.refs_0_, bf16[128,3840]{1,0:T(8,128)(2,1)S(1)} %get-tuple-element.58.refs_1_, f32[48,3840]{1,0:T(8,128)S(1)} %get-tuple-element.76.refs_2_, ...), custom_call_target="tpu_custom_call" | custom-call | flops 943718400 | bytes 5838336 | tf_op jit(solution)/shard_map/fields_3/pallas_call | solution.py:432
  96.7 1.3 %collective-permute-start.39 = (f32[8,256]{1,0:T(8,128)S(1)}, f32[8,256]{1,0:T(8,128)S(1)}, u32[]{:S(2)}, u32[]{:S(2)}) collective-permute-start(f32[8,256]{1,0:T(8,128)S(1)} %get-tuple-element.83.refs_7_), channel_id=1, source_target_pairs={{0,24},{1,25},{2,26},{3,27},{4,28},{5,29},{6,30},{7,31},{8,16},{9,... | collective-permute-start | bytes 24584 | tf_op jit(solution)/shard_map/ppermute | solution.py:60
  98.0 1.3 %collective-permute-start.38 = (f32[8,256]{1,0:T(8,128)S(1)}, f32[8,256]{1,0:T(8,128)S(1)}, u32[]{:S(2)}, u32[]{:S(2)}) collective-permute-start(f32[8,256]{1,0:T(8,128)S(1)} %get-tuple-element.83.refs_7_), channel_id=1, source_target_pairs={{0,8},{1,9},{2,10},{3,11},{4,12},{5,13},{6,14},{7,15},{8,0},{9,1},... | collective-permute-start | bytes 24584 | tf_op jit(solution)/shard_map/ppermute | solution.py:59
  99.3 2.0 %collective-permute-done.39.refs_9_ = f32[8,256]{1,0:T(8,128)S(1)} collective-permute-done((f32[8,256]{1,0:T(8,128)S(1)}, f32[8,256]{1,0:T(8,128)S(1)}, u32[]{:S(2)}, u32[]{:S(2)}) %collective-permute-start.39) | collective-permute-done | bytes 8224 | tf_op jit(solution)/shard_map/ppermute | solution.py:60
  101.7 2.4 %sums_3.1 = (f32[2,3968]{1,0:T(2,128)S(1)}, f32[8,256]{1,0:T(8,128)S(1)}) custom-call(bf16[512,3840]{1,0:T(8,128)(2,1)S(1)} %get-tuple-element.48.refs_3_.refs_0_, bf16[512,3840]{1,0:T(8,128)(2,1)S(1)} %get-tuple-element.51.refs_0_.refs_1_, f32[48,3840]{1,0:T(8,128)S(1)} %get-tuple-element.81.refs_2_.refs_0_, ...), custom_call_target="tpu_custom_call" | custom-call | flops 754974720 | bytes 8830992 | tf_op jit(solution)/shard_map/sums_3/pallas_call | solution.py:432
  104.1 1.2 collective-permute-done.40
  105.4 1.5 %collective-permute-start.43 = (f32[2,3968]{1,0:T(2,128)S(1)}, f32[2,3968]{1,0:T(2,128)S(1)}, u32[]{:S(2)}, u32[]{:S(2)}) collective-permute-start(f32[2,3968]{1,0:T(2,128)S(1)} %add.144), channel_id=1, source_target_pairs={{0,25},{1,24},{2,27},{3,26},{4,29},{5,28},{6,31},{7,30},{8,17},{9,... | collective-permute-start | bytes 95240 | tf_op jit(solution)/shard_map/ppermute | solution.py:32
  106.9 1.1 collective-permute-start.42
  108.4 1.3 %collective-permute-done.43 = f32[2,3968]{1,0:T(2,128)S(1)} collective-permute-done((f32[2,3968]{1,0:T(2,128)S(1)}, f32[2,3968]{1,0:T(2,128)S(1)}, u32[]{:S(2)}, u32[]{:S(2)}) %collective-permute-start.43) | collective-permute-done | bytes 31776 | tf_op jit(solution)/shard_map/ppermute | solution.py:32
  110.3 0.9 collective-permute-done.41
  111.3 1.1 collective-permute-start.46
  112.4 0.8 collective-permute-start.45
  113.2 2.0 %collective-permute-start.44 = (f32[2,3968]{1,0:T(2,128)S(1)}, f32[2,3968]{1,0:T(2,128)S(1)}, u32[]{:S(2)}, u32[]{:S(2)}) collective-permute-start(f32[2,3968]{1,0:T(2,128)S(1)} %add_add_fusion.1), channel_id=1, source_target_pairs={{0,3},{1,2},{2,1},{3,0},{4,7},{5,6},{6,5},{7,4},{8,11},{9,10},{10,... | collective-permute-start | bytes 95240 | tf_op jit(solution)/shard_map/ppermute | solution.py:32
  115.2 1.3 %collective-permute-done.46 = f32[2,3968]{1,0:T(2,128)S(1)} collective-permute-done((f32[2,3968]{1,0:T(2,128)S(1)}, f32[2,3968]{1,0:T(2,128)S(1)}, u32[]{:S(2)}, u32[]{:S(2)}) %collective-permute-start.46) | collective-permute-done | bytes 31776 | tf_op jit(solution)/shard_map/ppermute | solution.py:32
  116.5 1.6 %collective-permute-done.45 = f32[2,3968]{1,0:T(2,128)S(1)} collective-permute-done((f32[2,3968]{1,0:T(2,128)S(1)}, f32[2,3968]{1,0:T(2,128)S(1)}, u32[]{:S(2)}, u32[]{:S(2)}) %collective-permute-start.45) | collective-permute-done | bytes 31776 | tf_op jit(solution)/shard_map/ppermute | solution.py:32
  118.2 2.1 %last.1 = (f32[48,4,128]{2,1,0:T(4,128)}, f32[48,480]{1,0:T(8,128)}) custom-call(f32[48,3840]{1,0:T(8,128)S(1)} %get-tuple-element.81.refs_2_.refs_0_, f32[48,640]{1,0:T(8,128)S(1)} %get-tuple-element.82.refs_3_.refs_1_, f32[2,3968]{1,0:T(2,128)S(1)} %add_add_fusion.refs_2_, ...), custom_call_target="tpu_custom_call", output_to_operand_aliasing={{0}: (5, {}), {1}: (6, {})} | custom-call | bytes 1090576 | tf_op jit(solution)/shard_map/last/pallas_call | solution.py:432
  (61 shorter events, 12.3 us)
Async XLA Ops:
  0.6 17.4 %copy-start = (f32[48,480]{1,0:T(8,128)S(1)}, f32[48,480]{1,0:T(8,128)}, u32[]{:S(2)}) copy-start(f32[48,480]{1,0:T(8,128)} %refs_2_.1) | copy-start | bytes 276484
  0.6 11.1 %collective-permute-start.2 = (f32[48,480]{1,0:T(8,128)}, f32[48,480]{1,0:T(8,128)S(1)}, u32[]{:S(2)}, u32[]{:S(2)}) collective-permute-start(f32[48,480]{1,0:T(8,128)} %refs_2_.1), channel_id=1, source_target_pairs={{0,7},{1,6},{2,5},{3,4},{4,3},{5,2},{6,1},{7,0},{8,15},{9,14},{10,... | collective-permute-start | bytes 276488 | tf_op jit(solution)/shard_map/ppermute | solution.py:32
  5.2 9.5 %collective-permute-start.1 = (f32[48,480]{1,0:T(8,128)}, f32[48,480]{1,0:T(8,128)S(1)}, u32[]{:S(2)}, u32[]{:S(2)}) collective-permute-start(f32[48,480]{1,0:T(8,128)} %refs_2_.1), channel_id=1, source_target_pairs={{0,5},{1,4},{2,7},{3,6},{4,1},{5,0},{6,3},{7,2},{8,13},{9,12},{10,... | collective-permute-start | bytes 276488 | tf_op jit(solution)/shard_map/ppermute | solution.py:32
  5.2 9.5 %collective-permute-start = (f32[48,480]{1,0:T(8,128)}, f32[48,480]{1,0:T(8,128)S(1)}, u32[]{:S(2)}, u32[]{:S(2)}) collective-permute-start(f32[48,480]{1,0:T(8,128)} %refs_2_.1), channel_id=1, source_target_pairs={{0,3},{1,2},{2,1},{3,0},{4,7},{5,6},{6,5},{7,4},{8,11},{9,10},{10,... | collective-permute-start | bytes 276488 | tf_op jit(solution)/shard_map/ppermute | solution.py:32
  6.1 9.6 %collective-permute-start.5 = (f32[48,480]{1,0:T(8,128)}, f32[48,480]{1,0:T(8,128)S(1)}, u32[]{:S(2)}, u32[]{:S(2)}) collective-permute-start(f32[48,480]{1,0:T(8,128)} %refs_2_.1), channel_id=1, source_target_pairs={{0,1},{1,0},{2,3},{3,2},{4,5},{5,4},{6,7},{7,6},{8,9},{9,8},{10,11... | collective-permute-start | bytes 276488 | tf_op jit(solution)/shard_map/ppermute | solution.py:32
  14.7 3.3 %collective-permute-start.6 = (f32[48,480]{1,0:T(8,128)S(1)}, f32[48,480]{1,0:T(8,128)S(1)}, u32[]{:S(2)}, u32[]{:S(2)}) collective-permute-start(f32[48,480]{1,0:T(8,128)S(1)} %collective-permute-done.refs_5_), channel_id=1, source_target_pairs={{0,1},{1,0},{2,3},{3,2},{4,5},{5,4},{6,7},{7,6},{8,9},{9,8},{10,11... | collective-permute-start | bytes 276488 | tf_op jit(solution)/shard_map/ppermute | solution.py:32
  14.8 3.2 %collective-permute-start.7 = (f32[48,480]{1,0:T(8,128)S(1)}, f32[48,480]{1,0:T(8,128)S(1)}, u32[]{:S(2)}, u32[]{:S(2)}) collective-permute-start(f32[48,480]{1,0:T(8,128)S(1)} %collective-permute-done.1.refs_7_), channel_id=1, source_target_pairs={{0,1},{1,0},{2,3},{3,2},{4,5},{5,4},{6,7},{7,6},{8,9},{9,8},{10,11... | collective-permute-start | bytes 276488 | tf_op jit(solution)/shard_map/ppermute | solution.py:32
  15.2 2.8 %collective-permute-start.8 = (f32[48,480]{1,0:T(8,128)S(1)}, f32[48,480]{1,0:T(8,128)S(1)}, u32[]{:S(2)}, u32[]{:S(2)}) collective-permute-start(f32[48,480]{1,0:T(8,128)S(1)} %collective-permute-done.2.refs_9_), channel_id=1, source_target_pairs={{0,1},{1,0},{2,3},{3,2},{4,5},{5,4},{6,7},{7,6},{8,9},{9,8},{10,11... | collective-permute-start | bytes 276488 | tf_op jit(solution)/shard_map/ppermute | solution.py:32
  15.3 5.9 %collective-permute-start.3 = (f32[184,128]{1,0:T(8,128)S(1)}, f32[184,128]{1,0:T(8,128)S(1)}, u32[]{:S(2)}, u32[]{:S(2)}) collective-permute-start(f32[184,128]{1,0:T(8,128)S(1)} %get-tuple-element.49), channel_id=1, source_target_pairs={{0,1},{1,0},{2,3},{3,2},{4,5},{5,4},{6,7},{7,6},{8,9},{9,8},{10,11... | collective-permute-start | bytes 282632 | tf_op jit(solution)/shard_map/ppermute | solution.py:32
  15.7 6.2 %collective-permute-start.4 = (f32[184,128]{1,0:T(8,128)S(1)}, f32[184,128]{1,0:T(8,128)S(1)}, u32[]{:S(2)}, u32[]{:S(2)}) collective-permute-start(f32[184,128]{1,0:T(8,128)S(1)} %get-tuple-element.50), channel_id=1, source_target_pairs={{0,7},{1,2},{2,1},{3,4},{4,3},{5,6},{6,5},{7,0},{8,15},{9,10},{10,... | collective-permute-start | bytes 282632 | tf_op jit(solution)/shard_map/ppermute | solution.py:67
  19.8 5.1 %collective-permute-start.9 = (f32[8,128]{1,0:T(8,128)S(1)}, f32[8,128]{1,0:T(8,128)S(1)}, u32[]{:S(2)}, u32[]{:S(2)}) collective-permute-start(f32[8,128]{1,0:T(8,128)S(1)} %get-tuple-element.62), channel_id=1, source_target_pairs={{0,1},{1,0},{2,3},{3,2},{4,5},{5,4},{6,7},{7,6},{8,9},{9,8},{10,11... | collective-permute-start | bytes 12296 | tf_op jit(solution)/shard_map/ppermute | solution.py:32
  19.9 5.0 %collective-permute-start.10 = (f32[8,128]{1,0:T(8,128)S(1)}, f32[8,128]{1,0:T(8,128)S(1)}, u32[]{:S(2)}, u32[]{:S(2)}) collective-permute-start(f32[8,128]{1,0:T(8,128)S(1)} %get-tuple-element.63), channel_id=1, source_target_pairs={{0,7},{1,2},{2,1},{3,4},{4,3},{5,6},{6,5},{7,0},{8,15},{9,10},{10,... | collective-permute-start | bytes 12296 | tf_op jit(solution)/shard_map/ppermute | solution.py:67
  25.7 4.7 %collective-permute-start.12 = (f32[16,256]{1,0:T(8,128)S(1)}, f32[16,256]{1,0:T(8,128)S(1)}, u32[]{:S(2)}, u32[]{:S(2)}) collective-permute-start(f32[16,256]{1,0:T(8,128)S(1)} %get-tuple-element.68.refs_7_.refs_10_), channel_id=1, source_target_pairs={{0,24},{1,25},{2,26},{3,27},{4,28},{5,29},{6,30},{7,31},{8,16},{9,... | collective-permute-start | bytes 49160 | tf_op jit(solution)/shard_map/ppermute | solution.py:60
  28.3 3.7 %collective-permute-start.11 = (f32[16,256]{1,0:T(8,128)S(1)}, f32[16,256]{1,0:T(8,128)S(1)}, u32[]{:S(2)}, u32[]{:S(2)}) collective-permute-start(f32[16,256]{1,0:T(8,128)S(1)} %get-tuple-element.68.refs_7_.refs_10_), channel_id=1, source_target_pairs={{0,8},{1,9},{2,10},{3,11},{4,12},{5,13},{6,14},{7,15},{8,0},{9,1},... | collective-permute-start | bytes 49160 | tf_op jit(solution)/shard_map/ppermute | solution.py:59
  34.4 1.3 %collective-permute-start.13 = (f32[2,3968]{1,0:T(2,128)S(1)}, f32[2,3968]{1,0:T(2,128)S(1)}, u32[]{:S(2)}, u32[]{:S(2)}) collective-permute-start(f32[2,3968]{1,0:T(2,128)S(1)} %get-tuple-element.69), channel_id=1, source_target_pairs={{0,1},{1,0},{2,3},{3,2},{4,5},{5,4},{6,7},{7,6},{8,9},{9,8},{10,11... | collective-permute-start | bytes 95240 | tf_op jit(solution)/shard_map/ppermute | solution.py:32
  35.7 4.4 %collective-permute-start.16 = (f32[2,3968]{1,0:T(2,128)S(1)}, f32[2,3968]{1,0:T(2,128)S(1)}, u32[]{:S(2)}, u32[]{:S(2)}) collective-permute-start(f32[2,3968]{1,0:T(2,128)S(1)} %add.123), channel_id=1, source_target_pairs={{0,25},{1,24},{2,27},{3,26},{4,29},{5,28},{6,31},{7,30},{8,17},{9,... | collective-permute-start | bytes 95240 | tf_op jit(solution)/shard_map/ppermute | solution.py:32
  36.4 4.0 %collective-permute-start.15 = (f32[2,3968]{1,0:T(2,128)S(1)}, f32[2,3968]{1,0:T(2,128)S(1)}, u32[]{:S(2)}, u32[]{:S(2)}) collective-permute-start(f32[2,3968]{1,0:T(2,128)S(1)} %add.123), channel_id=1, source_target_pairs={{0,17},{1,16},{2,19},{3,18},{4,21},{5,20},{6,23},{7,22},{8,25},{9,... | collective-permute-start | bytes 95240 | tf_op jit(solution)/shard_map/ppermute | solution.py:32
  37.5 3.3 %collective-permute-start.14 = (f32[2,3968]{1,0:T(2,128)S(1)}, f32[2,3968]{1,0:T(2,128)S(1)}, u32[]{:S(2)}, u32[]{:S(2)}) collective-permute-start(f32[2,3968]{1,0:T(2,128)S(1)} %add.123), channel_id=1, source_target_pairs={{0,9},{1,8},{2,11},{3,10},{4,13},{5,12},{6,15},{7,14},{8,1},{9,0},... | collective-permute-start | bytes 95240 | tf_op jit(solution)/shard_map/ppermute | solution.py:32
  40.8 5.3 %collective-permute-start.19 = (f32[2,3968]{1,0:T(2,128)S(1)}, f32[2,3968]{1,0:T(2,128)S(1)}, u32[]{:S(2)}, u32[]{:S(2)}) collective-permute-start(f32[2,3968]{1,0:T(2,128)S(1)} %add_add_fusion.7), channel_id=1, source_target_pairs={{0,7},{1,6},{2,5},{3,4},{4,3},{5,2},{6,1},{7,0},{8,15},{9,14},{10,... | collective-permute-start | bytes 95240 | tf_op jit(solution)/shard_map/ppermute | solution.py:32
  41.4 4.7 %collective-permute-start.18 = (f32[2,3968]{1,0:T(2,128)S(1)}, f32[2,3968]{1,0:T(2,128)S(1)}, u32[]{:S(2)}, u32[]{:S(2)}) collective-permute-start(f32[2,3968]{1,0:T(2,128)S(1)} %add_add_fusion.7), channel_id=1, source_target_pairs={{0,5},{1,4},{2,7},{3,6},{4,1},{5,0},{6,3},{7,2},{8,13},{9,12},{10,... | collective-permute-start | bytes 95240 | tf_op jit(solution)/shard_map/ppermute | solution.py:32
  42.2 4.8 %collective-permute-start.17 = (f32[2,3968]{1,0:T(2,128)S(1)}, f32[2,3968]{1,0:T(2,128)S(1)}, u32[]{:S(2)}, u32[]{:S(2)}) collective-permute-start(f32[2,3968]{1,0:T(2,128)S(1)} %add_add_fusion.7), channel_id=1, source_target_pairs={{0,3},{1,2},{2,1},{3,0},{4,7},{5,6},{6,5},{7,4},{8,11},{9,10},{10,... | collective-permute-start | bytes 95240 | tf_op jit(solution)/shard_map/ppermute | solution.py:32
  49.3 4.6 %collective-permute-start.21 = (f32[8,256]{1,0:T(8,128)S(1)}, f32[8,256]{1,0:T(8,128)S(1)}, u32[]{:S(2)}, u32[]{:S(2)}) collective-permute-start(f32[8,256]{1,0:T(8,128)S(1)} %get-tuple-element.73.refs_7_), channel_id=1, source_target_pairs={{0,24},{1,25},{2,26},{3,27},{4,28},{5,29},{6,30},{7,31},{8,16},{9,... | collective-permute-start | bytes 24584 | tf_op jit(solution)/shard_map/ppermute | solution.py:60
  50.7 3.7 %collective-permute-start.20 = (f32[8,256]{1,0:T(8,128)S(1)}, f32[8,256]{1,0:T(8,128)S(1)}, u32[]{:S(2)}, u32[]{:S(2)}) collective-permute-start(f32[8,256]{1,0:T(8,128)S(1)} %get-tuple-element.73.refs_7_), channel_id=1, source_target_pairs={{0,8},{1,9},{2,10},{3,11},{4,12},{5,13},{6,14},{7,15},{8,0},{9,1},... | collective-permute-start | bytes 24584 | tf_op jit(solution)/shard_map/ppermute | solution.py:59
  56.8 1.3 %collective-permute-start.22 = (f32[2,3968]{1,0:T(2,128)S(1)}, f32[2,3968]{1,0:T(2,128)S(1)}, u32[]{:S(2)}, u32[]{:S(2)}) collective-permute-start(f32[2,3968]{1,0:T(2,128)S(1)} %get-tuple-element.74), channel_id=1, source_target_pairs={{0,1},{1,0},{2,3},{3,2},{4,5},{5,4},{6,7},{7,6},{8,9},{9,8},{10,11... | collective-permute-start | bytes 95240 | tf_op jit(solution)/shard_map/ppermute | solution.py:32
  58.1 4.3 %collective-permute-start.25 = (f32[2,3968]{1,0:T(2,128)S(1)}, f32[2,3968]{1,0:T(2,128)S(1)}, u32[]{:S(2)}, u32[]{:S(2)}) collective-permute-start(f32[2,3968]{1,0:T(2,128)S(1)} %add.130), channel_id=1, source_target_pairs={{0,25},{1,24},{2,27},{3,26},{4,29},{5,28},{6,31},{7,30},{8,17},{9,... | collective-permute-start | bytes 95240 | tf_op jit(solution)/shard_map/ppermute | solution.py:32
  59.4 3.8 %collective-permute-start.24 = (f32[2,3968]{1,0:T(2,128)S(1)}, f32[2,3968]{1,0:T(2,128)S(1)}, u32[]{:S(2)}, u32[]{:S(2)}) collective-permute-start(f32[2,3968]{1,0:T(2,128)S(1)} %add.130), channel_id=1, source_target_pairs={{0,17},{1,16},{2,19},{3,18},{4,21},{5,20},{6,23},{7,22},{8,25},{9,... | collective-permute-start | bytes 95240 | tf_op jit(solution)/shard_map/ppermute | solution.py:32
  60.7 3.3 %collective-permute-start.23 = (f32[2,3968]{1,0:T(2,128)S(1)}, f32[2,3968]{1,0:T(2,128)S(1)}, u32[]{:S(2)}, u32[]{:S(2)}) collective-permute-start(f32[2,3968]{1,0:T(2,128)S(1)} %add.130), channel_id=1, source_target_pairs={{0,9},{1,8},{2,11},{3,10},{4,13},{5,12},{6,15},{7,14},{8,1},{9,0},... | collective-permute-start | bytes 95240 | tf_op jit(solution)/shard_map/ppermute | solution.py:32
  64.0 5.4 %collective-permute-start.28 = (f32[2,3968]{1,0:T(2,128)S(1)}, f32[2,3968]{1,0:T(2,128)S(1)}, u32[]{:S(2)}, u32[]{:S(2)}) collective-permute-start(f32[2,3968]{1,0:T(2,128)S(1)} %add_add_fusion.5), channel_id=1, source_target_pairs={{0,7},{1,6},{2,5},{3,4},{4,3},{5,2},{6,1},{7,0},{8,15},{9,14},{10,... | collective-permute-start | bytes 95240 | tf_op jit(solution)/shard_map/ppermute | solution.py:32
  65.4 5.7 %collective-permute-start.27 = (f32[2,3968]{1,0:T(2,128)S(1)}, f32[2,3968]{1,0:T(2,128)S(1)}, u32[]{:S(2)}, u32[]{:S(2)}) collective-permute-start(f32[2,3968]{1,0:T(2,128)S(1)} %add_add_fusion.5), channel_id=1, source_target_pairs={{0,5},{1,4},{2,7},{3,6},{4,1},{5,0},{6,3},{7,2},{8,13},{9,12},{10,... | collective-permute-start | bytes 95240 | tf_op jit(solution)/shard_map/ppermute | solution.py:32
  66.4 4.7 %collective-permute-start.26 = (f32[2,3968]{1,0:T(2,128)S(1)}, f32[2,3968]{1,0:T(2,128)S(1)}, u32[]{:S(2)}, u32[]{:S(2)}) collective-permute-start(f32[2,3968]{1,0:T(2,128)S(1)} %add_add_fusion.5), channel_id=1, source_target_pairs={{0,3},{1,2},{2,1},{3,0},{4,7},{5,6},{6,5},{7,4},{8,11},{9,10},{10,... | collective-permute-start | bytes 95240 | tf_op jit(solution)/shard_map/ppermute | solution.py:32
  73.3 4.6 %collective-permute-start.30 = (f32[8,256]{1,0:T(8,128)S(1)}, f32[8,256]{1,0:T(8,128)S(1)}, u32[]{:S(2)}, u32[]{:S(2)}) collective-permute-start(f32[8,256]{1,0:T(8,128)S(1)} %get-tuple-element.78.refs_7_), channel_id=1, source_target_pairs={{0,24},{1,25},{2,26},{3,27},{4,28},{5,29},{6,30},{7,31},{8,16},{9,... | collective-permute-start | bytes 24584 | tf_op jit(solution)/shard_map/ppermute | solution.py:60
  75.0 3.7 %collective-permute-start.29 = (f32[8,256]{1,0:T(8,128)S(1)}, f32[8,256]{1,0:T(8,128)S(1)}, u32[]{:S(2)}, u32[]{:S(2)}) collective-permute-start(f32[8,256]{1,0:T(8,128)S(1)} %get-tuple-element.78.refs_7_), channel_id=1, source_target_pairs={{0,8},{1,9},{2,10},{3,11},{4,12},{5,13},{6,14},{7,15},{8,0},{9,1},... | collective-permute-start | bytes 24584 | tf_op jit(solution)/shard_map/ppermute | solution.py:59
  81.1 1.3 %collective-permute-start.31 = (f32[2,3968]{1,0:T(2,128)S(1)}, f32[2,3968]{1,0:T(2,128)S(1)}, u32[]{:S(2)}, u32[]{:S(2)}) collective-permute-start(f32[2,3968]{1,0:T(2,128)S(1)} %get-tuple-element.79), channel_id=1, source_target_pairs={{0,1},{1,0},{2,3},{3,2},{4,5},{5,4},{6,7},{7,6},{8,9},{9,8},{10,11... | collective-permute-start | bytes 95240 | tf_op jit(solution)/shard_map/ppermute | solution.py:32
  82.3 4.3 %collective-permute-start.34 = (f32[2,3968]{1,0:T(2,128)S(1)}, f32[2,3968]{1,0:T(2,128)S(1)}, u32[]{:S(2)}, u32[]{:S(2)}) collective-permute-start(f32[2,3968]{1,0:T(2,128)S(1)} %add.137), channel_id=1, source_target_pairs={{0,25},{1,24},{2,27},{3,26},{4,29},{5,28},{6,31},{7,30},{8,17},{9,... | collective-permute-start | bytes 95240 | tf_op jit(solution)/shard_map/ppermute | solution.py:32
  83.4 4.2 %collective-permute-start.33 = (f32[2,3968]{1,0:T(2,128)S(1)}, f32[2,3968]{1,0:T(2,128)S(1)}, u32[]{:S(2)}, u32[]{:S(2)}) collective-permute-start(f32[2,3968]{1,0:T(2,128)S(1)} %add.137), channel_id=1, source_target_pairs={{0,17},{1,16},{2,19},{3,18},{4,21},{5,20},{6,23},{7,22},{8,25},{9,... | collective-permute-start | bytes 95240 | tf_op jit(solution)/shard_map/ppermute | solution.py:32
  84.3 3.3 %collective-permute-start.32 = (f32[2,3968]{1,0:T(2,128)S(1)}, f32[2,3968]{1,0:T(2,128)S(1)}, u32[]{:S(2)}, u32[]{:S(2)}) collective-permute-start(f32[2,3968]{1,0:T(2,128)S(1)} %add.137), channel_id=1, source_target_pairs={{0,9},{1,8},{2,11},{3,10},{4,13},{5,12},{6,15},{7,14},{8,1},{9,0},... | collective-permute-start | bytes 95240 | tf_op jit(solution)/shard_map/ppermute | solution.py:32
  87.6 5.2 %collective-permute-start.37 = (f32[2,3968]{1,0:T(2,128)S(1)}, f32[2,3968]{1,0:T(2,128)S(1)}, u32[]{:S(2)}, u32[]{:S(2)}) collective-permute-start(f32[2,3968]{1,0:T(2,128)S(1)} %add_add_fusion.3), channel_id=1, source_target_pairs={{0,7},{1,6},{2,5},{3,4},{4,3},{5,2},{6,1},{7,0},{8,15},{9,14},{10,... | collective-permute-start | bytes 95240 | tf_op jit(solution)/shard_map/ppermute | solution.py:32
  89.0 5.5 %collective-permute-start.36 = (f32[2,3968]{1,0:T(2,128)S(1)}, f32[2,3968]{1,0:T(2,128)S(1)}, u32[]{:S(2)}, u32[]{:S(2)}) collective-permute-start(f32[2,3968]{1,0:T(2,128)S(1)} %add_add_fusion.3), channel_id=1, source_target_pairs={{0,5},{1,4},{2,7},{3,6},{4,1},{5,0},{6,3},{7,2},{8,13},{9,12},{10,... | collective-permute-start | bytes 95240 | tf_op jit(solution)/shard_map/ppermute | solution.py:32
  89.6 4.9 %collective-permute-start.35 = (f32[2,3968]{1,0:T(2,128)S(1)}, f32[2,3968]{1,0:T(2,128)S(1)}, u32[]{:S(2)}, u32[]{:S(2)}) collective-permute-start(f32[2,3968]{1,0:T(2,128)S(1)} %add_add_fusion.3), channel_id=1, source_target_pairs={{0,3},{1,2},{2,1},{3,0},{4,7},{5,6},{6,5},{7,4},{8,11},{9,10},{10,... | collective-permute-start | bytes 95240 | tf_op jit(solution)/shard_map/ppermute | solution.py:32
  96.7 4.6 %collective-permute-start.39 = (f32[8,256]{1,0:T(8,128)S(1)}, f32[8,256]{1,0:T(8,128)S(1)}, u32[]{:S(2)}, u32[]{:S(2)}) collective-permute-start(f32[8,256]{1,0:T(8,128)S(1)} %get-tuple-element.83.refs_7_), channel_id=1, source_target_pairs={{0,24},{1,25},{2,26},{3,27},{4,28},{5,29},{6,30},{7,31},{8,16},{9,... | collective-permute-start | bytes 24584 | tf_op jit(solution)/shard_map/ppermute | solution.py:60
  98.0 3.7 %collective-permute-start.38 = (f32[8,256]{1,0:T(8,128)S(1)}, f32[8,256]{1,0:T(8,128)S(1)}, u32[]{:S(2)}, u32[]{:S(2)}) collective-permute-start(f32[8,256]{1,0:T(8,128)S(1)} %get-tuple-element.83.refs_7_), channel_id=1, source_target_pairs={{0,8},{1,9},{2,10},{3,11},{4,12},{5,13},{6,14},{7,15},{8,0},{9,1},... | collective-permute-start | bytes 24584 | tf_op jit(solution)/shard_map/ppermute | solution.py:59
  104.1 1.3 %collective-permute-start.40 = (f32[2,3968]{1,0:T(2,128)S(1)}, f32[2,3968]{1,0:T(2,128)S(1)}, u32[]{:S(2)}, u32[]{:S(2)}) collective-permute-start(f32[2,3968]{1,0:T(2,128)S(1)} %get-tuple-element.84), channel_id=1, source_target_pairs={{0,1},{1,0},{2,3},{3,2},{4,5},{5,4},{6,7},{7,6},{8,9},{9,8},{10,11... | collective-permute-start | bytes 95240 | tf_op jit(solution)/shard_map/ppermute | solution.py:32
  105.4 4.3 %collective-permute-start.43 = (f32[2,3968]{1,0:T(2,128)S(1)}, f32[2,3968]{1,0:T(2,128)S(1)}, u32[]{:S(2)}, u32[]{:S(2)}) collective-permute-start(f32[2,3968]{1,0:T(2,128)S(1)} %add.144), channel_id=1, source_target_pairs={{0,25},{1,24},{2,27},{3,26},{4,29},{5,28},{6,31},{7,30},{8,17},{9,... | collective-permute-start | bytes 95240 | tf_op jit(solution)/shard_map/ppermute | solution.py:32
  106.9 3.5 %collective-permute-start.42 = (f32[2,3968]{1,0:T(2,128)S(1)}, f32[2,3968]{1,0:T(2,128)S(1)}, u32[]{:S(2)}, u32[]{:S(2)}) collective-permute-start(f32[2,3968]{1,0:T(2,128)S(1)} %add.144), channel_id=1, source_target_pairs={{0,17},{1,16},{2,19},{3,18},{4,21},{5,20},{6,23},{7,22},{8,25},{9,... | collective-permute-start | bytes 95240 | tf_op jit(solution)/shard_map/ppermute | solution.py:32
  107.9 3.3 %collective-permute-start.41 = (f32[2,3968]{1,0:T(2,128)S(1)}, f32[2,3968]{1,0:T(2,128)S(1)}, u32[]{:S(2)}, u32[]{:S(2)}) collective-permute-start(f32[2,3968]{1,0:T(2,128)S(1)} %add.144), channel_id=1, source_target_pairs={{0,9},{1,8},{2,11},{3,10},{4,13},{5,12},{6,15},{7,14},{8,1},{9,0},... | collective-permute-start | bytes 95240 | tf_op jit(solution)/shard_map/ppermute | solution.py:32
  111.3 5.2 %collective-permute-start.46 = (f32[2,3968]{1,0:T(2,128)S(1)}, f32[2,3968]{1,0:T(2,128)S(1)}, u32[]{:S(2)}, u32[]{:S(2)}) collective-permute-start(f32[2,3968]{1,0:T(2,128)S(1)} %add_add_fusion.1), channel_id=1, source_target_pairs={{0,7},{1,6},{2,5},{3,4},{4,3},{5,2},{6,1},{7,0},{8,15},{9,14},{10,... | collective-permute-start | bytes 95240 | tf_op jit(solution)/shard_map/ppermute | solution.py:32
  112.4 5.8 %collective-permute-start.45 = (f32[2,3968]{1,0:T(2,128)S(1)}, f32[2,3968]{1,0:T(2,128)S(1)}, u32[]{:S(2)}, u32[]{:S(2)}) collective-permute-start(f32[2,3968]{1,0:T(2,128)S(1)} %add_add_fusion.1), channel_id=1, source_target_pairs={{0,5},{1,4},{2,7},{3,6},{4,1},{5,0},{6,3},{7,2},{8,13},{9,12},{10,... | collective-permute-start | bytes 95240 | tf_op jit(solution)/shard_map/ppermute | solution.py:32
  113.2 4.9 %collective-permute-start.44 = (f32[2,3968]{1,0:T(2,128)S(1)}, f32[2,3968]{1,0:T(2,128)S(1)}, u32[]{:S(2)}, u32[]{:S(2)}) collective-permute-start(f32[2,3968]{1,0:T(2,128)S(1)} %add_add_fusion.1), channel_id=1, source_target_pairs={{0,3},{1,2},{2,1},{3,0},{4,7},{5,6},{6,5},{7,4},{8,11},{9,10},{10,... | collective-permute-start | bytes 95240 | tf_op jit(solution)/shard_map/ppermute | solution.py:32

commit v7 on v6

--- a/solution.py
+++ b/solution.py
@@ -136,14 +136,39 @@
     bit_ref[...] = jnp.left_shift(1, jnp.sum(word, axis=0, keepdims=True))
 
 
+def fill_spread_days(spread_ref):
+    days = spread_ref.shape[0]
+    rest = lax.broadcasted_iota(jnp.int32, (days, LANES), 0) - BITS * lane_ids((days, LANES))
+    hit = jnp.where((rest >= 0) & (rest < BITS), 1.0, 0.0).astype(BF16)
+    spread_ref[:, :LANES] = hit
+    spread_ref[:, LANES:] = hit
+
+
+def unpack_days(words, spread_ref, m_ref):
+    days = spread_ref.shape[0]
+    step = days // 5
+    for g in range(words.shape[1] // LANES):
+        group = words[:, g * LANES : (g + 1) * LANES]
+        top = ((group >> 8) << 8).astype(F32).astype(BF16)
+        bottom = (group & 255).astype(F32).astype(BF16)
+        both = jnp.concatenate([top, bottom], axis=1)
+        for first in range(0, days, step):
+            each = lax.dot_general(spread_ref[first : first + step], both, NT, preferred_element_type=F32).astype(jnp.int32)
+            day = first + lax.broadcasted_iota(jnp.int32, (step, LANES), 0)
+            bit = jnp.left_shift(1, day - BITS * ((day * 34953) >> 19))
+            for c in range(0, each.shape[1], LANES):
+                flags = jnp.where((each[:, c : c + LANES] & bit) == 0, 1.0, 0.0).astype(BF16)
+                m_ref[g * days + first : g * days + first + step, c : c + LANES] = flags
+
+
 def as_column(row):
     return jnp.transpose(jnp.broadcast_to(row, (8, LANES)))[:, :1]
 
 
 def own_flags_kernel(reach, *refs):
     words_hbm, coast_hbm, x_hbm, maps_hbm, series_hbm, place_ref = refs[:6]
-    m_ref, a_ref, u_ref, row_ref, near_ref, far_ref, maps_out, series_out = refs[6:14]
-    words_ref, coast_ref, x_ref, maps_ref, series_ref, spread_ref, bit_ref, sems = refs[14:]
+    m_ref, a_ref, mt_ref, spread_days_ref, u_ref, row_ref, near_ref, far_ref, maps_out, series_out = refs[6:16]
+    words_ref, coast_ref, x_ref, maps_ref, series_ref, spread_ref, bit_ref, sems = refs[16:]
     rows = coast_ref.shape[0]
     loads = [
         pltpu.make_async_copy(words_hbm, words_ref, sems.at[0]),
@@ -161,8 +186,12 @@
     for load in loads:
         load.start()
     fill_spread(spread_ref, bit_ref)
+    fill_spread_days(spread_days_ref)
     loads[0].wait()
     loads[1].wait()
+    for load, store in zip(loads[-2:], stores, strict=True):
+        load.wait()
+        store.start()
     days = spread_ref.shape[1]
     coast_own = coast_ref[...].astype(F32)
     coasts = jnp.transpose(jnp.concatenate([coast_own] * (8 // rows), axis=0))
@@ -178,9 +207,8 @@
             at = slice(g * days, (g + 1) * days)
             m_ref[cell, at] = given
             a_ref[cell, at] = x_ref[cell, at] * given * ocean
-    for load, store in zip(loads[-2:], stores, strict=True):
-        load.wait()
-        store.start()
+    column = jnp.concatenate([coasts[:, r : r + 1] for r in range(rows)], axis=0).astype(jnp.int32)
+    unpack_days(words_ref[...] * column, spread_days_ref, mt_ref)
     modes = maps_ref.shape[0]
     pieces = []
     for r in range(rows):
@@ -220,20 +248,23 @@
     return west, east
 
 
-def given_kernel(rows, reach, *refs):
-    a_ref, place_ref = refs[:2]
-    pieces = [ref[...] for ref in refs[2:-4]]
-    v_ref, xv_ref, near_ref, far_ref = refs[-4:]
-    here = place_ref[3]
+def in_order(pieces, here):
     bit = 1
     while bit < len(pieces):
         turn = (here // bit) % 2 == 1
         pieces = [jnp.where(turn, pieces[i ^ bit], pieces[i]) for i in range(len(pieces))]
         bit *= 2
-    share = pieces[0].shape[1]
-    for i, piece in enumerate(pieces):
+    return pieces
+
+
+def given_kernel(rows, reach, *refs):
+    a_ref, place_ref = refs[:2]
+    xv_ref, near_ref, far_ref, v_ref = refs[-4:]
+    here = place_ref[3]
+    share = refs[2].shape[1]
+    for i, piece in enumerate(in_order([ref[:PAIRS] for ref in refs[2:-4]], here)):
         v_ref[:, i * share : (i + 1) * share] = piece
-    high, low = split(v_ref[:PAIRS])
+    high, low = split(v_ref[...])
     both = lax.dot_general(jnp.concatenate([high, low], axis=0), a_ref[...], NT, preferred_element_type=F32)
     xv = both[:PAIRS] + both[PAIRS:]
     xv_ref[...] = xv
@@ -251,7 +282,7 @@
         v = vs[:, at]
         high, lower = split(jnp.concatenate([v * v[j : j + 1] for j in (low, low + 1)], axis=0))
         left = jnp.concatenate([high, lower], axis=0)
-        part = lax.dot_general(left, m_ref[:, at], NT, preferred_element_type=F32)
+        part = jnp.dot(left, m_ref[at], preferred_element_type=F32)
         acc = part if acc is None else acc + part
     acc = acc[: 2 * modes] + acc[2 * modes :]
     return jnp.concatenate(
@@ -260,9 +291,11 @@
 
 
 def first_products_kernel(chunk, *refs):
-    near_ref, far_ref, place_ref, m_ref, v_ref, u_own_ref, row_own_ref = refs[:7]
-    base_ref, mh_ref, u_ref, row_ref, spread_ref, bit_ref = refs[7:]
-    fill_spread(spread_ref, bit_ref)
+    near_ref, far_ref, place_ref, m_ref, spread_ref, u_own_ref, row_own_ref = refs[:7]
+    base_ref, v_ref, mh_ref, u_ref, row_ref = refs[-5:]
+    share = refs[7].shape[1]
+    for i, piece in enumerate(in_order([ref[...] for ref in refs[7:-5]], place_ref[3])):
+        v_ref[:, i * share : (i + 1) * share] = piece
     odd = place_ref[3] % 2 == 1
     west = jnp.where(odd, near_ref[...], far_ref[...])
     east = jnp.where(odd, far_ref[...], near_ref[...])
@@ -276,14 +309,35 @@
     row_ref[:, :own] = row_own_ref[...]
     row_ref[:, own:] = row_halo
     coast = as_column(row_halo).astype(jnp.int32)
-    days = spread_ref.shape[1]
     half = LANES // 2
-    for g in range(mh_ref.shape[1] // days):
-        at = slice(base + half * g, base + half * (g + 1))
-        words = jnp.concatenate([west[at], east[at]], axis=0).astype(jnp.int32) * coast
-        mh_ref[:, g * days : (g + 1) * days] = unpack_words(words, spread_ref, bit_ref)
+    groups = [slice(base + half * g, base + half * (g + 1)) for g in range((west.shape[0] - base) // half)]
+    words = jnp.concatenate([jnp.concatenate([west[at], east[at]], axis=0) for at in groups], axis=1)
+    unpack_days(words.astype(jnp.int32) * coast, spread_ref, mh_ref)
     base_ref[:, :own] = masked_products(v_ref, u_own, 0, chunk, m_ref)
     base_ref[:, own:] = masked_products(v_ref, u_halo, 0, chunk, mh_ref)
+
+
+def next_products_kernel(step, chunk, m_ref, mh_ref, v_ref, u_ref, base_ref):
+    low = 2 * step
+    own = m_ref.shape[1]
+    mode = lax.broadcasted_iota(jnp.int32, u_ref.shape, 0)
+    u = jnp.where((mode >= low - 2) & (mode < low), 0.0, u_ref[...])
+    base_ref[:, :own] = masked_products(v_ref, u[:, :own], low, chunk, m_ref)
+    base_ref[:, own:] = masked_products(v_ref, u[:, own:], low, chunk, mh_ref)
+
+
+def changed_products(vn, un, pair, m_ref, mh_ref):
+    high, lower = split(jnp.concatenate([vn * pair[0:1], vn * pair[1:2]], axis=0))
+    left = jnp.concatenate([high, lower], axis=0)
+    acc = jnp.concatenate(
+        [
+            jnp.dot(left, m_ref[...], preferred_element_type=F32),
+            jnp.dot(left, mh_ref[...], preferred_element_type=F32),
+        ],
+        axis=1,
+    )
+    acc = acc[:4] + acc[4:]
+    return jnp.concatenate([un[0:1] * acc[2 * j : 2 * j + 1] + un[1:2] * acc[2 * j + 1 : 2 * j + 2] for j in range(2)], axis=0)
 
 
 def new_fields(pair, u_pair, coast, proj):
@@ -306,17 +360,18 @@
     w_ref[count:] = to_block(jnp.concatenate([coast, coast], axis=0), rows, reach)
 
 
-def fields_kernel(step, rows, reach, total, chunk, *refs):
-    m_ref, mh_ref, v_ref, u_ref, row_ref, xv_ref, xh_ref, sum_ref, block_ref, w_ref, vs, us = refs
+def fields_kernel(step, rows, reach, total, *refs):
+    m_ref, mh_ref, v_ref, u_ref, row_ref, xv_ref, xh_ref, base_ref, sum_ref, block_ref, w_ref, v_out, u_out = refs
     low = 2 * step
-    own = rows * LANES
-    vs[...] = v_ref[...]
-    us[...] = u_ref[...]
-    vs[low - 2 : low], us[low - 2 : low] = new_pair(rows, reach, total, sum_ref, block_ref)
-    mid = xv_ref[low : low + 2] - masked_products(vs, us[:, :own], low, chunk, m_ref)
-    edge = xh_ref[low : low + 2] - masked_products(vs, us[:, own:], low, chunk, mh_ref)
-    proj = jnp.concatenate([mid, edge], axis=1)
-    w_ref[...] = to_block(new_fields(vs[low : low + 2], us[low : low + 2], row_ref[...], proj), rows, reach)
+    vn, un = new_pair(rows, reach, total, sum_ref, block_ref)
+    pair = v_ref[low : low + 2]
+    given = jnp.concatenate([xv_ref[low : low + 2], xh_ref[low : low + 2]], axis=1)
+    proj = given - base_ref[...] - changed_products(vn, un, pair, m_ref, mh_ref)
+    w_ref[...] = to_block(new_fields(pair, u_ref[low : low + 2], row_ref[...], proj), rows, reach)
+    v_out[...] = v_ref[...]
+    u_out[...] = u_ref[...]
+    v_out[low - 2 : low] = vn
+    u_out[low - 2 : low] = un
 
 
 def new_pair(rows, reach, total, sum_ref, block_ref):
@@ -336,12 +391,12 @@
 
 
 def sums_kernel(step, rows, chunk, *refs):
-    m_ref, a_ref, v_ref, u_ref, place_ref, klon_ref, cosl_ref, w_ref, ga_ref, gb_ref = refs[:10]
+    m_ref, a_ref, v_ref, u_ref, place_ref, klon_ref, cosl_ref, w_ref, gb_ref, ga_ref = refs[:10]
     refs = refs[10:]
     if step:
-        cw_ref, ca_ref, cb_ref = refs[:3]
-        refs = refs[3:]
-    sum_ref, block_ref = refs
+        coef_ref, sum_ref, block_ref = refs
+    else:
+        sum_ref, block_ref, coef_ref = refs
     days = v_ref.shape[1]
     low = 2 * step
     own = rows * LANES
@@ -353,21 +408,22 @@
         return jnp.concatenate([jnp.where(is_odd, a, b), mid, jnp.where(is_odd, b, a)], axis=0)
 
     w = assemble(w_ref[:count], ga_ref[:count], gb_ref[:count])
-    if step:
-        coast = assemble(cw_ref[count:], ca_ref[count:], cb_ref[count:])
-    else:
-        coast = assemble(w_ref[count:], ga_ref[count:], gb_ref[count:])
     tall = 3 * count
-    row = row0 - rows + lax.broadcasted_iota(jnp.int32, (tall, 2 * LANES), 0) // 2
-    coast = jnp.where((row >= 0) & (row < nlat), coast, 0.0)
     north = lambda z: pltpu.roll(z, 2, 0)
     south = lambda z: pltpu.roll(z, tall - 2, 0)
     west = lambda z: pltpu.roll(z, 1, 1)
     east = lambda z: pltpu.roll(z, 2 * LANES - 1, 1)
-    klon = klon_ref[...] * coast
-    klat = KLAT * coast
-    an, as_, aw, ae = (klat * north(coast), klat * south(coast), klon * west(coast), klon * east(coast))
-    stay = 1.0 - (an + as_ + aw + ae)
+    if step == 0:
+        coast = assemble(w_ref[count:], ga_ref[count:], gb_ref[count:])
+        row = row0 - rows + lax.broadcasted_iota(jnp.int32, (tall, 2 * LANES), 0) // 2
+        coast = jnp.where((row >= 0) & (row < nlat), coast, 0.0)
+        klon = klon_ref[...] * coast
+        klat = KLAT * coast
+        parts = [klat * north(coast), klat * south(coast), klon * west(coast), klon * east(coast)]
+        parts.append(1.0 - ((parts[0] + parts[1]) + (parts[2] + parts[3])))
+        for i, part in enumerate(parts):
+            coef_ref[i * tall : (i + 1) * tall] = part
+    an, as_, aw, ae, stay = (coef_ref[i * tall : (i + 1) * tall] for i in range(5))
     for _ in range(SWEEPS):
         w = stay * w + (an * north(w) + as_ * south(w)) + (aw * west(w) + ae * east(w))
     block = w[count : 2 * count]
@@ -471,51 +527,52 @@
     inputs = [missing_date_bitmask.reshape(own, words), ocean_binary_mask, sea_heat_deviations.reshape(own, days)]
     inputs += [mode_maps, mode_series]
     place, klon, cosl = lax.optimization_barrier((place, klon, cosl))
-    m, a, u, row, near, far, maps_out, series_out = call(
+    m, a, m_days, spread, u, row, near, far, maps_out, series_out = call(
         functools.partial(own_flags_kernel, reach),
         "own_flags",
-        [((own, days), BF16), ((own, days), BF16), ((modes, own), F32), ((1, own), F32), edge, edge]
+        [((own, days), BF16), ((own, days), BF16), ((days, own), BF16), ((days // words_per, 2 * LANES), BF16)]
+        + [((modes, own), F32), ((1, own), F32), edge, edge]
         + [(mode_maps.shape, F32), (mode_series.shape, F32)],
         [((own, words), jnp.int32), ((rows, LANES), jnp.int32), ((own, days), BF16)]
         + [(mode_maps.shape, F32), (mode_series.shape, F32), *flags_scratch],
         [*inputs, place],
         smem=(5,),
         in_hbm=range(5),
-        out_hbm=(6, 7),
+        out_hbm=(8, 9),
         copies=6 + rows,
         flops=4 * LANES * own * days,
     )
     if lax.axis_size("lon") == 8:
         pieces = [swap(mode_series, 0, b | 1) for b in (2, 4, 6)]
-        *pieces, m, a = lax.optimization_barrier((*pieces, m, a))
+        *pieces, m, a, m_days = lax.optimization_barrier((*pieces, m, a, m_days))
         pieces = [z for piece in pieces for z in (swap(piece, 0, 1), piece)]
         pieces = [mode_series, swap(mode_series, 0, 1), *pieces]
     else:
         pieces = [lax.all_gather(mode_series, "lon", axis=1, tiled=True)]
     near, far = lon_partners(near, far)
-    v, xv, near_xv, far_xv = call(
+    xv, near_xv, far_xv = call(
         functools.partial(given_kernel, rows, reach),
         "given",
-        [((modes, days), F32), ((PAIRS, own), F32), ((PAIRS, LANES), F32), ((PAIRS, LANES), F32)],
-        [],
+        [((PAIRS, own), F32), ((PAIRS, LANES), F32), ((PAIRS, LANES), F32)],
+        [((PAIRS, days), F32)],
         [a, place, *pieces],
         smem=(1,),
         flops=4 * PAIRS * own * days,
     )
     near_xv, far_xv = lon_partners(near_xv, far_xv)
-    base, m_halo, u, row = call(
+    base, v, m_halo, u, row = call(
         functools.partial(first_products_kernel, chunk),
         "first_products",
-        [((2, cells), F32), ((sides, days), BF16), ((modes, cells), F32), ((1, cells), F32)],
-        flags_scratch,
-        [near, far, place, m, v, u, row],
+        [((2, cells), F32), ((modes, days), F32), ((days, sides), BF16), ((modes, cells), F32), ((1, cells), F32)],
+        [],
+        [near, far, place, m_days, spread, u, row, *pieces],
         smem=(2,),
         flops=8 * modes * cells * days,
     )
 
     count = 2 * rows
     summed = block = None
-    coasts = ()
+    coefs = []
     for step in range(STEPS):
         if step == 0:
             fresh, xv_halo = call(
@@ -528,25 +585,35 @@
             )
         else:
             fresh, v, u = call(
-                functools.partial(fields_kernel, step, rows, reach, total, chunk),
+                functools.partial(fields_kernel, step, rows, reach, total),
                 f"fields_{step}",
                 [((count, 2 * LANES), F32), ((modes, days), F32), ((modes, cells), F32)],
                 [],
-                [m, m_halo, v, u, row, xv, xv_halo, summed, block],
+                [m_days, m_halo, v, u, row, xv, xv_halo, base, summed, block],
                 flops=8 * modes * cells * days,
             )
         got_a, got_b = lat_partners(fresh)
-        partial_sums, block = call(
+        outs = [((2, days + LANES), F32), ((count, 2 * LANES), F32)]
+        coef = ((5 * 3 * count, 2 * LANES), F32)
+        partial_sums, block, *made = call(
             functools.partial(sums_kernel, step, rows, chunk),
             f"sums_{step}",
-            [((2, days + LANES), F32), ((count, 2 * LANES), F32)],
+            outs if step else [*outs, coef],
             [],
-            [m, a, v, u, place, klon, cosl, fresh, got_a, got_b, *coasts],
+            [m, a, v, u, place, klon, cosl, fresh, got_b, got_a, *coefs],
             smem=(4,),
             flops=8 * modes * own * days,
         )
-        if step == 0:
-            coasts = (fresh, got_a, got_b)
+        coefs = coefs or made
+        if step + 1 < STEPS:
+            (base,) = call(
+                functools.partial(next_products_kernel, step + 1, chunk),
+                f"next_products_{step + 1}",
+                [((2, cells), F32)],
+                [],
+                [m_days, m_halo, v, u],
+                flops=8 * modes * cells * days,
+            )
         summed = sum_all(partial_sums)
     return call(
         functools.partial(last_kernel, rows, reach, total),

time: 121 us -> 117 us (0.967)
  waiting for transfers between devices: 40.1 us -> 36.1 us
  Pallas kernels: 29.3 us -> 32.5 us
  starting transfers between devices: 49.4 us -> 46.5 us
    ppermute x37, waiting for transfers between devices: 28.6 us -> 23 us  [swap(): lax.ppermute(x, ('lat', 'lon'), pairing(lambda i: i ^ lat_bits, lambda j:...]
    pallas_call x12 -> x15, Pallas kernels: 29.3 us -> 32.5 us  [call(): pl.pallas_call(kernel, out_shape=[jax.ShapeDtypeStruct(s, t) for s, t in...]
    ppermute x37, starting transfers between devices: 34.9 us -> 31.9 us  [swap(): lax.ppermute(x, ('lat', 'lon'), pairing(lambda i: i ^ lat_bits, lambda j:...]
    ppermute x4, starting transfers between devices: 3.9 us -> 2.53 us  [lat_partners(): got_a = lax.ppermute(x, ('lat', 'lon'), pairing(lambda i: i ^ 1, same))]
  transfers between devices with their start and end apart: 47 -> 47, of which waited for: 33 -> 33; matrix products, arithmetic and copies ran while one was open for 0% -> 0% of each run, Pallas kernels for 8% -> 14%
where the time goes in v7:
time: 117 us
  starting transfers between devices  46.5 us (40%)
  waiting for transfers between devices  36.1 us (31%)
  Pallas kernels  32.5 us (28%)
    pallas_call x15, Pallas kernels, call(): pl.pallas_call(kernel, out_shape=[jax.ShapeDtypeStruct(s, t) for s, t in...  32.5 us
    ppermute x37, starting transfers between devices, swap(): lax.ppermute(x, ('lat', 'lon'), pairing(lambda i: i ^ lat_bits, lambda j:...  31.9 us
    ppermute x37, waiting for transfers between devices, swap(): lax.ppermute(x, ('lat', 'lon'), pairing(lambda i: i ^ lat_bits, lambda j:...  23 us
    ppermute x4, waiting for transfers between devices, lat_partners(): lax.ppermute(x, ('lat', 'lon'), pairing(lambda i: (i + 1 if i % 2 else i...  8.64 us
    ppermute x4, starting transfers between devices, lat_partners(): lax.ppermute(x, ('lat', 'lon'), pairing(lambda i: (i + 1 if i % 2 else i...  7.28 us
    ppermute x2, starting transfers between devices, lon_partners(): lax.ppermute(far, ('lat', 'lon'), pairing(same, lambda j: (j + 1 if j % 2...  4.72 us
    ppermute x4, waiting for transfers between devices, lat_partners(): got_a = lax.ppermute(x, ('lat', 'lon'), pairing(lambda i: i ^ 1, same))  3.52 us
    ppermute x4, starting transfers between devices, lat_partners(): got_a = lax.ppermute(x, ('lat', 'lon'), pairing(lambda i: i ^ 1, same))  2.53 us
  transfers between devices with their start and end apart: 47, of which 33 were waited for; matrix products, arithmetic and copies ran while one was open for 0% of the time, Pallas kernels for 14%

profile of v7, /device:TPU:0, one launch (start us, length us, event | category | flops | bytes accessed | tf_op | source)
XLA Modules:
  0.0 116.7 jit_solution(16786070238364249769)
XLA Ops:
  0.6 2.5 %collective-permute-start = (f32[48,480]{1,0:T(8,128)}, f32[48,480]{1,0:T(8,128)S(1)}, u32[]{:S(2)}, u32[]{:S(2)}) collective-permute-start(f32[48,480]{1,0:T(8,128)} %refs_2_.1), channel_id=1, source_target_pairs={{0,3},{1,2},{2,1},{3,0},{4,7},{5,6},{6,5},{7,4},{8,11},{9,10},{10,... | collective-permute-start | bytes 276488 | tf_op jit(solution)/shard_map/ppermute | solution.py:32
  3.2 2.9 %collective-permute-start.1 = (f32[48,480]{1,0:T(8,128)}, f32[48,480]{1,0:T(8,128)S(1)}, u32[]{:S(2)}, u32[]{:S(2)}) collective-permute-start(f32[48,480]{1,0:T(8,128)} %refs_2_.1), channel_id=1, source_target_pairs={{0,5},{1,4},{2,7},{3,6},{4,1},{5,0},{6,3},{7,2},{8,13},{9,12},{10,... | collective-permute-start | bytes 276488 | tf_op jit(solution)/shard_map/ppermute | solution.py:32
  6.4 7.7 %own_flags.1 = (bf16[512,3840]{1,0:T(8,128)(2,1)S(1)}, bf16[512,3840]{1,0:T(8,128)(2,1)S(1)}, bf16[3840,512]{1,0:T(8,128)(2,1)S(1)}, bf16[1920,256]{1,0:T(8,128)...) custom-call(s32[512,256]{1,0:T(8,128)} %bitcast.6, ...), custom_call_target="tpu_custom_call" | custom-call | flops 1006632960 | bytes 4648976 | tf_op jit(solution)/shard_map/own_flags/pallas_call | solution.py:488
  15.3 3.5 %collective-permute-start.4 = (f32[184,128]{1,0:T(8,128)S(1)}, f32[184,128]{1,0:T(8,128)S(1)}, u32[]{:S(2)}, u32[]{:S(2)}) collective-permute-start(f32[184,128]{1,0:T(8,128)S(1)} %get-tuple-element.55), channel_id=1, source_target_pairs={{0,7},{1,2},{2,1},{3,4},{4,3},{5,6},{6,5},{7,0},{8,15},{9,10},{10,... | collective-permute-start | bytes 282632 | tf_op jit(solution)/shard_map/ppermute | solution.py:67
  18.8 1.7 %given.1 = (f32[8,512]{1,0:T(8,128)S(1)}, f32[8,128]{1,0:T(8,128)S(1)}, f32[8,128]{1,0:T(8,128)S(1)}) custom-call(bf16[512,3840]{1,0:T(8,128)(2,1)S(1)} %get-tuple-element.66.refs_0_.refs_1_, s32[4]{0:T(128)S(1)} %pad_add_fusion.refs_5_.refs_2_.refs_1_.place_ref.refs_4_, f32[48,480]{1,0:T(8,128)S(1)} %copy-done, ...), custom_call_target="tpu_custom_call" | custom-call | flops 62914560 | bytes 4669456 | tf_op jit(solution)/shard_map/given/pallas_call | solution.py:488
  20.6 1.2 %collective-permute-start.10 = (f32[8,128]{1,0:T(8,128)S(1)}, f32[8,128]{1,0:T(8,128)S(1)}, u32[]{:S(2)}, u32[]{:S(2)}) collective-permute-start(f32[8,128]{1,0:T(8,128)S(1)} %get-tuple-element.69), channel_id=1, source_target_pairs={{0,7},{1,2},{2,1},{3,4},{4,3},{5,6},{6,5},{7,0},{8,15},{9,10},{10,... | collective-permute-start | bytes 12296 | tf_op jit(solution)/shard_map/ppermute | solution.py:67
  21.8 2.8 %first_products.1 = (f32[2,640]{1,0:T(2,128)S(1)}, f32[48,3840]{1,0:T(8,128)S(1)}, bf16[3840,128]{1,0:T(8,128)(2,1)S(1)}, f32[48,640]{1,0:T(8,128)S(1)}, f32[1,640]{1,0:T(1,128)S(1)}) custom-call(f32[184,128]{1,0:T(8,128)S(1)} %collective-permute-done.3.refs_0_, f32[184,128]{1,0:T(8,128)S(1)} %collective-permute-done.4.refs_1_, ...), custom_call_target="tpu_custom_call" | custom-call | flops 943718400 | bytes 5941264 | tf_op jit(solution)/shard_map/first_products/pallas_call | solution.py:488
  24.6 0.9 collective-permute-done.10.far_ref
  25.5 0.8 fields_0.1
  26.3 2.5 %collective-permute-start.11 = (f32[16,256]{1,0:T(8,128)S(1)}, f32[16,256]{1,0:T(8,128)S(1)}, u32[]{:S(2)}, u32[]{:S(2)}) collective-permute-start(f32[16,256]{1,0:T(8,128)S(1)} %get-tuple-element.75.refs_7_), channel_id=1, source_target_pairs={{0,24},{1,25},{2,26},{3,27},{4,28},{5,29},{6,30},{7,31},{8,16},{9,... | collective-permute-start | bytes 49160 | tf_op jit(solution)/shard_map/ppermute | solution.py:60
  29.4 1.6 %collective-permute-done.11.refs_8_ = f32[16,256]{1,0:T(8,128)S(1)} collective-permute-done((f32[16,256]{1,0:T(8,128)S(1)}, f32[16,256]{1,0:T(8,128)S(1)}, u32[]{:S(2)}, u32[]{:S(2)}) %collective-permute-start.11) | collective-permute-done | bytes 16416 | tf_op jit(solution)/shard_map/ppermute | solution.py:60
  31.0 1.5 %collective-permute-done.12.refs_9_ = f32[16,256]{1,0:T(8,128)S(1)} collective-permute-done((f32[16,256]{1,0:T(8,128)S(1)}, f32[16,256]{1,0:T(8,128)S(1)}, u32[]{:S(2)}, u32[]{:S(2)}) %collective-permute-start.12) | collective-permute-done | bytes 16416 | tf_op jit(solution)/shard_map/ppermute | solution.py:59
  32.6 2.4 %sums_0.1 = (f32[2,3968]{1,0:T(2,128)S(1)}, f32[8,256]{1,0:T(8,128)S(1)}, f32[120,256]{1,0:T(8,128)S(1)}) custom-call(bf16[512,3840]{1,0:T(8,128)(2,1)S(1)} %get-tuple-element.72.refs_0_, bf16[512,3840]{1,0:T(8,128)(2,1)S(1)} %get-tuple-element.66.refs_0_.refs_1_, f32[48,3840]{1,0:T(8,128)S(1)} %get-tuple-element.63.v_ref.refs_2_, ...), custom_call_target="tpu_custom_call" | custom-call | flops 754974720 | bytes 8806416 | tf_op jit(solution)/shard_map/sums_0/pallas_call | solution.py:488
  35.1 1.2 %collective-permute-done.13 = f32[2,3968]{1,0:T(2,128)S(1)} collective-permute-done((f32[2,3968]{1,0:T(2,128)S(1)}, f32[2,3968]{1,0:T(2,128)S(1)}, u32[]{:S(2)}, u32[]{:S(2)}) %collective-permute-start.13) | collective-permute-done | bytes 31776 | tf_op jit(solution)/shard_map/ppermute | solution.py:32
  36.6 1.5 %collective-permute-start.16 = (f32[2,3968]{1,0:T(2,128)S(1)}, f32[2,3968]{1,0:T(2,128)S(1)}, u32[]{:S(2)}, u32[]{:S(2)}) collective-permute-start(f32[2,3968]{1,0:T(2,128)S(1)} %add.123), channel_id=1, source_target_pairs={{0,25},{1,24},{2,27},{3,26},{4,29},{5,28},{6,31},{7,30},{8,17},{9,... | collective-permute-start | bytes 95240 | tf_op jit(solution)/shard_map/ppermute | solution.py:32
  38.1 1.2 %collective-permute-start.14 = (f32[2,3968]{1,0:T(2,128)S(1)}, f32[2,3968]{1,0:T(2,128)S(1)}, u32[]{:S(2)}, u32[]{:S(2)}) collective-permute-start(f32[2,3968]{1,0:T(2,128)S(1)} %add.123), channel_id=1, source_target_pairs={{0,9},{1,8},{2,11},{3,10},{4,13},{5,12},{6,15},{7,14},{8,1},{9,0},... | collective-permute-start | bytes 95240 | tf_op jit(solution)/shard_map/ppermute | solution.py:32
  39.7 1.2 %collective-permute-done.16 = f32[2,3968]{1,0:T(2,128)S(1)} collective-permute-done((f32[2,3968]{1,0:T(2,128)S(1)}, f32[2,3968]{1,0:T(2,128)S(1)}, u32[]{:S(2)}, u32[]{:S(2)}) %collective-permute-start.16) | collective-permute-done | bytes 31776 | tf_op jit(solution)/shard_map/ppermute | solution.py:32
  40.8 0.9 collective-permute-done.14
  41.8 2.1 %collective-permute-start.19 = (f32[2,3968]{1,0:T(2,128)S(1)}, f32[2,3968]{1,0:T(2,128)S(1)}, u32[]{:S(2)}, u32[]{:S(2)}) collective-permute-start(f32[2,3968]{1,0:T(2,128)S(1)} %add_add_fusion.7), channel_id=1, source_target_pairs={{0,7},{1,6},{2,5},{3,4},{4,3},{5,2},{6,1},{7,0},{8,15},{9,14},{10,... | collective-permute-start | bytes 95240 | tf_op jit(solution)/shard_map/ppermute | solution.py:32
  44.0 0.8 collective-permute-start.17
  44.8 1.4 %next_products_1.1.refs_7_ = f32[2,640]{1,0:T(2,128)S(1)} custom-call(bf16[3840,512]{1,0:T(8,128)(2,1)S(1)} %get-tuple-element.53.refs_3_.m_ref.refs_0_, bf16[3840,128]{1,0:T(8,128)(2,1)S(1)} %get-tuple-element.62.mh_ref.refs_1_, f32[48,3840]{1,0:T(8,128)S(1)} %get-tuple-element.63.v_ref.refs_2_, f32[48,640]{1,0:T(8,128)S(1)} %get-tuple-element.64.u_ref.refs_3_), custom_call_target="tpu_custom_call" | custom-call | flops 943718400 | bytes 5775360 | tf_op jit(solution)/shard_map/next_products_1/pallas_call | solution.py:488
  47.1 1.0 collective-permute-done.17
  48.1 1.3 %fields_1.1 = (f32[8,256]{1,0:T(8,128)S(1)}, f32[48,3840]{1,0:T(8,128)S(1)}, f32[48,640]{1,0:T(8,128)S(1)}) custom-call(bf16[3840,512]{1,0:T(8,128)(2,1)S(1)} %get-tuple-element.53.refs_3_.m_ref.refs_0_, bf16[3840,128]{1,0:T(8,128)(2,1)S(1)} %get-tuple-element.62.mh_ref.refs_1_, f32[48,3840]{1,0:T(8,128)S(1)} %get-tuple-element.63.v_ref.refs_2_, ...), custom_call_target="tpu_custom_call" | custom-call | flops 943718400 | bytes 5843456 | tf_op jit(solution)/shard_map/fields_1/pallas_call | solution.py:488
  49.4 1.1 collective-permute-start.20
  51.1 2.9 %collective-permute-done.20.refs_8_ = f32[8,256]{1,0:T(8,128)S(1)} collective-permute-done((f32[8,256]{1,0:T(8,128)S(1)}, f32[8,256]{1,0:T(8,128)S(1)}, u32[]{:S(2)}, u32[]{:S(2)}) %collective-permute-start.20) | collective-permute-done | bytes 8224 | tf_op jit(solution)/shard_map/ppermute | solution.py:60
  54.2 2.4 %sums_1.1 = (f32[2,3968]{1,0:T(2,128)S(1)}, f32[8,256]{1,0:T(8,128)S(1)}) custom-call(bf16[512,3840]{1,0:T(8,128)(2,1)S(1)} %get-tuple-element.72.refs_0_, bf16[512,3840]{1,0:T(8,128)(2,1)S(1)} %get-tuple-element.66.refs_0_.refs_1_, f32[48,3840]{1,0:T(8,128)S(1)} %get-tuple-element.78.v_ref.refs_2_, f32[48,640]{1,0:T(8,128)S(1)} %get-tuple-element.79.u_ref.refs_3_, ...), custom_call_target="tpu_custom_call" | custom-call | flops 754974720 | bytes 8904720 | tf_op jit(solution)/shard_map/sums_1/pallas_call | solution.py:488
  56.6 1.2 %collective-permute-done.22 = f32[2,3968]{1,0:T(2,128)S(1)} collective-permute-done((f32[2,3968]{1,0:T(2,128)S(1)}, f32[2,3968]{1,0:T(2,128)S(1)}, u32[]{:S(2)}, u32[]{:S(2)}) %collective-permute-start.22) | collective-permute-done | bytes 31776 | tf_op jit(solution)/shard_map/ppermute | solution.py:32
  57.9 1.4 %collective-permute-start.24 = (f32[2,3968]{1,0:T(2,128)S(1)}, f32[2,3968]{1,0:T(2,128)S(1)}, u32[]{:S(2)}, u32[]{:S(2)}) collective-permute-start(f32[2,3968]{1,0:T(2,128)S(1)} %add.130), channel_id=1, source_target_pairs={{0,17},{1,16},{2,19},{3,18},{4,21},{5,20},{6,23},{7,22},{8,25},{9,... | collective-permute-start | bytes 95240 | tf_op jit(solution)/shard_map/ppermute | solution.py:32
  59.2 0.9 collective-permute-start.25
  60.1 0.8 collective-permute-start.23
  61.3 2.2 %collective-permute-done.25 = f32[2,3968]{1,0:T(2,128)S(1)} collective-permute-done((f32[2,3968]{1,0:T(2,128)S(1)}, f32[2,3968]{1,0:T(2,128)S(1)}, u32[]{:S(2)}, u32[]{:S(2)}) %collective-permute-start.25) | collective-permute-done | bytes 31776 | tf_op jit(solution)/shard_map/ppermute | solution.py:32
  63.5 1.0 collective-permute-start.27
  64.5 1.5 %collective-permute-start.28 = (f32[2,3968]{1,0:T(2,128)S(1)}, f32[2,3968]{1,0:T(2,128)S(1)}, u32[]{:S(2)}, u32[]{:S(2)}) collective-permute-start(f32[2,3968]{1,0:T(2,128)S(1)} %add_add_fusion.5), channel_id=1, source_target_pairs={{0,7},{1,6},{2,5},{3,4},{4,3},{5,2},{6,1},{7,0},{8,15},{9,14},{10,... | collective-permute-start | bytes 95240 | tf_op jit(solution)/shard_map/ppermute | solution.py:32
  66.1 0.8 collective-permute-start.26
  66.8 1.3 %next_products_2.1.refs_7_ = f32[2,640]{1,0:T(2,128)S(1)} custom-call(bf16[3840,512]{1,0:T(8,128)(2,1)S(1)} %get-tuple-element.53.refs_3_.m_ref.refs_0_, bf16[3840,128]{1,0:T(8,128)(2,1)S(1)} %get-tuple-element.62.mh_ref.refs_1_, f32[48,3840]{1,0:T(8,128)S(1)} %get-tuple-element.78.v_ref.refs_2_, f32[48,640]{1,0:T(8,128)S(1)} %get-tuple-element.79.u_ref.refs_3_), custom_call_target="tpu_custom_call" | custom-call | flops 943718400 | bytes 5775360 | tf_op jit(solution)/shard_map/next_products_2/pallas_call | solution.py:488
  68.6 1.2 %collective-permute-done.28 = f32[2,3968]{1,0:T(2,128)S(1)} collective-permute-done((f32[2,3968]{1,0:T(2,128)S(1)}, f32[2,3968]{1,0:T(2,128)S(1)}, u32[]{:S(2)}, u32[]{:S(2)}) %collective-permute-start.28) | collective-permute-done | bytes 31776 | tf_op jit(solution)/shard_map/ppermute | solution.py:32
  69.8 1.2 %fields_2.1 = (f32[8,256]{1,0:T(8,128)S(1)}, f32[48,3840]{1,0:T(8,128)S(1)}, f32[48,640]{1,0:T(8,128)S(1)}) custom-call(bf16[3840,512]{1,0:T(8,128)(2,1)S(1)} %get-tuple-element.53.refs_3_.m_ref.refs_0_, bf16[3840,128]{1,0:T(8,128)(2,1)S(1)} %get-tuple-element.62.mh_ref.refs_1_, f32[48,3840]{1,0:T(8,128)S(1)} %get-tuple-element.78.v_ref.refs_2_, ...), custom_call_target="tpu_custom_call" | custom-call | flops 943718400 | bytes 5843456 | tf_op jit(solution)/shard_map/fields_2/pallas_call | solution.py:488
  71.0 2.3 %collective-permute-start.29 = (f32[8,256]{1,0:T(8,128)S(1)}, f32[8,256]{1,0:T(8,128)S(1)}, u32[]{:S(2)}, u32[]{:S(2)}) collective-permute-start(f32[8,256]{1,0:T(8,128)S(1)} %get-tuple-element.86.refs_7_), channel_id=1, source_target_pairs={{0,24},{1,25},{2,26},{3,27},{4,28},{5,29},{6,30},{7,31},{8,16},{9,... | collective-permute-start | bytes 24584 | tf_op jit(solution)/shard_map/ppermute | solution.py:60
  74.0 1.6 %collective-permute-done.29.refs_8_ = f32[8,256]{1,0:T(8,128)S(1)} collective-permute-done((f32[8,256]{1,0:T(8,128)S(1)}, f32[8,256]{1,0:T(8,128)S(1)}, u32[]{:S(2)}, u32[]{:S(2)}) %collective-permute-start.29) | collective-permute-done | bytes 8224 | tf_op jit(solution)/shard_map/ppermute | solution.py:60
  75.6 1.4 %collective-permute-done.30.refs_9_ = f32[8,256]{1,0:T(8,128)S(1)} collective-permute-done((f32[8,256]{1,0:T(8,128)S(1)}, f32[8,256]{1,0:T(8,128)S(1)}, u32[]{:S(2)}, u32[]{:S(2)}) %collective-permute-start.30) | collective-permute-done | bytes 8224 | tf_op jit(solution)/shard_map/ppermute | solution.py:59
  76.9 2.4 %sums_2.1 = (f32[2,3968]{1,0:T(2,128)S(1)}, f32[8,256]{1,0:T(8,128)S(1)}) custom-call(bf16[512,3840]{1,0:T(8,128)(2,1)S(1)} %get-tuple-element.72.refs_0_, bf16[512,3840]{1,0:T(8,128)(2,1)S(1)} %get-tuple-element.66.refs_0_.refs_1_, f32[48,3840]{1,0:T(8,128)S(1)} %get-tuple-element.84.v_ref.refs_2_, f32[48,640]{1,0:T(8,128)S(1)} %get-tuple-element.85.u_ref.refs_3_, ...), custom_call_target="tpu_custom_call" | custom-call | flops 754974720 | bytes 8904720 | tf_op jit(solution)/shard_map/sums_2/pallas_call | solution.py:488
  79.4 1.2 %collective-permute-done.31 = f32[2,3968]{1,0:T(2,128)S(1)} collective-permute-done((f32[2,3968]{1,0:T(2,128)S(1)}, f32[2,3968]{1,0:T(2,128)S(1)}, u32[]{:S(2)}, u32[]{:S(2)}) %collective-permute-start.31) | collective-permute-done | bytes 31776 | tf_op jit(solution)/shard_map/ppermute | solution.py:32
  81.2 1.4 %collective-permute-start.34 = (f32[2,3968]{1,0:T(2,128)S(1)}, f32[2,3968]{1,0:T(2,128)S(1)}, u32[]{:S(2)}, u32[]{:S(2)}) collective-permute-start(f32[2,3968]{1,0:T(2,128)S(1)} %add.137), channel_id=1, source_target_pairs={{0,25},{1,24},{2,27},{3,26},{4,29},{5,28},{6,31},{7,30},{8,17},{9,... | collective-permute-start | bytes 95240 | tf_op jit(solution)/shard_map/ppermute | solution.py:32
  82.6 1.1 collective-permute-start.32
  84.0 1.4 %collective-permute-done.34 = f32[2,3968]{1,0:T(2,128)S(1)} collective-permute-done((f32[2,3968]{1,0:T(2,128)S(1)}, f32[2,3968]{1,0:T(2,128)S(1)}, u32[]{:S(2)}, u32[]{:S(2)}) %collective-permute-start.34) | collective-permute-done | bytes 31776 | tf_op jit(solution)/shard_map/ppermute | solution.py:32
  85.4 0.8 collective-permute-done.32
  86.3 2.3 %collective-permute-start.37 = (f32[2,3968]{1,0:T(2,128)S(1)}, f32[2,3968]{1,0:T(2,128)S(1)}, u32[]{:S(2)}, u32[]{:S(2)}) collective-permute-start(f32[2,3968]{1,0:T(2,128)S(1)} %add_add_fusion.3), channel_id=1, source_target_pairs={{0,7},{1,6},{2,5},{3,4},{4,3},{5,2},{6,1},{7,0},{8,15},{9,14},{10,... | collective-permute-start | bytes 95240 | tf_op jit(solution)/shard_map/ppermute | solution.py:32
  89.3 1.4 %next_products_3.1.refs_7_ = f32[2,640]{1,0:T(2,128)S(1)} custom-call(bf16[3840,512]{1,0:T(8,128)(2,1)S(1)} %get-tuple-element.53.refs_3_.m_ref.refs_0_, bf16[3840,128]{1,0:T(8,128)(2,1)S(1)} %get-tuple-element.62.mh_ref.refs_1_, f32[48,3840]{1,0:T(8,128)S(1)} %get-tuple-element.84.v_ref.refs_2_, f32[48,640]{1,0:T(8,128)S(1)} %get-tuple-element.85.u_ref.refs_3_), custom_call_target="tpu_custom_call" | custom-call | flops 943718400 | bytes 5775360 | tf_op jit(solution)/shard_map/next_products_3/pallas_call | solution.py:488
  91.6 0.9 collective-permute-done.35
  92.5 1.2 %fields_3.1 = (f32[8,256]{1,0:T(8,128)S(1)}, f32[48,3840]{1,0:T(8,128)S(1)}, f32[48,640]{1,0:T(8,128)S(1)}) custom-call(bf16[3840,512]{1,0:T(8,128)(2,1)S(1)} %get-tuple-element.53.refs_3_.m_ref.refs_0_, bf16[3840,128]{1,0:T(8,128)(2,1)S(1)} %get-tuple-element.62.mh_ref.refs_1_, f32[48,3840]{1,0:T(8,128)S(1)} %get-tuple-element.84.v_ref.refs_2_, ...), custom_call_target="tpu_custom_call" | custom-call | flops 943718400 | bytes 5843456 | tf_op jit(solution)/shard_map/fields_3/pallas_call | solution.py:488
  93.7 1.4 %collective-permute-start.38 = (f32[8,256]{1,0:T(8,128)S(1)}, f32[8,256]{1,0:T(8,128)S(1)}, u32[]{:S(2)}, u32[]{:S(2)}) collective-permute-start(f32[8,256]{1,0:T(8,128)S(1)} %get-tuple-element.91.refs_7_), channel_id=1, source_target_pairs={{0,24},{1,25},{2,26},{3,27},{4,28},{5,29},{6,30},{7,31},{8,16},{9,... | collective-permute-start | bytes 24584 | tf_op jit(solution)/shard_map/ppermute | solution.py:60
  95.8 2.6 %collective-permute-done.38.refs_8_ = f32[8,256]{1,0:T(8,128)S(1)} collective-permute-done((f32[8,256]{1,0:T(8,128)S(1)}, f32[8,256]{1,0:T(8,128)S(1)}, u32[]{:S(2)}, u32[]{:S(2)}) %collective-permute-start.38) | collective-permute-done | bytes 8224 | tf_op jit(solution)/shard_map/ppermute | solution.py:60
  98.8 2.4 %sums_3.1 = (f32[2,3968]{1,0:T(2,128)S(1)}, f32[8,256]{1,0:T(8,128)S(1)}) custom-call(bf16[512,3840]{1,0:T(8,128)(2,1)S(1)} %get-tuple-element.72.refs_0_, bf16[512,3840]{1,0:T(8,128)(2,1)S(1)} %get-tuple-element.66.refs_0_.refs_1_, f32[48,3840]{1,0:T(8,128)S(1)} %get-tuple-element.89.refs_2_.refs_0_, f32[48,640]{1,0:T(8,128)S(1)} %get-tuple-element.90.refs_3_.refs_1_, ...), custom_call_target="tpu_custom_call" | custom-call | flops 754974720 | bytes 8904720 | tf_op jit(solution)/shard_map/sums_3/pallas_call | solution.py:488
  101.2 1.2 %collective-permute-done.40 = f32[2,3968]{1,0:T(2,128)S(1)} collective-permute-done((f32[2,3968]{1,0:T(2,128)S(1)}, f32[2,3968]{1,0:T(2,128)S(1)}, u32[]{:S(2)}, u32[]{:S(2)}) %collective-permute-start.40) | collective-permute-done | bytes 31776 | tf_op jit(solution)/shard_map/ppermute | solution.py:32
  102.4 1.4 %collective-permute-start.42 = (f32[2,3968]{1,0:T(2,128)S(1)}, f32[2,3968]{1,0:T(2,128)S(1)}, u32[]{:S(2)}, u32[]{:S(2)}) collective-permute-start(f32[2,3968]{1,0:T(2,128)S(1)} %add.144), channel_id=1, source_target_pairs={{0,17},{1,16},{2,19},{3,18},{4,21},{5,20},{6,23},{7,22},{8,25},{9,... | collective-permute-start | bytes 95240 | tf_op jit(solution)/shard_map/ppermute | solution.py:32
  103.8 0.9 collective-permute-start.43
  104.7 0.8 collective-permute-start.41
  105.8 2.2 %collective-permute-done.43 = f32[2,3968]{1,0:T(2,128)S(1)} collective-permute-done((f32[2,3968]{1,0:T(2,128)S(1)}, f32[2,3968]{1,0:T(2,128)S(1)}, u32[]{:S(2)}, u32[]{:S(2)}) %collective-permute-start.43) | collective-permute-done | bytes 31776 | tf_op jit(solution)/shard_map/ppermute | solution.py:32
  108.1 1.1 collective-permute-start.45
  109.2 1.4 %collective-permute-start.46 = (f32[2,3968]{1,0:T(2,128)S(1)}, f32[2,3968]{1,0:T(2,128)S(1)}, u32[]{:S(2)}, u32[]{:S(2)}) collective-permute-start(f32[2,3968]{1,0:T(2,128)S(1)} %add_add_fusion.1), channel_id=1, source_target_pairs={{0,7},{1,6},{2,5},{3,4},{4,3},{5,2},{6,1},{7,0},{8,15},{9,14},{10,... | collective-permute-start | bytes 95240 | tf_op jit(solution)/shard_map/ppermute | solution.py:32
  110.5 1.1 collective-permute-start.44
  111.6 1.2 %collective-permute-done.45 = f32[2,3968]{1,0:T(2,128)S(1)} collective-permute-done((f32[2,3968]{1,0:T(2,128)S(1)}, f32[2,3968]{1,0:T(2,128)S(1)}, u32[]{:S(2)}, u32[]{:S(2)}) %collective-permute-start.45) | collective-permute-done | bytes 31776 | tf_op jit(solution)/shard_map/ppermute | solution.py:32
  112.8 1.6 %collective-permute-done.46 = f32[2,3968]{1,0:T(2,128)S(1)} collective-permute-done((f32[2,3968]{1,0:T(2,128)S(1)}, f32[2,3968]{1,0:T(2,128)S(1)}, u32[]{:S(2)}, u32[]{:S(2)}) %collective-permute-start.46) | collective-permute-done | bytes 31776 | tf_op jit(solution)/shard_map/ppermute | solution.py:32
  114.4 2.1 %last.1 = (f32[48,4,128]{2,1,0:T(4,128)}, f32[48,480]{1,0:T(8,128)}) custom-call(f32[48,3840]{1,0:T(8,128)S(1)} %get-tuple-element.89.refs_2_.refs_0_, f32[48,640]{1,0:T(8,128)S(1)} %get-tuple-element.90.refs_3_.refs_1_, f32[2,3968]{1,0:T(2,128)S(1)} %add_add_fusion.refs_2_, ...), custom_call_target="tpu_custom_call", output_to_operand_aliasing={{0}: (5, {}), {1}: (6, {})} | custom-call | bytes 1090576 | tf_op jit(solution)/shard_map/last/pallas_call | solution.py:488
  (64 shorter events, 10.7 us)
Async XLA Ops:
  0.6 18.2 %copy-start = (f32[48,480]{1,0:T(8,128)S(1)}, f32[48,480]{1,0:T(8,128)}, u32[]{:S(2)}) copy-start(f32[48,480]{1,0:T(8,128)} %refs_2_.1) | copy-start | bytes 276484
  0.6 13.4 %collective-permute-start = (f32[48,480]{1,0:T(8,128)}, f32[48,480]{1,0:T(8,128)S(1)}, u32[]{:S(2)}, u32[]{:S(2)}) collective-permute-start(f32[48,480]{1,0:T(8,128)} %refs_2_.1), channel_id=1, source_target_pairs={{0,3},{1,2},{2,1},{3,0},{4,7},{5,6},{6,5},{7,4},{8,11},{9,10},{10,... | collective-permute-start | bytes 276488 | tf_op jit(solution)/shard_map/ppermute | solution.py:32
  3.2 10.9 %collective-permute-start.1 = (f32[48,480]{1,0:T(8,128)}, f32[48,480]{1,0:T(8,128)S(1)}, u32[]{:S(2)}, u32[]{:S(2)}) collective-permute-start(f32[48,480]{1,0:T(8,128)} %refs_2_.1), channel_id=1, source_target_pairs={{0,5},{1,4},{2,7},{3,6},{4,1},{5,0},{6,3},{7,2},{8,13},{9,12},{10,... | collective-permute-start | bytes 276488 | tf_op jit(solution)/shard_map/ppermute | solution.py:32
  6.0 8.1 %collective-permute-start.2 = (f32[48,480]{1,0:T(8,128)}, f32[48,480]{1,0:T(8,128)S(1)}, u32[]{:S(2)}, u32[]{:S(2)}) collective-permute-start(f32[48,480]{1,0:T(8,128)} %refs_2_.1), channel_id=1, source_target_pairs={{0,7},{1,6},{2,5},{3,4},{4,3},{5,2},{6,1},{7,0},{8,15},{9,14},{10,... | collective-permute-start | bytes 276488 | tf_op jit(solution)/shard_map/ppermute | solution.py:32
  6.0 9.2 %collective-permute-start.5 = (f32[48,480]{1,0:T(8,128)}, f32[48,480]{1,0:T(8,128)S(1)}, u32[]{:S(2)}, u32[]{:S(2)}) collective-permute-start(f32[48,480]{1,0:T(8,128)} %refs_2_.1), channel_id=1, source_target_pairs={{0,1},{1,0},{2,3},{3,2},{4,5},{5,4},{6,7},{7,6},{8,9},{9,8},{10,11... | collective-permute-start | bytes 276488 | tf_op jit(solution)/shard_map/ppermute | solution.py:32
  14.1 4.7 %collective-permute-start.6 = (f32[48,480]{1,0:T(8,128)S(1)}, f32[48,480]{1,0:T(8,128)S(1)}, u32[]{:S(2)}, u32[]{:S(2)}) collective-permute-start(f32[48,480]{1,0:T(8,128)S(1)} %collective-permute-done.refs_10_.refs_5_), channel_id=1, source_target_pairs={{0,1},{1,0},{2,3},{3,2},{4,5},{5,4},{6,7},{7,6},{8,9},{9,8},{10,11... | collective-permute-start | bytes 276488 | tf_op jit(solution)/shard_map/ppermute | solution.py:32
  14.7 4.1 %collective-permute-start.7 = (f32[48,480]{1,0:T(8,128)S(1)}, f32[48,480]{1,0:T(8,128)S(1)}, u32[]{:S(2)}, u32[]{:S(2)}) collective-permute-start(f32[48,480]{1,0:T(8,128)S(1)} %collective-permute-done.1.refs_12_.refs_7_), channel_id=1, source_target_pairs={{0,1},{1,0},{2,3},{3,2},{4,5},{5,4},{6,7},{7,6},{8,9},{9,8},{10,11... | collective-permute-start | bytes 276488 | tf_op jit(solution)/shard_map/ppermute | solution.py:32
  14.8 4.1 %collective-permute-start.8 = (f32[48,480]{1,0:T(8,128)S(1)}, f32[48,480]{1,0:T(8,128)S(1)}, u32[]{:S(2)}, u32[]{:S(2)}) collective-permute-start(f32[48,480]{1,0:T(8,128)S(1)} %collective-permute-done.2.refs_14_.refs_9_), channel_id=1, source_target_pairs={{0,1},{1,0},{2,3},{3,2},{4,5},{5,4},{6,7},{7,6},{8,9},{9,8},{10,11... | collective-permute-start | bytes 276488 | tf_op jit(solution)/shard_map/ppermute | solution.py:32
  15.2 6.6 %collective-permute-start.3 = (f32[184,128]{1,0:T(8,128)S(1)}, f32[184,128]{1,0:T(8,128)S(1)}, u32[]{:S(2)}, u32[]{:S(2)}) collective-permute-start(f32[184,128]{1,0:T(8,128)S(1)} %get-tuple-element.54), channel_id=1, source_target_pairs={{0,1},{1,0},{2,3},{3,2},{4,5},{5,4},{6,7},{7,6},{8,9},{9,8},{10,11... | collective-permute-start | bytes 282632 | tf_op jit(solution)/shard_map/ppermute | solution.py:32
  15.3 6.5 %collective-permute-start.4 = (f32[184,128]{1,0:T(8,128)S(1)}, f32[184,128]{1,0:T(8,128)S(1)}, u32[]{:S(2)}, u32[]{:S(2)}) collective-permute-start(f32[184,128]{1,0:T(8,128)S(1)} %get-tuple-element.55), channel_id=1, source_target_pairs={{0,7},{1,2},{2,1},{3,4},{4,3},{5,6},{6,5},{7,0},{8,15},{9,10},{10,... | collective-permute-start | bytes 282632 | tf_op jit(solution)/shard_map/ppermute | solution.py:67
  20.6 4.0 %collective-permute-start.9 = (f32[8,128]{1,0:T(8,128)S(1)}, f32[8,128]{1,0:T(8,128)S(1)}, u32[]{:S(2)}, u32[]{:S(2)}) collective-permute-start(f32[8,128]{1,0:T(8,128)S(1)} %get-tuple-element.68), channel_id=1, source_target_pairs={{0,1},{1,0},{2,3},{3,2},{4,5},{5,4},{6,7},{7,6},{8,9},{9,8},{10,11... | collective-permute-start | bytes 12296 | tf_op jit(solution)/shard_map/ppermute | solution.py:32
  20.6 4.9 %collective-permute-start.10 = (f32[8,128]{1,0:T(8,128)S(1)}, f32[8,128]{1,0:T(8,128)S(1)}, u32[]{:S(2)}, u32[]{:S(2)}) collective-permute-start(f32[8,128]{1,0:T(8,128)S(1)} %get-tuple-element.69), channel_id=1, source_target_pairs={{0,7},{1,2},{2,1},{3,4},{4,3},{5,6},{6,5},{7,0},{8,15},{9,10},{10,... | collective-permute-start | bytes 12296 | tf_op jit(solution)/shard_map/ppermute | solution.py:67
  26.3 4.7 %collective-permute-start.11 = (f32[16,256]{1,0:T(8,128)S(1)}, f32[16,256]{1,0:T(8,128)S(1)}, u32[]{:S(2)}, u32[]{:S(2)}) collective-permute-start(f32[16,256]{1,0:T(8,128)S(1)} %get-tuple-element.75.refs_7_), channel_id=1, source_target_pairs={{0,24},{1,25},{2,26},{3,27},{4,28},{5,29},{6,30},{7,31},{8,16},{9,... | collective-permute-start | bytes 49160 | tf_op jit(solution)/shard_map/ppermute | solution.py:60
  28.8 3.7 %collective-permute-start.12 = (f32[16,256]{1,0:T(8,128)S(1)}, f32[16,256]{1,0:T(8,128)S(1)}, u32[]{:S(2)}, u32[]{:S(2)}) collective-permute-start(f32[16,256]{1,0:T(8,128)S(1)} %get-tuple-element.75.refs_7_), channel_id=1, source_target_pairs={{0,8},{1,9},{2,10},{3,11},{4,12},{5,13},{6,14},{7,15},{8,0},{9,1},... | collective-permute-start | bytes 49160 | tf_op jit(solution)/shard_map/ppermute | solution.py:59
  35.0 1.3 %collective-permute-start.13 = (f32[2,3968]{1,0:T(2,128)S(1)}, f32[2,3968]{1,0:T(2,128)S(1)}, u32[]{:S(2)}, u32[]{:S(2)}) collective-permute-start(f32[2,3968]{1,0:T(2,128)S(1)} %get-tuple-element.76), channel_id=1, source_target_pairs={{0,1},{1,0},{2,3},{3,2},{4,5},{5,4},{6,7},{7,6},{8,9},{9,8},{10,11... | collective-permute-start | bytes 95240 | tf_op jit(solution)/shard_map/ppermute | solution.py:32
  36.3 3.4 %collective-permute-start.15 = (f32[2,3968]{1,0:T(2,128)S(1)}, f32[2,3968]{1,0:T(2,128)S(1)}, u32[]{:S(2)}, u32[]{:S(2)}) collective-permute-start(f32[2,3968]{1,0:T(2,128)S(1)} %add.123), channel_id=1, source_target_pairs={{0,17},{1,16},{2,19},{3,18},{4,21},{5,20},{6,23},{7,22},{8,25},{9,... | collective-permute-start | bytes 95240 | tf_op jit(solution)/shard_map/ppermute | solution.py:32
  36.6 4.2 %collective-permute-start.16 = (f32[2,3968]{1,0:T(2,128)S(1)}, f32[2,3968]{1,0:T(2,128)S(1)}, u32[]{:S(2)}, u32[]{:S(2)}) collective-permute-start(f32[2,3968]{1,0:T(2,128)S(1)} %add.123), channel_id=1, source_target_pairs={{0,25},{1,24},{2,27},{3,26},{4,29},{5,28},{6,31},{7,30},{8,17},{9,... | collective-permute-start | bytes 95240 | tf_op jit(solution)/shard_map/ppermute | solution.py:32
  38.1 3.6 %collective-permute-start.14 = (f32[2,3968]{1,0:T(2,128)S(1)}, f32[2,3968]{1,0:T(2,128)S(1)}, u32[]{:S(2)}, u32[]{:S(2)}) collective-permute-start(f32[2,3968]{1,0:T(2,128)S(1)} %add.123), channel_id=1, source_target_pairs={{0,9},{1,8},{2,11},{3,10},{4,13},{5,12},{6,15},{7,14},{8,1},{9,0},... | collective-permute-start | bytes 95240 | tf_op jit(solution)/shard_map/ppermute | solution.py:32
  41.7 4.7 %collective-permute-start.18 = (f32[2,3968]{1,0:T(2,128)S(1)}, f32[2,3968]{1,0:T(2,128)S(1)}, u32[]{:S(2)}, u32[]{:S(2)}) collective-permute-start(f32[2,3968]{1,0:T(2,128)S(1)} %add_add_fusion.7), channel_id=1, source_target_pairs={{0,5},{1,4},{2,7},{3,6},{4,1},{5,0},{6,3},{7,2},{8,13},{9,12},{10,... | collective-permute-start | bytes 95240 | tf_op jit(solution)/shard_map/ppermute | solution.py:32
  41.8 5.3 %collective-permute-start.19 = (f32[2,3968]{1,0:T(2,128)S(1)}, f32[2,3968]{1,0:T(2,128)S(1)}, u32[]{:S(2)}, u32[]{:S(2)}) collective-permute-start(f32[2,3968]{1,0:T(2,128)S(1)} %add_add_fusion.7), channel_id=1, source_target_pairs={{0,7},{1,6},{2,5},{3,4},{4,3},{5,2},{6,1},{7,0},{8,15},{9,14},{10,... | collective-permute-start | bytes 95240 | tf_op jit(solution)/shard_map/ppermute | solution.py:32
  44.0 4.1 %collective-permute-start.17 = (f32[2,3968]{1,0:T(2,128)S(1)}, f32[2,3968]{1,0:T(2,128)S(1)}, u32[]{:S(2)}, u32[]{:S(2)}) collective-permute-start(f32[2,3968]{1,0:T(2,128)S(1)} %add_add_fusion.7), channel_id=1, source_target_pairs={{0,3},{1,2},{2,1},{3,0},{4,7},{5,6},{6,5},{7,4},{8,11},{9,10},{10,... | collective-permute-start | bytes 95240 | tf_op jit(solution)/shard_map/ppermute | solution.py:32
  49.4 4.6 %collective-permute-start.20 = (f32[8,256]{1,0:T(8,128)S(1)}, f32[8,256]{1,0:T(8,128)S(1)}, u32[]{:S(2)}, u32[]{:S(2)}) collective-permute-start(f32[8,256]{1,0:T(8,128)S(1)} %get-tuple-element.80.refs_7_), channel_id=1, source_target_pairs={{0,24},{1,25},{2,26},{3,27},{4,28},{5,29},{6,30},{7,31},{8,16},{9,... | collective-permute-start | bytes 24584 | tf_op jit(solution)/shard_map/ppermute | solution.py:60
  50.5 3.7 %collective-permute-start.21 = (f32[8,256]{1,0:T(8,128)S(1)}, f32[8,256]{1,0:T(8,128)S(1)}, u32[]{:S(2)}, u32[]{:S(2)}) collective-permute-start(f32[8,256]{1,0:T(8,128)S(1)} %get-tuple-element.80.refs_7_), channel_id=1, source_target_pairs={{0,8},{1,9},{2,10},{3,11},{4,12},{5,13},{6,14},{7,15},{8,0},{9,1},... | collective-permute-start | bytes 24584 | tf_op jit(solution)/shard_map/ppermute | solution.py:59
  56.6 1.3 %collective-permute-start.22 = (f32[2,3968]{1,0:T(2,128)S(1)}, f32[2,3968]{1,0:T(2,128)S(1)}, u32[]{:S(2)}, u32[]{:S(2)}) collective-permute-start(f32[2,3968]{1,0:T(2,128)S(1)} %get-tuple-element.82), channel_id=1, source_target_pairs={{0,1},{1,0},{2,3},{3,2},{4,5},{5,4},{6,7},{7,6},{8,9},{9,8},{10,11... | collective-permute-start | bytes 95240 | tf_op jit(solution)/shard_map/ppermute | solution.py:32
  57.9 3.4 %collective-permute-start.24 = (f32[2,3968]{1,0:T(2,128)S(1)}, f32[2,3968]{1,0:T(2,128)S(1)}, u32[]{:S(2)}, u32[]{:S(2)}) collective-permute-start(f32[2,3968]{1,0:T(2,128)S(1)} %add.130), channel_id=1, source_target_pairs={{0,17},{1,16},{2,19},{3,18},{4,21},{5,20},{6,23},{7,22},{8,25},{9,... | collective-permute-start | bytes 95240 | tf_op jit(solution)/shard_map/ppermute | solution.py:32
  59.2 4.2 %collective-permute-start.25 = (f32[2,3968]{1,0:T(2,128)S(1)}, f32[2,3968]{1,0:T(2,128)S(1)}, u32[]{:S(2)}, u32[]{:S(2)}) collective-permute-start(f32[2,3968]{1,0:T(2,128)S(1)} %add.130), channel_id=1, source_target_pairs={{0,25},{1,24},{2,27},{3,26},{4,29},{5,28},{6,31},{7,30},{8,17},{9,... | collective-permute-start | bytes 95240 | tf_op jit(solution)/shard_map/ppermute | solution.py:32
  60.1 3.4 %collective-permute-start.23 = (f32[2,3968]{1,0:T(2,128)S(1)}, f32[2,3968]{1,0:T(2,128)S(1)}, u32[]{:S(2)}, u32[]{:S(2)}) collective-permute-start(f32[2,3968]{1,0:T(2,128)S(1)} %add.130), channel_id=1, source_target_pairs={{0,9},{1,8},{2,11},{3,10},{4,13},{5,12},{6,15},{7,14},{8,1},{9,0},... | collective-permute-start | bytes 95240 | tf_op jit(solution)/shard_map/ppermute | solution.py:32
  63.5 5.1 %collective-permute-start.27 = (f32[2,3968]{1,0:T(2,128)S(1)}, f32[2,3968]{1,0:T(2,128)S(1)}, u32[]{:S(2)}, u32[]{:S(2)}) collective-permute-start(f32[2,3968]{1,0:T(2,128)S(1)} %add_add_fusion.5), channel_id=1, source_target_pairs={{0,5},{1,4},{2,7},{3,6},{4,1},{5,0},{6,3},{7,2},{8,13},{9,12},{10,... | collective-permute-start | bytes 95240 | tf_op jit(solution)/shard_map/ppermute | solution.py:32
  64.5 5.2 %collective-permute-start.28 = (f32[2,3968]{1,0:T(2,128)S(1)}, f32[2,3968]{1,0:T(2,128)S(1)}, u32[]{:S(2)}, u32[]{:S(2)}) collective-permute-start(f32[2,3968]{1,0:T(2,128)S(1)} %add_add_fusion.5), channel_id=1, source_target_pairs={{0,7},{1,6},{2,5},{3,4},{4,3},{5,2},{6,1},{7,0},{8,15},{9,14},{10,... | collective-permute-start | bytes 95240 | tf_op jit(solution)/shard_map/ppermute | solution.py:32
  66.1 3.7 %collective-permute-start.26 = (f32[2,3968]{1,0:T(2,128)S(1)}, f32[2,3968]{1,0:T(2,128)S(1)}, u32[]{:S(2)}, u32[]{:S(2)}) collective-permute-start(f32[2,3968]{1,0:T(2,128)S(1)} %add_add_fusion.5), channel_id=1, source_target_pairs={{0,3},{1,2},{2,1},{3,0},{4,7},{5,6},{6,5},{7,4},{8,11},{9,10},{10,... | collective-permute-start | bytes 95240 | tf_op jit(solution)/shard_map/ppermute | solution.py:32
  71.0 4.6 %collective-permute-start.29 = (f32[8,256]{1,0:T(8,128)S(1)}, f32[8,256]{1,0:T(8,128)S(1)}, u32[]{:S(2)}, u32[]{:S(2)}) collective-permute-start(f32[8,256]{1,0:T(8,128)S(1)} %get-tuple-element.86.refs_7_), channel_id=1, source_target_pairs={{0,24},{1,25},{2,26},{3,27},{4,28},{5,29},{6,30},{7,31},{8,16},{9,... | collective-permute-start | bytes 24584 | tf_op jit(solution)/shard_map/ppermute | solution.py:60
  73.3 3.7 %collective-permute-start.30 = (f32[8,256]{1,0:T(8,128)S(1)}, f32[8,256]{1,0:T(8,128)S(1)}, u32[]{:S(2)}, u32[]{:S(2)}) collective-permute-start(f32[8,256]{1,0:T(8,128)S(1)} %get-tuple-element.86.refs_7_), channel_id=1, source_target_pairs={{0,8},{1,9},{2,10},{3,11},{4,12},{5,13},{6,14},{7,15},{8,0},{9,1},... | collective-permute-start | bytes 24584 | tf_op jit(solution)/shard_map/ppermute | solution.py:59
  79.3 1.3 %collective-permute-start.31 = (f32[2,3968]{1,0:T(2,128)S(1)}, f32[2,3968]{1,0:T(2,128)S(1)}, u32[]{:S(2)}, u32[]{:S(2)}) collective-permute-start(f32[2,3968]{1,0:T(2,128)S(1)} %get-tuple-element.87), channel_id=1, source_target_pairs={{0,1},{1,0},{2,3},{3,2},{4,5},{5,4},{6,7},{7,6},{8,9},{9,8},{10,11... | collective-permute-start | bytes 95240 | tf_op jit(solution)/shard_map/ppermute | solution.py:32
  80.6 3.4 %collective-permute-start.33 = (f32[2,3968]{1,0:T(2,128)S(1)}, f32[2,3968]{1,0:T(2,128)S(1)}, u32[]{:S(2)}, u32[]{:S(2)}) collective-permute-start(f32[2,3968]{1,0:T(2,128)S(1)} %add.137), channel_id=1, source_target_pairs={{0,17},{1,16},{2,19},{3,18},{4,21},{5,20},{6,23},{7,22},{8,25},{9,... | collective-permute-start | bytes 95240 | tf_op jit(solution)/shard_map/ppermute | solution.py:32
  81.2 4.2 %collective-permute-start.34 = (f32[2,3968]{1,0:T(2,128)S(1)}, f32[2,3968]{1,0:T(2,128)S(1)}, u32[]{:S(2)}, u32[]{:S(2)}) collective-permute-start(f32[2,3968]{1,0:T(2,128)S(1)} %add.137), channel_id=1, source_target_pairs={{0,25},{1,24},{2,27},{3,26},{4,29},{5,28},{6,31},{7,30},{8,17},{9,... | collective-permute-start | bytes 95240 | tf_op jit(solution)/shard_map/ppermute | solution.py:32
  82.6 3.7 %collective-permute-start.32 = (f32[2,3968]{1,0:T(2,128)S(1)}, f32[2,3968]{1,0:T(2,128)S(1)}, u32[]{:S(2)}, u32[]{:S(2)}) collective-permute-start(f32[2,3968]{1,0:T(2,128)S(1)} %add.137), channel_id=1, source_target_pairs={{0,9},{1,8},{2,11},{3,10},{4,13},{5,12},{6,15},{7,14},{8,1},{9,0},... | collective-permute-start | bytes 95240 | tf_op jit(solution)/shard_map/ppermute | solution.py:32
  86.3 5.0 %collective-permute-start.36 = (f32[2,3968]{1,0:T(2,128)S(1)}, f32[2,3968]{1,0:T(2,128)S(1)}, u32[]{:S(2)}, u32[]{:S(2)}) collective-permute-start(f32[2,3968]{1,0:T(2,128)S(1)} %add_add_fusion.3), channel_id=1, source_target_pairs={{0,5},{1,4},{2,7},{3,6},{4,1},{5,0},{6,3},{7,2},{8,13},{9,12},{10,... | collective-permute-start | bytes 95240 | tf_op jit(solution)/shard_map/ppermute | solution.py:32
  86.3 5.3 %collective-permute-start.37 = (f32[2,3968]{1,0:T(2,128)S(1)}, f32[2,3968]{1,0:T(2,128)S(1)}, u32[]{:S(2)}, u32[]{:S(2)}) collective-permute-start(f32[2,3968]{1,0:T(2,128)S(1)} %add_add_fusion.3), channel_id=1, source_target_pairs={{0,7},{1,6},{2,5},{3,4},{4,3},{5,2},{6,1},{7,0},{8,15},{9,14},{10,... | collective-permute-start | bytes 95240 | tf_op jit(solution)/shard_map/ppermute | solution.py:32
  88.6 3.9 %collective-permute-start.35 = (f32[2,3968]{1,0:T(2,128)S(1)}, f32[2,3968]{1,0:T(2,128)S(1)}, u32[]{:S(2)}, u32[]{:S(2)}) collective-permute-start(f32[2,3968]{1,0:T(2,128)S(1)} %add_add_fusion.3), channel_id=1, source_target_pairs={{0,3},{1,2},{2,1},{3,0},{4,7},{5,6},{6,5},{7,4},{8,11},{9,10},{10,... | collective-permute-start | bytes 95240 | tf_op jit(solution)/shard_map/ppermute | solution.py:32
  93.7 4.6 %collective-permute-start.38 = (f32[8,256]{1,0:T(8,128)S(1)}, f32[8,256]{1,0:T(8,128)S(1)}, u32[]{:S(2)}, u32[]{:S(2)}) collective-permute-start(f32[8,256]{1,0:T(8,128)S(1)} %get-tuple-element.91.refs_7_), channel_id=1, source_target_pairs={{0,24},{1,25},{2,26},{3,27},{4,28},{5,29},{6,30},{7,31},{8,16},{9,... | collective-permute-start | bytes 24584 | tf_op jit(solution)/shard_map/ppermute | solution.py:60
  95.1 3.7 %collective-permute-start.39 = (f32[8,256]{1,0:T(8,128)S(1)}, f32[8,256]{1,0:T(8,128)S(1)}, u32[]{:S(2)}, u32[]{:S(2)}) collective-permute-start(f32[8,256]{1,0:T(8,128)S(1)} %get-tuple-element.91.refs_7_), channel_id=1, source_target_pairs={{0,8},{1,9},{2,10},{3,11},{4,12},{5,13},{6,14},{7,15},{8,0},{9,1},... | collective-permute-start | bytes 24584 | tf_op jit(solution)/shard_map/ppermute | solution.py:59
  101.1 1.3 %collective-permute-start.40 = (f32[2,3968]{1,0:T(2,128)S(1)}, f32[2,3968]{1,0:T(2,128)S(1)}, u32[]{:S(2)}, u32[]{:S(2)}) collective-permute-start(f32[2,3968]{1,0:T(2,128)S(1)} %get-tuple-element.92), channel_id=1, source_target_pairs={{0,1},{1,0},{2,3},{3,2},{4,5},{5,4},{6,7},{7,6},{8,9},{9,8},{10,11... | collective-permute-start | bytes 95240 | tf_op jit(solution)/shard_map/ppermute | solution.py:32
  102.4 3.4 %collective-permute-start.42 = (f32[2,3968]{1,0:T(2,128)S(1)}, f32[2,3968]{1,0:T(2,128)S(1)}, u32[]{:S(2)}, u32[]{:S(2)}) collective-permute-start(f32[2,3968]{1,0:T(2,128)S(1)} %add.144), channel_id=1, source_target_pairs={{0,17},{1,16},{2,19},{3,18},{4,21},{5,20},{6,23},{7,22},{8,25},{9,... | collective-permute-start | bytes 95240 | tf_op jit(solution)/shard_map/ppermute | solution.py:32
  103.8 4.2 %collective-permute-start.43 = (f32[2,3968]{1,0:T(2,128)S(1)}, f32[2,3968]{1,0:T(2,128)S(1)}, u32[]{:S(2)}, u32[]{:S(2)}) collective-permute-start(f32[2,3968]{1,0:T(2,128)S(1)} %add.144), channel_id=1, source_target_pairs={{0,25},{1,24},{2,27},{3,26},{4,29},{5,28},{6,31},{7,30},{8,17},{9,... | collective-permute-start | bytes 95240 | tf_op jit(solution)/shard_map/ppermute | solution.py:32
  104.7 3.4 %collective-permute-start.41 = (f32[2,3968]{1,0:T(2,128)S(1)}, f32[2,3968]{1,0:T(2,128)S(1)}, u32[]{:S(2)}, u32[]{:S(2)}) collective-permute-start(f32[2,3968]{1,0:T(2,128)S(1)} %add.144), channel_id=1, source_target_pairs={{0,9},{1,8},{2,11},{3,10},{4,13},{5,12},{6,15},{7,14},{8,1},{9,0},... | collective-permute-start | bytes 95240 | tf_op jit(solution)/shard_map/ppermute | solution.py:32
  108.1 4.7 %collective-permute-start.45 = (f32[2,3968]{1,0:T(2,128)S(1)}, f32[2,3968]{1,0:T(2,128)S(1)}, u32[]{:S(2)}, u32[]{:S(2)}) collective-permute-start(f32[2,3968]{1,0:T(2,128)S(1)} %add_add_fusion.1), channel_id=1, source_target_pairs={{0,5},{1,4},{2,7},{3,6},{4,1},{5,0},{6,3},{7,2},{8,13},{9,12},{10,... | collective-permute-start | bytes 95240 | tf_op jit(solution)/shard_map/ppermute | solution.py:32
  109.2 5.2 %collective-permute-start.46 = (f32[2,3968]{1,0:T(2,128)S(1)}, f32[2,3968]{1,0:T(2,128)S(1)}, u32[]{:S(2)}, u32[]{:S(2)}) collective-permute-start(f32[2,3968]{1,0:T(2,128)S(1)} %add_add_fusion.1), channel_id=1, source_target_pairs={{0,7},{1,6},{2,5},{3,4},{4,3},{5,2},{6,1},{7,0},{8,15},{9,14},{10,... | collective-permute-start | bytes 95240 | tf_op jit(solution)/shard_map/ppermute | solution.py:32
  110.5 3.9 %collective-permute-start.44 = (f32[2,3968]{1,0:T(2,128)S(1)}, f32[2,3968]{1,0:T(2,128)S(1)}, u32[]{:S(2)}, u32[]{:S(2)}) collective-permute-start(f32[2,3968]{1,0:T(2,128)S(1)} %add_add_fusion.1), channel_id=1, source_target_pairs={{0,3},{1,2},{2,1},{3,0},{4,7},{5,6},{6,5},{7,4},{8,11},{9,10},{10,... | collective-permute-start | bytes 95240 | tf_op jit(solution)/shard_map/ppermute | solution.py:32

commit v8 on v7

--- a/solution.py
+++ b/solution.py
@@ -45,7 +45,7 @@
             bits = lambda b: (b, core) if on_lat else (0, b | core)
             if 2 * bit < size:
                 near, far, both = (swap(x, *bits(b)) for b in (bit, 2 * bit, 3 * bit))
-                x = (x + near) + (far + both)
+                x = (x + near) + (both + far)
                 bit *= 4
             else:
                 x = x + swap(x, *bits(bit))
@@ -167,8 +167,8 @@
 
 def own_flags_kernel(reach, *refs):
     words_hbm, coast_hbm, x_hbm, maps_hbm, series_hbm, place_ref = refs[:6]
-    m_ref, a_ref, mt_ref, spread_days_ref, u_ref, row_ref, near_ref, far_ref, maps_out, series_out = refs[6:16]
-    words_ref, coast_ref, x_ref, maps_ref, series_ref, spread_ref, bit_ref, sems = refs[16:]
+    m_ref, a_ref, held_ref, u_ref, row_ref, near_ref, far_ref, maps_out, series_out = refs[6:15]
+    words_ref, coast_ref, x_ref, maps_ref, series_ref, spread_ref, bit_ref, sems = refs[15:]
     rows = coast_ref.shape[0]
     loads = [
         pltpu.make_async_copy(words_hbm, words_ref, sems.at[0]),
@@ -186,7 +186,6 @@
     for load in loads:
         load.start()
     fill_spread(spread_ref, bit_ref)
-    fill_spread_days(spread_days_ref)
     loads[0].wait()
     loads[1].wait()
     for load, store in zip(loads[-2:], stores, strict=True):
@@ -203,12 +202,11 @@
         cell = slice(r * LANES, (r + 1) * LANES)
         for g in range(words_ref.shape[1] // LANES):
             words = words_ref[cell, g * LANES : (g + 1) * LANES] * coast
+            held_ref[cell, g * LANES : (g + 1) * LANES] = words
             given = unpack_words(words, spread_ref, bit_ref)
             at = slice(g * days, (g + 1) * days)
             m_ref[cell, at] = given
             a_ref[cell, at] = x_ref[cell, at] * given * ocean
-    column = jnp.concatenate([coasts[:, r : r + 1] for r in range(rows)], axis=0).astype(jnp.int32)
-    unpack_days(words_ref[...] * column, spread_days_ref, mt_ref)
     modes = maps_ref.shape[0]
     pieces = []
     for r in range(rows):
@@ -274,7 +272,7 @@
     far_ref[...] = jnp.where(odd, east, west)
 
 
-def masked_products(vs, u, low, chunk, m_ref):
+def masked_products(vs, u, low, chunk, m_ref, by_day=True):
     modes, days = vs.shape
     acc = None
     for first in range(0, days, chunk):
@@ -282,7 +280,10 @@
         v = vs[:, at]
         high, lower = split(jnp.concatenate([v * v[j : j + 1] for j in (low, low + 1)], axis=0))
         left = jnp.concatenate([high, lower], axis=0)
-        part = jnp.dot(left, m_ref[at], preferred_element_type=F32)
+        if by_day:
+            part = jnp.dot(left, m_ref[at], preferred_element_type=F32)
+        else:
+            part = lax.dot_general(left, m_ref[:, at], NT, preferred_element_type=F32)
         acc = part if acc is None else acc + part
     acc = acc[: 2 * modes] + acc[2 * modes :]
     return jnp.concatenate(
@@ -291,10 +292,11 @@
 
 
 def first_products_kernel(chunk, *refs):
-    near_ref, far_ref, place_ref, m_ref, spread_ref, u_own_ref, row_own_ref = refs[:7]
-    base_ref, v_ref, mh_ref, u_ref, row_ref = refs[-5:]
-    share = refs[7].shape[1]
-    for i, piece in enumerate(in_order([ref[...] for ref in refs[7:-5]], place_ref[3])):
+    near_ref, far_ref, place_ref, m_ref, u_own_ref, row_own_ref = refs[:6]
+    base_ref, inv_ref, v_ref, mh_ref, u_ref, row_ref, spread_ref = refs[-7:]
+    fill_spread_days(spread_ref)
+    share = refs[6].shape[1]
+    for i, piece in enumerate(in_order([ref[...] for ref in refs[6:-7]], place_ref[3])):
         v_ref[:, i * share : (i + 1) * share] = piece
     odd = place_ref[3] % 2 == 1
     west = jnp.where(odd, near_ref[...], far_ref[...])
@@ -313,21 +315,40 @@
     groups = [slice(base + half * g, base + half * (g + 1)) for g in range((west.shape[0] - base) // half)]
     words = jnp.concatenate([jnp.concatenate([west[at], east[at]], axis=0) for at in groups], axis=1)
     unpack_days(words.astype(jnp.int32) * coast, spread_ref, mh_ref)
-    base_ref[:, :own] = masked_products(v_ref, u_own, 0, chunk, m_ref)
+    base_ref[:, :own] = masked_products(v_ref, u_own, 0, chunk, m_ref, by_day=False)
     base_ref[:, own:] = masked_products(v_ref, u_halo, 0, chunk, mh_ref)
-
-
-def next_products_kernel(step, chunk, m_ref, mh_ref, v_ref, u_ref, base_ref):
+    inv_ref[...] = inverse_rows(v_ref[:2])
+
+
+def days_flags_kernel(held_ref, spread_ref, m_ref):
+    unpack_days(held_ref[...], spread_ref, m_ref)
+
+
+def inverse_rows(pair):
+    v0, v1 = (pair[0:1], pair[1:2])
+    h00, h01, h11 = (total_of(v0 * v0), total_of(v0 * v1), total_of(v1 * v1))
+    determ = h00 * h11 - h01 * h01
+    rows = [h11 / determ, h01 / determ, h00 / determ]
+    rows = [jnp.broadcast_to(z, (1, LANES)) for z in rows]
+    return jnp.concatenate(rows + [jnp.zeros((5, LANES), F32)], axis=0)
+
+
+def along(row, length):
+    return jnp.concatenate([row] * (length // LANES), axis=1)
+
+
+def next_products_kernel(step, chunk, m_ref, mh_ref, v_ref, u_ref, base_ref, inv_ref):
     low = 2 * step
     own = m_ref.shape[1]
     mode = lax.broadcasted_iota(jnp.int32, u_ref.shape, 0)
     u = jnp.where((mode >= low - 2) & (mode < low), 0.0, u_ref[...])
     base_ref[:, :own] = masked_products(v_ref, u[:, :own], low, chunk, m_ref)
     base_ref[:, own:] = masked_products(v_ref, u[:, own:], low, chunk, mh_ref)
-
-
-def changed_products(vn, un, pair, m_ref, mh_ref):
-    high, lower = split(jnp.concatenate([vn * pair[0:1], vn * pair[1:2]], axis=0))
+    inv_ref[...] = inverse_rows(v_ref[low : low + 2])
+
+
+def masked_rows(first, second, m_ref, mh_ref):
+    high, lower = split(jnp.concatenate([first * second[0:1], first * second[1:2]], axis=0))
     left = jnp.concatenate([high, lower], axis=0)
     acc = jnp.concatenate(
         [
@@ -336,18 +357,16 @@
         ],
         axis=1,
     )
-    acc = acc[:4] + acc[4:]
-    return jnp.concatenate([un[0:1] * acc[2 * j : 2 * j + 1] + un[1:2] * acc[2 * j + 1 : 2 * j + 2] for j in range(2)], axis=0)
-
-
-def new_fields(pair, u_pair, coast, proj):
-    v0, v1 = (pair[0:1], pair[1:2])
-    h00, h01, h11 = (total_of(v0 * v0), total_of(v0 * v1), total_of(v1 * v1))
-    add0, add1 = solve_pair(h00, h01, h01, h11, proj[0:1], proj[1:2])
-    return coast * (u_pair + jnp.concatenate([add0, add1], axis=0))
-
-
-def first_fields_kernel(rows, reach, near_ref, far_ref, place_ref, v_ref, u_ref, row_ref, xv_ref, base_ref, w_ref, xh_ref):
+    return acc[:4] + acc[4:]
+
+
+def new_fields(inv_ref, u_pair, coast, proj):
+    first, other, last = (along(inv_ref[i : i + 1], proj.shape[1]) for i in range(3))
+    p0, p1 = (proj[0:1], proj[1:2])
+    return coast * (u_pair + jnp.concatenate([first * p0 - other * p1, last * p1 - other * p0], axis=0))
+
+
+def first_fields_kernel(rows, reach, near_ref, far_ref, place_ref, inv_ref, u_ref, row_ref, xv_ref, base_ref, w_ref, xh_ref):
     odd = place_ref[3] % 2 == 1
     west = jnp.where(odd, near_ref[...], far_ref[...])
     east = jnp.where(odd, far_ref[...], near_ref[...])
@@ -356,42 +375,56 @@
     proj = jnp.concatenate([xv_ref[:2], xh[:2]], axis=1) - base_ref[...]
     coast = row_ref[...]
     count = 2 * rows
-    w_ref[:count] = to_block(new_fields(v_ref[:2], u_ref[:2], coast, proj), rows, reach)
+    w_ref[:count] = to_block(new_fields(inv_ref, u_ref[:2], coast, proj), rows, reach)
     w_ref[count:] = to_block(jnp.concatenate([coast, coast], axis=0), rows, reach)
 
 
 def fields_kernel(step, rows, reach, total, *refs):
-    m_ref, mh_ref, v_ref, u_ref, row_ref, xv_ref, xh_ref, base_ref, sum_ref, block_ref, w_ref, v_out, u_out = refs
+    m_ref, mh_ref, v_ref, u_ref, row_ref, xv_ref, xh_ref, base_ref, inv_ref, sum_ref, block_ref, w_ref, v_out, u_out = refs
     low = 2 * step
-    vn, un = new_pair(rows, reach, total, sum_ref, block_ref)
-    pair = v_ref[low : low + 2]
+    days = v_ref.shape[1]
+    sums = sum_ref[:, :days]
+    masked = masked_rows(sums, v_ref[low : low + 2], m_ref, mh_ref)
+    mixes, norms = mixing(total, sum_ref)
+    un = new_units(rows, reach, norms, block_ref)
+    cells = un.shape[1]
+    mixes = [[along(z, cells) for z in mix] for mix in mixes]
+    changed = []
+    for j in range(2):
+        p0, p1 = (masked[2 * j : 2 * j + 1], masked[2 * j + 1 : 2 * j + 2])
+        changed.append(sum(un[k : k + 1] * (mixes[k][0] * p0 + mixes[k][1] * p1) for k in range(2)))
     given = jnp.concatenate([xv_ref[low : low + 2], xh_ref[low : low + 2]], axis=1)
-    proj = given - base_ref[...] - changed_products(vn, un, pair, m_ref, mh_ref)
-    w_ref[...] = to_block(new_fields(pair, u_ref[low : low + 2], row_ref[...], proj), rows, reach)
-    v_out[...] = v_ref[...]
-    u_out[...] = u_ref[...]
-    v_out[low - 2 : low] = vn
+    proj = given - base_ref[...] - jnp.concatenate(changed, axis=0)
+    w_ref[...] = to_block(new_fields(inv_ref, u_ref[low : low + 2], row_ref[...], proj), rows, reach)
+    v_out[low - 2 : low] = new_series(total, sum_ref)
     u_out[low - 2 : low] = un
 
 
-def new_pair(rows, reach, total, sum_ref, block_ref):
-    days = sum_ref.shape[1] - LANES
-    gram = sum_ref[:, days:]
-    g00, g01, g11 = (gram[0:1, 0:1], gram[0:1, 1:2], gram[1:2, 1:2])
+def mixing(total, sum_ref):
+    days = sum_ref.shape[1] - 2 * LANES
+    g00, g01 = (sum_ref[0:1, days : days + LANES], sum_ref[0:1, days + LANES :])
+    g11 = sum_ref[1:2, days + LANES :]
     n0, n1 = (jnp.sqrt(g00 / total + EPS), jnp.sqrt(g11 / total + EPS))
     g00, g01, g11 = (g00 / (n0 * n0), g01 / (n0 * n1), g11 / (n1 * n1))
     determ = g00 * g11 - g01 * g01
+    cross = g01 / determ
+    return [[g11 / determ / n0, -(cross / n1)], [-(cross / n0), g00 / determ / n1]], (n0, n1)
+
+
+def new_series(total, sum_ref):
+    days = sum_ref.shape[1] - 2 * LANES
     p0, p1 = (sum_ref[0:1, :days], sum_ref[1:2, :days])
-    cross = g01 / determ
-    first = (g11 / determ / n0) * p0 - (cross / n1) * p1
-    second = (g00 / determ / n1) * p1 - (cross / n0) * p0
+    mixes, _ = mixing(total, sum_ref)
+    return jnp.concatenate([along(mix[0], days) * p0 + along(mix[1], days) * p1 for mix in mixes], axis=0)
+
+
+def new_units(rows, reach, norms, block_ref):
     field = from_block(block_ref[...], rows, reach)
-    unit = jnp.concatenate([field[0:1] / n0, field[1:2] / n1], axis=0)
-    return jnp.concatenate([first, second], axis=0), unit
+    return jnp.concatenate([field[k : k + 1] / along(norms[k], field.shape[1]) for k in range(2)], axis=0)
 
 
 def sums_kernel(step, rows, chunk, *refs):
-    m_ref, a_ref, v_ref, u_ref, place_ref, klon_ref, cosl_ref, w_ref, gb_ref, ga_ref = refs[:10]
+    m_ref, a_ref, v_ref, u_ref, place_ref, klon_ref, cosl_ref, w_ref, ga_ref, gb_ref = refs[:10]
     refs = refs[10:]
     if step:
         coef_ref, sum_ref, block_ref = refs
@@ -437,10 +470,10 @@
     left = jnp.concatenate([high, lower], axis=0)
     high, lower = split(weighted)
     left_a = jnp.concatenate([high, lower], axis=0)
-    lane = lane_ids((1, LANES))
     for j in range(2):
-        gram = [total_of(weighted[j : j + 1] * fresh[i : i + 1]) for i in range(2)]
-        sum_ref[j : j + 1, days:] = jnp.where(lane == 0, gram[0], jnp.where(lane == 1, gram[1], 0.0))
+        for i in range(2):
+            gram = total_of(weighted[j : j + 1] * fresh[i : i + 1])
+            sum_ref[j : j + 1, days + i * LANES : days + (i + 1) * LANES] = jnp.broadcast_to(gram, (1, LANES))
     old = [[total_of(weighted[j : j + 1] * u[low + i : low + i + 1]) for i in range(2)] for j in range(2)]
     for first in range(0, days, chunk):
         at = slice(first, first + chunk)
@@ -466,7 +499,8 @@
         pltpu.make_async_copy(maps_new, maps_out.at[pl.ds(0, PAIRS)], sems.at[0]),
         pltpu.make_async_copy(series_new, series_out.at[pl.ds(0, PAIRS)], sems.at[1]),
     ]
-    vn, un = new_pair(rows, reach, total, sum_ref, block_ref)
+    un = new_units(rows, reach, mixing(total, sum_ref)[1], block_ref)
+    vn = new_series(total, sum_ref)
     u = jnp.concatenate([u_ref[: PAIRS - 2], un], axis=0)
     for r in range(rows):
         maps_new[:, r, :] = u[:, r * LANES : (r + 1) * LANES]
@@ -481,8 +515,8 @@
         store.wait()
 
 
-def call(kernel, name, outs, scratch, args, smem=(), mib=24, flops=0, copies=0, in_hbm=(), out_hbm=(), aliases={}):
-    moved = sum(z.size * z.dtype.itemsize for z in args)
+def call(kernel, name, outs, scratch, args, smem=(), mib=24, flops=0, copies=0, in_hbm=(), out_hbm=(), aliases={}, light=False):
+    moved = 0 if light else sum(z.size * z.dtype.itemsize for z in args)
     hbm = pl.BlockSpec(memory_space=pl.ANY)
     args = [pltpu.with_memory_space_constraint(z, pltpu.HBM) if i in in_hbm else z for i, z in enumerate(args)]
     return pl.pallas_call(
@@ -527,10 +561,10 @@
     inputs = [missing_date_bitmask.reshape(own, words), ocean_binary_mask, sea_heat_deviations.reshape(own, days)]
     inputs += [mode_maps, mode_series]
     place, klon, cosl = lax.optimization_barrier((place, klon, cosl))
-    m, a, m_days, spread, u, row, near, far, maps_out, series_out = call(
+    m, a, held, u, row, near, far, maps_out, series_out = call(
         functools.partial(own_flags_kernel, reach),
         "own_flags",
-        [((own, days), BF16), ((own, days), BF16), ((days, own), BF16), ((days // words_per, 2 * LANES), BF16)]
+        [((own, days), BF16), ((own, days), BF16), ((own, words), jnp.int32)]
         + [((modes, own), F32), ((1, own), F32), edge, edge]
         + [(mode_maps.shape, F32), (mode_series.shape, F32)],
         [((own, words), jnp.int32), ((rows, LANES), jnp.int32), ((own, days), BF16)]
@@ -538,13 +572,13 @@
         [*inputs, place],
         smem=(5,),
         in_hbm=range(5),
-        out_hbm=(8, 9),
+        out_hbm=(7, 8),
         copies=6 + rows,
         flops=4 * LANES * own * days,
     )
     if lax.axis_size("lon") == 8:
         pieces = [swap(mode_series, 0, b | 1) for b in (2, 4, 6)]
-        *pieces, m, a, m_days = lax.optimization_barrier((*pieces, m, a, m_days))
+        *pieces, m, a = lax.optimization_barrier((*pieces, m, a))
         pieces = [z for piece in pieces for z in (swap(piece, 0, 1), piece)]
         pieces = [mode_series, swap(mode_series, 0, 1), *pieces]
     else:
@@ -557,17 +591,27 @@
         [((PAIRS, days), F32)],
         [a, place, *pieces],
         smem=(1,),
-        flops=4 * PAIRS * own * days,
+        light=True,
     )
     near_xv, far_xv = lon_partners(near_xv, far_xv)
-    base, v, m_halo, u, row = call(
+    base, inverse, v, m_halo, u, row, spread = call(
         functools.partial(first_products_kernel, chunk),
         "first_products",
-        [((2, cells), F32), ((modes, days), F32), ((days, sides), BF16), ((modes, cells), F32), ((1, cells), F32)],
+        [((2, cells), F32), ((8, LANES), F32), ((modes, days), F32), ((days, sides), BF16), ((modes, cells), F32), ((1, cells), F32)]
+        + [((days // words_per, 2 * LANES), BF16)],
         [],
-        [near, far, place, m_days, spread, u, row, *pieces],
+        [near, far, place, m, u, row, *pieces],
         smem=(2,),
         flops=8 * modes * cells * days,
+    )
+
+    (m_days,) = call(
+        days_flags_kernel,
+        "days_flags",
+        [((days, own), BF16)],
+        [],
+        [held, spread],
+        flops=4 * LANES * own * days,
     )
 
     count = 2 * rows
@@ -580,7 +624,7 @@
                 "fields_0",
                 [((2 * count, 2 * LANES), F32), ((PAIRS, sides), F32)],
                 [],
-                [near_xv, far_xv, place, v, u, row, xv, base],
+                [near_xv, far_xv, place, inverse, u, row, xv, base],
                 smem=(2,),
             )
         else:
@@ -589,27 +633,28 @@
                 f"fields_{step}",
                 [((count, 2 * LANES), F32), ((modes, days), F32), ((modes, cells), F32)],
                 [],
-                [m_days, m_halo, v, u, row, xv, xv_halo, base, summed, block],
+                [m_days, m_halo, v, u, row, xv, xv_halo, base, inverse, summed, block],
                 flops=8 * modes * cells * days,
+                aliases={2: 1, 3: 2},
             )
         got_a, got_b = lat_partners(fresh)
-        outs = [((2, days + LANES), F32), ((count, 2 * LANES), F32)]
+        outs = [((2, days + 2 * LANES), F32), ((count, 2 * LANES), F32)]
         coef = ((5 * 3 * count, 2 * LANES), F32)
         partial_sums, block, *made = call(
             functools.partial(sums_kernel, step, rows, chunk),
             f"sums_{step}",
             outs if step else [*outs, coef],
             [],
-            [m, a, v, u, place, klon, cosl, fresh, got_b, got_a, *coefs],
+            [m, a, v, u, place, klon, cosl, fresh, got_a, got_b, *coefs],
             smem=(4,),
             flops=8 * modes * own * days,
         )
         coefs = coefs or made
         if step + 1 < STEPS:
-            (base,) = call(
+            base, inverse = call(
                 functools.partial(next_products_kernel, step + 1, chunk),
                 f"next_products_{step + 1}",
-                [((2, cells), F32)],
+                [((2, cells), F32), ((8, LANES), F32)],
                 [],
                 [m_days, m_halo, v, u],
                 flops=8 * modes * cells * days,

time: 117 us -> 115 us (0.983)
    pallas_call x15 -> x16, Pallas kernels: 32.5 us -> 31.8 us  [call(): pl.pallas_call(kernel, out_shape=[jax.ShapeDtypeStruct(s, t) for s, t in...]
  transfers between devices with their start and end apart: 47 -> 47, of which waited for: 33 -> 35; matrix products, arithmetic and copies ran while one was open for 0% -> 0% of each run, Pallas kernels for 14% -> 15%
where the time goes in v8:
time: 115 us
  starting transfers between devices  45.9 us (40%)
  waiting for transfers between devices  35.9 us (31%)
  Pallas kernels  31.8 us (28%)
    pallas_call x16, Pallas kernels, call(): pl.pallas_call(kernel, out_shape=[jax.ShapeDtypeStruct(s, t) for s, t in...  31.8 us
    ppermute x37, starting transfers between devices, swap(): lax.ppermute(x, ('lat', 'lon'), pairing(lambda i: i ^ lat_bits, lambda j:...  31.6 us
    ppermute x37, waiting for transfers between devices, swap(): lax.ppermute(x, ('lat', 'lon'), pairing(lambda i: i ^ lat_bits, lambda j:...  24.1 us
    ppermute x4, waiting for transfers between devices, lat_partners(): lax.ppermute(x, ('lat', 'lon'), pairing(lambda i: (i + 1 if i % 2 else i...  8.37 us
    ppermute x4, starting transfers between devices, lat_partners(): lax.ppermute(x, ('lat', 'lon'), pairing(lambda i: (i + 1 if i % 2 else i...  6.54 us
    ppermute x2, starting transfers between devices, lon_partners(): lax.ppermute(far, ('lat', 'lon'), pairing(same, lambda j: (j + 1 if j % 2...  4.07 us
    ppermute x4, starting transfers between devices, lat_partners(): got_a = lax.ppermute(x, ('lat', 'lon'), pairing(lambda i: i ^ 1, same))  3.67 us
    ppermute x4, waiting for transfers between devices, lat_partners(): got_a = lax.ppermute(x, ('lat', 'lon'), pairing(lambda i: i ^ 1, same))  2.64 us
  transfers between devices with their start and end apart: 47, of which 35 were waited for; matrix products, arithmetic and copies ran while one was open for 0% of the time, Pallas kernels for 15%

profile of v8, /device:TPU:0, one launch (start us, length us, event | category | flops | bytes accessed | tf_op | source)
XLA Modules:
  0.0 115.3 jit_solution(10696858233022006268)
XLA Ops:
  1.2 4.7 %collective-permute-start.4 = (f32[48,480]{1,0:T(8,128)}, f32[48,480]{1,0:T(8,128)S(1)}, u32[]{:S(2)}, u32[]{:S(2)}) collective-permute-start(f32[48,480]{1,0:T(8,128)} %refs_2_.1), channel_id=1, source_target_pairs={{0,7},{1,6},{2,5},{3,4},{4,3},{5,2},{6,1},{7,0},{8,15},{9,14},{10,... | collective-permute-start | bytes 276488 | tf_op jit(solution)/shard_map/ppermute | solution.py:32
  6.5 5.7 %own_flags.1 = (bf16[512,3840]{1,0:T(8,128)(2,1)S(1)}, bf16[512,3840]{1,0:T(8,128)(2,1)S(1)}, s32[512,256]{1,0:T(8,128)S(1)}, f32[48,512]{1,0:T(8,128)S(1)}, f32...) custom-call(s32[512,256]{1,0:T(8,128)} %bitcast.6, ...), custom_call_target="tpu_custom_call" | custom-call | flops 1006632960 | bytes 4648976 | tf_op jit(solution)/shard_map/own_flags/pallas_call | solution.py:522
  12.7 3.6 %collective-permute-start.1 = (f32[184,128]{1,0:T(8,128)S(1)}, f32[184,128]{1,0:T(8,128)S(1)}, u32[]{:S(2)}, u32[]{:S(2)}) collective-permute-start(f32[184,128]{1,0:T(8,128)S(1)} %get-tuple-element.58), channel_id=1, source_target_pairs={{0,7},{1,2},{2,1},{3,4},{4,3},{5,6},{6,5},{7,0},{8,15},{9,10},{10,... | collective-permute-start | bytes 282632 | tf_op jit(solution)/shard_map/ppermute | solution.py:67
  16.9 0.7 collective-permute-done.6.refs_8_.refs_4_
  18.1 1.7 %given.1 = (f32[8,512]{1,0:T(8,128)S(1)}, f32[8,128]{1,0:T(8,128)S(1)}, f32[8,128]{1,0:T(8,128)S(1)}) custom-call(bf16[512,3840]{1,0:T(8,128)(2,1)S(1)} %get-tuple-element.72.refs_0_.refs_1_, s32[4]{0:T(128)S(1)} %pad_add_fusion.refs_5_.refs_2_.refs_1_.place_ref.refs_4_, f32[48,480]{1,0:T(8,128)S(1)} %copy-done, ...), custom_call_target="tpu_custom_call" | custom-call | tf_op jit(solution)/shard_map/given/pallas_call | solution.py:522
  20.5 3.5 %first_products.1 = (f32[2,640]{1,0:T(2,128)S(1)}, f32[8,128]{1,0:T(8,128)S(1)}, f32[48,3840]{1,0:T(8,128)S(1)}, bf16[3840,128]{1,0:T(8,128)(2,1)S(1)}, f32[48,6...) custom-call(f32[184,128]{1,0:T(8,128)S(1)} %collective-permute-done.refs_0_, ...), custom_call_target="tpu_custom_call" | custom-call | flops 943718400 | bytes 4958224 | tf_op jit(solution)/shard_map/first_products/pallas_call | solution.py:522
  24.0 0.8 collective-permute-done.10.far_ref
  24.8 0.6 fields_0.1
  25.5 2.5 %collective-permute-start.12 = (f32[16,256]{1,0:T(8,128)S(1)}, f32[16,256]{1,0:T(8,128)S(1)}, u32[]{:S(2)}, u32[]{:S(2)}) collective-permute-start(f32[16,256]{1,0:T(8,128)S(1)} %get-tuple-element.83.refs_7_), channel_id=1, source_target_pairs={{0,24},{1,25},{2,26},{3,27},{4,28},{5,29},{6,30},{7,31},{8,16},{9,... | collective-permute-start | bytes 49160 | tf_op jit(solution)/shard_map/ppermute | solution.py:60
  28.5 1.7 %collective-permute-done.12.refs_9_ = f32[16,256]{1,0:T(8,128)S(1)} collective-permute-done((f32[16,256]{1,0:T(8,128)S(1)}, f32[16,256]{1,0:T(8,128)S(1)}, u32[]{:S(2)}, u32[]{:S(2)}) %collective-permute-start.12) | collective-permute-done | bytes 16416 | tf_op jit(solution)/shard_map/ppermute | solution.py:60
  30.2 1.5 %collective-permute-done.11.refs_8_ = f32[16,256]{1,0:T(8,128)S(1)} collective-permute-done((f32[16,256]{1,0:T(8,128)S(1)}, f32[16,256]{1,0:T(8,128)S(1)}, u32[]{:S(2)}, u32[]{:S(2)}) %collective-permute-start.11) | collective-permute-done | bytes 16416 | tf_op jit(solution)/shard_map/ppermute | solution.py:59
  31.7 2.4 %sums_0.1 = (f32[2,4096]{1,0:T(2,128)S(1)}, f32[8,256]{1,0:T(8,128)S(1)}, f32[120,256]{1,0:T(8,128)S(1)}) custom-call(bf16[512,3840]{1,0:T(8,128)(2,1)S(1)} %get-tuple-element.61.refs_3_.refs_0_, bf16[512,3840]{1,0:T(8,128)(2,1)S(1)} %get-tuple-element.72.refs_0_.refs_1_, f32[48,3840]{1,0:T(8,128)S(1)} %get-tuple-element.69.v_ref.refs_2_, ...), custom_call_target="tpu_custom_call" | custom-call | flops 754974720 | bytes 8806416 | tf_op jit(solution)/shard_map/sums_0/pallas_call | solution.py:522
  34.2 1.2 %collective-permute-done.13 = f32[2,4096]{1,0:T(2,128)S(1)} collective-permute-done((f32[2,4096]{1,0:T(2,128)S(1)}, f32[2,4096]{1,0:T(2,128)S(1)}, u32[]{:S(2)}, u32[]{:S(2)}) %collective-permute-start.13) | collective-permute-done | bytes 32800 | tf_op jit(solution)/shard_map/ppermute | solution.py:32
  35.8 1.4 %collective-permute-start.15 = (f32[2,4096]{1,0:T(2,128)S(1)}, f32[2,4096]{1,0:T(2,128)S(1)}, u32[]{:S(2)}, u32[]{:S(2)}) collective-permute-start(f32[2,4096]{1,0:T(2,128)S(1)} %add.123), channel_id=1, source_target_pairs={{0,25},{1,24},{2,27},{3,26},{4,29},{5,28},{6,31},{7,30},{8,17},{9,... | collective-permute-start | bytes 98312 | tf_op jit(solution)/shard_map/ppermute | solution.py:32
  37.2 1.2 %collective-permute-start.14 = (f32[2,4096]{1,0:T(2,128)S(1)}, f32[2,4096]{1,0:T(2,128)S(1)}, u32[]{:S(2)}, u32[]{:S(2)}) collective-permute-start(f32[2,4096]{1,0:T(2,128)S(1)} %add.123), channel_id=1, source_target_pairs={{0,9},{1,8},{2,11},{3,10},{4,13},{5,12},{6,15},{7,14},{8,1},{9,0},... | collective-permute-start | bytes 98312 | tf_op jit(solution)/shard_map/ppermute | solution.py:32
  38.5 2.0 %days_flags.1.m_ref.refs_0_ = bf16[3840,512]{1,0:T(8,128)(2,1)S(1)} custom-call(s32[512,256]{1,0:T(8,128)S(1)} %get-tuple-element.56.held_ref, bf16[1920,256]{1,0:T(8,128)(2,1)S(1)} %get-tuple-element.67.spread_ref), custom_call_target="tpu_custom_call" | custom-call | flops 1006632960 | bytes 1507328 | tf_op jit(solution)/shard_map/days_flags/pallas_call | solution.py:522
  41.0 2.7 %collective-permute-start.18 = (f32[2,4096]{1,0:T(2,128)S(1)}, f32[2,4096]{1,0:T(2,128)S(1)}, u32[]{:S(2)}, u32[]{:S(2)}) collective-permute-start(f32[2,4096]{1,0:T(2,128)S(1)} %add_add_fusion.7), channel_id=1, source_target_pairs={{0,7},{1,6},{2,5},{3,4},{4,3},{5,2},{6,1},{7,0},{8,15},{9,14},{10,... | collective-permute-start | bytes 98312 | tf_op jit(solution)/shard_map/ppermute | solution.py:32
  44.0 1.5 %next_products_1.1 = (f32[2,640]{1,0:T(2,128)S(1)}, f32[8,128]{1,0:T(8,128)S(1)}) custom-call(bf16[3840,512]{1,0:T(8,128)(2,1)S(1)} %days_flags.1.m_ref.refs_0_, bf16[3840,128]{1,0:T(8,128)(2,1)S(1)} %get-tuple-element.68.mh_ref.refs_1_, f32[48,3840]{1,0:T(8,128)S(1)} %get-tuple-element.69.v_ref.refs_2_, f32[48,640]{1,0:T(8,128)S(1)} %get-tuple-element.70.u_ref.refs_3_), custom_call_target="tpu_custom_call" | custom-call | flops 943718400 | bytes 5775360 | tf_op jit(solution)/shard_map/next_products_1/pallas_call | solution.py:522
  45.5 1.1 collective-permute-done.19
  46.7 0.8 collective-permute-done.17
  47.5 0.9 fields_1.1
  48.4 1.2 %collective-permute-start.21 = (f32[8,256]{1,0:T(8,128)S(1)}, f32[8,256]{1,0:T(8,128)S(1)}, u32[]{:S(2)}, u32[]{:S(2)}) collective-permute-start(f32[8,256]{1,0:T(8,128)S(1)} %get-tuple-element.90.refs_7_), channel_id=1, source_target_pairs={{0,24},{1,25},{2,26},{3,27},{4,28},{5,29},{6,30},{7,31},{8,16},{9,... | collective-permute-start | bytes 24584 | tf_op jit(solution)/shard_map/ppermute | solution.py:60
  49.6 1.1 collective-permute-start.20
  50.7 2.4 %collective-permute-done.21.refs_9_ = f32[8,256]{1,0:T(8,128)S(1)} collective-permute-done((f32[8,256]{1,0:T(8,128)S(1)}, f32[8,256]{1,0:T(8,128)S(1)}, u32[]{:S(2)}, u32[]{:S(2)}) %collective-permute-start.21) | collective-permute-done | bytes 8224 | tf_op jit(solution)/shard_map/ppermute | solution.py:60
  53.2 2.4 %sums_1.1 = (f32[2,4096]{1,0:T(2,128)S(1)}, f32[8,256]{1,0:T(8,128)S(1)}) custom-call(bf16[512,3840]{1,0:T(8,128)(2,1)S(1)} %get-tuple-element.61.refs_3_.refs_0_, bf16[512,3840]{1,0:T(8,128)(2,1)S(1)} %get-tuple-element.72.refs_0_.refs_1_, f32[48,3840]{1,0:T(8,128)S(1)} %get-tuple-element.86.v_ref.refs_2_, f32[48,640]{1,0:T(8,128)S(1)} %get-tuple-element.87.u_ref.refs_3_, ...), custom_call_target="tpu_custom_call" | custom-call | flops 754974720 | bytes 8904720 | tf_op jit(solution)/shard_map/sums_1/pallas_call | solution.py:522
  55.7 1.2 %collective-permute-done.22 = f32[2,4096]{1,0:T(2,128)S(1)} collective-permute-done((f32[2,4096]{1,0:T(2,128)S(1)}, f32[2,4096]{1,0:T(2,128)S(1)}, u32[]{:S(2)}, u32[]{:S(2)}) %collective-permute-start.22) | collective-permute-done | bytes 32800 | tf_op jit(solution)/shard_map/ppermute | solution.py:32
  56.9 1.3 %collective-permute-start.25 = (f32[2,4096]{1,0:T(2,128)S(1)}, f32[2,4096]{1,0:T(2,128)S(1)}, u32[]{:S(2)}, u32[]{:S(2)}) collective-permute-start(f32[2,4096]{1,0:T(2,128)S(1)} %add.130), channel_id=1, source_target_pairs={{0,17},{1,16},{2,19},{3,18},{4,21},{5,20},{6,23},{7,22},{8,25},{9,... | collective-permute-start | bytes 98312 | tf_op jit(solution)/shard_map/ppermute | solution.py:32
  58.3 1.0 collective-permute-start.24
  59.3 0.7 collective-permute-start.23
  60.4 2.2 %collective-permute-done.24 = f32[2,4096]{1,0:T(2,128)S(1)} collective-permute-done((f32[2,4096]{1,0:T(2,128)S(1)}, f32[2,4096]{1,0:T(2,128)S(1)}, u32[]{:S(2)}, u32[]{:S(2)}) %collective-permute-start.24) | collective-permute-done | bytes 32800 | tf_op jit(solution)/shard_map/ppermute | solution.py:32
  62.8 3.1 %collective-permute-start.27 = (f32[2,4096]{1,0:T(2,128)S(1)}, f32[2,4096]{1,0:T(2,128)S(1)}, u32[]{:S(2)}, u32[]{:S(2)}) collective-permute-start(f32[2,4096]{1,0:T(2,128)S(1)} %add_add_fusion.5), channel_id=1, source_target_pairs={{0,7},{1,6},{2,5},{3,4},{4,3},{5,2},{6,1},{7,0},{8,15},{9,14},{10,... | collective-permute-start | bytes 98312 | tf_op jit(solution)/shard_map/ppermute | solution.py:32
  65.9 1.4 %next_products_2.1 = (f32[2,640]{1,0:T(2,128)S(1)}, f32[8,128]{1,0:T(8,128)S(1)}) custom-call(bf16[3840,512]{1,0:T(8,128)(2,1)S(1)} %days_flags.1.m_ref.refs_0_, bf16[3840,128]{1,0:T(8,128)(2,1)S(1)} %get-tuple-element.68.mh_ref.refs_1_, f32[48,3840]{1,0:T(8,128)S(1)} %get-tuple-element.86.v_ref.refs_2_, f32[48,640]{1,0:T(8,128)S(1)} %get-tuple-element.87.u_ref.refs_3_), custom_call_target="tpu_custom_call" | custom-call | flops 943718400 | bytes 5775360 | tf_op jit(solution)/shard_map/next_products_2/pallas_call | solution.py:522
  67.2 1.1 collective-permute-done.27
  68.3 1.2 %collective-permute-done.26 = f32[2,4096]{1,0:T(2,128)S(1)} collective-permute-done((f32[2,4096]{1,0:T(2,128)S(1)}, f32[2,4096]{1,0:T(2,128)S(1)}, u32[]{:S(2)}, u32[]{:S(2)}) %collective-permute-start.26) | collective-permute-done | bytes 32800 | tf_op jit(solution)/shard_map/ppermute | solution.py:32
  69.5 0.9 fields_2.1
  70.4 1.8 %collective-permute-start.30 = (f32[8,256]{1,0:T(8,128)S(1)}, f32[8,256]{1,0:T(8,128)S(1)}, u32[]{:S(2)}, u32[]{:S(2)}) collective-permute-start(f32[8,256]{1,0:T(8,128)S(1)} %get-tuple-element.98.refs_7_), channel_id=1, source_target_pairs={{0,24},{1,25},{2,26},{3,27},{4,28},{5,29},{6,30},{7,31},{8,16},{9,... | collective-permute-start | bytes 24584 | tf_op jit(solution)/shard_map/ppermute | solution.py:60
  72.2 1.0 collective-permute-start.29
  73.2 1.8 %collective-permute-done.30.refs_9_ = f32[8,256]{1,0:T(8,128)S(1)} collective-permute-done((f32[8,256]{1,0:T(8,128)S(1)}, f32[8,256]{1,0:T(8,128)S(1)}, u32[]{:S(2)}, u32[]{:S(2)}) %collective-permute-start.30) | collective-permute-done | bytes 8224 | tf_op jit(solution)/shard_map/ppermute | solution.py:60
  75.0 0.8 collective-permute-done.29.refs_8_
  75.8 2.4 %sums_2.1 = (f32[2,4096]{1,0:T(2,128)S(1)}, f32[8,256]{1,0:T(8,128)S(1)}) custom-call(bf16[512,3840]{1,0:T(8,128)(2,1)S(1)} %get-tuple-element.61.refs_3_.refs_0_, bf16[512,3840]{1,0:T(8,128)(2,1)S(1)} %get-tuple-element.72.refs_0_.refs_1_, f32[48,3840]{1,0:T(8,128)S(1)} %get-tuple-element.94.v_ref.refs_2_, f32[48,640]{1,0:T(8,128)S(1)} %get-tuple-element.95.u_ref.refs_3_, ...), custom_call_target="tpu_custom_call" | custom-call | flops 754974720 | bytes 8904720 | tf_op jit(solution)/shard_map/sums_2/pallas_call | solution.py:522
  78.3 1.2 %collective-permute-done.31 = f32[2,4096]{1,0:T(2,128)S(1)} collective-permute-done((f32[2,4096]{1,0:T(2,128)S(1)}, f32[2,4096]{1,0:T(2,128)S(1)}, u32[]{:S(2)}, u32[]{:S(2)}) %collective-permute-start.31) | collective-permute-done | bytes 32800 | tf_op jit(solution)/shard_map/ppermute | solution.py:32
  79.8 2.0 %collective-permute-start.33 = (f32[2,4096]{1,0:T(2,128)S(1)}, f32[2,4096]{1,0:T(2,128)S(1)}, u32[]{:S(2)}, u32[]{:S(2)}) collective-permute-start(f32[2,4096]{1,0:T(2,128)S(1)} %add.137), channel_id=1, source_target_pairs={{0,25},{1,24},{2,27},{3,26},{4,29},{5,28},{6,31},{7,30},{8,17},{9,... | collective-permute-start | bytes 98312 | tf_op jit(solution)/shard_map/ppermute | solution.py:32
  81.8 0.8 collective-permute-start.32
  82.9 1.1 collective-permute-done.33
  84.0 1.1 collective-permute-done.32
  85.2 2.6 %collective-permute-start.36 = (f32[2,4096]{1,0:T(2,128)S(1)}, f32[2,4096]{1,0:T(2,128)S(1)}, u32[]{:S(2)}, u32[]{:S(2)}) collective-permute-start(f32[2,4096]{1,0:T(2,128)S(1)} %add_add_fusion.3), channel_id=1, source_target_pairs={{0,7},{1,6},{2,5},{3,4},{4,3},{5,2},{6,1},{7,0},{8,15},{9,14},{10,... | collective-permute-start | bytes 98312 | tf_op jit(solution)/shard_map/ppermute | solution.py:32
  88.2 1.4 %next_products_3.1 = (f32[2,640]{1,0:T(2,128)S(1)}, f32[8,128]{1,0:T(8,128)S(1)}) custom-call(bf16[3840,512]{1,0:T(8,128)(2,1)S(1)} %days_flags.1.m_ref.refs_0_, bf16[3840,128]{1,0:T(8,128)(2,1)S(1)} %get-tuple-element.68.mh_ref.refs_1_, f32[48,3840]{1,0:T(8,128)S(1)} %get-tuple-element.94.v_ref.refs_2_, f32[48,640]{1,0:T(8,128)S(1)} %get-tuple-element.95.u_ref.refs_3_), custom_call_target="tpu_custom_call" | custom-call | flops 943718400 | bytes 5775360 | tf_op jit(solution)/shard_map/next_products_3/pallas_call | solution.py:522
  89.6 1.6 %collective-permute-done.37 = f32[2,4096]{1,0:T(2,128)S(1)} collective-permute-done((f32[2,4096]{1,0:T(2,128)S(1)}, f32[2,4096]{1,0:T(2,128)S(1)}, u32[]{:S(2)}, u32[]{:S(2)}) %collective-permute-start.37) | collective-permute-done | bytes 32800 | tf_op jit(solution)/shard_map/ppermute | solution.py:32
  91.1 0.7 collective-permute-done.35
  91.9 0.9 fields_3.1
  92.8 1.1 collective-permute-start.39
  93.8 1.0 collective-permute-start.38
  94.9 2.5 %collective-permute-done.39.refs_9_ = f32[8,256]{1,0:T(8,128)S(1)} collective-permute-done((f32[8,256]{1,0:T(8,128)S(1)}, f32[8,256]{1,0:T(8,128)S(1)}, u32[]{:S(2)}, u32[]{:S(2)}) %collective-permute-start.39) | collective-permute-done | bytes 8224 | tf_op jit(solution)/shard_map/ppermute | solution.py:60
  97.5 2.4 %sums_3.1 = (f32[2,4096]{1,0:T(2,128)S(1)}, f32[8,256]{1,0:T(8,128)S(1)}) custom-call(bf16[512,3840]{1,0:T(8,128)(2,1)S(1)} %get-tuple-element.61.refs_3_.refs_0_, bf16[512,3840]{1,0:T(8,128)(2,1)S(1)} %get-tuple-element.72.refs_0_.refs_1_, f32[48,3840]{1,0:T(8,128)S(1)} %get-tuple-element.101.refs_2_.refs_0_, ...), custom_call_target="tpu_custom_call" | custom-call | flops 754974720 | bytes 8904720 | tf_op jit(solution)/shard_map/sums_3/pallas_call | solution.py:522
  100.0 1.2 %collective-permute-done.40 = f32[2,4096]{1,0:T(2,128)S(1)} collective-permute-done((f32[2,4096]{1,0:T(2,128)S(1)}, f32[2,4096]{1,0:T(2,128)S(1)}, u32[]{:S(2)}, u32[]{:S(2)}) %collective-permute-start.40) | collective-permute-done | bytes 32800 | tf_op jit(solution)/shard_map/ppermute | solution.py:32
  101.2 1.3 %collective-permute-start.43 = (f32[2,4096]{1,0:T(2,128)S(1)}, f32[2,4096]{1,0:T(2,128)S(1)}, u32[]{:S(2)}, u32[]{:S(2)}) collective-permute-start(f32[2,4096]{1,0:T(2,128)S(1)} %add.144), channel_id=1, source_target_pairs={{0,17},{1,16},{2,19},{3,18},{4,21},{5,20},{6,23},{7,22},{8,25},{9,... | collective-permute-start | bytes 98312 | tf_op jit(solution)/shard_map/ppermute | solution.py:32
  102.5 1.0 collective-permute-start.42
  103.5 0.8 collective-permute-start.41
  104.6 2.1 %collective-permute-done.42 = f32[2,4096]{1,0:T(2,128)S(1)} collective-permute-done((f32[2,4096]{1,0:T(2,128)S(1)}, f32[2,4096]{1,0:T(2,128)S(1)}, u32[]{:S(2)}, u32[]{:S(2)}) %collective-permute-start.42) | collective-permute-done | bytes 32800 | tf_op jit(solution)/shard_map/ppermute | solution.py:32
  107.2 2.2 %collective-permute-start.45 = (f32[2,4096]{1,0:T(2,128)S(1)}, f32[2,4096]{1,0:T(2,128)S(1)}, u32[]{:S(2)}, u32[]{:S(2)}) collective-permute-start(f32[2,4096]{1,0:T(2,128)S(1)} %add_add_fusion.1), channel_id=1, source_target_pairs={{0,7},{1,6},{2,5},{3,4},{4,3},{5,2},{6,1},{7,0},{8,15},{9,14},{10,... | collective-permute-start | bytes 98312 | tf_op jit(solution)/shard_map/ppermute | solution.py:32
  109.4 0.6 collective-permute-start.44
  110.0 1.9 %collective-permute-done.46 = f32[2,4096]{1,0:T(2,128)S(1)} collective-permute-done((f32[2,4096]{1,0:T(2,128)S(1)}, f32[2,4096]{1,0:T(2,128)S(1)}, u32[]{:S(2)}, u32[]{:S(2)}) %collective-permute-start.46) | collective-permute-done | bytes 32800 | tf_op jit(solution)/shard_map/ppermute | solution.py:32
  112.3 1.0 collective-permute-done.44
  113.4 1.8 %last.1 = (f32[48,4,128]{2,1,0:T(4,128)}, f32[48,480]{1,0:T(8,128)}) custom-call(f32[48,3840]{1,0:T(8,128)S(1)} %get-tuple-element.101.refs_2_.refs_0_, f32[48,640]{1,0:T(8,128)S(1)} %get-tuple-element.102.refs_3_.refs_1_, f32[2,4096]{1,0:T(2,128)S(1)} %add_add_fusion.refs_2_, ...), custom_call_target="tpu_custom_call", output_to_operand_aliasing={{0}: (5, {}), {1}: (6, {})} | custom-call | bytes 1091600 | tf_op jit(solution)/shard_map/last/pallas_call | solution.py:522
  (65 shorter events, 8.7 us)
Async XLA Ops:
  0.6 17.5 %copy-start = (f32[48,480]{1,0:T(8,128)S(1)}, f32[48,480]{1,0:T(8,128)}, u32[]{:S(2)}) copy-start(f32[48,480]{1,0:T(8,128)} %refs_2_.1) | copy-start | bytes 276484
  0.6 16.1 %collective-permute-start.5 = (f32[48,480]{1,0:T(8,128)}, f32[48,480]{1,0:T(8,128)S(1)}, u32[]{:S(2)}, u32[]{:S(2)}) collective-permute-start(f32[48,480]{1,0:T(8,128)} %refs_2_.1), channel_id=1, source_target_pairs={{0,1},{1,0},{2,3},{3,2},{4,5},{5,4},{6,7},{7,6},{8,9},{9,8},{10,11... | collective-permute-start | bytes 276488 | tf_op jit(solution)/shard_map/ppermute | solution.py:32
  1.2 11.5 %collective-permute-start.4 = (f32[48,480]{1,0:T(8,128)}, f32[48,480]{1,0:T(8,128)S(1)}, u32[]{:S(2)}, u32[]{:S(2)}) collective-permute-start(f32[48,480]{1,0:T(8,128)} %refs_2_.1), channel_id=1, source_target_pairs={{0,7},{1,6},{2,5},{3,4},{4,3},{5,2},{6,1},{7,0},{8,15},{9,14},{10,... | collective-permute-start | bytes 276488 | tf_op jit(solution)/shard_map/ppermute | solution.py:32
  5.9 10.4 %collective-permute-start.3 = (f32[48,480]{1,0:T(8,128)}, f32[48,480]{1,0:T(8,128)S(1)}, u32[]{:S(2)}, u32[]{:S(2)}) collective-permute-start(f32[48,480]{1,0:T(8,128)} %refs_2_.1), channel_id=1, source_target_pairs={{0,5},{1,4},{2,7},{3,6},{4,1},{5,0},{6,3},{7,2},{8,13},{9,12},{10,... | collective-permute-start | bytes 276488 | tf_op jit(solution)/shard_map/ppermute | solution.py:32
  5.9 10.4 %collective-permute-start.2 = (f32[48,480]{1,0:T(8,128)}, f32[48,480]{1,0:T(8,128)S(1)}, u32[]{:S(2)}, u32[]{:S(2)}) collective-permute-start(f32[48,480]{1,0:T(8,128)} %refs_2_.1), channel_id=1, source_target_pairs={{0,3},{1,2},{2,1},{3,0},{4,7},{5,6},{6,5},{7,4},{8,11},{9,10},{10,... | collective-permute-start | bytes 276488 | tf_op jit(solution)/shard_map/ppermute | solution.py:32
  12.3 8.2 %collective-permute-start = (f32[184,128]{1,0:T(8,128)S(1)}, f32[184,128]{1,0:T(8,128)S(1)}, u32[]{:S(2)}, u32[]{:S(2)}) collective-permute-start(f32[184,128]{1,0:T(8,128)S(1)} %get-tuple-element.57), channel_id=1, source_target_pairs={{0,1},{1,0},{2,3},{3,2},{4,5},{5,4},{6,7},{7,6},{8,9},{9,8},{10,11... | collective-permute-start | bytes 282632 | tf_op jit(solution)/shard_map/ppermute | solution.py:32
  12.7 7.8 %collective-permute-start.1 = (f32[184,128]{1,0:T(8,128)S(1)}, f32[184,128]{1,0:T(8,128)S(1)}, u32[]{:S(2)}, u32[]{:S(2)}) collective-permute-start(f32[184,128]{1,0:T(8,128)S(1)} %get-tuple-element.58), channel_id=1, source_target_pairs={{0,7},{1,2},{2,1},{3,4},{4,3},{5,6},{6,5},{7,0},{8,15},{9,10},{10,... | collective-permute-start | bytes 282632 | tf_op jit(solution)/shard_map/ppermute | solution.py:67
  16.3 1.3 %collective-permute-start.6 = (f32[48,480]{1,0:T(8,128)S(1)}, f32[48,480]{1,0:T(8,128)S(1)}, u32[]{:S(2)}, u32[]{:S(2)}) collective-permute-start(f32[48,480]{1,0:T(8,128)S(1)} %collective-permute-done.2.refs_9_.refs_5_), channel_id=1, source_target_pairs={{0,1},{1,0},{2,3},{3,2},{4,5},{5,4},{6,7},{7,6},{8,9},{9,8},{10,11... | collective-permute-start | bytes 276488 | tf_op jit(solution)/shard_map/ppermute | solution.py:32
  16.3 1.4 %collective-permute-start.7 = (f32[48,480]{1,0:T(8,128)S(1)}, f32[48,480]{1,0:T(8,128)S(1)}, u32[]{:S(2)}, u32[]{:S(2)}) collective-permute-start(f32[48,480]{1,0:T(8,128)S(1)} %collective-permute-done.3.refs_11_.refs_7_), channel_id=1, source_target_pairs={{0,1},{1,0},{2,3},{3,2},{4,5},{5,4},{6,7},{7,6},{8,9},{9,8},{10,11... | collective-permute-start | bytes 276488 | tf_op jit(solution)/shard_map/ppermute | solution.py:32
  16.8 1.3 %collective-permute-start.8 = (f32[48,480]{1,0:T(8,128)S(1)}, f32[48,480]{1,0:T(8,128)S(1)}, u32[]{:S(2)}, u32[]{:S(2)}) collective-permute-start(f32[48,480]{1,0:T(8,128)S(1)} %collective-permute-done.4.refs_13_.refs_9_), channel_id=1, source_target_pairs={{0,1},{1,0},{2,3},{3,2},{4,5},{5,4},{6,7},{7,6},{8,9},{9,8},{10,11... | collective-permute-start | bytes 276488 | tf_op jit(solution)/shard_map/ppermute | solution.py:32
  19.8 4.2 %collective-permute-start.9 = (f32[8,128]{1,0:T(8,128)S(1)}, f32[8,128]{1,0:T(8,128)S(1)}, u32[]{:S(2)}, u32[]{:S(2)}) collective-permute-start(f32[8,128]{1,0:T(8,128)S(1)} %get-tuple-element.74), channel_id=1, source_target_pairs={{0,1},{1,0},{2,3},{3,2},{4,5},{5,4},{6,7},{7,6},{8,9},{9,8},{10,11... | collective-permute-start | bytes 12296 | tf_op jit(solution)/shard_map/ppermute | solution.py:32
  20.0 4.8 %collective-permute-start.10 = (f32[8,128]{1,0:T(8,128)S(1)}, f32[8,128]{1,0:T(8,128)S(1)}, u32[]{:S(2)}, u32[]{:S(2)}) collective-permute-start(f32[8,128]{1,0:T(8,128)S(1)} %get-tuple-element.75), channel_id=1, source_target_pairs={{0,7},{1,2},{2,1},{3,4},{4,3},{5,6},{6,5},{7,0},{8,15},{9,10},{10,... | collective-permute-start | bytes 12296 | tf_op jit(solution)/shard_map/ppermute | solution.py:67
  25.5 4.7 %collective-permute-start.12 = (f32[16,256]{1,0:T(8,128)S(1)}, f32[16,256]{1,0:T(8,128)S(1)}, u32[]{:S(2)}, u32[]{:S(2)}) collective-permute-start(f32[16,256]{1,0:T(8,128)S(1)} %get-tuple-element.83.refs_7_), channel_id=1, source_target_pairs={{0,24},{1,25},{2,26},{3,27},{4,28},{5,29},{6,30},{7,31},{8,16},{9,... | collective-permute-start | bytes 49160 | tf_op jit(solution)/shard_map/ppermute | solution.py:60
  28.0 3.7 %collective-permute-start.11 = (f32[16,256]{1,0:T(8,128)S(1)}, f32[16,256]{1,0:T(8,128)S(1)}, u32[]{:S(2)}, u32[]{:S(2)}) collective-permute-start(f32[16,256]{1,0:T(8,128)S(1)} %get-tuple-element.83.refs_7_), channel_id=1, source_target_pairs={{0,8},{1,9},{2,10},{3,11},{4,12},{5,13},{6,14},{7,15},{8,0},{9,1},... | collective-permute-start | bytes 49160 | tf_op jit(solution)/shard_map/ppermute | solution.py:59
  34.1 1.3 %collective-permute-start.13 = (f32[2,4096]{1,0:T(2,128)S(1)}, f32[2,4096]{1,0:T(2,128)S(1)}, u32[]{:S(2)}, u32[]{:S(2)}) collective-permute-start(f32[2,4096]{1,0:T(2,128)S(1)} %get-tuple-element.84), channel_id=1, source_target_pairs={{0,1},{1,0},{2,3},{3,2},{4,5},{5,4},{6,7},{7,6},{8,9},{9,8},{10,11... | collective-permute-start | bytes 98312 | tf_op jit(solution)/shard_map/ppermute | solution.py:32
  35.4 5.1 %collective-permute-start.16 = (f32[2,4096]{1,0:T(2,128)S(1)}, f32[2,4096]{1,0:T(2,128)S(1)}, u32[]{:S(2)}, u32[]{:S(2)}) collective-permute-start(f32[2,4096]{1,0:T(2,128)S(1)} %add.123), channel_id=1, source_target_pairs={{0,17},{1,16},{2,19},{3,18},{4,21},{5,20},{6,23},{7,22},{8,25},{9,... | collective-permute-start | bytes 98312 | tf_op jit(solution)/shard_map/ppermute | solution.py:32
  35.8 4.7 %collective-permute-start.15 = (f32[2,4096]{1,0:T(2,128)S(1)}, f32[2,4096]{1,0:T(2,128)S(1)}, u32[]{:S(2)}, u32[]{:S(2)}) collective-permute-start(f32[2,4096]{1,0:T(2,128)S(1)} %add.123), channel_id=1, source_target_pairs={{0,25},{1,24},{2,27},{3,26},{4,29},{5,28},{6,31},{7,30},{8,17},{9,... | collective-permute-start | bytes 98312 | tf_op jit(solution)/shard_map/ppermute | solution.py:32
  37.2 3.7 %collective-permute-start.14 = (f32[2,4096]{1,0:T(2,128)S(1)}, f32[2,4096]{1,0:T(2,128)S(1)}, u32[]{:S(2)}, u32[]{:S(2)}) collective-permute-start(f32[2,4096]{1,0:T(2,128)S(1)} %add.123), channel_id=1, source_target_pairs={{0,9},{1,8},{2,11},{3,10},{4,13},{5,12},{6,15},{7,14},{8,1},{9,0},... | collective-permute-start | bytes 98312 | tf_op jit(solution)/shard_map/ppermute | solution.py:32
  40.9 5.8 %collective-permute-start.19 = (f32[2,4096]{1,0:T(2,128)S(1)}, f32[2,4096]{1,0:T(2,128)S(1)}, u32[]{:S(2)}, u32[]{:S(2)}) collective-permute-start(f32[2,4096]{1,0:T(2,128)S(1)} %add_add_fusion.7), channel_id=1, source_target_pairs={{0,5},{1,4},{2,7},{3,6},{4,1},{5,0},{6,3},{7,2},{8,13},{9,12},{10,... | collective-permute-start | bytes 98312 | tf_op jit(solution)/shard_map/ppermute | solution.py:32
  41.0 5.7 %collective-permute-start.18 = (f32[2,4096]{1,0:T(2,128)S(1)}, f32[2,4096]{1,0:T(2,128)S(1)}, u32[]{:S(2)}, u32[]{:S(2)}) collective-permute-start(f32[2,4096]{1,0:T(2,128)S(1)} %add_add_fusion.7), channel_id=1, source_target_pairs={{0,7},{1,6},{2,5},{3,4},{4,3},{5,2},{6,1},{7,0},{8,15},{9,14},{10,... | collective-permute-start | bytes 98312 | tf_op jit(solution)/shard_map/ppermute | solution.py:32
  43.7 3.8 %collective-permute-start.17 = (f32[2,4096]{1,0:T(2,128)S(1)}, f32[2,4096]{1,0:T(2,128)S(1)}, u32[]{:S(2)}, u32[]{:S(2)}) collective-permute-start(f32[2,4096]{1,0:T(2,128)S(1)} %add_add_fusion.7), channel_id=1, source_target_pairs={{0,3},{1,2},{2,1},{3,0},{4,7},{5,6},{6,5},{7,4},{8,11},{9,10},{10,... | collective-permute-start | bytes 98312 | tf_op jit(solution)/shard_map/ppermute | solution.py:32
  48.4 4.7 %collective-permute-start.21 = (f32[8,256]{1,0:T(8,128)S(1)}, f32[8,256]{1,0:T(8,128)S(1)}, u32[]{:S(2)}, u32[]{:S(2)}) collective-permute-start(f32[8,256]{1,0:T(8,128)S(1)} %get-tuple-element.90.refs_7_), channel_id=1, source_target_pairs={{0,24},{1,25},{2,26},{3,27},{4,28},{5,29},{6,30},{7,31},{8,16},{9,... | collective-permute-start | bytes 24584 | tf_op jit(solution)/shard_map/ppermute | solution.py:60
  49.6 3.7 %collective-permute-start.20 = (f32[8,256]{1,0:T(8,128)S(1)}, f32[8,256]{1,0:T(8,128)S(1)}, u32[]{:S(2)}, u32[]{:S(2)}) collective-permute-start(f32[8,256]{1,0:T(8,128)S(1)} %get-tuple-element.90.refs_7_), channel_id=1, source_target_pairs={{0,8},{1,9},{2,10},{3,11},{4,12},{5,13},{6,14},{7,15},{8,0},{9,1},... | collective-permute-start | bytes 24584 | tf_op jit(solution)/shard_map/ppermute | solution.py:59
  55.7 1.3 %collective-permute-start.22 = (f32[2,4096]{1,0:T(2,128)S(1)}, f32[2,4096]{1,0:T(2,128)S(1)}, u32[]{:S(2)}, u32[]{:S(2)}) collective-permute-start(f32[2,4096]{1,0:T(2,128)S(1)} %get-tuple-element.92), channel_id=1, source_target_pairs={{0,1},{1,0},{2,3},{3,2},{4,5},{5,4},{6,7},{7,6},{8,9},{9,8},{10,11... | collective-permute-start | bytes 98312 | tf_op jit(solution)/shard_map/ppermute | solution.py:32
  56.9 3.4 %collective-permute-start.25 = (f32[2,4096]{1,0:T(2,128)S(1)}, f32[2,4096]{1,0:T(2,128)S(1)}, u32[]{:S(2)}, u32[]{:S(2)}) collective-permute-start(f32[2,4096]{1,0:T(2,128)S(1)} %add.130), channel_id=1, source_target_pairs={{0,17},{1,16},{2,19},{3,18},{4,21},{5,20},{6,23},{7,22},{8,25},{9,... | collective-permute-start | bytes 98312 | tf_op jit(solution)/shard_map/ppermute | solution.py:32
  58.3 4.2 %collective-permute-start.24 = (f32[2,4096]{1,0:T(2,128)S(1)}, f32[2,4096]{1,0:T(2,128)S(1)}, u32[]{:S(2)}, u32[]{:S(2)}) collective-permute-start(f32[2,4096]{1,0:T(2,128)S(1)} %add.130), channel_id=1, source_target_pairs={{0,25},{1,24},{2,27},{3,26},{4,29},{5,28},{6,31},{7,30},{8,17},{9,... | collective-permute-start | bytes 98312 | tf_op jit(solution)/shard_map/ppermute | solution.py:32
  59.3 3.3 %collective-permute-start.23 = (f32[2,4096]{1,0:T(2,128)S(1)}, f32[2,4096]{1,0:T(2,128)S(1)}, u32[]{:S(2)}, u32[]{:S(2)}) collective-permute-start(f32[2,4096]{1,0:T(2,128)S(1)} %add.130), channel_id=1, source_target_pairs={{0,9},{1,8},{2,11},{3,10},{4,13},{5,12},{6,15},{7,14},{8,1},{9,0},... | collective-permute-start | bytes 98312 | tf_op jit(solution)/shard_map/ppermute | solution.py:32
  62.7 4.5 %collective-permute-start.28 = (f32[2,4096]{1,0:T(2,128)S(1)}, f32[2,4096]{1,0:T(2,128)S(1)}, u32[]{:S(2)}, u32[]{:S(2)}) collective-permute-start(f32[2,4096]{1,0:T(2,128)S(1)} %add_add_fusion.5), channel_id=1, source_target_pairs={{0,5},{1,4},{2,7},{3,6},{4,1},{5,0},{6,3},{7,2},{8,13},{9,12},{10,... | collective-permute-start | bytes 98312 | tf_op jit(solution)/shard_map/ppermute | solution.py:32
  62.8 5.5 %collective-permute-start.27 = (f32[2,4096]{1,0:T(2,128)S(1)}, f32[2,4096]{1,0:T(2,128)S(1)}, u32[]{:S(2)}, u32[]{:S(2)}) collective-permute-start(f32[2,4096]{1,0:T(2,128)S(1)} %add_add_fusion.5), channel_id=1, source_target_pairs={{0,7},{1,6},{2,5},{3,4},{4,3},{5,2},{6,1},{7,0},{8,15},{9,14},{10,... | collective-permute-start | bytes 98312 | tf_op jit(solution)/shard_map/ppermute | solution.py:32
  65.8 3.7 %collective-permute-start.26 = (f32[2,4096]{1,0:T(2,128)S(1)}, f32[2,4096]{1,0:T(2,128)S(1)}, u32[]{:S(2)}, u32[]{:S(2)}) collective-permute-start(f32[2,4096]{1,0:T(2,128)S(1)} %add_add_fusion.5), channel_id=1, source_target_pairs={{0,3},{1,2},{2,1},{3,0},{4,7},{5,6},{6,5},{7,4},{8,11},{9,10},{10,... | collective-permute-start | bytes 98312 | tf_op jit(solution)/shard_map/ppermute | solution.py:32
  70.4 4.6 %collective-permute-start.30 = (f32[8,256]{1,0:T(8,128)S(1)}, f32[8,256]{1,0:T(8,128)S(1)}, u32[]{:S(2)}, u32[]{:S(2)}) collective-permute-start(f32[8,256]{1,0:T(8,128)S(1)} %get-tuple-element.98.refs_7_), channel_id=1, source_target_pairs={{0,24},{1,25},{2,26},{3,27},{4,28},{5,29},{6,30},{7,31},{8,16},{9,... | collective-permute-start | bytes 24584 | tf_op jit(solution)/shard_map/ppermute | solution.py:60
  72.2 3.7 %collective-permute-start.29 = (f32[8,256]{1,0:T(8,128)S(1)}, f32[8,256]{1,0:T(8,128)S(1)}, u32[]{:S(2)}, u32[]{:S(2)}) collective-permute-start(f32[8,256]{1,0:T(8,128)S(1)} %get-tuple-element.98.refs_7_), channel_id=1, source_target_pairs={{0,8},{1,9},{2,10},{3,11},{4,12},{5,13},{6,14},{7,15},{8,0},{9,1},... | collective-permute-start | bytes 24584 | tf_op jit(solution)/shard_map/ppermute | solution.py:59
  78.2 1.3 %collective-permute-start.31 = (f32[2,4096]{1,0:T(2,128)S(1)}, f32[2,4096]{1,0:T(2,128)S(1)}, u32[]{:S(2)}, u32[]{:S(2)}) collective-permute-start(f32[2,4096]{1,0:T(2,128)S(1)} %get-tuple-element.99), channel_id=1, source_target_pairs={{0,1},{1,0},{2,3},{3,2},{4,5},{5,4},{6,7},{7,6},{8,9},{9,8},{10,11... | collective-permute-start | bytes 98312 | tf_op jit(solution)/shard_map/ppermute | solution.py:32
  79.5 3.4 %collective-permute-start.34 = (f32[2,4096]{1,0:T(2,128)S(1)}, f32[2,4096]{1,0:T(2,128)S(1)}, u32[]{:S(2)}, u32[]{:S(2)}) collective-permute-start(f32[2,4096]{1,0:T(2,128)S(1)} %add.137), channel_id=1, source_target_pairs={{0,17},{1,16},{2,19},{3,18},{4,21},{5,20},{6,23},{7,22},{8,25},{9,... | collective-permute-start | bytes 98312 | tf_op jit(solution)/shard_map/ppermute | solution.py:32
  79.8 4.2 %collective-permute-start.33 = (f32[2,4096]{1,0:T(2,128)S(1)}, f32[2,4096]{1,0:T(2,128)S(1)}, u32[]{:S(2)}, u32[]{:S(2)}) collective-permute-start(f32[2,4096]{1,0:T(2,128)S(1)} %add.137), channel_id=1, source_target_pairs={{0,25},{1,24},{2,27},{3,26},{4,29},{5,28},{6,31},{7,30},{8,17},{9,... | collective-permute-start | bytes 98312 | tf_op jit(solution)/shard_map/ppermute | solution.py:32
  81.8 3.3 %collective-permute-start.32 = (f32[2,4096]{1,0:T(2,128)S(1)}, f32[2,4096]{1,0:T(2,128)S(1)}, u32[]{:S(2)}, u32[]{:S(2)}) collective-permute-start(f32[2,4096]{1,0:T(2,128)S(1)} %add.137), channel_id=1, source_target_pairs={{0,9},{1,8},{2,11},{3,10},{4,13},{5,12},{6,15},{7,14},{8,1},{9,0},... | collective-permute-start | bytes 98312 | tf_op jit(solution)/shard_map/ppermute | solution.py:32
  85.2 6.0 %collective-permute-start.37 = (f32[2,4096]{1,0:T(2,128)S(1)}, f32[2,4096]{1,0:T(2,128)S(1)}, u32[]{:S(2)}, u32[]{:S(2)}) collective-permute-start(f32[2,4096]{1,0:T(2,128)S(1)} %add_add_fusion.3), channel_id=1, source_target_pairs={{0,5},{1,4},{2,7},{3,6},{4,1},{5,0},{6,3},{7,2},{8,13},{9,12},{10,... | collective-permute-start | bytes 98312 | tf_op jit(solution)/shard_map/ppermute | solution.py:32
  85.2 5.9 %collective-permute-start.36 = (f32[2,4096]{1,0:T(2,128)S(1)}, f32[2,4096]{1,0:T(2,128)S(1)}, u32[]{:S(2)}, u32[]{:S(2)}) collective-permute-start(f32[2,4096]{1,0:T(2,128)S(1)} %add_add_fusion.3), channel_id=1, source_target_pairs={{0,7},{1,6},{2,5},{3,4},{4,3},{5,2},{6,1},{7,0},{8,15},{9,14},{10,... | collective-permute-start | bytes 98312 | tf_op jit(solution)/shard_map/ppermute | solution.py:32
  87.9 4.0 %collective-permute-start.35 = (f32[2,4096]{1,0:T(2,128)S(1)}, f32[2,4096]{1,0:T(2,128)S(1)}, u32[]{:S(2)}, u32[]{:S(2)}) collective-permute-start(f32[2,4096]{1,0:T(2,128)S(1)} %add_add_fusion.3), channel_id=1, source_target_pairs={{0,3},{1,2},{2,1},{3,0},{4,7},{5,6},{6,5},{7,4},{8,11},{9,10},{10,... | collective-permute-start | bytes 98312 | tf_op jit(solution)/shard_map/ppermute | solution.py:32
  92.8 4.6 %collective-permute-start.39 = (f32[8,256]{1,0:T(8,128)S(1)}, f32[8,256]{1,0:T(8,128)S(1)}, u32[]{:S(2)}, u32[]{:S(2)}) collective-permute-start(f32[8,256]{1,0:T(8,128)S(1)} %get-tuple-element.103.refs_7_), channel_id=1, source_target_pairs={{0,24},{1,25},{2,26},{3,27},{4,28},{5,29},{6,30},{7,31},{8,16},{9,... | collective-permute-start | bytes 24584 | tf_op jit(solution)/shard_map/ppermute | solution.py:60
  93.8 3.7 %collective-permute-start.38 = (f32[8,256]{1,0:T(8,128)S(1)}, f32[8,256]{1,0:T(8,128)S(1)}, u32[]{:S(2)}, u32[]{:S(2)}) collective-permute-start(f32[8,256]{1,0:T(8,128)S(1)} %get-tuple-element.103.refs_7_), channel_id=1, source_target_pairs={{0,8},{1,9},{2,10},{3,11},{4,12},{5,13},{6,14},{7,15},{8,0},{9,1},... | collective-permute-start | bytes 24584 | tf_op jit(solution)/shard_map/ppermute | solution.py:59
  99.9 1.3 %collective-permute-start.40 = (f32[2,4096]{1,0:T(2,128)S(1)}, f32[2,4096]{1,0:T(2,128)S(1)}, u32[]{:S(2)}, u32[]{:S(2)}) collective-permute-start(f32[2,4096]{1,0:T(2,128)S(1)} %get-tuple-element.104), channel_id=1, source_target_pairs={{0,1},{1,0},{2,3},{3,2},{4,5},{5,4},{6,7},{7,6},{8,9},{9,8},{10,11... | collective-permute-start | bytes 98312 | tf_op jit(solution)/shard_map/ppermute | solution.py:32
  101.2 3.4 %collective-permute-start.43 = (f32[2,4096]{1,0:T(2,128)S(1)}, f32[2,4096]{1,0:T(2,128)S(1)}, u32[]{:S(2)}, u32[]{:S(2)}) collective-permute-start(f32[2,4096]{1,0:T(2,128)S(1)} %add.144), channel_id=1, source_target_pairs={{0,17},{1,16},{2,19},{3,18},{4,21},{5,20},{6,23},{7,22},{8,25},{9,... | collective-permute-start | bytes 98312 | tf_op jit(solution)/shard_map/ppermute | solution.py:32
  102.5 4.2 %collective-permute-start.42 = (f32[2,4096]{1,0:T(2,128)S(1)}, f32[2,4096]{1,0:T(2,128)S(1)}, u32[]{:S(2)}, u32[]{:S(2)}) collective-permute-start(f32[2,4096]{1,0:T(2,128)S(1)} %add.144), channel_id=1, source_target_pairs={{0,25},{1,24},{2,27},{3,26},{4,29},{5,28},{6,31},{7,30},{8,17},{9,... | collective-permute-start | bytes 98312 | tf_op jit(solution)/shard_map/ppermute | solution.py:32
  103.5 3.3 %collective-permute-start.41 = (f32[2,4096]{1,0:T(2,128)S(1)}, f32[2,4096]{1,0:T(2,128)S(1)}, u32[]{:S(2)}, u32[]{:S(2)}) collective-permute-start(f32[2,4096]{1,0:T(2,128)S(1)} %add.144), channel_id=1, source_target_pairs={{0,9},{1,8},{2,11},{3,10},{4,13},{5,12},{6,15},{7,14},{8,1},{9,0},... | collective-permute-start | bytes 98312 | tf_op jit(solution)/shard_map/ppermute | solution.py:32
  106.8 5.1 %collective-permute-start.46 = (f32[2,4096]{1,0:T(2,128)S(1)}, f32[2,4096]{1,0:T(2,128)S(1)}, u32[]{:S(2)}, u32[]{:S(2)}) collective-permute-start(f32[2,4096]{1,0:T(2,128)S(1)} %add_add_fusion.1), channel_id=1, source_target_pairs={{0,5},{1,4},{2,7},{3,6},{4,1},{5,0},{6,3},{7,2},{8,13},{9,12},{10,... | collective-permute-start | bytes 98312 | tf_op jit(solution)/shard_map/ppermute | solution.py:32
  107.2 5.1 %collective-permute-start.45 = (f32[2,4096]{1,0:T(2,128)S(1)}, f32[2,4096]{1,0:T(2,128)S(1)}, u32[]{:S(2)}, u32[]{:S(2)}) collective-permute-start(f32[2,4096]{1,0:T(2,128)S(1)} %add_add_fusion.1), channel_id=1, source_target_pairs={{0,7},{1,6},{2,5},{3,4},{4,3},{5,2},{6,1},{7,0},{8,15},{9,14},{10,... | collective-permute-start | bytes 98312 | tf_op jit(solution)/shard_map/ppermute | solution.py:32
  109.4 3.9 %collective-permute-start.44 = (f32[2,4096]{1,0:T(2,128)S(1)}, f32[2,4096]{1,0:T(2,128)S(1)}, u32[]{:S(2)}, u32[]{:S(2)}) collective-permute-start(f32[2,4096]{1,0:T(2,128)S(1)} %add_add_fusion.1), channel_id=1, source_target_pairs={{0,3},{1,2},{2,1},{3,0},{4,7},{5,6},{6,5},{7,4},{8,11},{9,10},{10,... | collective-permute-start | bytes 98312 | tf_op jit(solution)/shard_map/ppermute | solution.py:32

commit v9 on v8

--- a/solution.py
+++ b/solution.py
@@ -45,7 +45,7 @@
             bits = lambda b: (b, core) if on_lat else (0, b | core)
             if 2 * bit < size:
                 near, far, both = (swap(x, *bits(b)) for b in (bit, 2 * bit, 3 * bit))
-                x = (x + near) + (both + far)
+                x = (x + near) + (far + both) if on_lat else (x + near) + (both + far)
                 bit *= 4
             else:
                 x = x + swap(x, *bits(bit))
@@ -493,7 +493,7 @@
 
 def last_kernel(rows, reach, total, *refs):
     v_ref, u_ref, sum_ref, block_ref, place_ref = refs[:5]
-    maps_out, series_out, maps_new, series_new, sems = refs[7:]
+    maps_out, series_out, maps_new, series_new, held_ref, sems = refs[7:]
     share = series_new.shape[1]
     stores = [
         pltpu.make_async_copy(maps_new, maps_out.at[pl.ds(0, PAIRS)], sems.at[0]),
@@ -505,11 +505,14 @@
     for r in range(rows):
         maps_new[:, r, :] = u[:, r * LANES : (r + 1) * LANES]
     stores[0].start()
-    v = jnp.concatenate([v_ref[: PAIRS - 2], vn], axis=0)
-    mine = v[:, :share]
-    for i in range(1, v.shape[1] // share):
-        mine = jnp.where(place_ref[3] == i, v[:, i * share : (i + 1) * share], mine)
-    series_new[...] = mine
+    days = v_ref.shape[1]
+    held_ref[: PAIRS - 2, :days] = v_ref[: PAIRS - 2]
+    held_ref[PAIRS - 2 :, :days] = vn
+    start = place_ref[3] * share
+    tile = start // LANES
+    width = held_ref.shape[1] - days + (share // LANES) * LANES
+    window = held_ref[:, pl.ds(pl.multiple_of(tile * LANES, LANES), width)]
+    series_new[...] = pltpu.roll(window, (width - (start - tile * LANES)) % width, 1)[:, :share]
     stores[1].start()
     for store in stores:
         store.wait()
@@ -664,7 +667,7 @@
         functools.partial(last_kernel, rows, reach, total),
         "last",
         [(mode_maps.shape, F32), (mode_series.shape, F32)],
-        [((PAIRS, rows, columns), F32), ((PAIRS, mode_series.shape[1]), F32)],
+        [((PAIRS, rows, columns), F32), ((PAIRS, mode_series.shape[1]), F32), ((PAIRS, days + 2 * LANES), F32)],
         [v, u, summed, block, place, maps_out, series_out],
         smem=(4,),
         in_hbm=(5, 6),

time: 115 us -> 115 us (level)
  transfers between devices with their start and end apart: 47 -> 47, of which waited for: 35 -> 33; matrix products, arithmetic and copies ran while one was open for 0% -> 0% of each run, Pallas kernels for 15% -> 15%
where the time goes in v9:
time: 115 us
  starting transfers between devices  46.1 us (40%)
  waiting for transfers between devices  35.7 us (31%)
  Pallas kernels  31.4 us (27%)
    ppermute x37, starting transfers between devices, swap(): lax.ppermute(x, ('lat', 'lon'), pairing(lambda i: i ^ lat_bits, lambda j:...  31.5 us
    pallas_call x16, Pallas kernels, call(): pl.pallas_call(kernel, out_shape=[jax.ShapeDtypeStruct(s, t) for s, t in...  31.4 us
    ppermute x37, waiting for transfers between devices, swap(): lax.ppermute(x, ('lat', 'lon'), pairing(lambda i: i ^ lat_bits, lambda j:...  23.2 us
    ppermute x4, waiting for transfers between devices, lat_partners(): lax.ppermute(x, ('lat', 'lon'), pairing(lambda i: (i + 1 if i % 2 else i...  8.01 us
    ppermute x4, starting transfers between devices, lat_partners(): lax.ppermute(x, ('lat', 'lon'), pairing(lambda i: (i + 1 if i % 2 else i...  7.57 us
    ppermute x2, starting transfers between devices, lon_partners(): lax.ppermute(far, ('lat', 'lon'), pairing(same, lambda j: (j + 1 if j % 2...  4.07 us
    ppermute x4, waiting for transfers between devices, lat_partners(): got_a = lax.ppermute(x, ('lat', 'lon'), pairing(lambda i: i ^ 1, same))  3.69 us
    ppermute x4, starting transfers between devices, lat_partners(): got_a = lax.ppermute(x, ('lat', 'lon'), pairing(lambda i: i ^ 1, same))  2.99 us
  transfers between devices with their start and end apart: 47, of which 33 were waited for; matrix products, arithmetic and copies ran while one was open for 0% of the time, Pallas kernels for 15%

profile of v9, /device:TPU:0, one launch (start us, length us, event | category | flops | bytes accessed | tf_op | source)
XLA Modules:
  0.0 114.9 jit_solution(12496235942657215805)
XLA Ops:
  1.2 4.7 %collective-permute-start.4 = (f32[48,480]{1,0:T(8,128)}, f32[48,480]{1,0:T(8,128)S(1)}, u32[]{:S(2)}, u32[]{:S(2)}) collective-permute-start(f32[48,480]{1,0:T(8,128)} %refs_2_.1), channel_id=1, source_target_pairs={{0,7},{1,6},{2,5},{3,4},{4,3},{5,2},{6,1},{7,0},{8,15},{9,14},{10,... | collective-permute-start | bytes 276488 | tf_op jit(solution)/shard_map/ppermute | solution.py:32
  6.5 5.7 %own_flags.1 = (bf16[512,3840]{1,0:T(8,128)(2,1)S(1)}, bf16[512,3840]{1,0:T(8,128)(2,1)S(1)}, s32[512,256]{1,0:T(8,128)S(1)}, f32[48,512]{1,0:T(8,128)S(1)}, f32...) custom-call(s32[512,256]{1,0:T(8,128)} %bitcast.6, ...), custom_call_target="tpu_custom_call" | custom-call | flops 1006632960 | bytes 4648976 | tf_op jit(solution)/shard_map/own_flags/pallas_call | solution.py:525
  12.7 3.6 %collective-permute-start.1 = (f32[184,128]{1,0:T(8,128)S(1)}, f32[184,128]{1,0:T(8,128)S(1)}, u32[]{:S(2)}, u32[]{:S(2)}) collective-permute-start(f32[184,128]{1,0:T(8,128)S(1)} %get-tuple-element.58), channel_id=1, source_target_pairs={{0,7},{1,2},{2,1},{3,4},{4,3},{5,6},{6,5},{7,0},{8,15},{9,10},{10,... | collective-permute-start | bytes 282632 | tf_op jit(solution)/shard_map/ppermute | solution.py:67
  16.9 0.7 collective-permute-done.6.refs_8_.refs_4_
  18.1 1.7 %given.1 = (f32[8,512]{1,0:T(8,128)S(1)}, f32[8,128]{1,0:T(8,128)S(1)}, f32[8,128]{1,0:T(8,128)S(1)}) custom-call(bf16[512,3840]{1,0:T(8,128)(2,1)S(1)} %get-tuple-element.72.refs_0_.refs_1_, s32[4]{0:T(128)S(1)} %pad_add_fusion.refs_5_.refs_2_.refs_1_.place_ref.refs_4_, f32[48,480]{1,0:T(8,128)S(1)} %copy-done, ...), custom_call_target="tpu_custom_call" | custom-call | tf_op jit(solution)/shard_map/given/pallas_call | solution.py:525
  20.5 3.5 %first_products.1 = (f32[2,640]{1,0:T(2,128)S(1)}, f32[8,128]{1,0:T(8,128)S(1)}, f32[48,3840]{1,0:T(8,128)S(1)}, bf16[3840,128]{1,0:T(8,128)(2,1)S(1)}, f32[48,6...) custom-call(f32[184,128]{1,0:T(8,128)S(1)} %collective-permute-done.refs_0_, ...), custom_call_target="tpu_custom_call" | custom-call | flops 943718400 | bytes 4958224 | tf_op jit(solution)/shard_map/first_products/pallas_call | solution.py:525
  24.0 0.8 collective-permute-done.10.far_ref
  25.5 2.5 %collective-permute-start.12 = (f32[16,256]{1,0:T(8,128)S(1)}, f32[16,256]{1,0:T(8,128)S(1)}, u32[]{:S(2)}, u32[]{:S(2)}) collective-permute-start(f32[16,256]{1,0:T(8,128)S(1)} %get-tuple-element.83.refs_7_), channel_id=1, source_target_pairs={{0,24},{1,25},{2,26},{3,27},{4,28},{5,29},{6,30},{7,31},{8,16},{9,... | collective-permute-start | bytes 49160 | tf_op jit(solution)/shard_map/ppermute | solution.py:60
  28.5 1.7 %collective-permute-done.12.refs_9_ = f32[16,256]{1,0:T(8,128)S(1)} collective-permute-done((f32[16,256]{1,0:T(8,128)S(1)}, f32[16,256]{1,0:T(8,128)S(1)}, u32[]{:S(2)}, u32[]{:S(2)}) %collective-permute-start.12) | collective-permute-done | bytes 16416 | tf_op jit(solution)/shard_map/ppermute | solution.py:60
  30.2 1.5 %collective-permute-done.11.refs_8_ = f32[16,256]{1,0:T(8,128)S(1)} collective-permute-done((f32[16,256]{1,0:T(8,128)S(1)}, f32[16,256]{1,0:T(8,128)S(1)}, u32[]{:S(2)}, u32[]{:S(2)}) %collective-permute-start.11) | collective-permute-done | bytes 16416 | tf_op jit(solution)/shard_map/ppermute | solution.py:59
  31.7 2.4 %sums_0.1 = (f32[2,4096]{1,0:T(2,128)S(1)}, f32[8,256]{1,0:T(8,128)S(1)}, f32[120,256]{1,0:T(8,128)S(1)}) custom-call(bf16[512,3840]{1,0:T(8,128)(2,1)S(1)} %get-tuple-element.61.refs_3_.refs_0_, bf16[512,3840]{1,0:T(8,128)(2,1)S(1)} %get-tuple-element.72.refs_0_.refs_1_, f32[48,3840]{1,0:T(8,128)S(1)} %get-tuple-element.69.v_ref.refs_2_, ...), custom_call_target="tpu_custom_call" | custom-call | flops 754974720 | bytes 8806416 | tf_op jit(solution)/shard_map/sums_0/pallas_call | solution.py:525
  34.2 1.2 %collective-permute-done.13 = f32[2,4096]{1,0:T(2,128)S(1)} collective-permute-done((f32[2,4096]{1,0:T(2,128)S(1)}, f32[2,4096]{1,0:T(2,128)S(1)}, u32[]{:S(2)}, u32[]{:S(2)}) %collective-permute-start.13) | collective-permute-done | bytes 32800 | tf_op jit(solution)/shard_map/ppermute | solution.py:32
  35.4 0.7 collective-permute-start.16
  36.1 1.1 collective-permute-start.15
  37.2 1.2 %collective-permute-start.14 = (f32[2,4096]{1,0:T(2,128)S(1)}, f32[2,4096]{1,0:T(2,128)S(1)}, u32[]{:S(2)}, u32[]{:S(2)}) collective-permute-start(f32[2,4096]{1,0:T(2,128)S(1)} %add.123), channel_id=1, source_target_pairs={{0,9},{1,8},{2,11},{3,10},{4,13},{5,12},{6,15},{7,14},{8,1},{9,0},... | collective-permute-start | bytes 98312 | tf_op jit(solution)/shard_map/ppermute | solution.py:32
  38.5 2.0 %days_flags.1.m_ref.refs_0_ = bf16[3840,512]{1,0:T(8,128)(2,1)S(1)} custom-call(s32[512,256]{1,0:T(8,128)S(1)} %get-tuple-element.56.held_ref, bf16[1920,256]{1,0:T(8,128)(2,1)S(1)} %get-tuple-element.67.spread_ref), custom_call_target="tpu_custom_call" | custom-call | flops 1006632960 | bytes 1507328 | tf_op jit(solution)/shard_map/days_flags/pallas_call | solution.py:525
  40.7 2.7 %collective-permute-start.18 = (f32[2,4096]{1,0:T(2,128)S(1)}, f32[2,4096]{1,0:T(2,128)S(1)}, u32[]{:S(2)}, u32[]{:S(2)}) collective-permute-start(f32[2,4096]{1,0:T(2,128)S(1)} %add_add_fusion.7), channel_id=1, source_target_pairs={{0,7},{1,6},{2,5},{3,4},{4,3},{5,2},{6,1},{7,0},{8,15},{9,14},{10,... | collective-permute-start | bytes 98312 | tf_op jit(solution)/shard_map/ppermute | solution.py:32
  43.8 1.5 %next_products_1.1 = (f32[2,640]{1,0:T(2,128)S(1)}, f32[8,128]{1,0:T(8,128)S(1)}) custom-call(bf16[3840,512]{1,0:T(8,128)(2,1)S(1)} %days_flags.1.m_ref.refs_0_, bf16[3840,128]{1,0:T(8,128)(2,1)S(1)} %get-tuple-element.68.mh_ref.refs_1_, f32[48,3840]{1,0:T(8,128)S(1)} %get-tuple-element.69.v_ref.refs_2_, f32[48,640]{1,0:T(8,128)S(1)} %get-tuple-element.70.u_ref.refs_3_), custom_call_target="tpu_custom_call" | custom-call | flops 943718400 | bytes 5775360 | tf_op jit(solution)/shard_map/next_products_1/pallas_call | solution.py:525
  45.3 0.8 collective-permute-done.19
  46.2 1.1 collective-permute-done.17
  47.2 0.9 fields_1.1
  48.1 1.5 %collective-permute-start.21 = (f32[8,256]{1,0:T(8,128)S(1)}, f32[8,256]{1,0:T(8,128)S(1)}, u32[]{:S(2)}, u32[]{:S(2)}) collective-permute-start(f32[8,256]{1,0:T(8,128)S(1)} %get-tuple-element.90.refs_7_), channel_id=1, source_target_pairs={{0,24},{1,25},{2,26},{3,27},{4,28},{5,29},{6,30},{7,31},{8,16},{9,... | collective-permute-start | bytes 24584 | tf_op jit(solution)/shard_map/ppermute | solution.py:60
  49.6 0.9 collective-permute-start.20
  50.5 2.2 %collective-permute-done.21.refs_9_ = f32[8,256]{1,0:T(8,128)S(1)} collective-permute-done((f32[8,256]{1,0:T(8,128)S(1)}, f32[8,256]{1,0:T(8,128)S(1)}, u32[]{:S(2)}, u32[]{:S(2)}) %collective-permute-start.21) | collective-permute-done | bytes 8224 | tf_op jit(solution)/shard_map/ppermute | solution.py:60
  53.2 2.4 %sums_1.1 = (f32[2,4096]{1,0:T(2,128)S(1)}, f32[8,256]{1,0:T(8,128)S(1)}) custom-call(bf16[512,3840]{1,0:T(8,128)(2,1)S(1)} %get-tuple-element.61.refs_3_.refs_0_, bf16[512,3840]{1,0:T(8,128)(2,1)S(1)} %get-tuple-element.72.refs_0_.refs_1_, f32[48,3840]{1,0:T(8,128)S(1)} %get-tuple-element.86.v_ref.refs_2_, f32[48,640]{1,0:T(8,128)S(1)} %get-tuple-element.87.u_ref.refs_3_, ...), custom_call_target="tpu_custom_call" | custom-call | flops 754974720 | bytes 8904720 | tf_op jit(solution)/shard_map/sums_1/pallas_call | solution.py:525
  55.7 1.2 %collective-permute-done.22 = f32[2,4096]{1,0:T(2,128)S(1)} collective-permute-done((f32[2,4096]{1,0:T(2,128)S(1)}, f32[2,4096]{1,0:T(2,128)S(1)}, u32[]{:S(2)}, u32[]{:S(2)}) %collective-permute-start.22) | collective-permute-done | bytes 32800 | tf_op jit(solution)/shard_map/ppermute | solution.py:32
  56.9 1.3 %collective-permute-start.25 = (f32[2,4096]{1,0:T(2,128)S(1)}, f32[2,4096]{1,0:T(2,128)S(1)}, u32[]{:S(2)}, u32[]{:S(2)}) collective-permute-start(f32[2,4096]{1,0:T(2,128)S(1)} %add.130), channel_id=1, source_target_pairs={{0,25},{1,24},{2,27},{3,26},{4,29},{5,28},{6,31},{7,30},{8,17},{9,... | collective-permute-start | bytes 98312 | tf_op jit(solution)/shard_map/ppermute | solution.py:32
  58.3 0.9 collective-permute-start.24
  59.1 0.8 collective-permute-start.23
  60.0 1.3 %collective-permute-done.25 = f32[2,4096]{1,0:T(2,128)S(1)} collective-permute-done((f32[2,4096]{1,0:T(2,128)S(1)}, f32[2,4096]{1,0:T(2,128)S(1)}, u32[]{:S(2)}, u32[]{:S(2)}) %collective-permute-start.25) | collective-permute-done | bytes 32800 | tf_op jit(solution)/shard_map/ppermute | solution.py:32
  61.3 0.8 collective-permute-done.24
  62.6 2.6 %collective-permute-start.27 = (f32[2,4096]{1,0:T(2,128)S(1)}, f32[2,4096]{1,0:T(2,128)S(1)}, u32[]{:S(2)}, u32[]{:S(2)}) collective-permute-start(f32[2,4096]{1,0:T(2,128)S(1)} %add_add_fusion.5), channel_id=1, source_target_pairs={{0,7},{1,6},{2,5},{3,4},{4,3},{5,2},{6,1},{7,0},{8,15},{9,14},{10,... | collective-permute-start | bytes 98312 | tf_op jit(solution)/shard_map/ppermute | solution.py:32
  65.6 1.4 %next_products_2.1 = (f32[2,640]{1,0:T(2,128)S(1)}, f32[8,128]{1,0:T(8,128)S(1)}) custom-call(bf16[3840,512]{1,0:T(8,128)(2,1)S(1)} %days_flags.1.m_ref.refs_0_, bf16[3840,128]{1,0:T(8,128)(2,1)S(1)} %get-tuple-element.68.mh_ref.refs_1_, f32[48,3840]{1,0:T(8,128)S(1)} %get-tuple-element.86.v_ref.refs_2_, f32[48,640]{1,0:T(8,128)S(1)} %get-tuple-element.87.u_ref.refs_3_), custom_call_target="tpu_custom_call" | custom-call | flops 943718400 | bytes 5775360 | tf_op jit(solution)/shard_map/next_products_2/pallas_call | solution.py:525
  66.9 1.6 %collective-permute-done.28 = f32[2,4096]{1,0:T(2,128)S(1)} collective-permute-done((f32[2,4096]{1,0:T(2,128)S(1)}, f32[2,4096]{1,0:T(2,128)S(1)}, u32[]{:S(2)}, u32[]{:S(2)}) %collective-permute-start.28) | collective-permute-done | bytes 32800 | tf_op jit(solution)/shard_map/ppermute | solution.py:32
  68.5 0.7 collective-permute-done.26
  69.2 0.9 fields_2.1
  70.1 2.1 %collective-permute-start.30 = (f32[8,256]{1,0:T(8,128)S(1)}, f32[8,256]{1,0:T(8,128)S(1)}, u32[]{:S(2)}, u32[]{:S(2)}) collective-permute-start(f32[8,256]{1,0:T(8,128)S(1)} %get-tuple-element.98.refs_7_), channel_id=1, source_target_pairs={{0,24},{1,25},{2,26},{3,27},{4,28},{5,29},{6,30},{7,31},{8,16},{9,... | collective-permute-start | bytes 24584 | tf_op jit(solution)/shard_map/ppermute | solution.py:60
  72.7 2.0 %collective-permute-done.30.refs_9_ = f32[8,256]{1,0:T(8,128)S(1)} collective-permute-done((f32[8,256]{1,0:T(8,128)S(1)}, f32[8,256]{1,0:T(8,128)S(1)}, u32[]{:S(2)}, u32[]{:S(2)}) %collective-permute-start.30) | collective-permute-done | bytes 8224 | tf_op jit(solution)/shard_map/ppermute | solution.py:60
  74.7 1.1 collective-permute-done.29.refs_8_
  75.8 2.4 %sums_2.1 = (f32[2,4096]{1,0:T(2,128)S(1)}, f32[8,256]{1,0:T(8,128)S(1)}) custom-call(bf16[512,3840]{1,0:T(8,128)(2,1)S(1)} %get-tuple-element.61.refs_3_.refs_0_, bf16[512,3840]{1,0:T(8,128)(2,1)S(1)} %get-tuple-element.72.refs_0_.refs_1_, f32[48,3840]{1,0:T(8,128)S(1)} %get-tuple-element.94.v_ref.refs_2_, f32[48,640]{1,0:T(8,128)S(1)} %get-tuple-element.95.u_ref.refs_3_, ...), custom_call_target="tpu_custom_call" | custom-call | flops 754974720 | bytes 8904720 | tf_op jit(solution)/shard_map/sums_2/pallas_call | solution.py:525
  78.3 1.2 %collective-permute-done.31 = f32[2,4096]{1,0:T(2,128)S(1)} collective-permute-done((f32[2,4096]{1,0:T(2,128)S(1)}, f32[2,4096]{1,0:T(2,128)S(1)}, u32[]{:S(2)}, u32[]{:S(2)}) %collective-permute-start.31) | collective-permute-done | bytes 32800 | tf_op jit(solution)/shard_map/ppermute | solution.py:32
  79.5 0.7 collective-permute-start.34
  80.3 1.1 collective-permute-start.33
  81.3 1.2 %collective-permute-start.32 = (f32[2,4096]{1,0:T(2,128)S(1)}, f32[2,4096]{1,0:T(2,128)S(1)}, u32[]{:S(2)}, u32[]{:S(2)}) collective-permute-start(f32[2,4096]{1,0:T(2,128)S(1)} %add.137), channel_id=1, source_target_pairs={{0,9},{1,8},{2,11},{3,10},{4,13},{5,12},{6,15},{7,14},{8,1},{9,0},... | collective-permute-start | bytes 98312 | tf_op jit(solution)/shard_map/ppermute | solution.py:32
  82.6 1.4 %collective-permute-done.34 = f32[2,4096]{1,0:T(2,128)S(1)} collective-permute-done((f32[2,4096]{1,0:T(2,128)S(1)}, f32[2,4096]{1,0:T(2,128)S(1)}, u32[]{:S(2)}, u32[]{:S(2)}) %collective-permute-start.34) | collective-permute-done | bytes 32800 | tf_op jit(solution)/shard_map/ppermute | solution.py:32
  84.8 2.6 %collective-permute-start.36 = (f32[2,4096]{1,0:T(2,128)S(1)}, f32[2,4096]{1,0:T(2,128)S(1)}, u32[]{:S(2)}, u32[]{:S(2)}) collective-permute-start(f32[2,4096]{1,0:T(2,128)S(1)} %add_add_fusion.3), channel_id=1, source_target_pairs={{0,7},{1,6},{2,5},{3,4},{4,3},{5,2},{6,1},{7,0},{8,15},{9,14},{10,... | collective-permute-start | bytes 98312 | tf_op jit(solution)/shard_map/ppermute | solution.py:32
  87.8 1.4 %next_products_3.1 = (f32[2,640]{1,0:T(2,128)S(1)}, f32[8,128]{1,0:T(8,128)S(1)}) custom-call(bf16[3840,512]{1,0:T(8,128)(2,1)S(1)} %days_flags.1.m_ref.refs_0_, bf16[3840,128]{1,0:T(8,128)(2,1)S(1)} %get-tuple-element.68.mh_ref.refs_1_, f32[48,3840]{1,0:T(8,128)S(1)} %get-tuple-element.94.v_ref.refs_2_, f32[48,640]{1,0:T(8,128)S(1)} %get-tuple-element.95.u_ref.refs_3_), custom_call_target="tpu_custom_call" | custom-call | flops 943718400 | bytes 5775360 | tf_op jit(solution)/shard_map/next_products_3/pallas_call | solution.py:525
  89.1 1.6 %collective-permute-done.37 = f32[2,4096]{1,0:T(2,128)S(1)} collective-permute-done((f32[2,4096]{1,0:T(2,128)S(1)}, f32[2,4096]{1,0:T(2,128)S(1)}, u32[]{:S(2)}, u32[]{:S(2)}) %collective-permute-start.37) | collective-permute-done | bytes 32800 | tf_op jit(solution)/shard_map/ppermute | solution.py:32
  90.7 0.7 collective-permute-done.35
  91.5 0.9 fields_3.1
  92.3 1.5 %collective-permute-start.39 = (f32[8,256]{1,0:T(8,128)S(1)}, f32[8,256]{1,0:T(8,128)S(1)}, u32[]{:S(2)}, u32[]{:S(2)}) collective-permute-start(f32[8,256]{1,0:T(8,128)S(1)} %get-tuple-element.103.refs_7_), channel_id=1, source_target_pairs={{0,24},{1,25},{2,26},{3,27},{4,28},{5,29},{6,30},{7,31},{8,16},{9,... | collective-permute-start | bytes 24584 | tf_op jit(solution)/shard_map/ppermute | solution.py:60
  93.8 0.9 collective-permute-start.38
  94.8 2.2 %collective-permute-done.39.refs_9_ = f32[8,256]{1,0:T(8,128)S(1)} collective-permute-done((f32[8,256]{1,0:T(8,128)S(1)}, f32[8,256]{1,0:T(8,128)S(1)}, u32[]{:S(2)}, u32[]{:S(2)}) %collective-permute-start.39) | collective-permute-done | bytes 8224 | tf_op jit(solution)/shard_map/ppermute | solution.py:60
  97.5 2.4 %sums_3.1 = (f32[2,4096]{1,0:T(2,128)S(1)}, f32[8,256]{1,0:T(8,128)S(1)}) custom-call(bf16[512,3840]{1,0:T(8,128)(2,1)S(1)} %get-tuple-element.61.refs_3_.refs_0_, bf16[512,3840]{1,0:T(8,128)(2,1)S(1)} %get-tuple-element.72.refs_0_.refs_1_, f32[48,3840]{1,0:T(8,128)S(1)} %get-tuple-element.101.refs_2_.refs_0_, ...), custom_call_target="tpu_custom_call" | custom-call | flops 754974720 | bytes 8904720 | tf_op jit(solution)/shard_map/sums_3/pallas_call | solution.py:525
  100.0 1.2 %collective-permute-done.40 = f32[2,4096]{1,0:T(2,128)S(1)} collective-permute-done((f32[2,4096]{1,0:T(2,128)S(1)}, f32[2,4096]{1,0:T(2,128)S(1)}, u32[]{:S(2)}, u32[]{:S(2)}) %collective-permute-start.40) | collective-permute-done | bytes 32800 | tf_op jit(solution)/shard_map/ppermute | solution.py:32
  101.2 1.3 %collective-permute-start.43 = (f32[2,4096]{1,0:T(2,128)S(1)}, f32[2,4096]{1,0:T(2,128)S(1)}, u32[]{:S(2)}, u32[]{:S(2)}) collective-permute-start(f32[2,4096]{1,0:T(2,128)S(1)} %add.144), channel_id=1, source_target_pairs={{0,25},{1,24},{2,27},{3,26},{4,29},{5,28},{6,31},{7,30},{8,17},{9,... | collective-permute-start | bytes 98312 | tf_op jit(solution)/shard_map/ppermute | solution.py:32
  102.5 0.9 collective-permute-start.42
  103.3 0.9 collective-permute-start.41
  104.2 1.3 %collective-permute-done.43 = f32[2,4096]{1,0:T(2,128)S(1)} collective-permute-done((f32[2,4096]{1,0:T(2,128)S(1)}, f32[2,4096]{1,0:T(2,128)S(1)}, u32[]{:S(2)}, u32[]{:S(2)}) %collective-permute-start.43) | collective-permute-done | bytes 32800 | tf_op jit(solution)/shard_map/ppermute | solution.py:32
  105.5 0.9 collective-permute-done.42
  106.8 2.6 %collective-permute-start.45 = (f32[2,4096]{1,0:T(2,128)S(1)}, f32[2,4096]{1,0:T(2,128)S(1)}, u32[]{:S(2)}, u32[]{:S(2)}) collective-permute-start(f32[2,4096]{1,0:T(2,128)S(1)} %add_add_fusion.1), channel_id=1, source_target_pairs={{0,7},{1,6},{2,5},{3,4},{4,3},{5,2},{6,1},{7,0},{8,15},{9,14},{10,... | collective-permute-start | bytes 98312 | tf_op jit(solution)/shard_map/ppermute | solution.py:32
  109.8 3.0 %collective-permute-done.46 = f32[2,4096]{1,0:T(2,128)S(1)} collective-permute-done((f32[2,4096]{1,0:T(2,128)S(1)}, f32[2,4096]{1,0:T(2,128)S(1)}, u32[]{:S(2)}, u32[]{:S(2)}) %collective-permute-start.46) | collective-permute-done | bytes 32800 | tf_op jit(solution)/shard_map/ppermute | solution.py:32
  112.7 0.7 collective-permute-done.44
  113.4 1.3 %last.1 = (f32[48,4,128]{2,1,0:T(4,128)}, f32[48,480]{1,0:T(8,128)}) custom-call(f32[48,3840]{1,0:T(8,128)S(1)} %get-tuple-element.101.refs_2_.refs_0_, f32[48,640]{1,0:T(8,128)S(1)} %get-tuple-element.102.refs_3_.refs_1_, f32[2,4096]{1,0:T(2,128)S(1)} %add_add_fusion.refs_2_, ...), custom_call_target="tpu_custom_call", output_to_operand_aliasing={{0}: (5, {}), {1}: (6, {})} | custom-call | bytes 1091600 | tf_op jit(solution)/shard_map/last/pallas_call | solution.py:525
  (65 shorter events, 10.1 us)
Async XLA Ops:
  0.6 17.5 %copy-start = (f32[48,480]{1,0:T(8,128)S(1)}, f32[48,480]{1,0:T(8,128)}, u32[]{:S(2)}) copy-start(f32[48,480]{1,0:T(8,128)} %refs_2_.1) | copy-start | bytes 276484
  0.6 16.1 %collective-permute-start.5 = (f32[48,480]{1,0:T(8,128)}, f32[48,480]{1,0:T(8,128)S(1)}, u32[]{:S(2)}, u32[]{:S(2)}) collective-permute-start(f32[48,480]{1,0:T(8,128)} %refs_2_.1), channel_id=1, source_target_pairs={{0,1},{1,0},{2,3},{3,2},{4,5},{5,4},{6,7},{7,6},{8,9},{9,8},{10,11... | collective-permute-start | bytes 276488 | tf_op jit(solution)/shard_map/ppermute | solution.py:32
  1.2 11.5 %collective-permute-start.4 = (f32[48,480]{1,0:T(8,128)}, f32[48,480]{1,0:T(8,128)S(1)}, u32[]{:S(2)}, u32[]{:S(2)}) collective-permute-start(f32[48,480]{1,0:T(8,128)} %refs_2_.1), channel_id=1, source_target_pairs={{0,7},{1,6},{2,5},{3,4},{4,3},{5,2},{6,1},{7,0},{8,15},{9,14},{10,... | collective-permute-start | bytes 276488 | tf_op jit(solution)/shard_map/ppermute | solution.py:32
  5.9 10.4 %collective-permute-start.3 = (f32[48,480]{1,0:T(8,128)}, f32[48,480]{1,0:T(8,128)S(1)}, u32[]{:S(2)}, u32[]{:S(2)}) collective-permute-start(f32[48,480]{1,0:T(8,128)} %refs_2_.1), channel_id=1, source_target_pairs={{0,5},{1,4},{2,7},{3,6},{4,1},{5,0},{6,3},{7,2},{8,13},{9,12},{10,... | collective-permute-start | bytes 276488 | tf_op jit(solution)/shard_map/ppermute | solution.py:32
  5.9 10.4 %collective-permute-start.2 = (f32[48,480]{1,0:T(8,128)}, f32[48,480]{1,0:T(8,128)S(1)}, u32[]{:S(2)}, u32[]{:S(2)}) collective-permute-start(f32[48,480]{1,0:T(8,128)} %refs_2_.1), channel_id=1, source_target_pairs={{0,3},{1,2},{2,1},{3,0},{4,7},{5,6},{6,5},{7,4},{8,11},{9,10},{10,... | collective-permute-start | bytes 276488 | tf_op jit(solution)/shard_map/ppermute | solution.py:32
  12.3 8.2 %collective-permute-start = (f32[184,128]{1,0:T(8,128)S(1)}, f32[184,128]{1,0:T(8,128)S(1)}, u32[]{:S(2)}, u32[]{:S(2)}) collective-permute-start(f32[184,128]{1,0:T(8,128)S(1)} %get-tuple-element.57), channel_id=1, source_target_pairs={{0,1},{1,0},{2,3},{3,2},{4,5},{5,4},{6,7},{7,6},{8,9},{9,8},{10,11... | collective-permute-start | bytes 282632 | tf_op jit(solution)/shard_map/ppermute | solution.py:32
  12.7 7.8 %collective-permute-start.1 = (f32[184,128]{1,0:T(8,128)S(1)}, f32[184,128]{1,0:T(8,128)S(1)}, u32[]{:S(2)}, u32[]{:S(2)}) collective-permute-start(f32[184,128]{1,0:T(8,128)S(1)} %get-tuple-element.58), channel_id=1, source_target_pairs={{0,7},{1,2},{2,1},{3,4},{4,3},{5,6},{6,5},{7,0},{8,15},{9,10},{10,... | collective-permute-start | bytes 282632 | tf_op jit(solution)/shard_map/ppermute | solution.py:67
  16.3 1.3 %collective-permute-start.6 = (f32[48,480]{1,0:T(8,128)S(1)}, f32[48,480]{1,0:T(8,128)S(1)}, u32[]{:S(2)}, u32[]{:S(2)}) collective-permute-start(f32[48,480]{1,0:T(8,128)S(1)} %collective-permute-done.2.refs_9_.refs_5_), channel_id=1, source_target_pairs={{0,1},{1,0},{2,3},{3,2},{4,5},{5,4},{6,7},{7,6},{8,9},{9,8},{10,11... | collective-permute-start | bytes 276488 | tf_op jit(solution)/shard_map/ppermute | solution.py:32
  16.3 1.4 %collective-permute-start.7 = (f32[48,480]{1,0:T(8,128)S(1)}, f32[48,480]{1,0:T(8,128)S(1)}, u32[]{:S(2)}, u32[]{:S(2)}) collective-permute-start(f32[48,480]{1,0:T(8,128)S(1)} %collective-permute-done.3.refs_11_.refs_7_), channel_id=1, source_target_pairs={{0,1},{1,0},{2,3},{3,2},{4,5},{5,4},{6,7},{7,6},{8,9},{9,8},{10,11... | collective-permute-start | bytes 276488 | tf_op jit(solution)/shard_map/ppermute | solution.py:32
  16.8 1.3 %collective-permute-start.8 = (f32[48,480]{1,0:T(8,128)S(1)}, f32[48,480]{1,0:T(8,128)S(1)}, u32[]{:S(2)}, u32[]{:S(2)}) collective-permute-start(f32[48,480]{1,0:T(8,128)S(1)} %collective-permute-done.4.refs_13_.refs_9_), channel_id=1, source_target_pairs={{0,1},{1,0},{2,3},{3,2},{4,5},{5,4},{6,7},{7,6},{8,9},{9,8},{10,11... | collective-permute-start | bytes 276488 | tf_op jit(solution)/shard_map/ppermute | solution.py:32
  19.8 4.2 %collective-permute-start.9 = (f32[8,128]{1,0:T(8,128)S(1)}, f32[8,128]{1,0:T(8,128)S(1)}, u32[]{:S(2)}, u32[]{:S(2)}) collective-permute-start(f32[8,128]{1,0:T(8,128)S(1)} %get-tuple-element.74), channel_id=1, source_target_pairs={{0,1},{1,0},{2,3},{3,2},{4,5},{5,4},{6,7},{7,6},{8,9},{9,8},{10,11... | collective-permute-start | bytes 12296 | tf_op jit(solution)/shard_map/ppermute | solution.py:32
  20.0 4.8 %collective-permute-start.10 = (f32[8,128]{1,0:T(8,128)S(1)}, f32[8,128]{1,0:T(8,128)S(1)}, u32[]{:S(2)}, u32[]{:S(2)}) collective-permute-start(f32[8,128]{1,0:T(8,128)S(1)} %get-tuple-element.75), channel_id=1, source_target_pairs={{0,7},{1,2},{2,1},{3,4},{4,3},{5,6},{6,5},{7,0},{8,15},{9,10},{10,... | collective-permute-start | bytes 12296 | tf_op jit(solution)/shard_map/ppermute | solution.py:67
  25.5 4.7 %collective-permute-start.12 = (f32[16,256]{1,0:T(8,128)S(1)}, f32[16,256]{1,0:T(8,128)S(1)}, u32[]{:S(2)}, u32[]{:S(2)}) collective-permute-start(f32[16,256]{1,0:T(8,128)S(1)} %get-tuple-element.83.refs_7_), channel_id=1, source_target_pairs={{0,24},{1,25},{2,26},{3,27},{4,28},{5,29},{6,30},{7,31},{8,16},{9,... | collective-permute-start | bytes 49160 | tf_op jit(solution)/shard_map/ppermute | solution.py:60
  28.0 3.7 %collective-permute-start.11 = (f32[16,256]{1,0:T(8,128)S(1)}, f32[16,256]{1,0:T(8,128)S(1)}, u32[]{:S(2)}, u32[]{:S(2)}) collective-permute-start(f32[16,256]{1,0:T(8,128)S(1)} %get-tuple-element.83.refs_7_), channel_id=1, source_target_pairs={{0,8},{1,9},{2,10},{3,11},{4,12},{5,13},{6,14},{7,15},{8,0},{9,1},... | collective-permute-start | bytes 49160 | tf_op jit(solution)/shard_map/ppermute | solution.py:59
  34.1 1.3 %collective-permute-start.13 = (f32[2,4096]{1,0:T(2,128)S(1)}, f32[2,4096]{1,0:T(2,128)S(1)}, u32[]{:S(2)}, u32[]{:S(2)}) collective-permute-start(f32[2,4096]{1,0:T(2,128)S(1)} %get-tuple-element.84), channel_id=1, source_target_pairs={{0,1},{1,0},{2,3},{3,2},{4,5},{5,4},{6,7},{7,6},{8,9},{9,8},{10,11... | collective-permute-start | bytes 98312 | tf_op jit(solution)/shard_map/ppermute | solution.py:32
  35.4 5.1 %collective-permute-start.16 = (f32[2,4096]{1,0:T(2,128)S(1)}, f32[2,4096]{1,0:T(2,128)S(1)}, u32[]{:S(2)}, u32[]{:S(2)}) collective-permute-start(f32[2,4096]{1,0:T(2,128)S(1)} %add.123), channel_id=1, source_target_pairs={{0,25},{1,24},{2,27},{3,26},{4,29},{5,28},{6,31},{7,30},{8,17},{9,... | collective-permute-start | bytes 98312 | tf_op jit(solution)/shard_map/ppermute | solution.py:32
  36.1 4.4 %collective-permute-start.15 = (f32[2,4096]{1,0:T(2,128)S(1)}, f32[2,4096]{1,0:T(2,128)S(1)}, u32[]{:S(2)}, u32[]{:S(2)}) collective-permute-start(f32[2,4096]{1,0:T(2,128)S(1)} %add.123), channel_id=1, source_target_pairs={{0,17},{1,16},{2,19},{3,18},{4,21},{5,20},{6,23},{7,22},{8,25},{9,... | collective-permute-start | bytes 98312 | tf_op jit(solution)/shard_map/ppermute | solution.py:32
  37.2 3.3 %collective-permute-start.14 = (f32[2,4096]{1,0:T(2,128)S(1)}, f32[2,4096]{1,0:T(2,128)S(1)}, u32[]{:S(2)}, u32[]{:S(2)}) collective-permute-start(f32[2,4096]{1,0:T(2,128)S(1)} %add.123), channel_id=1, source_target_pairs={{0,9},{1,8},{2,11},{3,10},{4,13},{5,12},{6,15},{7,14},{8,1},{9,0},... | collective-permute-start | bytes 98312 | tf_op jit(solution)/shard_map/ppermute | solution.py:32
  40.6 5.6 %collective-permute-start.19 = (f32[2,4096]{1,0:T(2,128)S(1)}, f32[2,4096]{1,0:T(2,128)S(1)}, u32[]{:S(2)}, u32[]{:S(2)}) collective-permute-start(f32[2,4096]{1,0:T(2,128)S(1)} %add_add_fusion.7), channel_id=1, source_target_pairs={{0,5},{1,4},{2,7},{3,6},{4,1},{5,0},{6,3},{7,2},{8,13},{9,12},{10,... | collective-permute-start | bytes 98312 | tf_op jit(solution)/shard_map/ppermute | solution.py:32
  40.7 5.5 %collective-permute-start.18 = (f32[2,4096]{1,0:T(2,128)S(1)}, f32[2,4096]{1,0:T(2,128)S(1)}, u32[]{:S(2)}, u32[]{:S(2)}) collective-permute-start(f32[2,4096]{1,0:T(2,128)S(1)} %add_add_fusion.7), channel_id=1, source_target_pairs={{0,7},{1,6},{2,5},{3,4},{4,3},{5,2},{6,1},{7,0},{8,15},{9,14},{10,... | collective-permute-start | bytes 98312 | tf_op jit(solution)/shard_map/ppermute | solution.py:32
  43.4 3.8 %collective-permute-start.17 = (f32[2,4096]{1,0:T(2,128)S(1)}, f32[2,4096]{1,0:T(2,128)S(1)}, u32[]{:S(2)}, u32[]{:S(2)}) collective-permute-start(f32[2,4096]{1,0:T(2,128)S(1)} %add_add_fusion.7), channel_id=1, source_target_pairs={{0,3},{1,2},{2,1},{3,0},{4,7},{5,6},{6,5},{7,4},{8,11},{9,10},{10,... | collective-permute-start | bytes 98312 | tf_op jit(solution)/shard_map/ppermute | solution.py:32
  48.1 4.6 %collective-permute-start.21 = (f32[8,256]{1,0:T(8,128)S(1)}, f32[8,256]{1,0:T(8,128)S(1)}, u32[]{:S(2)}, u32[]{:S(2)}) collective-permute-start(f32[8,256]{1,0:T(8,128)S(1)} %get-tuple-element.90.refs_7_), channel_id=1, source_target_pairs={{0,24},{1,25},{2,26},{3,27},{4,28},{5,29},{6,30},{7,31},{8,16},{9,... | collective-permute-start | bytes 24584 | tf_op jit(solution)/shard_map/ppermute | solution.py:60
  49.6 3.7 %collective-permute-start.20 = (f32[8,256]{1,0:T(8,128)S(1)}, f32[8,256]{1,0:T(8,128)S(1)}, u32[]{:S(2)}, u32[]{:S(2)}) collective-permute-start(f32[8,256]{1,0:T(8,128)S(1)} %get-tuple-element.90.refs_7_), channel_id=1, source_target_pairs={{0,8},{1,9},{2,10},{3,11},{4,12},{5,13},{6,14},{7,15},{8,0},{9,1},... | collective-permute-start | bytes 24584 | tf_op jit(solution)/shard_map/ppermute | solution.py:59
  55.7 1.3 %collective-permute-start.22 = (f32[2,4096]{1,0:T(2,128)S(1)}, f32[2,4096]{1,0:T(2,128)S(1)}, u32[]{:S(2)}, u32[]{:S(2)}) collective-permute-start(f32[2,4096]{1,0:T(2,128)S(1)} %get-tuple-element.92), channel_id=1, source_target_pairs={{0,1},{1,0},{2,3},{3,2},{4,5},{5,4},{6,7},{7,6},{8,9},{9,8},{10,11... | collective-permute-start | bytes 98312 | tf_op jit(solution)/shard_map/ppermute | solution.py:32
  56.9 4.3 %collective-permute-start.25 = (f32[2,4096]{1,0:T(2,128)S(1)}, f32[2,4096]{1,0:T(2,128)S(1)}, u32[]{:S(2)}, u32[]{:S(2)}) collective-permute-start(f32[2,4096]{1,0:T(2,128)S(1)} %add.130), channel_id=1, source_target_pairs={{0,25},{1,24},{2,27},{3,26},{4,29},{5,28},{6,31},{7,30},{8,17},{9,... | collective-permute-start | bytes 98312 | tf_op jit(solution)/shard_map/ppermute | solution.py:32
  58.3 3.8 %collective-permute-start.24 = (f32[2,4096]{1,0:T(2,128)S(1)}, f32[2,4096]{1,0:T(2,128)S(1)}, u32[]{:S(2)}, u32[]{:S(2)}) collective-permute-start(f32[2,4096]{1,0:T(2,128)S(1)} %add.130), channel_id=1, source_target_pairs={{0,17},{1,16},{2,19},{3,18},{4,21},{5,20},{6,23},{7,22},{8,25},{9,... | collective-permute-start | bytes 98312 | tf_op jit(solution)/shard_map/ppermute | solution.py:32
  59.1 3.3 %collective-permute-start.23 = (f32[2,4096]{1,0:T(2,128)S(1)}, f32[2,4096]{1,0:T(2,128)S(1)}, u32[]{:S(2)}, u32[]{:S(2)}) collective-permute-start(f32[2,4096]{1,0:T(2,128)S(1)} %add.130), channel_id=1, source_target_pairs={{0,9},{1,8},{2,11},{3,10},{4,13},{5,12},{6,15},{7,14},{8,1},{9,0},... | collective-permute-start | bytes 98312 | tf_op jit(solution)/shard_map/ppermute | solution.py:32
  62.5 6.0 %collective-permute-start.28 = (f32[2,4096]{1,0:T(2,128)S(1)}, f32[2,4096]{1,0:T(2,128)S(1)}, u32[]{:S(2)}, u32[]{:S(2)}) collective-permute-start(f32[2,4096]{1,0:T(2,128)S(1)} %add_add_fusion.5), channel_id=1, source_target_pairs={{0,5},{1,4},{2,7},{3,6},{4,1},{5,0},{6,3},{7,2},{8,13},{9,12},{10,... | collective-permute-start | bytes 98312 | tf_op jit(solution)/shard_map/ppermute | solution.py:32
  62.6 5.9 %collective-permute-start.27 = (f32[2,4096]{1,0:T(2,128)S(1)}, f32[2,4096]{1,0:T(2,128)S(1)}, u32[]{:S(2)}, u32[]{:S(2)}) collective-permute-start(f32[2,4096]{1,0:T(2,128)S(1)} %add_add_fusion.5), channel_id=1, source_target_pairs={{0,7},{1,6},{2,5},{3,4},{4,3},{5,2},{6,1},{7,0},{8,15},{9,14},{10,... | collective-permute-start | bytes 98312 | tf_op jit(solution)/shard_map/ppermute | solution.py:32
  65.2 4.0 %collective-permute-start.26 = (f32[2,4096]{1,0:T(2,128)S(1)}, f32[2,4096]{1,0:T(2,128)S(1)}, u32[]{:S(2)}, u32[]{:S(2)}) collective-permute-start(f32[2,4096]{1,0:T(2,128)S(1)} %add_add_fusion.5), channel_id=1, source_target_pairs={{0,3},{1,2},{2,1},{3,0},{4,7},{5,6},{6,5},{7,4},{8,11},{9,10},{10,... | collective-permute-start | bytes 98312 | tf_op jit(solution)/shard_map/ppermute | solution.py:32
  70.1 4.6 %collective-permute-start.30 = (f32[8,256]{1,0:T(8,128)S(1)}, f32[8,256]{1,0:T(8,128)S(1)}, u32[]{:S(2)}, u32[]{:S(2)}) collective-permute-start(f32[8,256]{1,0:T(8,128)S(1)} %get-tuple-element.98.refs_7_), channel_id=1, source_target_pairs={{0,24},{1,25},{2,26},{3,27},{4,28},{5,29},{6,30},{7,31},{8,16},{9,... | collective-permute-start | bytes 24584 | tf_op jit(solution)/shard_map/ppermute | solution.py:60
  72.2 3.7 %collective-permute-start.29 = (f32[8,256]{1,0:T(8,128)S(1)}, f32[8,256]{1,0:T(8,128)S(1)}, u32[]{:S(2)}, u32[]{:S(2)}) collective-permute-start(f32[8,256]{1,0:T(8,128)S(1)} %get-tuple-element.98.refs_7_), channel_id=1, source_target_pairs={{0,8},{1,9},{2,10},{3,11},{4,12},{5,13},{6,14},{7,15},{8,0},{9,1},... | collective-permute-start | bytes 24584 | tf_op jit(solution)/shard_map/ppermute | solution.py:59
  78.2 1.3 %collective-permute-start.31 = (f32[2,4096]{1,0:T(2,128)S(1)}, f32[2,4096]{1,0:T(2,128)S(1)}, u32[]{:S(2)}, u32[]{:S(2)}) collective-permute-start(f32[2,4096]{1,0:T(2,128)S(1)} %get-tuple-element.99), channel_id=1, source_target_pairs={{0,1},{1,0},{2,3},{3,2},{4,5},{5,4},{6,7},{7,6},{8,9},{9,8},{10,11... | collective-permute-start | bytes 98312 | tf_op jit(solution)/shard_map/ppermute | solution.py:32
  79.5 4.4 %collective-permute-start.34 = (f32[2,4096]{1,0:T(2,128)S(1)}, f32[2,4096]{1,0:T(2,128)S(1)}, u32[]{:S(2)}, u32[]{:S(2)}) collective-permute-start(f32[2,4096]{1,0:T(2,128)S(1)} %add.137), channel_id=1, source_target_pairs={{0,25},{1,24},{2,27},{3,26},{4,29},{5,28},{6,31},{7,30},{8,17},{9,... | collective-permute-start | bytes 98312 | tf_op jit(solution)/shard_map/ppermute | solution.py:32
  80.3 4.1 %collective-permute-start.33 = (f32[2,4096]{1,0:T(2,128)S(1)}, f32[2,4096]{1,0:T(2,128)S(1)}, u32[]{:S(2)}, u32[]{:S(2)}) collective-permute-start(f32[2,4096]{1,0:T(2,128)S(1)} %add.137), channel_id=1, source_target_pairs={{0,17},{1,16},{2,19},{3,18},{4,21},{5,20},{6,23},{7,22},{8,25},{9,... | collective-permute-start | bytes 98312 | tf_op jit(solution)/shard_map/ppermute | solution.py:32
  81.3 3.3 %collective-permute-start.32 = (f32[2,4096]{1,0:T(2,128)S(1)}, f32[2,4096]{1,0:T(2,128)S(1)}, u32[]{:S(2)}, u32[]{:S(2)}) collective-permute-start(f32[2,4096]{1,0:T(2,128)S(1)} %add.137), channel_id=1, source_target_pairs={{0,9},{1,8},{2,11},{3,10},{4,13},{5,12},{6,15},{7,14},{8,1},{9,0},... | collective-permute-start | bytes 98312 | tf_op jit(solution)/shard_map/ppermute | solution.py:32
  84.7 6.0 %collective-permute-start.37 = (f32[2,4096]{1,0:T(2,128)S(1)}, f32[2,4096]{1,0:T(2,128)S(1)}, u32[]{:S(2)}, u32[]{:S(2)}) collective-permute-start(f32[2,4096]{1,0:T(2,128)S(1)} %add_add_fusion.3), channel_id=1, source_target_pairs={{0,5},{1,4},{2,7},{3,6},{4,1},{5,0},{6,3},{7,2},{8,13},{9,12},{10,... | collective-permute-start | bytes 98312 | tf_op jit(solution)/shard_map/ppermute | solution.py:32
  84.8 5.9 %collective-permute-start.36 = (f32[2,4096]{1,0:T(2,128)S(1)}, f32[2,4096]{1,0:T(2,128)S(1)}, u32[]{:S(2)}, u32[]{:S(2)}) collective-permute-start(f32[2,4096]{1,0:T(2,128)S(1)} %add_add_fusion.3), channel_id=1, source_target_pairs={{0,7},{1,6},{2,5},{3,4},{4,3},{5,2},{6,1},{7,0},{8,15},{9,14},{10,... | collective-permute-start | bytes 98312 | tf_op jit(solution)/shard_map/ppermute | solution.py:32
  87.4 4.0 %collective-permute-start.35 = (f32[2,4096]{1,0:T(2,128)S(1)}, f32[2,4096]{1,0:T(2,128)S(1)}, u32[]{:S(2)}, u32[]{:S(2)}) collective-permute-start(f32[2,4096]{1,0:T(2,128)S(1)} %add_add_fusion.3), channel_id=1, source_target_pairs={{0,3},{1,2},{2,1},{3,0},{4,7},{5,6},{6,5},{7,4},{8,11},{9,10},{10,... | collective-permute-start | bytes 98312 | tf_op jit(solution)/shard_map/ppermute | solution.py:32
  92.3 4.6 %collective-permute-start.39 = (f32[8,256]{1,0:T(8,128)S(1)}, f32[8,256]{1,0:T(8,128)S(1)}, u32[]{:S(2)}, u32[]{:S(2)}) collective-permute-start(f32[8,256]{1,0:T(8,128)S(1)} %get-tuple-element.103.refs_7_), channel_id=1, source_target_pairs={{0,24},{1,25},{2,26},{3,27},{4,28},{5,29},{6,30},{7,31},{8,16},{9,... | collective-permute-start | bytes 24584 | tf_op jit(solution)/shard_map/ppermute | solution.py:60
  93.8 3.7 %collective-permute-start.38 = (f32[8,256]{1,0:T(8,128)S(1)}, f32[8,256]{1,0:T(8,128)S(1)}, u32[]{:S(2)}, u32[]{:S(2)}) collective-permute-start(f32[8,256]{1,0:T(8,128)S(1)} %get-tuple-element.103.refs_7_), channel_id=1, source_target_pairs={{0,8},{1,9},{2,10},{3,11},{4,12},{5,13},{6,14},{7,15},{8,0},{9,1},... | collective-permute-start | bytes 24584 | tf_op jit(solution)/shard_map/ppermute | solution.py:59
  99.9 1.3 %collective-permute-start.40 = (f32[2,4096]{1,0:T(2,128)S(1)}, f32[2,4096]{1,0:T(2,128)S(1)}, u32[]{:S(2)}, u32[]{:S(2)}) collective-permute-start(f32[2,4096]{1,0:T(2,128)S(1)} %get-tuple-element.104), channel_id=1, source_target_pairs={{0,1},{1,0},{2,3},{3,2},{4,5},{5,4},{6,7},{7,6},{8,9},{9,8},{10,11... | collective-permute-start | bytes 98312 | tf_op jit(solution)/shard_map/ppermute | solution.py:32
  101.2 4.3 %collective-permute-start.43 = (f32[2,4096]{1,0:T(2,128)S(1)}, f32[2,4096]{1,0:T(2,128)S(1)}, u32[]{:S(2)}, u32[]{:S(2)}) collective-permute-start(f32[2,4096]{1,0:T(2,128)S(1)} %add.144), channel_id=1, source_target_pairs={{0,25},{1,24},{2,27},{3,26},{4,29},{5,28},{6,31},{7,30},{8,17},{9,... | collective-permute-start | bytes 98312 | tf_op jit(solution)/shard_map/ppermute | solution.py:32
  102.5 3.9 %collective-permute-start.42 = (f32[2,4096]{1,0:T(2,128)S(1)}, f32[2,4096]{1,0:T(2,128)S(1)}, u32[]{:S(2)}, u32[]{:S(2)}) collective-permute-start(f32[2,4096]{1,0:T(2,128)S(1)} %add.144), channel_id=1, source_target_pairs={{0,17},{1,16},{2,19},{3,18},{4,21},{5,20},{6,23},{7,22},{8,25},{9,... | collective-permute-start | bytes 98312 | tf_op jit(solution)/shard_map/ppermute | solution.py:32
  103.3 3.3 %collective-permute-start.41 = (f32[2,4096]{1,0:T(2,128)S(1)}, f32[2,4096]{1,0:T(2,128)S(1)}, u32[]{:S(2)}, u32[]{:S(2)}) collective-permute-start(f32[2,4096]{1,0:T(2,128)S(1)} %add.144), channel_id=1, source_target_pairs={{0,9},{1,8},{2,11},{3,10},{4,13},{5,12},{6,15},{7,14},{8,1},{9,0},... | collective-permute-start | bytes 98312 | tf_op jit(solution)/shard_map/ppermute | solution.py:32
  106.7 6.0 %collective-permute-start.46 = (f32[2,4096]{1,0:T(2,128)S(1)}, f32[2,4096]{1,0:T(2,128)S(1)}, u32[]{:S(2)}, u32[]{:S(2)}) collective-permute-start(f32[2,4096]{1,0:T(2,128)S(1)} %add_add_fusion.1), channel_id=1, source_target_pairs={{0,5},{1,4},{2,7},{3,6},{4,1},{5,0},{6,3},{7,2},{8,13},{9,12},{10,... | collective-permute-start | bytes 98312 | tf_op jit(solution)/shard_map/ppermute | solution.py:32
  106.8 5.9 %collective-permute-start.45 = (f32[2,4096]{1,0:T(2,128)S(1)}, f32[2,4096]{1,0:T(2,128)S(1)}, u32[]{:S(2)}, u32[]{:S(2)}) collective-permute-start(f32[2,4096]{1,0:T(2,128)S(1)} %add_add_fusion.1), channel_id=1, source_target_pairs={{0,7},{1,6},{2,5},{3,4},{4,3},{5,2},{6,1},{7,0},{8,15},{9,14},{10,... | collective-permute-start | bytes 98312 | tf_op jit(solution)/shard_map/ppermute | solution.py:32
  109.4 4.0 %collective-permute-start.44 = (f32[2,4096]{1,0:T(2,128)S(1)}, f32[2,4096]{1,0:T(2,128)S(1)}, u32[]{:S(2)}, u32[]{:S(2)}) collective-permute-start(f32[2,4096]{1,0:T(2,128)S(1)} %add_add_fusion.1), channel_id=1, source_target_pairs={{0,3},{1,2},{2,1},{3,0},{4,7},{5,6},{6,5},{7,4},{8,11},{9,10},{10,... | collective-permute-start | bytes 98312 | tf_op jit(solution)/shard_map/ppermute | solution.py:32

commit v10 on v9

--- a/solution.py
+++ b/solution.py
@@ -644,7 +644,7 @@
         outs = [((2, days + 2 * LANES), F32), ((count, 2 * LANES), F32)]
         coef = ((5 * 3 * count, 2 * LANES), F32)
         partial_sums, block, *made = call(
-            functools.partial(sums_kernel, step, rows, chunk),
+            functools.partial(sums_kernel, step, rows, days),
             f"sums_{step}",
             outs if step else [*outs, coef],
             [],

time: 115 us -> 115 us (level)
  no operation moved by 1% of the time
where the time goes in v10:
time: 115 us; the launch traced here: 114 us
  starting transfers between devices  46.1 us (40%)
  waiting for transfers between devices  35.7 us (31%)
  Pallas kernels  30.9 us (27%)
    ppermute x37, starting transfers between devices, swap(): lax.ppermute(x, ('lat', 'lon'), pairing(lambda i: i ^ lat_bits, lambda j:...  31.5 us
    pallas_call x16, Pallas kernels, call(): pl.pallas_call(kernel, out_shape=[jax.ShapeDtypeStruct(s, t) for s, t in...  30.9 us
    ppermute x37, waiting for transfers between devices, swap(): lax.ppermute(x, ('lat', 'lon'), pairing(lambda i: i ^ lat_bits, lambda j:...  23.2 us
    ppermute x4, waiting for transfers between devices, lat_partners(): lax.ppermute(x, ('lat', 'lon'), pairing(lambda i: (i + 1 if i % 2 else i...  7.98 us
    ppermute x4, starting transfers between devices, lat_partners(): lax.ppermute(x, ('lat', 'lon'), pairing(lambda i: (i + 1 if i % 2 else i...  7.55 us
    ppermute x2, starting transfers between devices, lon_partners(): lax.ppermute(far, ('lat', 'lon'), pairing(same, lambda j: (j + 1 if j % 2...  4.07 us
    ppermute x4, waiting for transfers between devices, lat_partners(): got_a = lax.ppermute(x, ('lat', 'lon'), pairing(lambda i: i ^ 1, same))  3.69 us
    ppermute x4, starting transfers between devices, lat_partners(): got_a = lax.ppermute(x, ('lat', 'lon'), pairing(lambda i: i ^ 1, same))  3.02 us
  transfers between devices with their start and end apart: 47, of which 33 were waited for; matrix products, arithmetic and copies ran while one was open for 0% of the time, Pallas kernels for 15%

profile of v10, /device:TPU:0, one launch (start us, length us, event | category | flops | bytes accessed | tf_op | source)
XLA Modules:
  0.0 114.4 jit_solution(3508318278300833182)
XLA Ops:
  1.2 4.7 %collective-permute-start.4 = (f32[48,480]{1,0:T(8,128)}, f32[48,480]{1,0:T(8,128)S(1)}, u32[]{:S(2)}, u32[]{:S(2)}) collective-permute-start(f32[48,480]{1,0:T(8,128)} %refs_2_.1), channel_id=1, source_target_pairs={{0,7},{1,6},{2,5},{3,4},{4,3},{5,2},{6,1},{7,0},{8,15},{9,14},{10,... | collective-permute-start | bytes 276488 | tf_op jit(solution)/shard_map/ppermute | solution.py:32
  6.5 5.7 %own_flags.1 = (bf16[512,3840]{1,0:T(8,128)(2,1)S(1)}, bf16[512,3840]{1,0:T(8,128)(2,1)S(1)}, s32[512,256]{1,0:T(8,128)S(1)}, f32[48,512]{1,0:T(8,128)S(1)}, f32...) custom-call(s32[512,256]{1,0:T(8,128)} %bitcast.6, ...), custom_call_target="tpu_custom_call" | custom-call | flops 1006632960 | bytes 4648976 | tf_op jit(solution)/shard_map/own_flags/pallas_call | solution.py:525
  12.7 3.6 %collective-permute-start.1 = (f32[184,128]{1,0:T(8,128)S(1)}, f32[184,128]{1,0:T(8,128)S(1)}, u32[]{:S(2)}, u32[]{:S(2)}) collective-permute-start(f32[184,128]{1,0:T(8,128)S(1)} %get-tuple-element.58), channel_id=1, source_target_pairs={{0,7},{1,2},{2,1},{3,4},{4,3},{5,6},{6,5},{7,0},{8,15},{9,10},{10,... | collective-permute-start | bytes 282632 | tf_op jit(solution)/shard_map/ppermute | solution.py:67
  16.9 0.7 collective-permute-done.6.refs_8_.refs_4_
  18.1 1.7 %given.1 = (f32[8,512]{1,0:T(8,128)S(1)}, f32[8,128]{1,0:T(8,128)S(1)}, f32[8,128]{1,0:T(8,128)S(1)}) custom-call(bf16[512,3840]{1,0:T(8,128)(2,1)S(1)} %get-tuple-element.72.refs_0_.refs_1_, s32[4]{0:T(128)S(1)} %pad_add_fusion.refs_5_.refs_2_.refs_1_.place_ref.refs_4_, f32[48,480]{1,0:T(8,128)S(1)} %copy-done, ...), custom_call_target="tpu_custom_call" | custom-call | tf_op jit(solution)/shard_map/given/pallas_call | solution.py:525
  20.5 3.5 %first_products.1 = (f32[2,640]{1,0:T(2,128)S(1)}, f32[8,128]{1,0:T(8,128)S(1)}, f32[48,3840]{1,0:T(8,128)S(1)}, bf16[3840,128]{1,0:T(8,128)(2,1)S(1)}, f32[48,6...) custom-call(f32[184,128]{1,0:T(8,128)S(1)} %collective-permute-done.refs_0_, ...), custom_call_target="tpu_custom_call" | custom-call | flops 943718400 | bytes 4958224 | tf_op jit(solution)/shard_map/first_products/pallas_call | solution.py:525
  24.0 0.8 collective-permute-done.10.far_ref
  25.5 2.5 %collective-permute-start.12 = (f32[16,256]{1,0:T(8,128)S(1)}, f32[16,256]{1,0:T(8,128)S(1)}, u32[]{:S(2)}, u32[]{:S(2)}) collective-permute-start(f32[16,256]{1,0:T(8,128)S(1)} %get-tuple-element.83.refs_7_), channel_id=1, source_target_pairs={{0,24},{1,25},{2,26},{3,27},{4,28},{5,29},{6,30},{7,31},{8,16},{9,... | collective-permute-start | bytes 49160 | tf_op jit(solution)/shard_map/ppermute | solution.py:60
  28.5 1.7 %collective-permute-done.12.refs_9_ = f32[16,256]{1,0:T(8,128)S(1)} collective-permute-done((f32[16,256]{1,0:T(8,128)S(1)}, f32[16,256]{1,0:T(8,128)S(1)}, u32[]{:S(2)}, u32[]{:S(2)}) %collective-permute-start.12) | collective-permute-done | bytes 16416 | tf_op jit(solution)/shard_map/ppermute | solution.py:60
  30.2 1.5 %collective-permute-done.11.refs_8_ = f32[16,256]{1,0:T(8,128)S(1)} collective-permute-done((f32[16,256]{1,0:T(8,128)S(1)}, f32[16,256]{1,0:T(8,128)S(1)}, u32[]{:S(2)}, u32[]{:S(2)}) %collective-permute-start.11) | collective-permute-done | bytes 16416 | tf_op jit(solution)/shard_map/ppermute | solution.py:59
  31.7 2.3 %sums_0.1 = (f32[2,4096]{1,0:T(2,128)S(1)}, f32[8,256]{1,0:T(8,128)S(1)}, f32[120,256]{1,0:T(8,128)S(1)}) custom-call(bf16[512,3840]{1,0:T(8,128)(2,1)S(1)} %get-tuple-element.61.refs_3_.refs_0_, bf16[512,3840]{1,0:T(8,128)(2,1)S(1)} %get-tuple-element.72.refs_0_.refs_1_, f32[48,3840]{1,0:T(8,128)S(1)} %get-tuple-element.69.v_ref.refs_2_, ...), custom_call_target="tpu_custom_call" | custom-call | flops 754974720 | bytes 8806416 | tf_op jit(solution)/shard_map/sums_0/pallas_call | solution.py:525
  34.1 1.2 %collective-permute-done.13 = f32[2,4096]{1,0:T(2,128)S(1)} collective-permute-done((f32[2,4096]{1,0:T(2,128)S(1)}, f32[2,4096]{1,0:T(2,128)S(1)}, u32[]{:S(2)}, u32[]{:S(2)}) %collective-permute-start.13) | collective-permute-done | bytes 32800 | tf_op jit(solution)/shard_map/ppermute | solution.py:32
  35.3 0.7 collective-permute-start.16
  36.0 1.1 collective-permute-start.15
  37.1 1.3 %collective-permute-start.14 = (f32[2,4096]{1,0:T(2,128)S(1)}, f32[2,4096]{1,0:T(2,128)S(1)}, u32[]{:S(2)}, u32[]{:S(2)}) collective-permute-start(f32[2,4096]{1,0:T(2,128)S(1)} %add.123), channel_id=1, source_target_pairs={{0,9},{1,8},{2,11},{3,10},{4,13},{5,12},{6,15},{7,14},{8,1},{9,0},... | collective-permute-start | bytes 98312 | tf_op jit(solution)/shard_map/ppermute | solution.py:32
  38.3 2.0 %days_flags.1.m_ref.refs_0_ = bf16[3840,512]{1,0:T(8,128)(2,1)S(1)} custom-call(s32[512,256]{1,0:T(8,128)S(1)} %get-tuple-element.56.held_ref, bf16[1920,256]{1,0:T(8,128)(2,1)S(1)} %get-tuple-element.67.spread_ref), custom_call_target="tpu_custom_call" | custom-call | flops 1006632960 | bytes 1507328 | tf_op jit(solution)/shard_map/days_flags/pallas_call | solution.py:525
  40.5 2.7 %collective-permute-start.18 = (f32[2,4096]{1,0:T(2,128)S(1)}, f32[2,4096]{1,0:T(2,128)S(1)}, u32[]{:S(2)}, u32[]{:S(2)}) collective-permute-start(f32[2,4096]{1,0:T(2,128)S(1)} %add_add_fusion.7), channel_id=1, source_target_pairs={{0,7},{1,6},{2,5},{3,4},{4,3},{5,2},{6,1},{7,0},{8,15},{9,14},{10,... | collective-permute-start | bytes 98312 | tf_op jit(solution)/shard_map/ppermute | solution.py:32
  43.7 1.6 %next_products_1.1 = (f32[2,640]{1,0:T(2,128)S(1)}, f32[8,128]{1,0:T(8,128)S(1)}) custom-call(bf16[3840,512]{1,0:T(8,128)(2,1)S(1)} %days_flags.1.m_ref.refs_0_, bf16[3840,128]{1,0:T(8,128)(2,1)S(1)} %get-tuple-element.68.mh_ref.refs_1_, f32[48,3840]{1,0:T(8,128)S(1)} %get-tuple-element.69.v_ref.refs_2_, f32[48,640]{1,0:T(8,128)S(1)} %get-tuple-element.70.u_ref.refs_3_), custom_call_target="tpu_custom_call" | custom-call | flops 943718400 | bytes 5775360 | tf_op jit(solution)/shard_map/next_products_1/pallas_call | solution.py:525
  45.2 0.8 collective-permute-done.19
  46.0 1.1 collective-permute-done.17
  47.1 0.9 fields_1.1
  48.0 1.5 %collective-permute-start.21 = (f32[8,256]{1,0:T(8,128)S(1)}, f32[8,256]{1,0:T(8,128)S(1)}, u32[]{:S(2)}, u32[]{:S(2)}) collective-permute-start(f32[8,256]{1,0:T(8,128)S(1)} %get-tuple-element.90.refs_7_), channel_id=1, source_target_pairs={{0,24},{1,25},{2,26},{3,27},{4,28},{5,29},{6,30},{7,31},{8,16},{9,... | collective-permute-start | bytes 24584 | tf_op jit(solution)/shard_map/ppermute | solution.py:60
  49.5 1.0 collective-permute-start.20
  50.4 2.2 %collective-permute-done.21.refs_9_ = f32[8,256]{1,0:T(8,128)S(1)} collective-permute-done((f32[8,256]{1,0:T(8,128)S(1)}, f32[8,256]{1,0:T(8,128)S(1)}, u32[]{:S(2)}, u32[]{:S(2)}) %collective-permute-start.21) | collective-permute-done | bytes 8224 | tf_op jit(solution)/shard_map/ppermute | solution.py:60
  53.1 2.3 %sums_1.1 = (f32[2,4096]{1,0:T(2,128)S(1)}, f32[8,256]{1,0:T(8,128)S(1)}) custom-call(bf16[512,3840]{1,0:T(8,128)(2,1)S(1)} %get-tuple-element.61.refs_3_.refs_0_, bf16[512,3840]{1,0:T(8,128)(2,1)S(1)} %get-tuple-element.72.refs_0_.refs_1_, f32[48,3840]{1,0:T(8,128)S(1)} %get-tuple-element.86.v_ref.refs_2_, f32[48,640]{1,0:T(8,128)S(1)} %get-tuple-element.87.u_ref.refs_3_, ...), custom_call_target="tpu_custom_call" | custom-call | flops 754974720 | bytes 8904720 | tf_op jit(solution)/shard_map/sums_1/pallas_call | solution.py:525
  55.5 1.2 %collective-permute-done.22 = f32[2,4096]{1,0:T(2,128)S(1)} collective-permute-done((f32[2,4096]{1,0:T(2,128)S(1)}, f32[2,4096]{1,0:T(2,128)S(1)}, u32[]{:S(2)}, u32[]{:S(2)}) %collective-permute-start.22) | collective-permute-done | bytes 32800 | tf_op jit(solution)/shard_map/ppermute | solution.py:32
  56.7 1.3 %collective-permute-start.25 = (f32[2,4096]{1,0:T(2,128)S(1)}, f32[2,4096]{1,0:T(2,128)S(1)}, u32[]{:S(2)}, u32[]{:S(2)}) collective-permute-start(f32[2,4096]{1,0:T(2,128)S(1)} %add.130), channel_id=1, source_target_pairs={{0,25},{1,24},{2,27},{3,26},{4,29},{5,28},{6,31},{7,30},{8,17},{9,... | collective-permute-start | bytes 98312 | tf_op jit(solution)/shard_map/ppermute | solution.py:32
  58.0 0.9 collective-permute-start.24
  58.9 0.8 collective-permute-start.23
  59.7 1.3 %collective-permute-done.25 = f32[2,4096]{1,0:T(2,128)S(1)} collective-permute-done((f32[2,4096]{1,0:T(2,128)S(1)}, f32[2,4096]{1,0:T(2,128)S(1)}, u32[]{:S(2)}, u32[]{:S(2)}) %collective-permute-start.25) | collective-permute-done | bytes 32800 | tf_op jit(solution)/shard_map/ppermute | solution.py:32
  61.0 0.9 collective-permute-done.24
  62.3 2.6 %collective-permute-start.27 = (f32[2,4096]{1,0:T(2,128)S(1)}, f32[2,4096]{1,0:T(2,128)S(1)}, u32[]{:S(2)}, u32[]{:S(2)}) collective-permute-start(f32[2,4096]{1,0:T(2,128)S(1)} %add_add_fusion.5), channel_id=1, source_target_pairs={{0,7},{1,6},{2,5},{3,4},{4,3},{5,2},{6,1},{7,0},{8,15},{9,14},{10,... | collective-permute-start | bytes 98312 | tf_op jit(solution)/shard_map/ppermute | solution.py:32
  65.3 1.4 %next_products_2.1 = (f32[2,640]{1,0:T(2,128)S(1)}, f32[8,128]{1,0:T(8,128)S(1)}) custom-call(bf16[3840,512]{1,0:T(8,128)(2,1)S(1)} %days_flags.1.m_ref.refs_0_, bf16[3840,128]{1,0:T(8,128)(2,1)S(1)} %get-tuple-element.68.mh_ref.refs_1_, f32[48,3840]{1,0:T(8,128)S(1)} %get-tuple-element.86.v_ref.refs_2_, f32[48,640]{1,0:T(8,128)S(1)} %get-tuple-element.87.u_ref.refs_3_), custom_call_target="tpu_custom_call" | custom-call | flops 943718400 | bytes 5775360 | tf_op jit(solution)/shard_map/next_products_2/pallas_call | solution.py:525
  66.7 1.6 %collective-permute-done.28 = f32[2,4096]{1,0:T(2,128)S(1)} collective-permute-done((f32[2,4096]{1,0:T(2,128)S(1)}, f32[2,4096]{1,0:T(2,128)S(1)}, u32[]{:S(2)}, u32[]{:S(2)}) %collective-permute-start.28) | collective-permute-done | bytes 32800 | tf_op jit(solution)/shard_map/ppermute | solution.py:32
  68.3 0.7 collective-permute-done.26
  69.0 0.9 fields_2.1
  69.8 2.1 %collective-permute-start.30 = (f32[8,256]{1,0:T(8,128)S(1)}, f32[8,256]{1,0:T(8,128)S(1)}, u32[]{:S(2)}, u32[]{:S(2)}) collective-permute-start(f32[8,256]{1,0:T(8,128)S(1)} %get-tuple-element.98.refs_7_), channel_id=1, source_target_pairs={{0,24},{1,25},{2,26},{3,27},{4,28},{5,29},{6,30},{7,31},{8,16},{9,... | collective-permute-start | bytes 24584 | tf_op jit(solution)/shard_map/ppermute | solution.py:60
  72.5 2.0 %collective-permute-done.30.refs_9_ = f32[8,256]{1,0:T(8,128)S(1)} collective-permute-done((f32[8,256]{1,0:T(8,128)S(1)}, f32[8,256]{1,0:T(8,128)S(1)}, u32[]{:S(2)}, u32[]{:S(2)}) %collective-permute-start.30) | collective-permute-done | bytes 8224 | tf_op jit(solution)/shard_map/ppermute | solution.py:60
  74.5 1.1 collective-permute-done.29.refs_8_
  75.6 2.3 %sums_2.1 = (f32[2,4096]{1,0:T(2,128)S(1)}, f32[8,256]{1,0:T(8,128)S(1)}) custom-call(bf16[512,3840]{1,0:T(8,128)(2,1)S(1)} %get-tuple-element.61.refs_3_.refs_0_, bf16[512,3840]{1,0:T(8,128)(2,1)S(1)} %get-tuple-element.72.refs_0_.refs_1_, f32[48,3840]{1,0:T(8,128)S(1)} %get-tuple-element.94.v_ref.refs_2_, f32[48,640]{1,0:T(8,128)S(1)} %get-tuple-element.95.u_ref.refs_3_, ...), custom_call_target="tpu_custom_call" | custom-call | flops 754974720 | bytes 8904720 | tf_op jit(solution)/shard_map/sums_2/pallas_call | solution.py:525
  77.9 1.2 %collective-permute-done.31 = f32[2,4096]{1,0:T(2,128)S(1)} collective-permute-done((f32[2,4096]{1,0:T(2,128)S(1)}, f32[2,4096]{1,0:T(2,128)S(1)}, u32[]{:S(2)}, u32[]{:S(2)}) %collective-permute-start.31) | collective-permute-done | bytes 32800 | tf_op jit(solution)/shard_map/ppermute | solution.py:32
  79.1 0.7 collective-permute-start.34
  79.9 1.1 collective-permute-start.33
  80.9 1.2 %collective-permute-start.32 = (f32[2,4096]{1,0:T(2,128)S(1)}, f32[2,4096]{1,0:T(2,128)S(1)}, u32[]{:S(2)}, u32[]{:S(2)}) collective-permute-start(f32[2,4096]{1,0:T(2,128)S(1)} %add.137), channel_id=1, source_target_pairs={{0,9},{1,8},{2,11},{3,10},{4,13},{5,12},{6,15},{7,14},{8,1},{9,0},... | collective-permute-start | bytes 98312 | tf_op jit(solution)/shard_map/ppermute | solution.py:32
  82.2 1.4 %collective-permute-done.34 = f32[2,4096]{1,0:T(2,128)S(1)} collective-permute-done((f32[2,4096]{1,0:T(2,128)S(1)}, f32[2,4096]{1,0:T(2,128)S(1)}, u32[]{:S(2)}, u32[]{:S(2)}) %collective-permute-start.34) | collective-permute-done | bytes 32800 | tf_op jit(solution)/shard_map/ppermute | solution.py:32
  84.4 2.6 %collective-permute-start.36 = (f32[2,4096]{1,0:T(2,128)S(1)}, f32[2,4096]{1,0:T(2,128)S(1)}, u32[]{:S(2)}, u32[]{:S(2)}) collective-permute-start(f32[2,4096]{1,0:T(2,128)S(1)} %add_add_fusion.3), channel_id=1, source_target_pairs={{0,7},{1,6},{2,5},{3,4},{4,3},{5,2},{6,1},{7,0},{8,15},{9,14},{10,... | collective-permute-start | bytes 98312 | tf_op jit(solution)/shard_map/ppermute | solution.py:32
  87.4 1.4 %next_products_3.1 = (f32[2,640]{1,0:T(2,128)S(1)}, f32[8,128]{1,0:T(8,128)S(1)}) custom-call(bf16[3840,512]{1,0:T(8,128)(2,1)S(1)} %days_flags.1.m_ref.refs_0_, bf16[3840,128]{1,0:T(8,128)(2,1)S(1)} %get-tuple-element.68.mh_ref.refs_1_, f32[48,3840]{1,0:T(8,128)S(1)} %get-tuple-element.94.v_ref.refs_2_, f32[48,640]{1,0:T(8,128)S(1)} %get-tuple-element.95.u_ref.refs_3_), custom_call_target="tpu_custom_call" | custom-call | flops 943718400 | bytes 5775360 | tf_op jit(solution)/shard_map/next_products_3/pallas_call | solution.py:525
  88.7 1.6 %collective-permute-done.37 = f32[2,4096]{1,0:T(2,128)S(1)} collective-permute-done((f32[2,4096]{1,0:T(2,128)S(1)}, f32[2,4096]{1,0:T(2,128)S(1)}, u32[]{:S(2)}, u32[]{:S(2)}) %collective-permute-start.37) | collective-permute-done | bytes 32800 | tf_op jit(solution)/shard_map/ppermute | solution.py:32
  90.3 0.7 collective-permute-done.35
  91.1 0.9 fields_3.1
  91.9 1.5 %collective-permute-start.39 = (f32[8,256]{1,0:T(8,128)S(1)}, f32[8,256]{1,0:T(8,128)S(1)}, u32[]{:S(2)}, u32[]{:S(2)}) collective-permute-start(f32[8,256]{1,0:T(8,128)S(1)} %get-tuple-element.103.refs_7_), channel_id=1, source_target_pairs={{0,24},{1,25},{2,26},{3,27},{4,28},{5,29},{6,30},{7,31},{8,16},{9,... | collective-permute-start | bytes 24584 | tf_op jit(solution)/shard_map/ppermute | solution.py:60
  93.4 1.0 collective-permute-start.38
  94.4 2.2 %collective-permute-done.39.refs_9_ = f32[8,256]{1,0:T(8,128)S(1)} collective-permute-done((f32[8,256]{1,0:T(8,128)S(1)}, f32[8,256]{1,0:T(8,128)S(1)}, u32[]{:S(2)}, u32[]{:S(2)}) %collective-permute-start.39) | collective-permute-done | bytes 8224 | tf_op jit(solution)/shard_map/ppermute | solution.py:60
  97.1 2.3 %sums_3.1 = (f32[2,4096]{1,0:T(2,128)S(1)}, f32[8,256]{1,0:T(8,128)S(1)}) custom-call(bf16[512,3840]{1,0:T(8,128)(2,1)S(1)} %get-tuple-element.61.refs_3_.refs_0_, bf16[512,3840]{1,0:T(8,128)(2,1)S(1)} %get-tuple-element.72.refs_0_.refs_1_, f32[48,3840]{1,0:T(8,128)S(1)} %get-tuple-element.101.refs_2_.refs_0_, ...), custom_call_target="tpu_custom_call" | custom-call | flops 754974720 | bytes 8904720 | tf_op jit(solution)/shard_map/sums_3/pallas_call | solution.py:525
  99.4 1.2 %collective-permute-done.40 = f32[2,4096]{1,0:T(2,128)S(1)} collective-permute-done((f32[2,4096]{1,0:T(2,128)S(1)}, f32[2,4096]{1,0:T(2,128)S(1)}, u32[]{:S(2)}, u32[]{:S(2)}) %collective-permute-start.40) | collective-permute-done | bytes 32800 | tf_op jit(solution)/shard_map/ppermute | solution.py:32
  100.6 1.3 %collective-permute-start.43 = (f32[2,4096]{1,0:T(2,128)S(1)}, f32[2,4096]{1,0:T(2,128)S(1)}, u32[]{:S(2)}, u32[]{:S(2)}) collective-permute-start(f32[2,4096]{1,0:T(2,128)S(1)} %add.144), channel_id=1, source_target_pairs={{0,25},{1,24},{2,27},{3,26},{4,29},{5,28},{6,31},{7,30},{8,17},{9,... | collective-permute-start | bytes 98312 | tf_op jit(solution)/shard_map/ppermute | solution.py:32
  102.0 0.9 collective-permute-start.42
  102.8 0.8 collective-permute-start.41
  103.7 1.3 %collective-permute-done.43 = f32[2,4096]{1,0:T(2,128)S(1)} collective-permute-done((f32[2,4096]{1,0:T(2,128)S(1)}, f32[2,4096]{1,0:T(2,128)S(1)}, u32[]{:S(2)}, u32[]{:S(2)}) %collective-permute-start.43) | collective-permute-done | bytes 32800 | tf_op jit(solution)/shard_map/ppermute | solution.py:32
  104.9 0.8 collective-permute-done.42
  106.3 2.6 %collective-permute-start.45 = (f32[2,4096]{1,0:T(2,128)S(1)}, f32[2,4096]{1,0:T(2,128)S(1)}, u32[]{:S(2)}, u32[]{:S(2)}) collective-permute-start(f32[2,4096]{1,0:T(2,128)S(1)} %add_add_fusion.1), channel_id=1, source_target_pairs={{0,7},{1,6},{2,5},{3,4},{4,3},{5,2},{6,1},{7,0},{8,15},{9,14},{10,... | collective-permute-start | bytes 98312 | tf_op jit(solution)/shard_map/ppermute | solution.py:32
  109.2 3.0 %collective-permute-done.46 = f32[2,4096]{1,0:T(2,128)S(1)} collective-permute-done((f32[2,4096]{1,0:T(2,128)S(1)}, f32[2,4096]{1,0:T(2,128)S(1)}, u32[]{:S(2)}, u32[]{:S(2)}) %collective-permute-start.46) | collective-permute-done | bytes 32800 | tf_op jit(solution)/shard_map/ppermute | solution.py:32
  112.2 0.7 collective-permute-done.44
  112.9 1.3 %last.1 = (f32[48,4,128]{2,1,0:T(4,128)}, f32[48,480]{1,0:T(8,128)}) custom-call(f32[48,3840]{1,0:T(8,128)S(1)} %get-tuple-element.101.refs_2_.refs_0_, f32[48,640]{1,0:T(8,128)S(1)} %get-tuple-element.102.refs_3_.refs_1_, f32[2,4096]{1,0:T(2,128)S(1)} %add_add_fusion.refs_2_, ...), custom_call_target="tpu_custom_call", output_to_operand_aliasing={{0}: (5, {}), {1}: (6, {})} | custom-call | bytes 1091600 | tf_op jit(solution)/shard_map/last/pallas_call | solution.py:525
  (65 shorter events, 10.2 us)
Async XLA Ops:
  0.6 17.5 %copy-start = (f32[48,480]{1,0:T(8,128)S(1)}, f32[48,480]{1,0:T(8,128)}, u32[]{:S(2)}) copy-start(f32[48,480]{1,0:T(8,128)} %refs_2_.1) | copy-start | bytes 276484
  0.6 16.1 %collective-permute-start.5 = (f32[48,480]{1,0:T(8,128)}, f32[48,480]{1,0:T(8,128)S(1)}, u32[]{:S(2)}, u32[]{:S(2)}) collective-permute-start(f32[48,480]{1,0:T(8,128)} %refs_2_.1), channel_id=1, source_target_pairs={{0,1},{1,0},{2,3},{3,2},{4,5},{5,4},{6,7},{7,6},{8,9},{9,8},{10,11... | collective-permute-start | bytes 276488 | tf_op jit(solution)/shard_map/ppermute | solution.py:32
  1.2 11.5 %collective-permute-start.4 = (f32[48,480]{1,0:T(8,128)}, f32[48,480]{1,0:T(8,128)S(1)}, u32[]{:S(2)}, u32[]{:S(2)}) collective-permute-start(f32[48,480]{1,0:T(8,128)} %refs_2_.1), channel_id=1, source_target_pairs={{0,7},{1,6},{2,5},{3,4},{4,3},{5,2},{6,1},{7,0},{8,15},{9,14},{10,... | collective-permute-start | bytes 276488 | tf_op jit(solution)/shard_map/ppermute | solution.py:32
  5.9 10.4 %collective-permute-start.3 = (f32[48,480]{1,0:T(8,128)}, f32[48,480]{1,0:T(8,128)S(1)}, u32[]{:S(2)}, u32[]{:S(2)}) collective-permute-start(f32[48,480]{1,0:T(8,128)} %refs_2_.1), channel_id=1, source_target_pairs={{0,5},{1,4},{2,7},{3,6},{4,1},{5,0},{6,3},{7,2},{8,13},{9,12},{10,... | collective-permute-start | bytes 276488 | tf_op jit(solution)/shard_map/ppermute | solution.py:32
  5.9 10.4 %collective-permute-start.2 = (f32[48,480]{1,0:T(8,128)}, f32[48,480]{1,0:T(8,128)S(1)}, u32[]{:S(2)}, u32[]{:S(2)}) collective-permute-start(f32[48,480]{1,0:T(8,128)} %refs_2_.1), channel_id=1, source_target_pairs={{0,3},{1,2},{2,1},{3,0},{4,7},{5,6},{6,5},{7,4},{8,11},{9,10},{10,... | collective-permute-start | bytes 276488 | tf_op jit(solution)/shard_map/ppermute | solution.py:32
  12.3 8.2 %collective-permute-start = (f32[184,128]{1,0:T(8,128)S(1)}, f32[184,128]{1,0:T(8,128)S(1)}, u32[]{:S(2)}, u32[]{:S(2)}) collective-permute-start(f32[184,128]{1,0:T(8,128)S(1)} %get-tuple-element.57), channel_id=1, source_target_pairs={{0,1},{1,0},{2,3},{3,2},{4,5},{5,4},{6,7},{7,6},{8,9},{9,8},{10,11... | collective-permute-start | bytes 282632 | tf_op jit(solution)/shard_map/ppermute | solution.py:32
  12.7 7.8 %collective-permute-start.1 = (f32[184,128]{1,0:T(8,128)S(1)}, f32[184,128]{1,0:T(8,128)S(1)}, u32[]{:S(2)}, u32[]{:S(2)}) collective-permute-start(f32[184,128]{1,0:T(8,128)S(1)} %get-tuple-element.58), channel_id=1, source_target_pairs={{0,7},{1,2},{2,1},{3,4},{4,3},{5,6},{6,5},{7,0},{8,15},{9,10},{10,... | collective-permute-start | bytes 282632 | tf_op jit(solution)/shard_map/ppermute | solution.py:67
  16.3 1.3 %collective-permute-start.6 = (f32[48,480]{1,0:T(8,128)S(1)}, f32[48,480]{1,0:T(8,128)S(1)}, u32[]{:S(2)}, u32[]{:S(2)}) collective-permute-start(f32[48,480]{1,0:T(8,128)S(1)} %collective-permute-done.2.refs_9_.refs_5_), channel_id=1, source_target_pairs={{0,1},{1,0},{2,3},{3,2},{4,5},{5,4},{6,7},{7,6},{8,9},{9,8},{10,11... | collective-permute-start | bytes 276488 | tf_op jit(solution)/shard_map/ppermute | solution.py:32
  16.3 1.4 %collective-permute-start.7 = (f32[48,480]{1,0:T(8,128)S(1)}, f32[48,480]{1,0:T(8,128)S(1)}, u32[]{:S(2)}, u32[]{:S(2)}) collective-permute-start(f32[48,480]{1,0:T(8,128)S(1)} %collective-permute-done.3.refs_11_.refs_7_), channel_id=1, source_target_pairs={{0,1},{1,0},{2,3},{3,2},{4,5},{5,4},{6,7},{7,6},{8,9},{9,8},{10,11... | collective-permute-start | bytes 276488 | tf_op jit(solution)/shard_map/ppermute | solution.py:32
  16.8 1.3 %collective-permute-start.8 = (f32[48,480]{1,0:T(8,128)S(1)}, f32[48,480]{1,0:T(8,128)S(1)}, u32[]{:S(2)}, u32[]{:S(2)}) collective-permute-start(f32[48,480]{1,0:T(8,128)S(1)} %collective-permute-done.4.refs_13_.refs_9_), channel_id=1, source_target_pairs={{0,1},{1,0},{2,3},{3,2},{4,5},{5,4},{6,7},{7,6},{8,9},{9,8},{10,11... | collective-permute-start | bytes 276488 | tf_op jit(solution)/shard_map/ppermute | solution.py:32
  19.8 4.2 %collective-permute-start.9 = (f32[8,128]{1,0:T(8,128)S(1)}, f32[8,128]{1,0:T(8,128)S(1)}, u32[]{:S(2)}, u32[]{:S(2)}) collective-permute-start(f32[8,128]{1,0:T(8,128)S(1)} %get-tuple-element.74), channel_id=1, source_target_pairs={{0,1},{1,0},{2,3},{3,2},{4,5},{5,4},{6,7},{7,6},{8,9},{9,8},{10,11... | collective-permute-start | bytes 12296 | tf_op jit(solution)/shard_map/ppermute | solution.py:32
  20.0 4.8 %collective-permute-start.10 = (f32[8,128]{1,0:T(8,128)S(1)}, f32[8,128]{1,0:T(8,128)S(1)}, u32[]{:S(2)}, u32[]{:S(2)}) collective-permute-start(f32[8,128]{1,0:T(8,128)S(1)} %get-tuple-element.75), channel_id=1, source_target_pairs={{0,7},{1,2},{2,1},{3,4},{4,3},{5,6},{6,5},{7,0},{8,15},{9,10},{10,... | collective-permute-start | bytes 12296 | tf_op jit(solution)/shard_map/ppermute | solution.py:67
  25.5 4.7 %collective-permute-start.12 = (f32[16,256]{1,0:T(8,128)S(1)}, f32[16,256]{1,0:T(8,128)S(1)}, u32[]{:S(2)}, u32[]{:S(2)}) collective-permute-start(f32[16,256]{1,0:T(8,128)S(1)} %get-tuple-element.83.refs_7_), channel_id=1, source_target_pairs={{0,24},{1,25},{2,26},{3,27},{4,28},{5,29},{6,30},{7,31},{8,16},{9,... | collective-permute-start | bytes 49160 | tf_op jit(solution)/shard_map/ppermute | solution.py:60
  28.0 3.7 %collective-permute-start.11 = (f32[16,256]{1,0:T(8,128)S(1)}, f32[16,256]{1,0:T(8,128)S(1)}, u32[]{:S(2)}, u32[]{:S(2)}) collective-permute-start(f32[16,256]{1,0:T(8,128)S(1)} %get-tuple-element.83.refs_7_), channel_id=1, source_target_pairs={{0,8},{1,9},{2,10},{3,11},{4,12},{5,13},{6,14},{7,15},{8,0},{9,1},... | collective-permute-start | bytes 49160 | tf_op jit(solution)/shard_map/ppermute | solution.py:59
  34.0 1.3 %collective-permute-start.13 = (f32[2,4096]{1,0:T(2,128)S(1)}, f32[2,4096]{1,0:T(2,128)S(1)}, u32[]{:S(2)}, u32[]{:S(2)}) collective-permute-start(f32[2,4096]{1,0:T(2,128)S(1)} %get-tuple-element.84), channel_id=1, source_target_pairs={{0,1},{1,0},{2,3},{3,2},{4,5},{5,4},{6,7},{7,6},{8,9},{9,8},{10,11... | collective-permute-start | bytes 98312 | tf_op jit(solution)/shard_map/ppermute | solution.py:32
  35.3 5.1 %collective-permute-start.16 = (f32[2,4096]{1,0:T(2,128)S(1)}, f32[2,4096]{1,0:T(2,128)S(1)}, u32[]{:S(2)}, u32[]{:S(2)}) collective-permute-start(f32[2,4096]{1,0:T(2,128)S(1)} %add.123), channel_id=1, source_target_pairs={{0,25},{1,24},{2,27},{3,26},{4,29},{5,28},{6,31},{7,30},{8,17},{9,... | collective-permute-start | bytes 98312 | tf_op jit(solution)/shard_map/ppermute | solution.py:32
  36.0 4.4 %collective-permute-start.15 = (f32[2,4096]{1,0:T(2,128)S(1)}, f32[2,4096]{1,0:T(2,128)S(1)}, u32[]{:S(2)}, u32[]{:S(2)}) collective-permute-start(f32[2,4096]{1,0:T(2,128)S(1)} %add.123), channel_id=1, source_target_pairs={{0,17},{1,16},{2,19},{3,18},{4,21},{5,20},{6,23},{7,22},{8,25},{9,... | collective-permute-start | bytes 98312 | tf_op jit(solution)/shard_map/ppermute | solution.py:32
  37.1 3.3 %collective-permute-start.14 = (f32[2,4096]{1,0:T(2,128)S(1)}, f32[2,4096]{1,0:T(2,128)S(1)}, u32[]{:S(2)}, u32[]{:S(2)}) collective-permute-start(f32[2,4096]{1,0:T(2,128)S(1)} %add.123), channel_id=1, source_target_pairs={{0,9},{1,8},{2,11},{3,10},{4,13},{5,12},{6,15},{7,14},{8,1},{9,0},... | collective-permute-start | bytes 98312 | tf_op jit(solution)/shard_map/ppermute | solution.py:32
  40.5 5.6 %collective-permute-start.19 = (f32[2,4096]{1,0:T(2,128)S(1)}, f32[2,4096]{1,0:T(2,128)S(1)}, u32[]{:S(2)}, u32[]{:S(2)}) collective-permute-start(f32[2,4096]{1,0:T(2,128)S(1)} %add_add_fusion.7), channel_id=1, source_target_pairs={{0,5},{1,4},{2,7},{3,6},{4,1},{5,0},{6,3},{7,2},{8,13},{9,12},{10,... | collective-permute-start | bytes 98312 | tf_op jit(solution)/shard_map/ppermute | solution.py:32
  40.5 5.5 %collective-permute-start.18 = (f32[2,4096]{1,0:T(2,128)S(1)}, f32[2,4096]{1,0:T(2,128)S(1)}, u32[]{:S(2)}, u32[]{:S(2)}) collective-permute-start(f32[2,4096]{1,0:T(2,128)S(1)} %add_add_fusion.7), channel_id=1, source_target_pairs={{0,7},{1,6},{2,5},{3,4},{4,3},{5,2},{6,1},{7,0},{8,15},{9,14},{10,... | collective-permute-start | bytes 98312 | tf_op jit(solution)/shard_map/ppermute | solution.py:32
  43.3 3.8 %collective-permute-start.17 = (f32[2,4096]{1,0:T(2,128)S(1)}, f32[2,4096]{1,0:T(2,128)S(1)}, u32[]{:S(2)}, u32[]{:S(2)}) collective-permute-start(f32[2,4096]{1,0:T(2,128)S(1)} %add_add_fusion.7), channel_id=1, source_target_pairs={{0,3},{1,2},{2,1},{3,0},{4,7},{5,6},{6,5},{7,4},{8,11},{9,10},{10,... | collective-permute-start | bytes 98312 | tf_op jit(solution)/shard_map/ppermute | solution.py:32
  48.0 4.6 %collective-permute-start.21 = (f32[8,256]{1,0:T(8,128)S(1)}, f32[8,256]{1,0:T(8,128)S(1)}, u32[]{:S(2)}, u32[]{:S(2)}) collective-permute-start(f32[8,256]{1,0:T(8,128)S(1)} %get-tuple-element.90.refs_7_), channel_id=1, source_target_pairs={{0,24},{1,25},{2,26},{3,27},{4,28},{5,29},{6,30},{7,31},{8,16},{9,... | collective-permute-start | bytes 24584 | tf_op jit(solution)/shard_map/ppermute | solution.py:60
  49.5 3.7 %collective-permute-start.20 = (f32[8,256]{1,0:T(8,128)S(1)}, f32[8,256]{1,0:T(8,128)S(1)}, u32[]{:S(2)}, u32[]{:S(2)}) collective-permute-start(f32[8,256]{1,0:T(8,128)S(1)} %get-tuple-element.90.refs_7_), channel_id=1, source_target_pairs={{0,8},{1,9},{2,10},{3,11},{4,12},{5,13},{6,14},{7,15},{8,0},{9,1},... | collective-permute-start | bytes 24584 | tf_op jit(solution)/shard_map/ppermute | solution.py:59
  55.4 1.3 %collective-permute-start.22 = (f32[2,4096]{1,0:T(2,128)S(1)}, f32[2,4096]{1,0:T(2,128)S(1)}, u32[]{:S(2)}, u32[]{:S(2)}) collective-permute-start(f32[2,4096]{1,0:T(2,128)S(1)} %get-tuple-element.92), channel_id=1, source_target_pairs={{0,1},{1,0},{2,3},{3,2},{4,5},{5,4},{6,7},{7,6},{8,9},{9,8},{10,11... | collective-permute-start | bytes 98312 | tf_op jit(solution)/shard_map/ppermute | solution.py:32
  56.7 4.3 %collective-permute-start.25 = (f32[2,4096]{1,0:T(2,128)S(1)}, f32[2,4096]{1,0:T(2,128)S(1)}, u32[]{:S(2)}, u32[]{:S(2)}) collective-permute-start(f32[2,4096]{1,0:T(2,128)S(1)} %add.130), channel_id=1, source_target_pairs={{0,25},{1,24},{2,27},{3,26},{4,29},{5,28},{6,31},{7,30},{8,17},{9,... | collective-permute-start | bytes 98312 | tf_op jit(solution)/shard_map/ppermute | solution.py:32
  58.0 3.8 %collective-permute-start.24 = (f32[2,4096]{1,0:T(2,128)S(1)}, f32[2,4096]{1,0:T(2,128)S(1)}, u32[]{:S(2)}, u32[]{:S(2)}) collective-permute-start(f32[2,4096]{1,0:T(2,128)S(1)} %add.130), channel_id=1, source_target_pairs={{0,17},{1,16},{2,19},{3,18},{4,21},{5,20},{6,23},{7,22},{8,25},{9,... | collective-permute-start | bytes 98312 | tf_op jit(solution)/shard_map/ppermute | solution.py:32
  58.9 3.3 %collective-permute-start.23 = (f32[2,4096]{1,0:T(2,128)S(1)}, f32[2,4096]{1,0:T(2,128)S(1)}, u32[]{:S(2)}, u32[]{:S(2)}) collective-permute-start(f32[2,4096]{1,0:T(2,128)S(1)} %add.130), channel_id=1, source_target_pairs={{0,9},{1,8},{2,11},{3,10},{4,13},{5,12},{6,15},{7,14},{8,1},{9,0},... | collective-permute-start | bytes 98312 | tf_op jit(solution)/shard_map/ppermute | solution.py:32
  62.3 6.0 %collective-permute-start.28 = (f32[2,4096]{1,0:T(2,128)S(1)}, f32[2,4096]{1,0:T(2,128)S(1)}, u32[]{:S(2)}, u32[]{:S(2)}) collective-permute-start(f32[2,4096]{1,0:T(2,128)S(1)} %add_add_fusion.5), channel_id=1, source_target_pairs={{0,5},{1,4},{2,7},{3,6},{4,1},{5,0},{6,3},{7,2},{8,13},{9,12},{10,... | collective-permute-start | bytes 98312 | tf_op jit(solution)/shard_map/ppermute | solution.py:32
  62.3 5.9 %collective-permute-start.27 = (f32[2,4096]{1,0:T(2,128)S(1)}, f32[2,4096]{1,0:T(2,128)S(1)}, u32[]{:S(2)}, u32[]{:S(2)}) collective-permute-start(f32[2,4096]{1,0:T(2,128)S(1)} %add_add_fusion.5), channel_id=1, source_target_pairs={{0,7},{1,6},{2,5},{3,4},{4,3},{5,2},{6,1},{7,0},{8,15},{9,14},{10,... | collective-permute-start | bytes 98312 | tf_op jit(solution)/shard_map/ppermute | solution.py:32
  64.9 4.0 %collective-permute-start.26 = (f32[2,4096]{1,0:T(2,128)S(1)}, f32[2,4096]{1,0:T(2,128)S(1)}, u32[]{:S(2)}, u32[]{:S(2)}) collective-permute-start(f32[2,4096]{1,0:T(2,128)S(1)} %add_add_fusion.5), channel_id=1, source_target_pairs={{0,3},{1,2},{2,1},{3,0},{4,7},{5,6},{6,5},{7,4},{8,11},{9,10},{10,... | collective-permute-start | bytes 98312 | tf_op jit(solution)/shard_map/ppermute | solution.py:32
  69.8 4.6 %collective-permute-start.30 = (f32[8,256]{1,0:T(8,128)S(1)}, f32[8,256]{1,0:T(8,128)S(1)}, u32[]{:S(2)}, u32[]{:S(2)}) collective-permute-start(f32[8,256]{1,0:T(8,128)S(1)} %get-tuple-element.98.refs_7_), channel_id=1, source_target_pairs={{0,24},{1,25},{2,26},{3,27},{4,28},{5,29},{6,30},{7,31},{8,16},{9,... | collective-permute-start | bytes 24584 | tf_op jit(solution)/shard_map/ppermute | solution.py:60
  71.9 3.7 %collective-permute-start.29 = (f32[8,256]{1,0:T(8,128)S(1)}, f32[8,256]{1,0:T(8,128)S(1)}, u32[]{:S(2)}, u32[]{:S(2)}) collective-permute-start(f32[8,256]{1,0:T(8,128)S(1)} %get-tuple-element.98.refs_7_), channel_id=1, source_target_pairs={{0,8},{1,9},{2,10},{3,11},{4,12},{5,13},{6,14},{7,15},{8,0},{9,1},... | collective-permute-start | bytes 24584 | tf_op jit(solution)/shard_map/ppermute | solution.py:59
  77.8 1.3 %collective-permute-start.31 = (f32[2,4096]{1,0:T(2,128)S(1)}, f32[2,4096]{1,0:T(2,128)S(1)}, u32[]{:S(2)}, u32[]{:S(2)}) collective-permute-start(f32[2,4096]{1,0:T(2,128)S(1)} %get-tuple-element.99), channel_id=1, source_target_pairs={{0,1},{1,0},{2,3},{3,2},{4,5},{5,4},{6,7},{7,6},{8,9},{9,8},{10,11... | collective-permute-start | bytes 98312 | tf_op jit(solution)/shard_map/ppermute | solution.py:32
  79.1 4.4 %collective-permute-start.34 = (f32[2,4096]{1,0:T(2,128)S(1)}, f32[2,4096]{1,0:T(2,128)S(1)}, u32[]{:S(2)}, u32[]{:S(2)}) collective-permute-start(f32[2,4096]{1,0:T(2,128)S(1)} %add.137), channel_id=1, source_target_pairs={{0,25},{1,24},{2,27},{3,26},{4,29},{5,28},{6,31},{7,30},{8,17},{9,... | collective-permute-start | bytes 98312 | tf_op jit(solution)/shard_map/ppermute | solution.py:32
  79.9 4.1 %collective-permute-start.33 = (f32[2,4096]{1,0:T(2,128)S(1)}, f32[2,4096]{1,0:T(2,128)S(1)}, u32[]{:S(2)}, u32[]{:S(2)}) collective-permute-start(f32[2,4096]{1,0:T(2,128)S(1)} %add.137), channel_id=1, source_target_pairs={{0,17},{1,16},{2,19},{3,18},{4,21},{5,20},{6,23},{7,22},{8,25},{9,... | collective-permute-start | bytes 98312 | tf_op jit(solution)/shard_map/ppermute | solution.py:32
  80.9 3.3 %collective-permute-start.32 = (f32[2,4096]{1,0:T(2,128)S(1)}, f32[2,4096]{1,0:T(2,128)S(1)}, u32[]{:S(2)}, u32[]{:S(2)}) collective-permute-start(f32[2,4096]{1,0:T(2,128)S(1)} %add.137), channel_id=1, source_target_pairs={{0,9},{1,8},{2,11},{3,10},{4,13},{5,12},{6,15},{7,14},{8,1},{9,0},... | collective-permute-start | bytes 98312 | tf_op jit(solution)/shard_map/ppermute | solution.py:32
  84.3 6.0 %collective-permute-start.37 = (f32[2,4096]{1,0:T(2,128)S(1)}, f32[2,4096]{1,0:T(2,128)S(1)}, u32[]{:S(2)}, u32[]{:S(2)}) collective-permute-start(f32[2,4096]{1,0:T(2,128)S(1)} %add_add_fusion.3), channel_id=1, source_target_pairs={{0,5},{1,4},{2,7},{3,6},{4,1},{5,0},{6,3},{7,2},{8,13},{9,12},{10,... | collective-permute-start | bytes 98312 | tf_op jit(solution)/shard_map/ppermute | solution.py:32
  84.4 5.9 %collective-permute-start.36 = (f32[2,4096]{1,0:T(2,128)S(1)}, f32[2,4096]{1,0:T(2,128)S(1)}, u32[]{:S(2)}, u32[]{:S(2)}) collective-permute-start(f32[2,4096]{1,0:T(2,128)S(1)} %add_add_fusion.3), channel_id=1, source_target_pairs={{0,7},{1,6},{2,5},{3,4},{4,3},{5,2},{6,1},{7,0},{8,15},{9,14},{10,... | collective-permute-start | bytes 98312 | tf_op jit(solution)/shard_map/ppermute | solution.py:32
  87.0 4.0 %collective-permute-start.35 = (f32[2,4096]{1,0:T(2,128)S(1)}, f32[2,4096]{1,0:T(2,128)S(1)}, u32[]{:S(2)}, u32[]{:S(2)}) collective-permute-start(f32[2,4096]{1,0:T(2,128)S(1)} %add_add_fusion.3), channel_id=1, source_target_pairs={{0,3},{1,2},{2,1},{3,0},{4,7},{5,6},{6,5},{7,4},{8,11},{9,10},{10,... | collective-permute-start | bytes 98312 | tf_op jit(solution)/shard_map/ppermute | solution.py:32
  91.9 4.6 %collective-permute-start.39 = (f32[8,256]{1,0:T(8,128)S(1)}, f32[8,256]{1,0:T(8,128)S(1)}, u32[]{:S(2)}, u32[]{:S(2)}) collective-permute-start(f32[8,256]{1,0:T(8,128)S(1)} %get-tuple-element.103.refs_7_), channel_id=1, source_target_pairs={{0,24},{1,25},{2,26},{3,27},{4,28},{5,29},{6,30},{7,31},{8,16},{9,... | collective-permute-start | bytes 24584 | tf_op jit(solution)/shard_map/ppermute | solution.py:60
  93.4 3.7 %collective-permute-start.38 = (f32[8,256]{1,0:T(8,128)S(1)}, f32[8,256]{1,0:T(8,128)S(1)}, u32[]{:S(2)}, u32[]{:S(2)}) collective-permute-start(f32[8,256]{1,0:T(8,128)S(1)} %get-tuple-element.103.refs_7_), channel_id=1, source_target_pairs={{0,8},{1,9},{2,10},{3,11},{4,12},{5,13},{6,14},{7,15},{8,0},{9,1},... | collective-permute-start | bytes 24584 | tf_op jit(solution)/shard_map/ppermute | solution.py:59
  99.3 1.3 %collective-permute-start.40 = (f32[2,4096]{1,0:T(2,128)S(1)}, f32[2,4096]{1,0:T(2,128)S(1)}, u32[]{:S(2)}, u32[]{:S(2)}) collective-permute-start(f32[2,4096]{1,0:T(2,128)S(1)} %get-tuple-element.104), channel_id=1, source_target_pairs={{0,1},{1,0},{2,3},{3,2},{4,5},{5,4},{6,7},{7,6},{8,9},{9,8},{10,11... | collective-permute-start | bytes 98312 | tf_op jit(solution)/shard_map/ppermute | solution.py:32
  100.6 4.3 %collective-permute-start.43 = (f32[2,4096]{1,0:T(2,128)S(1)}, f32[2,4096]{1,0:T(2,128)S(1)}, u32[]{:S(2)}, u32[]{:S(2)}) collective-permute-start(f32[2,4096]{1,0:T(2,128)S(1)} %add.144), channel_id=1, source_target_pairs={{0,25},{1,24},{2,27},{3,26},{4,29},{5,28},{6,31},{7,30},{8,17},{9,... | collective-permute-start | bytes 98312 | tf_op jit(solution)/shard_map/ppermute | solution.py:32
  102.0 3.8 %collective-permute-start.42 = (f32[2,4096]{1,0:T(2,128)S(1)}, f32[2,4096]{1,0:T(2,128)S(1)}, u32[]{:S(2)}, u32[]{:S(2)}) collective-permute-start(f32[2,4096]{1,0:T(2,128)S(1)} %add.144), channel_id=1, source_target_pairs={{0,17},{1,16},{2,19},{3,18},{4,21},{5,20},{6,23},{7,22},{8,25},{9,... | collective-permute-start | bytes 98312 | tf_op jit(solution)/shard_map/ppermute | solution.py:32
  102.8 3.3 %collective-permute-start.41 = (f32[2,4096]{1,0:T(2,128)S(1)}, f32[2,4096]{1,0:T(2,128)S(1)}, u32[]{:S(2)}, u32[]{:S(2)}) collective-permute-start(f32[2,4096]{1,0:T(2,128)S(1)} %add.144), channel_id=1, source_target_pairs={{0,9},{1,8},{2,11},{3,10},{4,13},{5,12},{6,15},{7,14},{8,1},{9,0},... | collective-permute-start | bytes 98312 | tf_op jit(solution)/shard_map/ppermute | solution.py:32
  106.2 6.0 %collective-permute-start.46 = (f32[2,4096]{1,0:T(2,128)S(1)}, f32[2,4096]{1,0:T(2,128)S(1)}, u32[]{:S(2)}, u32[]{:S(2)}) collective-permute-start(f32[2,4096]{1,0:T(2,128)S(1)} %add_add_fusion.1), channel_id=1, source_target_pairs={{0,5},{1,4},{2,7},{3,6},{4,1},{5,0},{6,3},{7,2},{8,13},{9,12},{10,... | collective-permute-start | bytes 98312 | tf_op jit(solution)/shard_map/ppermute | solution.py:32
  106.3 5.9 %collective-permute-start.45 = (f32[2,4096]{1,0:T(2,128)S(1)}, f32[2,4096]{1,0:T(2,128)S(1)}, u32[]{:S(2)}, u32[]{:S(2)}) collective-permute-start(f32[2,4096]{1,0:T(2,128)S(1)} %add_add_fusion.1), channel_id=1, source_target_pairs={{0,7},{1,6},{2,5},{3,4},{4,3},{5,2},{6,1},{7,0},{8,15},{9,14},{10,... | collective-permute-start | bytes 98312 | tf_op jit(solution)/shard_map/ppermute | solution.py:32
  108.9 4.0 %collective-permute-start.44 = (f32[2,4096]{1,0:T(2,128)S(1)}, f32[2,4096]{1,0:T(2,128)S(1)}, u32[]{:S(2)}, u32[]{:S(2)}) collective-permute-start(f32[2,4096]{1,0:T(2,128)S(1)} %add_add_fusion.1), channel_id=1, source_target_pairs={{0,3},{1,2},{2,1},{3,0},{4,7},{5,6},{6,5},{7,4},{8,11},{9,10},{10,... | collective-permute-start | bytes 98312 | tf_op jit(solution)/shard_map/ppermute | solution.py:32

commit v11 on v10

--- a/solution.py
+++ b/solution.py
@@ -466,7 +466,12 @@
     weighted = cells(block * cosl_ref[...])
     u = u_ref[:, :own]
     modes = u.shape[0]
-    high, lower = split(jnp.concatenate([u * weighted[0:1], u * weighted[1:2]], axis=0))
+    scaled = block * cosl_ref[...]
+    parts = []
+    for j in range(2):
+        tiles = [u[:, r * LANES : (r + 1) * LANES] * scaled[2 * r + j : 2 * r + j + 1, :LANES] for r in range(rows)]
+        parts.append(jnp.concatenate(tiles, axis=1))
+    high, lower = split(jnp.concatenate(parts, axis=0))
     left = jnp.concatenate([high, lower], axis=0)
     high, lower = split(weighted)
     left_a = jnp.concatenate([high, lower], axis=0)
@@ -518,8 +523,8 @@
         store.wait()
 
 
-def call(kernel, name, outs, scratch, args, smem=(), mib=24, flops=0, copies=0, in_hbm=(), out_hbm=(), aliases={}, light=False):
-    moved = 0 if light else sum(z.size * z.dtype.itemsize for z in args)
+def call(kernel, name, outs, scratch, args, smem=(), mib=24, flops=0, copies=0, in_hbm=(), out_hbm=(), aliases={}):
+    moved = sum(z.size * z.dtype.itemsize for z in args)
     hbm = pl.BlockSpec(memory_space=pl.ANY)
     args = [pltpu.with_memory_space_constraint(z, pltpu.HBM) if i in in_hbm else z for i, z in enumerate(args)]
     return pl.pallas_call(
@@ -594,7 +599,7 @@
         [((PAIRS, days), F32)],
         [a, place, *pieces],
         smem=(1,),
-        light=True,
+        flops=4 * PAIRS * own * days,
     )
     near_xv, far_xv = lon_partners(near_xv, far_xv)
     base, inverse, v, m_halo, u, row, spread = call(
@@ -641,6 +646,19 @@
                 aliases={2: 1, 3: 2},
             )
         got_a, got_b = lat_partners(fresh)
+        if step == 0:
+            got_a, got_b, m_days = lax.optimization_barrier((got_a, got_b, m_days))
+        if step + 1 < STEPS:
+            base, inverse = call(
+                functools.partial(next_products_kernel, step + 1, chunk),
+                f"next_products_{step + 1}",
+                [((2, cells), F32), ((8, LANES), F32)],
+                [],
+                [m_days, m_halo, v, u],
+                flops=8 * modes * cells * days,
+            )
+            if step:
+                got_a, got_b, base, inverse = lax.optimization_barrier((got_a, got_b, base, inverse))
         outs = [((2, days + 2 * LANES), F32), ((count, 2 * LANES), F32)]
         coef = ((5 * 3 * count, 2 * LANES), F32)
         partial_sums, block, *made = call(
@@ -653,15 +671,6 @@
             flops=8 * modes * own * days,
         )
         coefs = coefs or made
-        if step + 1 < STEPS:
-            base, inverse = call(
-                functools.partial(next_products_kernel, step + 1, chunk),
-                f"next_products_{step + 1}",
-                [((2, cells), F32), ((8, LANES), F32)],
-                [],
-                [m_days, m_halo, v, u],
-                flops=8 * modes * cells * days,
-            )
         summed = sum_all(partial_sums)
     return call(
         functools.partial(last_kernel, rows, reach, total),

time: 115 us -> 115 us (level)
    ppermute x37, waiting for transfers between devices: 23.2 us -> 28.9 us  [swap(): lax.ppermute(x, ('lat', 'lon'), pairing(lambda i: i ^ lat_bits, lambda j:...]
    ppermute x4, waiting for transfers between devices: 7.98 us -> 3.55 us  [lat_partners(): lax.ppermute(x, ('lat', 'lon'), pairing(lambda i: (i + 1 if i % 2 else i...]
where the time goes in v11:
time: 115 us; the launch traced here: 114 us
  starting transfers between devices  45.4 us (39%)
  waiting for transfers between devices  36.5 us (32%)
  Pallas kernels  30.8 us (27%)
    ppermute x37, starting transfers between devices, swap(): lax.ppermute(x, ('lat', 'lon'), pairing(lambda i: i ^ lat_bits, lambda j:...  31.2 us
    pallas_call x16, Pallas kernels, call(): pl.pallas_call(kernel, out_shape=[jax.ShapeDtypeStruct(s, t) for s, t in...  30.8 us
    ppermute x37, waiting for transfers between devices, swap(): lax.ppermute(x, ('lat', 'lon'), pairing(lambda i: i ^ lat_bits, lambda j:...  28.9 us
    ppermute x4, starting transfers between devices, lat_partners(): lax.ppermute(x, ('lat', 'lon'), pairing(lambda i: (i + 1 if i % 2 else i...  7.57 us
    ppermute x2, starting transfers between devices, lon_partners(): lax.ppermute(far, ('lat', 'lon'), pairing(same, lambda j: (j + 1 if j % 2...  3.61 us
    ppermute x4, waiting for transfers between devices, lat_partners(): lax.ppermute(x, ('lat', 'lon'), pairing(lambda i: (i + 1 if i % 2 else i...  3.55 us
    ppermute x4, waiting for transfers between devices, lat_partners(): got_a = lax.ppermute(x, ('lat', 'lon'), pairing(lambda i: i ^ 1, same))  3.34 us
    ppermute x4, starting transfers between devices, lat_partners(): got_a = lax.ppermute(x, ('lat', 'lon'), pairing(lambda i: i ^ 1, same))  3.01 us
  transfers between devices with their start and end apart: 47, of which 33 were waited for; matrix products, arithmetic and copies ran while one was open for 0% of the time, Pallas kernels for 15%

profile of v11, /device:TPU:0, one launch (start us, length us, event | category | flops | bytes accessed | tf_op | source)
XLA Modules:
  0.0 114.4 jit_solution(2316029709738141880)
XLA Ops:
  1.2 4.7 %collective-permute-start.2 = (f32[48,480]{1,0:T(8,128)}, f32[48,480]{1,0:T(8,128)S(1)}, u32[]{:S(2)}, u32[]{:S(2)}) collective-permute-start(f32[48,480]{1,0:T(8,128)} %refs_6_.1), channel_id=1, source_target_pairs={{0,7},{1,6},{2,5},{3,4},{4,3},{5,2},{6,1},{7,0},{8,15},{9,14},{10,... | collective-permute-start | bytes 276488 | tf_op jit(solution)/shard_map/ppermute | solution.py:32
  6.5 5.7 %own_flags.1 = (bf16[512,3840]{1,0:T(8,128)(2,1)S(1)}, bf16[512,3840]{1,0:T(8,128)(2,1)S(1)}, s32[512,256]{1,0:T(8,128)S(1)}, f32[48,512]{1,0:T(8,128)S(1)}, f32...) custom-call(s32[512,256]{1,0:T(8,128)} %bitcast.6, ...), custom_call_target="tpu_custom_call" | custom-call | flops 1006632960 | bytes 4648976 | tf_op jit(solution)/shard_map/own_flags/pallas_call | solution.py:530
  12.3 2.0 %collective-permute-done.1.refs_7_.refs_11_ = f32[48,480]{1,0:T(8,128)S(1)} collective-permute-done((f32[48,480]{1,0:T(8,128)}, f32[48,480]{1,0:T(8,128)S(1)}, u32[]{:S(2)}, u32[]{:S(2)}) %collective-permute-start.1) | collective-permute-done | bytes 92192 | tf_op jit(solution)/shard_map/ppermute | solution.py:32
  15.3 2.5 %collective-permute-start.10 = (f32[184,128]{1,0:T(8,128)S(1)}, f32[184,128]{1,0:T(8,128)S(1)}, u32[]{:S(2)}, u32[]{:S(2)}) collective-permute-start(f32[184,128]{1,0:T(8,128)S(1)} %get-tuple-element.76), channel_id=1, source_target_pairs={{0,7},{1,2},{2,1},{3,4},{4,3},{5,6},{6,5},{7,0},{8,15},{9,10},{10,... | collective-permute-start | bytes 282632 | tf_op jit(solution)/shard_map/ppermute | solution.py:67
  17.8 1.7 %given.1 = (f32[8,512]{1,0:T(8,128)S(1)}, f32[8,128]{1,0:T(8,128)S(1)}, f32[8,128]{1,0:T(8,128)S(1)}) custom-call(bf16[512,3840]{1,0:T(8,128)(2,1)S(1)} %get-tuple-element.69.refs_0_.refs_1_, s32[4]{0:T(128)S(1)} %pad_add_fusion.refs_5_.refs_1_.refs_2_.place_ref.refs_4_, f32[48,480]{1,0:T(8,128)S(1)} %copy-done, ...), custom_call_target="tpu_custom_call" | custom-call | flops 62914560 | bytes 4669456 | tf_op jit(solution)/shard_map/given/pallas_call | solution.py:530
  19.6 1.1 collective-permute-start.8
  21.4 3.5 %first_products.1 = (f32[2,640]{1,0:T(2,128)S(1)}, f32[8,128]{1,0:T(8,128)S(1)}, f32[48,3840]{1,0:T(8,128)S(1)}, bf16[3840,128]{1,0:T(8,128)(2,1)S(1)}, f32[48,6...) custom-call(f32[184,128]{1,0:T(8,128)S(1)} %collective-permute-done.9.refs_0_, ...), custom_call_target="tpu_custom_call" | custom-call | flops 943718400 | bytes 4958224 | tf_op jit(solution)/shard_map/first_products/pallas_call | solution.py:530
  25.5 2.5 %collective-permute-start.12 = (f32[16,256]{1,0:T(8,128)S(1)}, f32[16,256]{1,0:T(8,128)S(1)}, u32[]{:S(2)}, u32[]{:S(2)}) collective-permute-start(f32[16,256]{1,0:T(8,128)S(1)} %get-tuple-element.85.refs_7_), channel_id=1, source_target_pairs={{0,24},{1,25},{2,26},{3,27},{4,28},{5,29},{6,30},{7,31},{8,16},{9,... | collective-permute-start | bytes 49160 | tf_op jit(solution)/shard_map/ppermute | solution.py:60
  28.5 2.0 %days_flags.1.m_ref.refs_0_ = bf16[3840,512]{1,0:T(8,128)(2,1)S(1)} custom-call(s32[512,256]{1,0:T(8,128)S(1)} %get-tuple-element.86.held_ref, bf16[1920,256]{1,0:T(8,128)(2,1)S(1)} %get-tuple-element.87.spread_ref), custom_call_target="tpu_custom_call" | custom-call | flops 1006632960 | bytes 1507328 | tf_op jit(solution)/shard_map/days_flags/pallas_call | solution.py:530
  30.6 1.2 %collective-permute-done.11.refs_8_ = f32[16,256]{1,0:T(8,128)S(1)} collective-permute-done((f32[16,256]{1,0:T(8,128)S(1)}, f32[16,256]{1,0:T(8,128)S(1)}, u32[]{:S(2)}, u32[]{:S(2)}) %collective-permute-start.11) | collective-permute-done | bytes 16416 | tf_op jit(solution)/shard_map/ppermute | solution.py:59
  31.7 2.3 %sums_0.1 = (f32[2,4096]{1,0:T(2,128)S(1)}, f32[8,256]{1,0:T(8,128)S(1)}, f32[120,256]{1,0:T(8,128)S(1)}) custom-call(bf16[512,3840]{1,0:T(8,128)(2,1)S(1)} %get-tuple-element.77.refs_3_.refs_0_, bf16[512,3840]{1,0:T(8,128)(2,1)S(1)} %get-tuple-element.69.refs_0_.refs_1_, f32[48,3840]{1,0:T(8,128)S(1)} %get-tuple-element.90.v_ref.refs_2_, ...), custom_call_target="tpu_custom_call" | custom-call | flops 754974720 | bytes 8806416 | tf_op jit(solution)/shard_map/sums_0/pallas_call | solution.py:530
  34.1 1.2 %collective-permute-done.13 = f32[2,4096]{1,0:T(2,128)S(1)} collective-permute-done((f32[2,4096]{1,0:T(2,128)S(1)}, f32[2,4096]{1,0:T(2,128)S(1)}, u32[]{:S(2)}, u32[]{:S(2)}) %collective-permute-start.13) | collective-permute-done | bytes 32800 | tf_op jit(solution)/shard_map/ppermute | solution.py:32
  35.3 0.7 collective-permute-start.16
  36.0 1.0 collective-permute-start.15
  37.1 1.3 %collective-permute-start.14 = (f32[2,4096]{1,0:T(2,128)S(1)}, f32[2,4096]{1,0:T(2,128)S(1)}, u32[]{:S(2)}, u32[]{:S(2)}) collective-permute-start(f32[2,4096]{1,0:T(2,128)S(1)} %add.123), channel_id=1, source_target_pairs={{0,9},{1,8},{2,11},{3,10},{4,13},{5,12},{6,15},{7,14},{8,1},{9,0},... | collective-permute-start | bytes 98312 | tf_op jit(solution)/shard_map/ppermute | solution.py:32
  38.3 1.4 %collective-permute-done.16 = f32[2,4096]{1,0:T(2,128)S(1)} collective-permute-done((f32[2,4096]{1,0:T(2,128)S(1)}, f32[2,4096]{1,0:T(2,128)S(1)}, u32[]{:S(2)}, u32[]{:S(2)}) %collective-permute-start.16) | collective-permute-done | bytes 32800 | tf_op jit(solution)/shard_map/ppermute | solution.py:32
  40.5 2.4 %collective-permute-start.18 = (f32[2,4096]{1,0:T(2,128)S(1)}, f32[2,4096]{1,0:T(2,128)S(1)}, u32[]{:S(2)}, u32[]{:S(2)}) collective-permute-start(f32[2,4096]{1,0:T(2,128)S(1)} %add_add_fusion.7), channel_id=1, source_target_pairs={{0,7},{1,6},{2,5},{3,4},{4,3},{5,2},{6,1},{7,0},{8,15},{9,14},{10,... | collective-permute-start | bytes 98312 | tf_op jit(solution)/shard_map/ppermute | solution.py:32
  43.5 1.6 %next_products_1.1 = (f32[2,640]{1,0:T(2,128)S(1)}, f32[8,128]{1,0:T(8,128)S(1)}) custom-call(bf16[3840,512]{1,0:T(8,128)(2,1)S(1)} %days_flags.1.m_ref.refs_0_, bf16[3840,128]{1,0:T(8,128)(2,1)S(1)} %get-tuple-element.89.mh_ref.refs_1_, f32[48,3840]{1,0:T(8,128)S(1)} %get-tuple-element.90.v_ref.refs_2_, f32[48,640]{1,0:T(8,128)S(1)} %get-tuple-element.81.u_ref.refs_3_), custom_call_target="tpu_custom_call" | custom-call | flops 943718400 | bytes 5775360 | tf_op jit(solution)/shard_map/next_products_1/pallas_call | solution.py:530
  45.1 1.2 %collective-permute-done.19 = f32[2,4096]{1,0:T(2,128)S(1)} collective-permute-done((f32[2,4096]{1,0:T(2,128)S(1)}, f32[2,4096]{1,0:T(2,128)S(1)}, u32[]{:S(2)}, u32[]{:S(2)}) %collective-permute-start.19) | collective-permute-done | bytes 32800 | tf_op jit(solution)/shard_map/ppermute | solution.py:32
  46.3 0.7 collective-permute-done.17
  47.0 0.9 fields_1.1
  47.9 1.5 %collective-permute-start.21 = (f32[8,256]{1,0:T(8,128)S(1)}, f32[8,256]{1,0:T(8,128)S(1)}, u32[]{:S(2)}, u32[]{:S(2)}) collective-permute-start(f32[8,256]{1,0:T(8,128)S(1)} %get-tuple-element.102.refs_7_), channel_id=1, source_target_pairs={{0,24},{1,25},{2,26},{3,27},{4,28},{5,29},{6,30},{7,31},{8,16},{9,... | collective-permute-start | bytes 24584 | tf_op jit(solution)/shard_map/ppermute | solution.py:60
  49.4 1.0 collective-permute-start.20
  50.4 1.4 %next_products_2.1 = (f32[2,640]{1,0:T(2,128)S(1)}, f32[8,128]{1,0:T(8,128)S(1)}) custom-call(bf16[3840,512]{1,0:T(8,128)(2,1)S(1)} %days_flags.1.m_ref.refs_0_, bf16[3840,128]{1,0:T(8,128)(2,1)S(1)} %get-tuple-element.89.mh_ref.refs_1_, f32[48,3840]{1,0:T(8,128)S(1)} %get-tuple-element.100.v_ref.refs_2_, f32[48,640]{1,0:T(8,128)S(1)} %get-tuple-element.101.u_ref.refs_3_), custom_call_target="tpu_custom_call" | custom-call | flops 943718400 | bytes 5775360 | tf_op jit(solution)/shard_map/next_products_2/pallas_call | solution.py:530
  51.7 0.8 collective-permute-done.21.refs_9_
  53.0 2.3 %sums_1.1 = (f32[2,4096]{1,0:T(2,128)S(1)}, f32[8,256]{1,0:T(8,128)S(1)}) custom-call(bf16[512,3840]{1,0:T(8,128)(2,1)S(1)} %get-tuple-element.77.refs_3_.refs_0_, bf16[512,3840]{1,0:T(8,128)(2,1)S(1)} %get-tuple-element.69.refs_0_.refs_1_, f32[48,3840]{1,0:T(8,128)S(1)} %get-tuple-element.100.v_ref.refs_2_, f32[48,640]{1,0:T(8,128)S(1)} %get-tuple-element.101.u_ref.refs_3_, ...), custom_call_target="tpu_custom_call" | custom-call | flops 754974720 | bytes 8904720 | tf_op jit(solution)/shard_map/sums_1/pallas_call | solution.py:530
  55.4 1.2 %collective-permute-done.22 = f32[2,4096]{1,0:T(2,128)S(1)} collective-permute-done((f32[2,4096]{1,0:T(2,128)S(1)}, f32[2,4096]{1,0:T(2,128)S(1)}, u32[]{:S(2)}, u32[]{:S(2)}) %collective-permute-start.22) | collective-permute-done | bytes 32800 | tf_op jit(solution)/shard_map/ppermute | solution.py:32
  56.6 1.3 %collective-permute-start.25 = (f32[2,4096]{1,0:T(2,128)S(1)}, f32[2,4096]{1,0:T(2,128)S(1)}, u32[]{:S(2)}, u32[]{:S(2)}) collective-permute-start(f32[2,4096]{1,0:T(2,128)S(1)} %add.130), channel_id=1, source_target_pairs={{0,25},{1,24},{2,27},{3,26},{4,29},{5,28},{6,31},{7,30},{8,17},{9,... | collective-permute-start | bytes 98312 | tf_op jit(solution)/shard_map/ppermute | solution.py:32
  57.9 0.9 collective-permute-start.24
  58.8 0.8 collective-permute-start.23
  59.6 1.3 %collective-permute-done.25 = f32[2,4096]{1,0:T(2,128)S(1)} collective-permute-done((f32[2,4096]{1,0:T(2,128)S(1)}, f32[2,4096]{1,0:T(2,128)S(1)}, u32[]{:S(2)}, u32[]{:S(2)}) %collective-permute-start.25) | collective-permute-done | bytes 32800 | tf_op jit(solution)/shard_map/ppermute | solution.py:32
  60.9 0.9 collective-permute-done.24
  62.3 2.6 %collective-permute-start.27 = (f32[2,4096]{1,0:T(2,128)S(1)}, f32[2,4096]{1,0:T(2,128)S(1)}, u32[]{:S(2)}, u32[]{:S(2)}) collective-permute-start(f32[2,4096]{1,0:T(2,128)S(1)} %add_add_fusion.5), channel_id=1, source_target_pairs={{0,7},{1,6},{2,5},{3,4},{4,3},{5,2},{6,1},{7,0},{8,15},{9,14},{10,... | collective-permute-start | bytes 98312 | tf_op jit(solution)/shard_map/ppermute | solution.py:32
  65.2 2.9 %collective-permute-done.28 = f32[2,4096]{1,0:T(2,128)S(1)} collective-permute-done((f32[2,4096]{1,0:T(2,128)S(1)}, f32[2,4096]{1,0:T(2,128)S(1)}, u32[]{:S(2)}, u32[]{:S(2)}) %collective-permute-start.28) | collective-permute-done | bytes 32800 | tf_op jit(solution)/shard_map/ppermute | solution.py:32
  68.2 0.7 collective-permute-done.26
  68.9 0.9 fields_2.1
  69.8 2.1 %collective-permute-start.30 = (f32[8,256]{1,0:T(8,128)S(1)}, f32[8,256]{1,0:T(8,128)S(1)}, u32[]{:S(2)}, u32[]{:S(2)}) collective-permute-start(f32[8,256]{1,0:T(8,128)S(1)} %get-tuple-element.114.refs_7_), channel_id=1, source_target_pairs={{0,24},{1,25},{2,26},{3,27},{4,28},{5,29},{6,30},{7,31},{8,16},{9,... | collective-permute-start | bytes 24584 | tf_op jit(solution)/shard_map/ppermute | solution.py:60
  72.4 1.4 %next_products_3.1 = (f32[2,640]{1,0:T(2,128)S(1)}, f32[8,128]{1,0:T(8,128)S(1)}) custom-call(bf16[3840,512]{1,0:T(8,128)(2,1)S(1)} %days_flags.1.m_ref.refs_0_, bf16[3840,128]{1,0:T(8,128)(2,1)S(1)} %get-tuple-element.89.mh_ref.refs_1_, f32[48,3840]{1,0:T(8,128)S(1)} %get-tuple-element.112.v_ref.refs_2_, f32[48,640]{1,0:T(8,128)S(1)} %get-tuple-element.113.u_ref.refs_3_), custom_call_target="tpu_custom_call" | custom-call | flops 943718400 | bytes 5775360 | tf_op jit(solution)/shard_map/next_products_3/pallas_call | solution.py:530
  73.8 0.7 collective-permute-done.30.refs_9_
  74.4 1.1 collective-permute-done.29.refs_8_
  75.5 2.3 %sums_2.1 = (f32[2,4096]{1,0:T(2,128)S(1)}, f32[8,256]{1,0:T(8,128)S(1)}) custom-call(bf16[512,3840]{1,0:T(8,128)(2,1)S(1)} %get-tuple-element.77.refs_3_.refs_0_, bf16[512,3840]{1,0:T(8,128)(2,1)S(1)} %get-tuple-element.69.refs_0_.refs_1_, f32[48,3840]{1,0:T(8,128)S(1)} %get-tuple-element.112.v_ref.refs_2_, f32[48,640]{1,0:T(8,128)S(1)} %get-tuple-element.113.u_ref.refs_3_, ...), custom_call_target="tpu_custom_call" | custom-call | flops 754974720 | bytes 8904720 | tf_op jit(solution)/shard_map/sums_2/pallas_call | solution.py:530
  77.9 1.2 %collective-permute-done.31 = f32[2,4096]{1,0:T(2,128)S(1)} collective-permute-done((f32[2,4096]{1,0:T(2,128)S(1)}, f32[2,4096]{1,0:T(2,128)S(1)}, u32[]{:S(2)}, u32[]{:S(2)}) %collective-permute-start.31) | collective-permute-done | bytes 32800 | tf_op jit(solution)/shard_map/ppermute | solution.py:32
  79.1 0.7 collective-permute-start.34
  79.8 1.0 collective-permute-start.33
  80.8 1.3 %collective-permute-start.32 = (f32[2,4096]{1,0:T(2,128)S(1)}, f32[2,4096]{1,0:T(2,128)S(1)}, u32[]{:S(2)}, u32[]{:S(2)}) collective-permute-start(f32[2,4096]{1,0:T(2,128)S(1)} %add.137), channel_id=1, source_target_pairs={{0,9},{1,8},{2,11},{3,10},{4,13},{5,12},{6,15},{7,14},{8,1},{9,0},... | collective-permute-start | bytes 98312 | tf_op jit(solution)/shard_map/ppermute | solution.py:32
  82.1 1.4 %collective-permute-done.34 = f32[2,4096]{1,0:T(2,128)S(1)} collective-permute-done((f32[2,4096]{1,0:T(2,128)S(1)}, f32[2,4096]{1,0:T(2,128)S(1)}, u32[]{:S(2)}, u32[]{:S(2)}) %collective-permute-start.34) | collective-permute-done | bytes 32800 | tf_op jit(solution)/shard_map/ppermute | solution.py:32
  84.3 2.6 %collective-permute-start.36 = (f32[2,4096]{1,0:T(2,128)S(1)}, f32[2,4096]{1,0:T(2,128)S(1)}, u32[]{:S(2)}, u32[]{:S(2)}) collective-permute-start(f32[2,4096]{1,0:T(2,128)S(1)} %add_add_fusion.3), channel_id=1, source_target_pairs={{0,7},{1,6},{2,5},{3,4},{4,3},{5,2},{6,1},{7,0},{8,15},{9,14},{10,... | collective-permute-start | bytes 98312 | tf_op jit(solution)/shard_map/ppermute | solution.py:32
  87.3 3.0 %collective-permute-done.37 = f32[2,4096]{1,0:T(2,128)S(1)} collective-permute-done((f32[2,4096]{1,0:T(2,128)S(1)}, f32[2,4096]{1,0:T(2,128)S(1)}, u32[]{:S(2)}, u32[]{:S(2)}) %collective-permute-start.37) | collective-permute-done | bytes 32800 | tf_op jit(solution)/shard_map/ppermute | solution.py:32
  90.2 0.7 collective-permute-done.35
  90.9 0.9 fields_3.1
  91.8 1.5 %collective-permute-start.39 = (f32[8,256]{1,0:T(8,128)S(1)}, f32[8,256]{1,0:T(8,128)S(1)}, u32[]{:S(2)}, u32[]{:S(2)}) collective-permute-start(f32[8,256]{1,0:T(8,128)S(1)} %get-tuple-element.125.refs_7_), channel_id=1, source_target_pairs={{0,24},{1,25},{2,26},{3,27},{4,28},{5,29},{6,30},{7,31},{8,16},{9,... | collective-permute-start | bytes 24584 | tf_op jit(solution)/shard_map/ppermute | solution.py:60
  93.3 1.0 collective-permute-start.38
  94.3 2.1 %collective-permute-done.39.refs_9_ = f32[8,256]{1,0:T(8,128)S(1)} collective-permute-done((f32[8,256]{1,0:T(8,128)S(1)}, f32[8,256]{1,0:T(8,128)S(1)}, u32[]{:S(2)}, u32[]{:S(2)}) %collective-permute-start.39) | collective-permute-done | bytes 8224 | tf_op jit(solution)/shard_map/ppermute | solution.py:60
  96.9 2.3 %sums_3.1 = (f32[2,4096]{1,0:T(2,128)S(1)}, f32[8,256]{1,0:T(8,128)S(1)}) custom-call(bf16[512,3840]{1,0:T(8,128)(2,1)S(1)} %get-tuple-element.77.refs_3_.refs_0_, bf16[512,3840]{1,0:T(8,128)(2,1)S(1)} %get-tuple-element.69.refs_0_.refs_1_, f32[48,3840]{1,0:T(8,128)S(1)} %get-tuple-element.123.refs_2_.refs_0_, ...), custom_call_target="tpu_custom_call" | custom-call | flops 754974720 | bytes 8904720 | tf_op jit(solution)/shard_map/sums_3/pallas_call | solution.py:530
  99.3 1.2 %collective-permute-done.40 = f32[2,4096]{1,0:T(2,128)S(1)} collective-permute-done((f32[2,4096]{1,0:T(2,128)S(1)}, f32[2,4096]{1,0:T(2,128)S(1)}, u32[]{:S(2)}, u32[]{:S(2)}) %collective-permute-start.40) | collective-permute-done | bytes 32800 | tf_op jit(solution)/shard_map/ppermute | solution.py:32
  100.5 1.3 %collective-permute-start.43 = (f32[2,4096]{1,0:T(2,128)S(1)}, f32[2,4096]{1,0:T(2,128)S(1)}, u32[]{:S(2)}, u32[]{:S(2)}) collective-permute-start(f32[2,4096]{1,0:T(2,128)S(1)} %add.144), channel_id=1, source_target_pairs={{0,25},{1,24},{2,27},{3,26},{4,29},{5,28},{6,31},{7,30},{8,17},{9,... | collective-permute-start | bytes 98312 | tf_op jit(solution)/shard_map/ppermute | solution.py:32
  101.8 0.9 collective-permute-start.42
  102.7 0.8 collective-permute-start.41
  103.5 1.3 %collective-permute-done.43 = f32[2,4096]{1,0:T(2,128)S(1)} collective-permute-done((f32[2,4096]{1,0:T(2,128)S(1)}, f32[2,4096]{1,0:T(2,128)S(1)}, u32[]{:S(2)}, u32[]{:S(2)}) %collective-permute-start.43) | collective-permute-done | bytes 32800 | tf_op jit(solution)/shard_map/ppermute | solution.py:32
  104.8 0.9 collective-permute-done.42
  106.2 2.6 %collective-permute-start.45 = (f32[2,4096]{1,0:T(2,128)S(1)}, f32[2,4096]{1,0:T(2,128)S(1)}, u32[]{:S(2)}, u32[]{:S(2)}) collective-permute-start(f32[2,4096]{1,0:T(2,128)S(1)} %add_add_fusion.1), channel_id=1, source_target_pairs={{0,7},{1,6},{2,5},{3,4},{4,3},{5,2},{6,1},{7,0},{8,15},{9,14},{10,... | collective-permute-start | bytes 98312 | tf_op jit(solution)/shard_map/ppermute | solution.py:32
  109.1 3.0 %collective-permute-done.46 = f32[2,4096]{1,0:T(2,128)S(1)} collective-permute-done((f32[2,4096]{1,0:T(2,128)S(1)}, f32[2,4096]{1,0:T(2,128)S(1)}, u32[]{:S(2)}, u32[]{:S(2)}) %collective-permute-start.46) | collective-permute-done | bytes 32800 | tf_op jit(solution)/shard_map/ppermute | solution.py:32
  112.2 0.7 collective-permute-done.44
  112.9 1.3 %last.1 = (f32[48,4,128]{2,1,0:T(4,128)}, f32[48,480]{1,0:T(8,128)}) custom-call(f32[48,3840]{1,0:T(8,128)S(1)} %get-tuple-element.123.refs_2_.refs_0_, f32[48,640]{1,0:T(8,128)S(1)} %get-tuple-element.124.refs_3_.refs_1_, f32[2,4096]{1,0:T(2,128)S(1)} %add_add_fusion.refs_2_, ...), custom_call_target="tpu_custom_call", output_to_operand_aliasing={{0}: (5, {}), {1}: (6, {})} | custom-call | bytes 1091600 | tf_op jit(solution)/shard_map/last/pallas_call | solution.py:530
  (65 shorter events, 10.3 us)
Async XLA Ops:
  0.6 17.2 %copy-start = (f32[48,480]{1,0:T(8,128)S(1)}, f32[48,480]{1,0:T(8,128)}, u32[]{:S(2)}) copy-start(f32[48,480]{1,0:T(8,128)} %refs_6_.1) | copy-start | bytes 276484
  0.6 14.7 %collective-permute-start.3 = (f32[48,480]{1,0:T(8,128)}, f32[48,480]{1,0:T(8,128)S(1)}, u32[]{:S(2)}, u32[]{:S(2)}) collective-permute-start(f32[48,480]{1,0:T(8,128)} %refs_6_.1), channel_id=1, source_target_pairs={{0,1},{1,0},{2,3},{3,2},{4,5},{5,4},{6,7},{7,6},{8,9},{9,8},{10,11... | collective-permute-start | bytes 276488 | tf_op jit(solution)/shard_map/ppermute | solution.py:32
  1.2 11.1 %collective-permute-start.2 = (f32[48,480]{1,0:T(8,128)}, f32[48,480]{1,0:T(8,128)S(1)}, u32[]{:S(2)}, u32[]{:S(2)}) collective-permute-start(f32[48,480]{1,0:T(8,128)} %refs_6_.1), channel_id=1, source_target_pairs={{0,7},{1,6},{2,5},{3,4},{4,3},{5,2},{6,1},{7,0},{8,15},{9,14},{10,... | collective-permute-start | bytes 276488 | tf_op jit(solution)/shard_map/ppermute | solution.py:32
  5.9 8.4 %collective-permute-start.1 = (f32[48,480]{1,0:T(8,128)}, f32[48,480]{1,0:T(8,128)S(1)}, u32[]{:S(2)}, u32[]{:S(2)}) collective-permute-start(f32[48,480]{1,0:T(8,128)} %refs_6_.1), channel_id=1, source_target_pairs={{0,5},{1,4},{2,7},{3,6},{4,1},{5,0},{6,3},{7,2},{8,13},{9,12},{10,... | collective-permute-start | bytes 276488 | tf_op jit(solution)/shard_map/ppermute | solution.py:32
  5.9 8.4 %collective-permute-start = (f32[48,480]{1,0:T(8,128)}, f32[48,480]{1,0:T(8,128)S(1)}, u32[]{:S(2)}, u32[]{:S(2)}) collective-permute-start(f32[48,480]{1,0:T(8,128)} %refs_6_.1), channel_id=1, source_target_pairs={{0,3},{1,2},{2,1},{3,0},{4,7},{5,6},{6,5},{7,4},{8,11},{9,10},{10,... | collective-permute-start | bytes 276488 | tf_op jit(solution)/shard_map/ppermute | solution.py:32
  14.3 3.5 %collective-permute-start.4 = (f32[48,480]{1,0:T(8,128)S(1)}, f32[48,480]{1,0:T(8,128)S(1)}, u32[]{:S(2)}, u32[]{:S(2)}) collective-permute-start(f32[48,480]{1,0:T(8,128)S(1)} %collective-permute-done.refs_5_.refs_9_), channel_id=1, source_target_pairs={{0,1},{1,0},{2,3},{3,2},{4,5},{5,4},{6,7},{7,6},{8,9},{9,8},{10,11... | collective-permute-start | bytes 276488 | tf_op jit(solution)/shard_map/ppermute | solution.py:32
  14.7 3.1 %collective-permute-start.5 = (f32[48,480]{1,0:T(8,128)S(1)}, f32[48,480]{1,0:T(8,128)S(1)}, u32[]{:S(2)}, u32[]{:S(2)}) collective-permute-start(f32[48,480]{1,0:T(8,128)S(1)} %collective-permute-done.1.refs_7_.refs_11_), channel_id=1, source_target_pairs={{0,1},{1,0},{2,3},{3,2},{4,5},{5,4},{6,7},{7,6},{8,9},{9,8},{10,11... | collective-permute-start | bytes 276488 | tf_op jit(solution)/shard_map/ppermute | solution.py:32
  14.8 3.0 %collective-permute-start.6 = (f32[48,480]{1,0:T(8,128)S(1)}, f32[48,480]{1,0:T(8,128)S(1)}, u32[]{:S(2)}, u32[]{:S(2)}) collective-permute-start(f32[48,480]{1,0:T(8,128)S(1)} %collective-permute-done.2.refs_9_.refs_13_), channel_id=1, source_target_pairs={{0,1},{1,0},{2,3},{3,2},{4,5},{5,4},{6,7},{7,6},{8,9},{9,8},{10,11... | collective-permute-start | bytes 276488 | tf_op jit(solution)/shard_map/ppermute | solution.py:32
  15.2 5.5 %collective-permute-start.9 = (f32[184,128]{1,0:T(8,128)S(1)}, f32[184,128]{1,0:T(8,128)S(1)}, u32[]{:S(2)}, u32[]{:S(2)}) collective-permute-start(f32[184,128]{1,0:T(8,128)S(1)} %get-tuple-element.75), channel_id=1, source_target_pairs={{0,1},{1,0},{2,3},{3,2},{4,5},{5,4},{6,7},{7,6},{8,9},{9,8},{10,11... | collective-permute-start | bytes 282632 | tf_op jit(solution)/shard_map/ppermute | solution.py:32
  15.3 6.0 %collective-permute-start.10 = (f32[184,128]{1,0:T(8,128)S(1)}, f32[184,128]{1,0:T(8,128)S(1)}, u32[]{:S(2)}, u32[]{:S(2)}) collective-permute-start(f32[184,128]{1,0:T(8,128)S(1)} %get-tuple-element.76), channel_id=1, source_target_pairs={{0,7},{1,2},{2,1},{3,4},{4,3},{5,6},{6,5},{7,0},{8,15},{9,10},{10,... | collective-permute-start | bytes 282632 | tf_op jit(solution)/shard_map/ppermute | solution.py:67
  19.6 5.3 %collective-permute-start.7 = (f32[8,128]{1,0:T(8,128)S(1)}, f32[8,128]{1,0:T(8,128)S(1)}, u32[]{:S(2)}, u32[]{:S(2)}) collective-permute-start(f32[8,128]{1,0:T(8,128)S(1)} %get-tuple-element.73), channel_id=1, source_target_pairs={{0,1},{1,0},{2,3},{3,2},{4,5},{5,4},{6,7},{7,6},{8,9},{9,8},{10,11... | collective-permute-start | bytes 12296 | tf_op jit(solution)/shard_map/ppermute | solution.py:32
  19.6 5.3 %collective-permute-start.8 = (f32[8,128]{1,0:T(8,128)S(1)}, f32[8,128]{1,0:T(8,128)S(1)}, u32[]{:S(2)}, u32[]{:S(2)}) collective-permute-start(f32[8,128]{1,0:T(8,128)S(1)} %get-tuple-element.74), channel_id=1, source_target_pairs={{0,7},{1,2},{2,1},{3,4},{4,3},{5,6},{6,5},{7,0},{8,15},{9,10},{10,... | collective-permute-start | bytes 12296 | tf_op jit(solution)/shard_map/ppermute | solution.py:67
  25.5 5.1 %collective-permute-start.12 = (f32[16,256]{1,0:T(8,128)S(1)}, f32[16,256]{1,0:T(8,128)S(1)}, u32[]{:S(2)}, u32[]{:S(2)}) collective-permute-start(f32[16,256]{1,0:T(8,128)S(1)} %get-tuple-element.85.refs_7_), channel_id=1, source_target_pairs={{0,24},{1,25},{2,26},{3,27},{4,28},{5,29},{6,30},{7,31},{8,16},{9,... | collective-permute-start | bytes 49160 | tf_op jit(solution)/shard_map/ppermute | solution.py:60
  28.0 3.7 %collective-permute-start.11 = (f32[16,256]{1,0:T(8,128)S(1)}, f32[16,256]{1,0:T(8,128)S(1)}, u32[]{:S(2)}, u32[]{:S(2)}) collective-permute-start(f32[16,256]{1,0:T(8,128)S(1)} %get-tuple-element.85.refs_7_), channel_id=1, source_target_pairs={{0,8},{1,9},{2,10},{3,11},{4,12},{5,13},{6,14},{7,15},{8,0},{9,1},... | collective-permute-start | bytes 49160 | tf_op jit(solution)/shard_map/ppermute | solution.py:59
  34.0 1.3 %collective-permute-start.13 = (f32[2,4096]{1,0:T(2,128)S(1)}, f32[2,4096]{1,0:T(2,128)S(1)}, u32[]{:S(2)}, u32[]{:S(2)}) collective-permute-start(f32[2,4096]{1,0:T(2,128)S(1)} %get-tuple-element.98), channel_id=1, source_target_pairs={{0,1},{1,0},{2,3},{3,2},{4,5},{5,4},{6,7},{7,6},{8,9},{9,8},{10,11... | collective-permute-start | bytes 98312 | tf_op jit(solution)/shard_map/ppermute | solution.py:32
  35.3 4.4 %collective-permute-start.16 = (f32[2,4096]{1,0:T(2,128)S(1)}, f32[2,4096]{1,0:T(2,128)S(1)}, u32[]{:S(2)}, u32[]{:S(2)}) collective-permute-start(f32[2,4096]{1,0:T(2,128)S(1)} %add.123), channel_id=1, source_target_pairs={{0,25},{1,24},{2,27},{3,26},{4,29},{5,28},{6,31},{7,30},{8,17},{9,... | collective-permute-start | bytes 98312 | tf_op jit(solution)/shard_map/ppermute | solution.py:32
  36.0 4.1 %collective-permute-start.15 = (f32[2,4096]{1,0:T(2,128)S(1)}, f32[2,4096]{1,0:T(2,128)S(1)}, u32[]{:S(2)}, u32[]{:S(2)}) collective-permute-start(f32[2,4096]{1,0:T(2,128)S(1)} %add.123), channel_id=1, source_target_pairs={{0,17},{1,16},{2,19},{3,18},{4,21},{5,20},{6,23},{7,22},{8,25},{9,... | collective-permute-start | bytes 98312 | tf_op jit(solution)/shard_map/ppermute | solution.py:32
  37.1 3.3 %collective-permute-start.14 = (f32[2,4096]{1,0:T(2,128)S(1)}, f32[2,4096]{1,0:T(2,128)S(1)}, u32[]{:S(2)}, u32[]{:S(2)}) collective-permute-start(f32[2,4096]{1,0:T(2,128)S(1)} %add.123), channel_id=1, source_target_pairs={{0,9},{1,8},{2,11},{3,10},{4,13},{5,12},{6,15},{7,14},{8,1},{9,0},... | collective-permute-start | bytes 98312 | tf_op jit(solution)/shard_map/ppermute | solution.py:32
  40.5 5.9 %collective-permute-start.19 = (f32[2,4096]{1,0:T(2,128)S(1)}, f32[2,4096]{1,0:T(2,128)S(1)}, u32[]{:S(2)}, u32[]{:S(2)}) collective-permute-start(f32[2,4096]{1,0:T(2,128)S(1)} %add_add_fusion.7), channel_id=1, source_target_pairs={{0,5},{1,4},{2,7},{3,6},{4,1},{5,0},{6,3},{7,2},{8,13},{9,12},{10,... | collective-permute-start | bytes 98312 | tf_op jit(solution)/shard_map/ppermute | solution.py:32
  40.5 5.8 %collective-permute-start.18 = (f32[2,4096]{1,0:T(2,128)S(1)}, f32[2,4096]{1,0:T(2,128)S(1)}, u32[]{:S(2)}, u32[]{:S(2)}) collective-permute-start(f32[2,4096]{1,0:T(2,128)S(1)} %add_add_fusion.7), channel_id=1, source_target_pairs={{0,7},{1,6},{2,5},{3,4},{4,3},{5,2},{6,1},{7,0},{8,15},{9,14},{10,... | collective-permute-start | bytes 98312 | tf_op jit(solution)/shard_map/ppermute | solution.py:32
  43.0 4.0 %collective-permute-start.17 = (f32[2,4096]{1,0:T(2,128)S(1)}, f32[2,4096]{1,0:T(2,128)S(1)}, u32[]{:S(2)}, u32[]{:S(2)}) collective-permute-start(f32[2,4096]{1,0:T(2,128)S(1)} %add_add_fusion.7), channel_id=1, source_target_pairs={{0,3},{1,2},{2,1},{3,0},{4,7},{5,6},{6,5},{7,4},{8,11},{9,10},{10,... | collective-permute-start | bytes 98312 | tf_op jit(solution)/shard_map/ppermute | solution.py:32
  47.9 4.6 %collective-permute-start.21 = (f32[8,256]{1,0:T(8,128)S(1)}, f32[8,256]{1,0:T(8,128)S(1)}, u32[]{:S(2)}, u32[]{:S(2)}) collective-permute-start(f32[8,256]{1,0:T(8,128)S(1)} %get-tuple-element.102.refs_7_), channel_id=1, source_target_pairs={{0,24},{1,25},{2,26},{3,27},{4,28},{5,29},{6,30},{7,31},{8,16},{9,... | collective-permute-start | bytes 24584 | tf_op jit(solution)/shard_map/ppermute | solution.py:60
  49.4 3.7 %collective-permute-start.20 = (f32[8,256]{1,0:T(8,128)S(1)}, f32[8,256]{1,0:T(8,128)S(1)}, u32[]{:S(2)}, u32[]{:S(2)}) collective-permute-start(f32[8,256]{1,0:T(8,128)S(1)} %get-tuple-element.102.refs_7_), channel_id=1, source_target_pairs={{0,8},{1,9},{2,10},{3,11},{4,12},{5,13},{6,14},{7,15},{8,0},{9,1},... | collective-permute-start | bytes 24584 | tf_op jit(solution)/shard_map/ppermute | solution.py:59
  55.3 1.3 %collective-permute-start.22 = (f32[2,4096]{1,0:T(2,128)S(1)}, f32[2,4096]{1,0:T(2,128)S(1)}, u32[]{:S(2)}, u32[]{:S(2)}) collective-permute-start(f32[2,4096]{1,0:T(2,128)S(1)} %get-tuple-element.110), channel_id=1, source_target_pairs={{0,1},{1,0},{2,3},{3,2},{4,5},{5,4},{6,7},{7,6},{8,9},{9,8},{10,11... | collective-permute-start | bytes 98312 | tf_op jit(solution)/shard_map/ppermute | solution.py:32
  56.6 4.3 %collective-permute-start.25 = (f32[2,4096]{1,0:T(2,128)S(1)}, f32[2,4096]{1,0:T(2,128)S(1)}, u32[]{:S(2)}, u32[]{:S(2)}) collective-permute-start(f32[2,4096]{1,0:T(2,128)S(1)} %add.130), channel_id=1, source_target_pairs={{0,25},{1,24},{2,27},{3,26},{4,29},{5,28},{6,31},{7,30},{8,17},{9,... | collective-permute-start | bytes 98312 | tf_op jit(solution)/shard_map/ppermute | solution.py:32
  57.9 3.8 %collective-permute-start.24 = (f32[2,4096]{1,0:T(2,128)S(1)}, f32[2,4096]{1,0:T(2,128)S(1)}, u32[]{:S(2)}, u32[]{:S(2)}) collective-permute-start(f32[2,4096]{1,0:T(2,128)S(1)} %add.130), channel_id=1, source_target_pairs={{0,17},{1,16},{2,19},{3,18},{4,21},{5,20},{6,23},{7,22},{8,25},{9,... | collective-permute-start | bytes 98312 | tf_op jit(solution)/shard_map/ppermute | solution.py:32
  58.8 3.3 %collective-permute-start.23 = (f32[2,4096]{1,0:T(2,128)S(1)}, f32[2,4096]{1,0:T(2,128)S(1)}, u32[]{:S(2)}, u32[]{:S(2)}) collective-permute-start(f32[2,4096]{1,0:T(2,128)S(1)} %add.130), channel_id=1, source_target_pairs={{0,9},{1,8},{2,11},{3,10},{4,13},{5,12},{6,15},{7,14},{8,1},{9,0},... | collective-permute-start | bytes 98312 | tf_op jit(solution)/shard_map/ppermute | solution.py:32
  62.2 6.0 %collective-permute-start.28 = (f32[2,4096]{1,0:T(2,128)S(1)}, f32[2,4096]{1,0:T(2,128)S(1)}, u32[]{:S(2)}, u32[]{:S(2)}) collective-permute-start(f32[2,4096]{1,0:T(2,128)S(1)} %add_add_fusion.5), channel_id=1, source_target_pairs={{0,5},{1,4},{2,7},{3,6},{4,1},{5,0},{6,3},{7,2},{8,13},{9,12},{10,... | collective-permute-start | bytes 98312 | tf_op jit(solution)/shard_map/ppermute | solution.py:32
  62.3 5.9 %collective-permute-start.27 = (f32[2,4096]{1,0:T(2,128)S(1)}, f32[2,4096]{1,0:T(2,128)S(1)}, u32[]{:S(2)}, u32[]{:S(2)}) collective-permute-start(f32[2,4096]{1,0:T(2,128)S(1)} %add_add_fusion.5), channel_id=1, source_target_pairs={{0,7},{1,6},{2,5},{3,4},{4,3},{5,2},{6,1},{7,0},{8,15},{9,14},{10,... | collective-permute-start | bytes 98312 | tf_op jit(solution)/shard_map/ppermute | solution.py:32
  64.9 4.0 %collective-permute-start.26 = (f32[2,4096]{1,0:T(2,128)S(1)}, f32[2,4096]{1,0:T(2,128)S(1)}, u32[]{:S(2)}, u32[]{:S(2)}) collective-permute-start(f32[2,4096]{1,0:T(2,128)S(1)} %add_add_fusion.5), channel_id=1, source_target_pairs={{0,3},{1,2},{2,1},{3,0},{4,7},{5,6},{6,5},{7,4},{8,11},{9,10},{10,... | collective-permute-start | bytes 98312 | tf_op jit(solution)/shard_map/ppermute | solution.py:32
  69.8 4.6 %collective-permute-start.30 = (f32[8,256]{1,0:T(8,128)S(1)}, f32[8,256]{1,0:T(8,128)S(1)}, u32[]{:S(2)}, u32[]{:S(2)}) collective-permute-start(f32[8,256]{1,0:T(8,128)S(1)} %get-tuple-element.114.refs_7_), channel_id=1, source_target_pairs={{0,24},{1,25},{2,26},{3,27},{4,28},{5,29},{6,30},{7,31},{8,16},{9,... | collective-permute-start | bytes 24584 | tf_op jit(solution)/shard_map/ppermute | solution.py:60
  71.9 3.7 %collective-permute-start.29 = (f32[8,256]{1,0:T(8,128)S(1)}, f32[8,256]{1,0:T(8,128)S(1)}, u32[]{:S(2)}, u32[]{:S(2)}) collective-permute-start(f32[8,256]{1,0:T(8,128)S(1)} %get-tuple-element.114.refs_7_), channel_id=1, source_target_pairs={{0,8},{1,9},{2,10},{3,11},{4,12},{5,13},{6,14},{7,15},{8,0},{9,1},... | collective-permute-start | bytes 24584 | tf_op jit(solution)/shard_map/ppermute | solution.py:59
  77.8 1.3 %collective-permute-start.31 = (f32[2,4096]{1,0:T(2,128)S(1)}, f32[2,4096]{1,0:T(2,128)S(1)}, u32[]{:S(2)}, u32[]{:S(2)}) collective-permute-start(f32[2,4096]{1,0:T(2,128)S(1)} %get-tuple-element.121), channel_id=1, source_target_pairs={{0,1},{1,0},{2,3},{3,2},{4,5},{5,4},{6,7},{7,6},{8,9},{9,8},{10,11... | collective-permute-start | bytes 98312 | tf_op jit(solution)/shard_map/ppermute | solution.py:32
  79.1 4.4 %collective-permute-start.34 = (f32[2,4096]{1,0:T(2,128)S(1)}, f32[2,4096]{1,0:T(2,128)S(1)}, u32[]{:S(2)}, u32[]{:S(2)}) collective-permute-start(f32[2,4096]{1,0:T(2,128)S(1)} %add.137), channel_id=1, source_target_pairs={{0,25},{1,24},{2,27},{3,26},{4,29},{5,28},{6,31},{7,30},{8,17},{9,... | collective-permute-start | bytes 98312 | tf_op jit(solution)/shard_map/ppermute | solution.py:32
  79.8 4.1 %collective-permute-start.33 = (f32[2,4096]{1,0:T(2,128)S(1)}, f32[2,4096]{1,0:T(2,128)S(1)}, u32[]{:S(2)}, u32[]{:S(2)}) collective-permute-start(f32[2,4096]{1,0:T(2,128)S(1)} %add.137), channel_id=1, source_target_pairs={{0,17},{1,16},{2,19},{3,18},{4,21},{5,20},{6,23},{7,22},{8,25},{9,... | collective-permute-start | bytes 98312 | tf_op jit(solution)/shard_map/ppermute | solution.py:32
  80.8 3.3 %collective-permute-start.32 = (f32[2,4096]{1,0:T(2,128)S(1)}, f32[2,4096]{1,0:T(2,128)S(1)}, u32[]{:S(2)}, u32[]{:S(2)}) collective-permute-start(f32[2,4096]{1,0:T(2,128)S(1)} %add.137), channel_id=1, source_target_pairs={{0,9},{1,8},{2,11},{3,10},{4,13},{5,12},{6,15},{7,14},{8,1},{9,0},... | collective-permute-start | bytes 98312 | tf_op jit(solution)/shard_map/ppermute | solution.py:32
  84.2 6.0 %collective-permute-start.37 = (f32[2,4096]{1,0:T(2,128)S(1)}, f32[2,4096]{1,0:T(2,128)S(1)}, u32[]{:S(2)}, u32[]{:S(2)}) collective-permute-start(f32[2,4096]{1,0:T(2,128)S(1)} %add_add_fusion.3), channel_id=1, source_target_pairs={{0,5},{1,4},{2,7},{3,6},{4,1},{5,0},{6,3},{7,2},{8,13},{9,12},{10,... | collective-permute-start | bytes 98312 | tf_op jit(solution)/shard_map/ppermute | solution.py:32
  84.3 5.9 %collective-permute-start.36 = (f32[2,4096]{1,0:T(2,128)S(1)}, f32[2,4096]{1,0:T(2,128)S(1)}, u32[]{:S(2)}, u32[]{:S(2)}) collective-permute-start(f32[2,4096]{1,0:T(2,128)S(1)} %add_add_fusion.3), channel_id=1, source_target_pairs={{0,7},{1,6},{2,5},{3,4},{4,3},{5,2},{6,1},{7,0},{8,15},{9,14},{10,... | collective-permute-start | bytes 98312 | tf_op jit(solution)/shard_map/ppermute | solution.py:32
  86.9 4.0 %collective-permute-start.35 = (f32[2,4096]{1,0:T(2,128)S(1)}, f32[2,4096]{1,0:T(2,128)S(1)}, u32[]{:S(2)}, u32[]{:S(2)}) collective-permute-start(f32[2,4096]{1,0:T(2,128)S(1)} %add_add_fusion.3), channel_id=1, source_target_pairs={{0,3},{1,2},{2,1},{3,0},{4,7},{5,6},{6,5},{7,4},{8,11},{9,10},{10,... | collective-permute-start | bytes 98312 | tf_op jit(solution)/shard_map/ppermute | solution.py:32
  91.8 4.6 %collective-permute-start.39 = (f32[8,256]{1,0:T(8,128)S(1)}, f32[8,256]{1,0:T(8,128)S(1)}, u32[]{:S(2)}, u32[]{:S(2)}) collective-permute-start(f32[8,256]{1,0:T(8,128)S(1)} %get-tuple-element.125.refs_7_), channel_id=1, source_target_pairs={{0,24},{1,25},{2,26},{3,27},{4,28},{5,29},{6,30},{7,31},{8,16},{9,... | collective-permute-start | bytes 24584 | tf_op jit(solution)/shard_map/ppermute | solution.py:60
  93.3 3.7 %collective-permute-start.38 = (f32[8,256]{1,0:T(8,128)S(1)}, f32[8,256]{1,0:T(8,128)S(1)}, u32[]{:S(2)}, u32[]{:S(2)}) collective-permute-start(f32[8,256]{1,0:T(8,128)S(1)} %get-tuple-element.125.refs_7_), channel_id=1, source_target_pairs={{0,8},{1,9},{2,10},{3,11},{4,12},{5,13},{6,14},{7,15},{8,0},{9,1},... | collective-permute-start | bytes 24584 | tf_op jit(solution)/shard_map/ppermute | solution.py:59
  99.2 1.3 %collective-permute-start.40 = (f32[2,4096]{1,0:T(2,128)S(1)}, f32[2,4096]{1,0:T(2,128)S(1)}, u32[]{:S(2)}, u32[]{:S(2)}) collective-permute-start(f32[2,4096]{1,0:T(2,128)S(1)} %get-tuple-element.126), channel_id=1, source_target_pairs={{0,1},{1,0},{2,3},{3,2},{4,5},{5,4},{6,7},{7,6},{8,9},{9,8},{10,11... | collective-permute-start | bytes 98312 | tf_op jit(solution)/shard_map/ppermute | solution.py:32
  100.5 4.3 %collective-permute-start.43 = (f32[2,4096]{1,0:T(2,128)S(1)}, f32[2,4096]{1,0:T(2,128)S(1)}, u32[]{:S(2)}, u32[]{:S(2)}) collective-permute-start(f32[2,4096]{1,0:T(2,128)S(1)} %add.144), channel_id=1, source_target_pairs={{0,25},{1,24},{2,27},{3,26},{4,29},{5,28},{6,31},{7,30},{8,17},{9,... | collective-permute-start | bytes 98312 | tf_op jit(solution)/shard_map/ppermute | solution.py:32
  101.8 3.8 %collective-permute-start.42 = (f32[2,4096]{1,0:T(2,128)S(1)}, f32[2,4096]{1,0:T(2,128)S(1)}, u32[]{:S(2)}, u32[]{:S(2)}) collective-permute-start(f32[2,4096]{1,0:T(2,128)S(1)} %add.144), channel_id=1, source_target_pairs={{0,17},{1,16},{2,19},{3,18},{4,21},{5,20},{6,23},{7,22},{8,25},{9,... | collective-permute-start | bytes 98312 | tf_op jit(solution)/shard_map/ppermute | solution.py:32
  102.7 3.3 %collective-permute-start.41 = (f32[2,4096]{1,0:T(2,128)S(1)}, f32[2,4096]{1,0:T(2,128)S(1)}, u32[]{:S(2)}, u32[]{:S(2)}) collective-permute-start(f32[2,4096]{1,0:T(2,128)S(1)} %add.144), channel_id=1, source_target_pairs={{0,9},{1,8},{2,11},{3,10},{4,13},{5,12},{6,15},{7,14},{8,1},{9,0},... | collective-permute-start | bytes 98312 | tf_op jit(solution)/shard_map/ppermute | solution.py:32
  106.1 6.1 %collective-permute-start.46 = (f32[2,4096]{1,0:T(2,128)S(1)}, f32[2,4096]{1,0:T(2,128)S(1)}, u32[]{:S(2)}, u32[]{:S(2)}) collective-permute-start(f32[2,4096]{1,0:T(2,128)S(1)} %add_add_fusion.1), channel_id=1, source_target_pairs={{0,5},{1,4},{2,7},{3,6},{4,1},{5,0},{6,3},{7,2},{8,13},{9,12},{10,... | collective-permute-start | bytes 98312 | tf_op jit(solution)/shard_map/ppermute | solution.py:32
  106.2 6.0 %collective-permute-start.45 = (f32[2,4096]{1,0:T(2,128)S(1)}, f32[2,4096]{1,0:T(2,128)S(1)}, u32[]{:S(2)}, u32[]{:S(2)}) collective-permute-start(f32[2,4096]{1,0:T(2,128)S(1)} %add_add_fusion.1), channel_id=1, source_target_pairs={{0,7},{1,6},{2,5},{3,4},{4,3},{5,2},{6,1},{7,0},{8,15},{9,14},{10,... | collective-permute-start | bytes 98312 | tf_op jit(solution)/shard_map/ppermute | solution.py:32
  108.8 4.0 %collective-permute-start.44 = (f32[2,4096]{1,0:T(2,128)S(1)}, f32[2,4096]{1,0:T(2,128)S(1)}, u32[]{:S(2)}, u32[]{:S(2)}) collective-permute-start(f32[2,4096]{1,0:T(2,128)S(1)} %add_add_fusion.1), channel_id=1, source_target_pairs={{0,3},{1,2},{2,1},{3,0},{4,7},{5,6},{6,5},{7,4},{8,11},{9,10},{10,... | collective-permute-start | bytes 98312 | tf_op jit(solution)/shard_map/ppermute | solution.py:32
